TPU v7x, 32 devices: a whole 2x2x4 slice. The times are simulated.
32 devices in a mesh: gx: 8 (over z, y), gy: 4 (over x, core).
Axes of the slice: x: 2, y: 2, z: 4, core: 2. Of those that a mesh axis runs over, the one named last changes fastest.
Arguments:
- layer_input: bfloat16 [8192, 2560], P('gx'), may hold values from -6 to 6
- norm_gain: float32 [2560], replicated, may hold values from 0.5 to 1.5
- gate_weight: bfloat16 [2560, 5120], P('gx', 'gy'), may hold values from -0.125 to 0.125
- value_weight: bfloat16 [2560, 5120], P('gx', 'gy'), may hold values from -0.125 to 0.125
- state_weight: bfloat16 [2560, 256], P('gx'), may hold values from -0.125 to 0.125
- step_weight: bfloat16 [2560, 80], P('gx', 'gy'), may hold values from -0.125 to 0.125
- conv_value: float32 [4, 5120], P(None, 'gy'), may hold values from -3 to 3
- conv_value_bias: float32 [5120], P('gy'), may hold values from -1.5 to 1.5
- conv_state: float32 [4, 256], replicated, may hold values from -3 to 3
- conv_state_bias: float32 [256], replicated, may hold values from -1.5 to 1.5
- step_bias: float32 [80], P('gy'), may hold values from -6.5 to -2
- decay_log: float32 [80], P('gy'), may hold values from 0 to 2.7
- skip_scale: float32 [80], P('gy'), may hold values from 0.5 to 1.5
- gated_gain: float32 [5120], P('gy'), may hold values from 0.5 to 1.5
- out_weight: bfloat16 [5120, 2560], P('gy', 'gx'), may hold values from -0.125 to 0.125
- segment_ids: int32 [8192], P('gx'), may hold values from 0 to 20, as said below
- cotangent: bfloat16 [8192, 2560], P('gx', 'gy'), may hold values from -6 to 6
Outputs:
- layer_output: bfloat16 [8192, 2560], P('gx', 'gy')
- grad_input: float32 [8192, 2560], P('gx', 'gy')
- grad_norm_gain: float32 [2560], P('gy')
- grad_gate_weight: float32 [2560, 5120], P('gx', 'gy')
- grad_value_weight: float32 [2560, 5120], P('gx', 'gy')
- grad_state_weight: float32 [2560, 256], P('gx')
- grad_step_weight: float32 [2560, 80], P('gx', 'gy')
- grad_conv_value: float32 [4, 5120], P(None, 'gy')
- grad_conv_value_bias: float32 [5120], P('gy')
- grad_conv_state: float32 [4, 256], replicated
- grad_conv_state_bias: float32 [256], replicated
- grad_step_bias: float32 [80], P('gy')
- grad_decay_log: float32 [80], P('gy')
- grad_skip_scale: float32 [80], P('gy')
- grad_gated_gain: float32 [5120], P('gy')
- grad_out_weight: float32 [5120, 2560], P('gy', 'gx')
Inputs may be any that keep to these rules, and one draw needn't show every extreme that they name: `segment_ids`: within each packed row of 1024 tokens the ids count documents from 0 upward and never fall; every document holds 51 to 512 tokens, except that the last one of a row may be shorter.
All inputs are finite; a program needn't handle non-finite values.
Results may differ from a plain program's by a relative error of at most 0.011.
Values may be sent and summed in bfloat16 or wider, within the bound.
No kernel may reach another device: no remote copies, remote signals or barrier semaphores. Data moves between devices by JAX's collectives and lax.ppermute only.
A program may use at most 256 MiB of HBM per device.

v0:
```python
import jax
import jax.numpy as jnp
from jax import lax
from jax.sharding import PartitionSpec as P

GROUP = 256
INNER = 5120


epsilon = 1e-05
highest = lax.Precision.HIGHEST


def causal_conv(values, kernel, offset_bias, segments):
    seq_len = values.shape[0]
    total = offset_bias + kernel[0] * values
    for offset in range(1, kernel.shape[0]):
        moved = jnp.concatenate(
            [jnp.zeros((offset, values.shape[1]), values.dtype), values[: seq_len - offset]], 0
        )
        moved_seg = jnp.concatenate(
            [jnp.full((offset,), -1, jnp.int32), segments[: seq_len - offset]], 0
        )
        same_doc = (moved_seg == segments).astype(values.dtype)
        total = total + kernel[offset] * moved * same_doc[:, None]
    return total


def group_step(running, inputs):
    memory, previous = running
    x_block, b_block, c_block, decay_rate, step_size, seg_block = inputs
    block_len = seg_block.shape[0]
    cumulative = jnp.cumsum(decay_rate, axis=0)
    row_index = lax.broadcasted_iota(jnp.int32, (block_len, block_len), 0)
    col_index = lax.broadcasted_iota(jnp.int32, (block_len, block_len), 1)
    visible = (row_index >= col_index) & (seg_block[:, None] == seg_block[None, :])
    log_decay = cumulative.T[:, :, None] - cumulative.T[:, None, :]
    decay_mask = jnp.where(visible[None], jnp.exp(jnp.where(visible[None], log_decay, 0.0)), 0.0)
    intersection = jnp.dot(c_block, b_block.T, precision=highest)
    mixing = decay_mask * intersection[None] * step_size.T[:, None, :]
    within = jnp.einsum("hts,shp->thp", mixing, x_block, precision=highest)
    carried = (seg_block == previous).astype(memory.dtype)
    from_state = jnp.einsum("tn,hpn->thp", c_block, memory, precision=highest)
    from_state = from_state * (jnp.exp(cumulative) * carried[:, None])[:, :, None]
    last_seg = seg_block[block_len - 1]
    tail_weight = (
        (seg_block == last_seg).astype(memory.dtype)[:, None]
        * jnp.exp(cumulative[block_len - 1][None, :] - cumulative)
        * step_size
    )
    fresh_state = jnp.einsum("sh,shp,sn->hpn", tail_weight, x_block, b_block, precision=highest)
    survives = (last_seg == previous).astype(memory.dtype)
    memory = survives * jnp.exp(cumulative[block_len - 1])[:, None, None] * memory + fresh_state
    return ((memory, last_seg), within + from_state)


def ssm_mixer(
    projected,
    conv_value,
    conv_value_bias,
    conv_state,
    conv_state_bias,
    step_bias,
    decay_log,
    skip_scale,
    segments,
):
    inner_width = conv_value.shape[1]
    head_count = step_bias.shape[0]
    head_dim = inner_width // head_count
    states = conv_state.shape[1] // 2
    seq_len = projected.shape[0]
    blocks = seq_len // GROUP
    gate_in = projected[:, :inner_width]
    value_in = projected[:, inner_width : 2 * inner_width]
    state_in = projected[:, 2 * inner_width : 2 * inner_width + 2 * states]
    step_in = projected[:, 2 * inner_width + 2 * states :]
    values = jax.nn.silu(causal_conv(value_in, conv_value, conv_value_bias, segments))
    state_act = jax.nn.silu(causal_conv(state_in, conv_state, conv_state_bias, segments))
    step_size = jax.nn.softplus(step_in + step_bias)
    decay_rate = -jnp.exp(decay_log) * step_size
    inputs = (
        values.reshape(blocks, GROUP, head_count, head_dim),
        state_act[:, :states].reshape(blocks, GROUP, states),
        state_act[:, states:].reshape(blocks, GROUP, states),
        decay_rate.reshape(blocks, GROUP, head_count),
        step_size.reshape(blocks, GROUP, head_count),
        segments.reshape(blocks, GROUP),
    )
    initial = (jnp.zeros((head_count, head_dim, states), projected.dtype), jnp.array(-1, jnp.int32))
    finished, outputs = lax.scan(jax.checkpoint(group_step), initial, inputs)
    combined = outputs.reshape(seq_len, head_count, head_dim) + skip_scale[
        None, :, None
    ] * values.reshape(seq_len, head_count, head_dim)
    return combined.reshape(seq_len, inner_width) * jax.nn.silu(gate_in)


def contract_rows(left, right):
    return lax.dot_general(
        left, right, (((0,), (0,)), ((), ())), preferred_element_type=jnp.float32
    )


def contract_cols(left, right):
    return lax.dot_general(
        left, right, (((1,), (1,)), ((), ())), preferred_element_type=jnp.float32
    )


def on_device(
    layer_input,
    norm_gain,
    gate_weight,
    value_weight,
    state_weight,
    step_weight,
    conv_value,
    conv_value_bias,
    conv_state,
    conv_state_bias,
    step_bias,
    decay_log,
    skip_scale,
    gated_gain,
    out_weight,
    segment_ids,
    cotangent,
):
    model_width = layer_input.shape[1]
    col_width = cotangent.shape[1]
    inner_local = gate_weight.shape[1]
    state_cols = state_weight.shape[1]
    proj_width = 2 * inner_local + state_cols + step_weight.shape[1]
    col_start = lax.axis_index("gy") * col_width
    tokens = layer_input.astype(jnp.float32)
    scale_in = lax.rsqrt(jnp.mean(tokens * tokens, axis=1, keepdims=True) + epsilon)
    normed = (tokens * scale_in * norm_gain).astype(jnp.bfloat16)
    local_in = jnp.concatenate([gate_weight, value_weight, state_weight, step_weight], 1)
    full_in, full_out = (
        lax.all_gather(local_in, "gx", axis=0, tiled=True),
        lax.all_gather(out_weight, "gx", axis=1, tiled=True),
    )
    projected = jnp.dot(normed, full_in, preferred_element_type=jnp.float32)

    def local_mixer(
        proj_in, value_kernel, value_bias, state_kernel, state_bias, bias_step, log_rate, skip_part
    ):
        return ssm_mixer(
            proj_in,
            value_kernel,
            value_bias,
            state_kernel,
            state_bias,
            bias_step,
            log_rate,
            skip_part,
            segment_ids,
        )

    gated, mixer_pull = jax.vjp(
        local_mixer,
        projected,
        conv_value,
        conv_value_bias,
        conv_state,
        conv_state_bias,
        step_bias,
        decay_log,
        skip_scale,
    )
    squares = jnp.sum(gated * gated, axis=1, keepdims=True)
    scaled = (gated * gated_gain).astype(jnp.bfloat16)
    partial_value = jnp.dot(scaled, full_out, preferred_element_type=jnp.float32)
    square_total = lax.psum(squares, "gy")
    scale_out = lax.rsqrt(square_total / INNER + epsilon)
    product = (
        lax.psum_scatter(partial_value * scale_out, "gy", scatter_dimension=1, tiled=True)
        / scale_out
    )
    token_cols = lax.dynamic_slice_in_dim(tokens, col_start, col_width, 1)
    layer_output = (token_cols + scale_out * product).astype(jnp.bfloat16)
    upstream = lax.all_gather(cotangent, "gy", axis=1, tiled=True)
    upstream_cols = cotangent.astype(jnp.float32)
    grad_scale = lax.psum(jnp.sum(upstream_cols * product, axis=1, keepdims=True), "gy")
    grad_product = (scale_out * upstream).astype(jnp.bfloat16)
    grad_scaled = contract_cols(grad_product, full_out)
    grad_gated = grad_scaled * gated_gain - grad_scale * scale_out**3 * gated / INNER
    gate_gain_part = jnp.sum(grad_scaled * gated, axis=0)
    pulled = mixer_pull(grad_gated)
    state_start = 2 * inner_local
    state_sum, conv_state_sum, conv_bias_sum = lax.psum(
        (pulled[0][:, state_start : state_start + state_cols], pulled[3], pulled[4]), "gy"
    )
    grad_proj = jnp.concatenate(
        [pulled[0][:, :state_start], state_sum, pulled[0][:, state_start + state_cols :]], 1
    ).astype(jnp.bfloat16)
    positions = lax.broadcasted_iota(jnp.int32, (1, proj_width), 1)
    shared_cols = (positions >= state_start) & (positions < state_start + state_cols)
    other_rank = lax.axis_index("gy") != 0
    grad_proj_own = jnp.where(shared_cols & other_rank, jnp.zeros_like(grad_proj), grad_proj)
    grad_normed = lax.psum_scatter(
        contract_cols(grad_proj_own, full_in), "gy", scatter_dimension=1, tiled=True
    )
    gain_cols = lax.dynamic_slice_in_dim(norm_gain, col_start, col_width, 0)
    weighted = grad_normed * gain_cols
    inner_dot = lax.psum(jnp.sum(weighted * token_cols, axis=1, keepdims=True), "gy")
    grad_input = (
        upstream_cols + scale_in * weighted - token_cols * scale_in**3 * inner_dot / model_width
    )
    norm_gain_part = jnp.sum(grad_normed * token_cols * scale_in, axis=0)
    weight_sums = lax.psum_scatter(
        jnp.concatenate([contract_rows(normed, grad_proj), contract_rows(grad_product, scaled)], 1),
        "gx",
        scatter_dimension=0,
        tiled=True,
    )
    small_sums = lax.psum(
        (
            norm_gain_part,
            gate_gain_part,
            pulled[1],
            pulled[2],
            conv_state_sum,
            conv_bias_sum,
            pulled[5],
            pulled[6],
            pulled[7],
        ),
        "gx",
    )
    value_end = 2 * inner_local
    state_end = value_end + state_cols
    return (
        layer_output,
        grad_input,
        small_sums[0],
        weight_sums[:, :inner_local],
        weight_sums[:, inner_local:value_end],
        weight_sums[:, value_end:state_end],
        weight_sums[:, state_end:proj_width],
        small_sums[2],
        small_sums[3],
        small_sums[4],
        small_sums[5],
        small_sums[6],
        small_sums[7],
        small_sums[8],
        small_sums[1],
        weight_sums[:, proj_width:].T,
    )


def solution(mesh):
    return jax.shard_map(
        on_device,
        mesh=mesh,
        in_specs=(
            P("gx", None),
            P(),
            P("gx", "gy"),
            P("gx", "gy"),
            P("gx", None),
            P("gx", "gy"),
            P(None, "gy"),
            P("gy"),
            P(),
            P(),
            P("gy"),
            P("gy"),
            P("gy"),
            P("gy"),
            P("gy", "gx"),
            P("gx"),
            P("gx", "gy"),
        ),
        out_specs=(
            P("gx", "gy"),
            P("gx", "gy"),
            P("gy"),
            P("gx", "gy"),
            P("gx", "gy"),
            P("gx", None),
            P("gx", "gy"),
            P(None, "gy"),
            P("gy"),
            P(),
            P(),
            P("gy"),
            P("gy"),
            P("gy"),
            P("gy"),
            P("gy", "gx"),
        ),
        check_vma=False,
    )
```

profile of v0, /device:TPU:0, one launch (start us, length us, event | category | flops | bytes accessed | tf_op | source)
XLA Modules:
  0.0 2051.1 jit_solution(13020040875051077625)
XLA Ops:
  11.9 3.6 multiply_reduce_fusion.4
  16.5 204.2 %all-gather.4.cloned.1.call-done = bf16[2560,2836]{1,0:T(8,128)(2,1)} async-done(((bf16[320,2836]{1,0:T(8,128)(2,1)}), bf16[2560,2836]{1,0:T(8,128)(2,1)}) %all-gather.4.cloned.1.call-update) | async-done | bytes 14520336 | tf_op jit(solution)/shard_map/all_gather | solution.py:140
  220.7 21.8 %fusion.113 = f32[1024,2836]{0,1:T(8,128)S(1)} fusion(bf16[2560,2836]{1,0:T(8,128)(2,1)} %all-gather.4.cloned.1.call-done, f32[2560]{0:T(1024)S(1)} %copy-done.70, f32[1024]{0:T(1024)S(1)} %get-tuple-element.969, bf16[1024,2560]{1,0:T(8,128)(2,1)} %param.21), kind=kOutput, calls=%fused_computation.189 | convolution fusion | flops 14879293440 | bytes 31393792 | tf_op jit(solution)/shard_map/dot_general | solution.py:143
  255.0 14.7 fusion.106
  269.8 7.6 reshape.485
  277.3 6.0 copy.173
  288.9 3.5 broadcast.288.clone2
  292.4 206.8 %while.46 = (s32[]{:T(128)}, f32[20,64,128]{2,1,0:T(8,128)S(1)}, s32[]{:T(128)}, f32[4,256,20,64]{1,0,3,2:T(4,128)}, f32[4,20,64,128]{3,2,1,0:T(8,128)}, /*index...) while((s32[]{:T(128)}, f32[20,64,128]{2,1,0:T(8,128)S(1)}, ...), condition=%wide.region_4.5_spmd.clone, body=%wide.region_1.4_spmd.clone.sunk | while | flops 2123158656 | bytes 16843172 | solution.py:91
  296.9 7.4 fusion.209
  313.5 29.0 %dynamic_update_slice.88 = f32[4,256,20,64]{1,0,3,2:T(4,128)} dynamic-update-slice(f32[4,256,20,64]{1,0,3,2:T(4,128)} %get-tuple-element.1240, f32[1,256,20,64]{1,0,3,2:T(1,128)S(1)} %copy.293, s32[]{:T(128)S(6)} %copy.320, s32[]{:T(128)} %constant.143.clone.1..sunk, s32[]{:T(128)} %constant.143.clone.1..sunk, s32[]{:T(128)} %constant.143.clone.1..sunk) | dynamic-update-slice | bytes 2621444 | tf_op jit(solution)/shard_map/jvp()/while/body/jit(dynamic_update_index_in_dim)/dynamic_update_slice | solution.py:91
  348.5 7.4 fusion.209
  365.1 29.0 %dynamic_update_slice.88 = f32[4,256,20,64]{1,0,3,2:T(4,128)} dynamic-update-slice(f32[4,256,20,64]{1,0,3,2:T(4,128)} %get-tuple-element.1240, f32[1,256,20,64]{1,0,3,2:T(1,128)S(1)} %copy.293, s32[]{:T(128)S(6)} %copy.320, s32[]{:T(128)} %constant.143.clone.1..sunk, s32[]{:T(128)} %constant.143.clone.1..sunk, s32[]{:T(128)} %constant.143.clone.1..sunk) | dynamic-update-slice | bytes 2621444 | tf_op jit(solution)/shard_map/jvp()/while/body/jit(dynamic_update_index_in_dim)/dynamic_update_slice | solution.py:91
  400.1 7.4 fusion.209
  416.8 29.0 %dynamic_update_slice.88 = f32[4,256,20,64]{1,0,3,2:T(4,128)} dynamic-update-slice(f32[4,256,20,64]{1,0,3,2:T(4,128)} %get-tuple-element.1240, f32[1,256,20,64]{1,0,3,2:T(1,128)S(1)} %copy.293, s32[]{:T(128)S(6)} %copy.320, s32[]{:T(128)} %constant.143.clone.1..sunk, s32[]{:T(128)} %constant.143.clone.1..sunk, s32[]{:T(128)} %constant.143.clone.1..sunk) | dynamic-update-slice | bytes 2621444 | tf_op jit(solution)/shard_map/jvp()/while/body/jit(dynamic_update_index_in_dim)/dynamic_update_slice | solution.py:91
  451.7 7.4 fusion.209
  468.4 29.0 %dynamic_update_slice.88 = f32[4,256,20,64]{1,0,3,2:T(4,128)} dynamic-update-slice(f32[4,256,20,64]{1,0,3,2:T(4,128)} %get-tuple-element.1240, f32[1,256,20,64]{1,0,3,2:T(1,128)S(1)} %copy.293, s32[]{:T(128)S(6)} %copy.320, s32[]{:T(128)} %constant.143.clone.1..sunk, s32[]{:T(128)} %constant.143.clone.1..sunk, s32[]{:T(128)} %constant.143.clone.1..sunk) | dynamic-update-slice | bytes 2621444 | tf_op jit(solution)/shard_map/jvp()/while/body/jit(dynamic_update_index_in_dim)/dynamic_update_slice | solution.py:91
  499.3 3.8 copy.269
  503.1 9.5 multiply_reduce_fusion.11
  512.6 5.6 psum.105
  518.3 14.6 convolution_multiply_fusion.2
  534.2 82.1 %reduce-scatter.6.cloned.1.call-done = f32[1024,640]{1,0:T(8,128)} async-done(((f32[1024,2560]{1,0:T(8,128)}), f32[1024,640]{1,0:T(8,128)}) %reduce-scatter.6.cloned.1.call-update) | async-done | bytes 2621456 | tf_op jit(solution)/shard_map/reduce_scatter | solution.py:177
  618.5 5.8 psum.106
  624.3 33.8 %all-gather.8.cloned.1.call-done = bf16[1024,2560]{1,0:T(8,128)(2,1)} async-done(((bf16[1024,640]{1,0:T(8,128)(2,1)}), bf16[1024,2560]{1,0:T(8,128)(2,1)}) %all-gather.8.cloned.1.call-update) | async-done | bytes 5242896 | tf_op jit(solution)/shard_map/all_gather | solution.py:182
  658.1 23.6 %multiply_reduce_fusion.6 = (f32[1280]{0:T(1024)}, f32[1024,1280]{0,1:T(8,128)}, f32[1024,1280]{0,1:T(8,128)}, f32[1280]{0:T(1024)}) fusion(f32[1024,1280]{0,1:T(8,128)} %get-tuple-element.924, f32[1024,2836]{0,1:T(8,128)} %copy-done.1, f32[1024,1280]{0,1:T(8,128)} %get-tuple-element.920, f32[1024]{0:T(1024)S(1)} %bitcast.398, f32[1280]{0:T(1024)S(1)} %copy-done.75, ...), kind=kOutput, calls=%fused_computation.157 | convolution fusion | flops 6752827392 | bytes 43282432 | tf_op jit(solution)/shard_map/dot_general | solution.py:105
  681.8 7.6 reshape.489
  689.4 3.5 broadcast.288.clone
  695.9 411.0 %while.47 = (s32[]{:T(128)}, f32[20,64,128]{2,1,0:T(8,128)}, f32[4,256,20,64]{1,0,3,2:T(4,128)}, f32[4,256,128]{2,1,0:T(8,128)}, f32[4,256,128]{2,1,0:T(8,128)},...) while((s32[]{:T(128)}, f32[20,64,128]{2,1,0:T(8,128)}, ...), condition=%wide.region_22.23_spmd.clone, body=%wide.region_10.22_spmd.clone.sunk | while | flops 4863421440 | bytes 43898548 | solution.py:91
  699.5 3.9 constant_dynamic-slice_fusion.7
  715.0 10.2 fusion.231
  742.4 6.1 fusion.235
  751.0 29.1 %dynamic_update_slice.92 = f32[4,256,20,64]{1,0,3,2:T(4,128)} dynamic-update-slice(f32[4,256,20,64]{1,0,3,2:T(4,128)} %get-tuple-element.1291, f32[1,256,20,64]{1,0,3,2:T(1,128)} %copy.300, s32[]{:T(128)S(6)} %sub.296, s32[]{:T(128)} %constant.143.clone.1..sunk.1, s32[]{:T(128)} %constant.143.clone.1..sunk.1, s32[]{:T(128)} %constant.143.clone.1..sunk.1) | dynamic-update-slice | bytes 2621444 | tf_op jit(solution)/shard_map/transpose(jvp())/while/body/jit(dynamic_update_index_in_dim)/dynamic_update_slice | solution.py:91
  801.3 3.9 constant_dynamic-slice_fusion.7
  817.9 10.2 fusion.231
  845.3 6.1 fusion.235
  853.9 29.1 %dynamic_update_slice.92 = f32[4,256,20,64]{1,0,3,2:T(4,128)} dynamic-update-slice(f32[4,256,20,64]{1,0,3,2:T(4,128)} %get-tuple-element.1291, f32[1,256,20,64]{1,0,3,2:T(1,128)} %copy.300, s32[]{:T(128)S(6)} %sub.296, s32[]{:T(128)} %constant.143.clone.1..sunk.1, s32[]{:T(128)} %constant.143.clone.1..sunk.1, s32[]{:T(128)} %constant.143.clone.1..sunk.1) | dynamic-update-slice | bytes 2621444 | tf_op jit(solution)/shard_map/transpose(jvp())/while/body/jit(dynamic_update_index_in_dim)/dynamic_update_slice | solution.py:91
  904.2 3.9 constant_dynamic-slice_fusion.7
  920.8 10.2 fusion.231
  948.2 6.1 fusion.235
  956.7 29.1 %dynamic_update_slice.92 = f32[4,256,20,64]{1,0,3,2:T(4,128)} dynamic-update-slice(f32[4,256,20,64]{1,0,3,2:T(4,128)} %get-tuple-element.1291, f32[1,256,20,64]{1,0,3,2:T(1,128)} %copy.300, s32[]{:T(128)S(6)} %sub.296, s32[]{:T(128)} %constant.143.clone.1..sunk.1, s32[]{:T(128)} %constant.143.clone.1..sunk.1, s32[]{:T(128)} %constant.143.clone.1..sunk.1) | dynamic-update-slice | bytes 2621444 | tf_op jit(solution)/shard_map/transpose(jvp())/while/body/jit(dynamic_update_index_in_dim)/dynamic_update_slice | solution.py:91
  1007.1 3.9 constant_dynamic-slice_fusion.7
  1023.7 10.2 fusion.231
  1051.1 6.1 fusion.235
  1059.6 29.1 %dynamic_update_slice.92 = f32[4,256,20,64]{1,0,3,2:T(4,128)} dynamic-update-slice(f32[4,256,20,64]{1,0,3,2:T(4,128)} %get-tuple-element.1291, f32[1,256,20,64]{1,0,3,2:T(1,128)} %copy.300, s32[]{:T(128)S(6)} %sub.296, s32[]{:T(128)} %constant.143.clone.1..sunk.1, s32[]{:T(128)} %constant.143.clone.1..sunk.1, s32[]{:T(128)} %constant.143.clone.1..sunk.1) | dynamic-update-slice | bytes 2621444 | tf_op jit(solution)/shard_map/transpose(jvp())/while/body/jit(dynamic_update_index_in_dim)/dynamic_update_slice | solution.py:91
  1106.9 4.0 copy.272
  1111.0 9.6 multiply_reduce_fusion.10
  1120.7 6.8 multiply_reduce_fusion.9
  1127.5 6.5 slice_multiply_fusion
  1134.0 4.1 slice_multiply_fusion.1
  1138.2 4.0 slice_multiply_fusion.2
  1155.3 5.5 fusion.132
  1163.1 8.1 pad_add_fusion
  1175.3 25.9 %all-reduce.33 = bf16[1024,256]{0,1:T(8,128)(2,1)S(1)} all-reduce(f32[1024,256]{0,1:T(8,128)S(1)} %slice.242), channel_id=1, replica_groups=mesh['gx'=8,'gy'=4] {'gy'}, use_global_device_ids=true, to_apply=%region_23.24 | all-reduce | flops 262144 | bytes 1572864 | tf_op jit(solution)/shard_map/psum | solution.py:191
  1201.2 28.2 %fusion.98 = f32[1024,2560]{1,0:T(8,128)} fusion(bf16[2560,2836]{1,0:T(8,128)(2,1)} %all-gather.4.cloned.1.call-done, pred[2836]{0:T(1024)(128)(4,1)S(1)} %copy-done.64, bf16[1024,20]{0,1:T(8,128)(2,1)S(1)} %slice.243, bf16[1024,256]{0,1:T(8,128)(2,1)S(1)} %all-reduce.33, bf16[1024,2560]{0,1:T(8,128)(2,1)} %slice.241), kind=kOutput, calls=%fused_computation.146 | convolution fusion | flops 14889136128 | bytes 30817044 | tf_op jit(solution)/shard_map/dot_general | solution.py:105
  1230.1 14.8 fusion.111
  1244.9 27.8 %fusion.110 = f32[2560,2836]{0,1:T(8,128)} fusion(bf16[1024,20]{0,1:T(8,128)(2,1)S(1)} %slice.243, bf16[1024,256]{0,1:T(8,128)(2,1)S(1)} %all-reduce.33, bf16[1024,2560]{0,1:T(8,128)(2,1)} %slice.241, f32[2560]{0:T(1024)S(1)} %copy-done.71, f32[1024]{0:T(1024)S(1)} %copy-done.41, bf16[1024,2560]{1,0:T(8,128)(2,1)} %param.21), kind=kOutput, calls=%fused_computation.183 | convolution fusion | flops 14896717824 | bytes 40105984 | tf_op jit(solution)/shard_map/dot_general | solution.py:99
  1272.7 28.6 %pad_maximum_fusion = f32[2560,4116]{0,1:T(8,128)} fusion(f32[2560,1280]{0,1:T(8,128)} %fusion.111, f32[2560,2836]{0,1:T(8,128)} %fusion.110), kind=kLoop, calls=%fused_computation.137 | loop fusion | flops 10536960 | bytes 84295680 | tf_op jit(solution)/shard_map/concatenate | solution.py:212
  1301.3 43.4 %copy.201 = f32[2560,4116]{1,0:T(8,128)} copy(f32[2560,4116]{0,1:T(8,128)} %pad_maximum_fusion) | data formatting | bytes 84295680
  1344.8 7.9 convert_element_type.87
  1353.2 3.8 multiply_reduce_fusion.12
  1357.0 8.0 all-reduce.31
  1365.0 41.2 %all-reduce.30 = (f32[640]{0:T(1024)}, f32[4,1280]{1,0:T(4,128)}, f32[1280]{0:T(1024)}, f32[4,256]{1,0:T(4,128)}, f32[256]{0:T(256)}, /*index=5*/f32[20]{0:T(128)}, f32[20]{0:T(128)}, f32[20]{0:T(128)}, f32[1280]{0:T(1024)}) all-reduce(f32[640]{0:T(1024)S(1)} %get-tuple-element.823, ...), channel_id=1, replica_groups=mesh['gx'=8,'gy'=4] {'gx'}, use_global_device_ids=true, to_apply=%region_28.29 | all-reduce | flops 9660 | bytes 77280 | tf_op jit(solution)/shard_map/psum | solution.py:217
  1406.2 5.2 fusion.109
  1411.4 623.8 %reduce-scatter.10.cloned.1.call-done = f32[320,4116]{1,0:T(8,128)} async-done(((f32[2560,4116]{1,0:T(8,128)}), f32[320,4116]{1,0:T(8,128)}) %reduce-scatter.10.cloned.1.call-update) | async-done | bytes 5268496
  2036.8 5.2 slice_bitcast_fusion
  (616 shorter events, 316.6 us)
Async XLA Ops:
  7.2 213.5 %all-gather.4.cloned.1.call-start = ((), (), s32[]{:S(2)}) async-start(), calls=%async_computation.3 | async-start | bytes 16957440 | tf_op jit(solution)/shard_map/all_gather | solution.py:140
  8.1 212.6 %copy-start.70 = (f32[2560]{0:T(1024)S(1)}, f32[2560]{0:T(1024)}, u32[]{:S(2)}) copy-start(f32[2560]{0:T(1024)} %param.22) | copy-start | bytes 30724
  11.1 507.2 %all-gather.6.cloned.1.call-start = ((), (), s32[]{:S(2)}) async-start(), calls=%async_computation.4 | async-start | bytes 7372800 | tf_op jit(solution)/shard_map/all_gather | solution.py:141
  11.8 604.5 %reduce-scatter.6.cloned.1.call-start = ((), (), s32[]{:S(2)}) async-start(), calls=%async_computation.5 | async-start | bytes 13107200 | tf_op jit(solution)/shard_map/reduce_scatter | solution.py:177
  16.1 226.5 %copy-start.40 = (f32[1024]{0:T(1024)}, f32[1024]{0:T(1024)S(1)}, u32[]{:S(2)}) copy-start(f32[1024]{0:T(1024)S(1)} %get-tuple-element.969) | copy-start | bytes 12292
  16.1 238.9 %copy-start.28 = (f32[1280]{0:T(1024)}, f32[1280]{0:T(1024)S(1)}, u32[]{:S(2)}) copy-start(f32[1280]{0:T(1024)S(1)} %get-tuple-element.831) | copy-start | bytes 15364
  16.1 238.9 %copy-start.30 = (f32[1280]{0:T(1024)}, f32[1280]{0:T(1024)S(1)}, u32[]{:S(2)}) copy-start(f32[1280]{0:T(1024)S(1)} %get-tuple-element.832) | copy-start | bytes 15364
  16.2 238.9 %copy-start.32 = (f32[1280]{0:T(1024)}, f32[1280]{0:T(1024)S(1)}, u32[]{:S(2)}) copy-start(f32[1280]{0:T(1024)S(1)} %get-tuple-element.830) | copy-start | bytes 15364
  16.2 238.9 %copy-start.36 = (f32[1280]{0:T(1024)}, f32[1280]{0:T(1024)S(1)}, u32[]{:S(2)}) copy-start(f32[1280]{0:T(1024)S(1)} %get-tuple-element.829) | copy-start | bytes 15364
  16.2 236.9 %copy-start.67 = (f32[20]{0:T(128)}, f32[20]{0:T(128)S(1)}, u32[]{:S(2)}) copy-start(f32[20]{0:T(128)S(1)} %exponential_negate_fusion) | copy-start | bytes 244
  16.3 267.1 %copy-start.49 = (f32[1,256]{1,0:T(1,128)}, f32[1,256]{1,0:T(1,128)S(1)}, u32[]{:S(2)}) copy-start(f32[1,256]{1,0:T(1,128)S(1)} %get-tuple-element.970) | copy-start | bytes 3076
  16.3 267.1 %copy-start.51 = (f32[1,256]{1,0:T(1,128)}, f32[1,256]{1,0:T(1,128)S(1)}, u32[]{:S(2)}) copy-start(f32[1,256]{1,0:T(1,128)S(1)} %get-tuple-element.972) | copy-start | bytes 3076
  16.3 267.1 %copy-start.53 = (f32[1,256]{1,0:T(1,128)}, f32[1,256]{1,0:T(1,128)S(1)}, u32[]{:S(2)}) copy-start(f32[1,256]{1,0:T(1,128)S(1)} %get-tuple-element.973) | copy-start | bytes 3076
  16.3 267.1 %copy-start.55 = (f32[1,256]{1,0:T(1,128)}, f32[1,256]{1,0:T(1,128)S(1)}, u32[]{:S(2)}) copy-start(f32[1,256]{1,0:T(1,128)S(1)} %get-tuple-element.971) | copy-start | bytes 3076
  16.4 641.7 %copy-start.34 = (f32[1280]{0:T(1024)}, f32[1280]{0:T(1024)S(1)}, u32[]{:S(2)}) copy-start(f32[1280]{0:T(1024)S(1)} %mul.955) | copy-start | bytes 15364
  16.5 266.9 %copy-start.22 = (f32[1024]{0:T(1024)}, f32[1024]{0:T(1024)S(1)}, u32[]{:S(2)}) copy-start(f32[1024]{0:T(1024)S(1)} %get-tuple-element.974) | copy-start | bytes 12292
  16.5 266.9 %copy-start.24 = (f32[1024]{0:T(1024)}, f32[1024]{0:T(1024)S(1)}, u32[]{:S(2)}) copy-start(f32[1024]{0:T(1024)S(1)} %get-tuple-element.975) | copy-start | bytes 12292
  16.5 266.9 %copy-start.26 = (f32[1024]{0:T(1024)}, f32[1024]{0:T(1024)S(1)}, u32[]{:S(2)}) copy-start(f32[1024]{0:T(1024)S(1)} %get-tuple-element.976) | copy-start | bytes 12292
  242.6 10.6 copy-start.1
  253.0 30.4 %copy-start.6 = (f32[1022,256]{0,1:T(8,128)}, f32[1022,256]{0,1:T(8,128)S(1)}, u32[]{:S(2)}) copy-start(f32[1022,256]{0,1:T(8,128)S(1)} %slice.236) | copy-start | bytes 3139588
  253.2 30.3 %copy-start.8 = (f32[1023,256]{0,1:T(8,128)}, f32[1023,256]{0,1:T(8,128)S(1)}, u32[]{:S(2)}) copy-start(f32[1023,256]{0,1:T(8,128)S(1)} %slice.235) | copy-start | bytes 3142660
  253.3 16.5 copy-start.15
  503.1 15.2 copy-start.75
  518.2 139.9 %copy-start.42 = (f32[1024,1]{0,1:T(1,128)}, f32[1024,1]{0,1:T(1,128)S(1)}, u32[]{:S(2)}) copy-start(f32[1024,1]{0,1:T(1,128)S(1)} %add_rsqrt_fusion) | copy-start | bytes 12292
  532.9 83.4 %copy-start.4 = (bf16[1024,640]{1,0:T(8,128)(2,1)S(1)}, bf16[1024,640]{1,0:T(8,128)(2,1)}, u32[]{:S(2)}) copy-start(bf16[1024,640]{1,0:T(8,128)(2,1)} %param.37) | copy-start | bytes 3932164
  532.9 125.2 %all-gather.8.cloned.1.call-start = ((), (), s32[]{:S(2)}) async-start(), calls=%async_computation.6 | async-start | bytes 6553600 | tf_op jit(solution)/shard_map/all_gather | solution.py:182
  533.5 819.7 %reduce-scatter.8.cloned.1.call-start = ((), (), s32[]{:S(2)}) async-start(), calls=%async_computation.7 | async-start | bytes 13107200 | tf_op jit(solution)/shard_map/reduce_scatter | solution.py:201
  696.3 11.1 copy-start.38
  714.9 10.3 copy-start.10
  715.0 10.2 copy-start.14
  715.0 10.2 copy-start
  748.6 49.5 %copy-start.39 = (s32[4,256]{1,0:T(4,128)S(1)}, s32[4,256]{1,0:T(4,128)}, u32[]{:S(2)}) copy-start(s32[4,256]{1,0:T(4,128)} %copy-done.38) | copy-start | bytes 12292 | tf_op jit(solution)/shard_map/transpose(jvp())/while
  798.1 12.2 copy-start.38
  817.8 10.3 copy-start.10
  817.9 10.2 copy-start.14
  817.9 10.2 copy-start
  851.5 49.5 %copy-start.39 = (s32[4,256]{1,0:T(4,128)S(1)}, s32[4,256]{1,0:T(4,128)}, u32[]{:S(2)}) copy-start(s32[4,256]{1,0:T(4,128)} %copy-done.38) | copy-start | bytes 12292 | tf_op jit(solution)/shard_map/transpose(jvp())/while
  901.0 12.2 copy-start.38
  920.7 10.3 copy-start.10
  920.8 10.2 copy-start.14
  920.8 10.2 copy-start
  954.3 49.5 %copy-start.39 = (s32[4,256]{1,0:T(4,128)S(1)}, s32[4,256]{1,0:T(4,128)}, u32[]{:S(2)}) copy-start(s32[4,256]{1,0:T(4,128)} %copy-done.38) | copy-start | bytes 12292 | tf_op jit(solution)/shard_map/transpose(jvp())/while
  1003.8 12.2 copy-start.38
  1023.5 10.3 copy-start.10
  1023.7 10.2 copy-start.14
  1023.7 10.2 copy-start
  1057.2 49.5 %copy-start.39 = (s32[4,256]{1,0:T(4,128)S(1)}, s32[4,256]{1,0:T(4,128)}, u32[]{:S(2)}) copy-start(s32[4,256]{1,0:T(4,128)} %copy-done.38) | copy-start | bytes 12292 | tf_op jit(solution)/shard_map/transpose(jvp())/while
  1106.9 13.7 slice-start
  1106.9 13.7 slice-start.2
  1110.9 9.7 slice-start.1
  1110.9 9.7 slice-start.3
  1110.9 9.7 copy-start.23
  1127.5 10.7 slice-start.10
  1138.2 17.1 slice-start.8
  1144.2 11.0 slice-start.6
  1144.2 11.0 slice-start.9
  1171.2 30.1 %copy-start.64 = (pred[2836]{0:T(1024)(128)(4,1)S(1)}, pred[2836]{0:T(1024)(128)(4,1)}, u32[]{:S(2)}) copy-start(pred[2836]{0:T(1024)(128)(4,1)} %fusion.123) | copy-start | bytes 8512
  1229.4 15.4 copy-start.41
  1229.4 15.4 copy-start.71
  1229.4 805.7 %reduce-scatter.10.cloned.1.call-start = ((), (), s32[]{:S(2)}) async-start(), calls=%async_computation.8 | async-start | bytes 48660480
  1352.7 12.2 copy-start.59
  1352.7 12.3 copy-start.69
  1352.8 53.5 %copy-start.5 = (bf16[1024,640]{1,0:T(8,128)(2,1)S(1)}, bf16[1024,640]{1,0:T(8,128)(2,1)}, u32[]{:S(2)}) copy-start(bf16[1024,640]{1,0:T(8,128)(2,1)} %param.37) | copy-start | bytes 3932164
  1352.8 53.5 %copy-start.48 = (f32[1024]{0:T(1024)S(1)}, f32[1024]{0:T(1024)}, u32[]{:S(2)}) copy-start(f32[1024]{0:T(1024)} %get-tuple-element.968) | copy-start | bytes 12292
  (57 other events, 315.3 us)
Sparse Core Ops, SparseCore 0:
  11.2 209.4 all-gather.3
  222.9 100.4 all-gather.5
  533.0 83.1 reduce-scatter.5
  617.7 40.4 all-gather.7
  1229.5 86.4 reduce-scatter.7
  1344.8 690.3 reduce-scatter.9
where the time goes:
time: 2070 us; the launch traced here: 2050 us
  waiting for transfers between devices  945 us (46%)
  local copies, waits for them, and re-layouts  457 us (22%)
  matrix products  323 us (16%)
  other arithmetic  210 us (10%)
  blocking collectives  86.4 us (4%)
    unnamed x7, waiting for transfers between devices  625 us
    dynamic_update_slice x36, local copies, waits for them, and re-layouts, ssm_mixer(): finished, outputs = lax.scan(jax.checkpoint(group_step), initial, inputs)  269 us
    all_gather x1, waiting for transfers between devices, on_device(): lax.all_gather(local_in, 'gx', axis=0, tiled=True)  204 us
    dot_general x12, matrix products, group_step(): within = jnp.einsum('hts,shp->thp', mixing, x_block, precision=highest)  95 us
    reduce_scatter x1, waiting for transfers between devices, on_device(): lax.psum_scatter(partial_value * scale_out, 'gy', scatter_dimension=1, ti...  82.1 us
    unnamed x180, local copies, waits for them, and re-layouts  63.4 us
    dot_general x2, matrix products, contract_cols(): lax.dot_general(left, right, (((1,), (1,)), ((), ())), preferred_element_...  51.8 us
    dot_general x2, matrix products, contract_rows(): lax.dot_general(left, right, (((0,), (0,)), ((), ())), preferred_element_...  42.6 us
  transfers between devices with their start and end apart: 6, of which 4 were waited for; matrix products, arithmetic and copies ran while one was open for 21% of the time, Pallas kernels for 0%

commit v1 on v0

v1 whole, which is shorter than its diff:
```python
import jax
import jax.numpy as jnp
from jax import lax
from jax.sharding import PartitionSpec as P

GROUP = 256
INNER = 5120


epsilon = 1e-05
highest = lax.Precision.HIGHEST


def causal_conv(values, kernel, offset_bias, segments):
    seq_len = values.shape[0]
    total = offset_bias + kernel[0] * values
    for offset in range(1, kernel.shape[0]):
        moved = jnp.concatenate(
            [jnp.zeros((offset, values.shape[1]), values.dtype), values[: seq_len - offset]], 0
        )
        moved_seg = jnp.concatenate(
            [jnp.full((offset,), -1, jnp.int32), segments[: seq_len - offset]], 0
        )
        same_doc = (moved_seg == segments).astype(values.dtype)
        total = total + kernel[offset] * moved * same_doc[:, None]
    return total


def group_step(running, inputs):
    memory, previous = running
    x_block, b_block, c_block, decay_rate, step_size, seg_block = inputs
    block_len = seg_block.shape[0]
    cumulative = jnp.cumsum(decay_rate, axis=0)
    row_index = lax.broadcasted_iota(jnp.int32, (block_len, block_len), 0)
    col_index = lax.broadcasted_iota(jnp.int32, (block_len, block_len), 1)
    visible = (row_index >= col_index) & (seg_block[:, None] == seg_block[None, :])
    log_decay = cumulative.T[:, :, None] - cumulative.T[:, None, :]
    decay_mask = jnp.where(visible[None], jnp.exp(jnp.where(visible[None], log_decay, 0.0)), 0.0)
    intersection = jnp.dot(c_block, b_block.T, precision=highest)
    mixing = decay_mask * intersection[None] * step_size.T[:, None, :]
    within = jnp.einsum("hts,shp->thp", mixing, x_block, precision=highest)
    carried = (seg_block == previous).astype(memory.dtype)
    from_state = jnp.einsum("tn,hpn->thp", c_block, memory, precision=highest)
    from_state = from_state * (jnp.exp(cumulative) * carried[:, None])[:, :, None]
    last_seg = seg_block[block_len - 1]
    tail_weight = (
        (seg_block == last_seg).astype(memory.dtype)[:, None]
        * jnp.exp(cumulative[block_len - 1][None, :] - cumulative)
        * step_size
    )
    fresh_state = jnp.einsum("sh,shp,sn->hpn", tail_weight, x_block, b_block, precision=highest)
    survives = (last_seg == previous).astype(memory.dtype)
    memory = survives * jnp.exp(cumulative[block_len - 1])[:, None, None] * memory + fresh_state
    return ((memory, last_seg), within + from_state)


def ssm_mixer(
    value_in,
    state_in,
    step_in,
    conv_value,
    conv_value_bias,
    conv_state,
    conv_state_bias,
    step_bias,
    decay_log,
    skip_scale,
    segments,
):
    inner_width = conv_value.shape[1]
    head_count = step_bias.shape[0]
    head_dim = inner_width // head_count
    states = conv_state.shape[1] // 2
    seq_len = value_in.shape[0]
    blocks = seq_len // GROUP
    values = jax.nn.silu(causal_conv(value_in, conv_value, conv_value_bias, segments))
    state_act = jax.nn.silu(causal_conv(state_in, conv_state, conv_state_bias, segments))
    step_size = jax.nn.softplus(step_in + step_bias)
    decay_rate = -jnp.exp(decay_log) * step_size
    inputs = (
        values.reshape(blocks, GROUP, head_count, head_dim),
        state_act[:, :states].reshape(blocks, GROUP, states),
        state_act[:, states:].reshape(blocks, GROUP, states),
        decay_rate.reshape(blocks, GROUP, head_count),
        step_size.reshape(blocks, GROUP, head_count),
        segments.reshape(blocks, GROUP),
    )
    initial = (jnp.zeros((head_count, head_dim, states), value_in.dtype), jnp.array(-1, jnp.int32))
    finished, outputs = lax.scan(jax.checkpoint(group_step), initial, inputs)
    combined = outputs.reshape(seq_len, head_count, head_dim) + skip_scale[
        None, :, None
    ] * values.reshape(seq_len, head_count, head_dim)
    return combined.reshape(seq_len, inner_width)


def contract_rows(left, right):
    return lax.dot_general(
        left, right, (((0,), (0,)), ((), ())), preferred_element_type=jnp.float32
    )


def contract_cols(left, right):
    return lax.dot_general(
        left, right, (((1,), (1,)), ((), ())), preferred_element_type=jnp.float32
    )


def scatter_rows(partial):
    return lax.psum_scatter(
        partial.astype(jnp.bfloat16), "gx", scatter_dimension=0, tiled=True
    ).astype(jnp.float32)


def on_device(
    layer_input,
    norm_gain,
    gate_weight,
    value_weight,
    state_weight,
    step_weight,
    conv_value,
    conv_value_bias,
    conv_state,
    conv_state_bias,
    step_bias,
    decay_log,
    skip_scale,
    gated_gain,
    out_weight,
    segment_ids,
    cotangent,
):
    model_width = layer_input.shape[1]
    col_width = cotangent.shape[1]
    state_cols = state_weight.shape[1]
    col_start = lax.axis_index("gy") * col_width

    full_value = lax.all_gather(value_weight, "gx", axis=0, tiled=True)
    full_state = lax.all_gather(
        jnp.concatenate([state_weight, step_weight], 1), "gx", axis=0, tiled=True
    )
    gate_weight, full_value = lax.optimization_barrier((gate_weight, full_value))
    full_gate = lax.all_gather(gate_weight, "gx", axis=0, tiled=True)
    out_rows, full_gate = lax.optimization_barrier((out_weight.T, full_gate))
    full_out = lax.all_gather(out_rows, "gx", axis=0, tiled=True)
    upstream = lax.all_gather(cotangent, "gy", axis=1, tiled=True)

    tokens = layer_input.astype(jnp.float32)
    scale_in = lax.rsqrt(jnp.mean(tokens * tokens, axis=1, keepdims=True) + epsilon)
    normed = (tokens * scale_in * norm_gain).astype(jnp.bfloat16)

    value_in = jnp.dot(normed, full_value, preferred_element_type=jnp.float32)
    state_step = jnp.dot(normed, full_state, preferred_element_type=jnp.float32)
    mixed, mixer_pull = jax.vjp(
        lambda *operands: ssm_mixer(*operands, segment_ids),
        value_in,
        state_step[:, :state_cols],
        state_step[:, state_cols:],
        conv_value,
        conv_value_bias,
        conv_state,
        conv_state_bias,
        step_bias,
        decay_log,
        skip_scale,
    )
    gate_in = jnp.dot(normed, full_gate, preferred_element_type=jnp.float32)
    gate_open = jax.nn.sigmoid(gate_in)
    gate_act = gate_in * gate_open
    gated = mixed * gate_act
    squares = lax.psum(jnp.sum(gated * gated, axis=1), "gy")
    scale_out = lax.rsqrt(squares / INNER + epsilon)[:, None]
    scaled = (gated * gated_gain).astype(jnp.bfloat16)

    scaled_out = (gated * gated_gain * scale_out).astype(jnp.bfloat16)
    grad_out = scatter_rows(contract_rows(upstream, scaled_out))

    up_back = jnp.dot(upstream, full_out, preferred_element_type=jnp.float32)
    grad_scale = lax.psum(jnp.sum(gated * gated_gain * up_back, axis=1), "gy")[:, None]
    grad_scaled = scale_out * up_back
    grad_gated = grad_scaled * gated_gain - grad_scale * scale_out**3 * gated / INNER
    gate_gain_part = jnp.sum(grad_scaled * gated, axis=0)
    grad_gate_in = (
        grad_gated * mixed * gate_open * (1.0 + gate_in * (1.0 - gate_open))
    ).astype(jnp.bfloat16)
    grad_gate = scatter_rows(contract_rows(normed, grad_gate_in))

    pulled = mixer_pull(grad_gated * gate_act)
    grad_value_in = pulled[0].astype(jnp.bfloat16)
    grad_state_in = jnp.concatenate([pulled[1], pulled[2]], 1).astype(jnp.bfloat16)
    grad_state_step = scatter_rows(contract_rows(normed, grad_state_in))
    grad_value = scatter_rows(contract_rows(normed, grad_value_in))

    product = lax.psum_scatter(
        (contract_cols(scaled, full_out) * scale_out).astype(jnp.bfloat16),
        "gy",
        scatter_dimension=1,
        tiled=True,
    )
    token_cols = lax.dynamic_slice_in_dim(layer_input, col_start, col_width, 1).astype(jnp.float32)
    layer_output = (token_cols + product.astype(jnp.float32)).astype(jnp.bfloat16)

    grad_normed_part = (
        contract_cols(grad_gate_in, full_gate)
        + contract_cols(grad_value_in, full_value)
        + contract_cols(grad_state_in, full_state)
    )
    grad_normed = lax.psum_scatter(
        grad_normed_part.astype(jnp.bfloat16), "gy", scatter_dimension=1, tiled=True
    ).astype(jnp.float32)
    gain_cols = lax.dynamic_slice_in_dim(norm_gain, col_start, col_width, 0)
    weighted = grad_normed * gain_cols
    inner_dot = lax.psum(jnp.sum(weighted * token_cols, axis=1), "gy")[:, None]
    grad_input = (
        cotangent.astype(jnp.float32)
        + scale_in * weighted
        - token_cols * scale_in**3 * inner_dot / model_width
    )
    norm_gain_part = jnp.sum(grad_normed * token_cols * scale_in, axis=0)
    conv_state_sum, conv_bias_sum = lax.psum((pulled[5], pulled[6]), ("gx", "gy"))
    grad_state = lax.psum(grad_state_step[:, :state_cols], "gy")
    small_sums = lax.psum(
        (norm_gain_part, gate_gain_part, pulled[3], pulled[4], pulled[7], pulled[8], pulled[9]),
        "gx",
    )
    return (
        layer_output,
        grad_input,
        small_sums[0],
        grad_gate,
        grad_value,
        grad_state,
        grad_state_step[:, state_cols:],
        small_sums[2],
        small_sums[3],
        conv_state_sum,
        conv_bias_sum,
        small_sums[4],
        small_sums[5],
        small_sums[6],
        small_sums[1],
        grad_out.T,
    )


def solution(mesh):
    return jax.shard_map(
        on_device,
        mesh=mesh,
        in_specs=(
            P("gx", None),
            P(),
            P("gx", "gy"),
            P("gx", "gy"),
            P("gx", None),
            P("gx", "gy"),
            P(None, "gy"),
            P("gy"),
            P(),
            P(),
            P("gy"),
            P("gy"),
            P("gy"),
            P("gy"),
            P("gy", "gx"),
            P("gx"),
            P("gx", "gy"),
        ),
        out_specs=(
            P("gx", "gy"),
            P("gx", "gy"),
            P("gy"),
            P("gx", "gy"),
            P("gx", "gy"),
            P("gx", None),
            P("gx", "gy"),
            P(None, "gy"),
            P("gy"),
            P(),
            P(),
            P("gy"),
            P("gy"),
            P("gy"),
            P("gy"),
            P("gy", "gx"),
        ),
        check_vma=False,
    )
```

time: 2070 us -> 1600 us (0.77)
  waiting for transfers between devices: 945 us -> 512 us
  other arithmetic: 210 us -> 149 us
  local copies, waits for them, and re-layouts: 457 us -> 484 us
    unnamed x7 -> x16, waiting for transfers between devices: 625 us -> 130 us
    reduce_scatter x2, waiting for transfers between devices: 82.1 us -> 194 us  [scatter_rows(): lax.psum_scatter(partial.astype(jnp.bfloat16), 'gx', scatter_dimension=0,...]
    all_gather x1, waiting for transfers between devices: 33.8 us -> 0.02 us  [on_device(): upstream = lax.all_gather(cotangent, 'gy', axis=1, tiled=True)]
    concatenate x2 -> x0, other arithmetic: 31.5 us -> none  [the longest x1 28.6 us: on_device(): jnp.concatenate([contract_rows(normed, grad_proj), contract_rows(grad_pro...]
    all_gather x2 -> x4, waiting for transfers between devices: 204 us -> 188 us  [the longest x1 105 us: on_device(): full_value = lax.all_gather(value_weight, 'gx', axis=0, tiled=True)]
    dot_general x2 -> x4, matrix products: 36.5 us -> 48.3 us  [the longest x1 18.5 us: on_device(): gate_in = jnp.dot(normed, full_gate, preferred_element_type=jnp.float32)]
    dot_general x2 -> x4, matrix products: 51.8 us -> 41.5 us  [contract_cols(): lax.dot_general(left, right, (((1,), (1,)), ((), ())), preferred_element_...]
    unnamed x180 -> x156, local copies, waits for them, and re-layouts: 63.4 us -> 70.3 us
  transfers between devices with their start and end apart: 6 -> 12, of which waited for: 4 -> 8; matrix products, arithmetic and copies ran while one was open for 21% -> 30% of each run, Pallas kernels for 0% -> 0%
where the time goes in v1:
time: 1600 us; the launch traced here: 1580 us
  waiting for transfers between devices  512 us (32%)
  local copies, waits for them, and re-layouts  484 us (30%)
  matrix products  310 us (19%)
  other arithmetic  149 us (9%)
  blocking collectives  98.4 us (6%)
    dynamic_update_slice x36, local copies, waits for them, and re-layouts, ssm_mixer(): finished, outputs = lax.scan(jax.checkpoint(group_step), initial, inputs)  268 us
    reduce_scatter x2, waiting for transfers between devices, scatter_rows(): lax.psum_scatter(partial.astype(jnp.bfloat16), 'gx', scatter_dimension=0,...  194 us
    unnamed x16, waiting for transfers between devices  130 us
    all_gather x1, waiting for transfers between devices, on_device(): full_value = lax.all_gather(value_weight, 'gx', axis=0, tiled=True)  105 us
    dot_general x12, matrix products, group_step(): within = jnp.einsum('hts,shp->thp', mixing, x_block, precision=highest)  89.6 us
    unnamed x156, local copies, waits for them, and re-layouts  70.3 us
    all_gather x1, waiting for transfers between devices, on_device(): full_gate = lax.all_gather(gate_weight, 'gx', axis=0, tiled=True)  46.7 us
    dot_general x16, matrix products, group_step(): from_state = jnp.einsum('tn,hpn->thp', c_block, memory, precision=highest)  42.7 us
  transfers between devices with their start and end apart: 12, of which 8 were waited for; matrix products, arithmetic and copies ran while one was open for 30% of the time, Pallas kernels for 0%

profile of v1, /device:TPU:0, one launch (start us, length us, event | category | flops | bytes accessed | tf_op | source)
XLA Modules:
  0.0 1582.1 jit_solution(265056863544697353)
XLA Ops:
  10.6 104.6 %all-gather.7.cloned.1.call-done = bf16[2560,1280]{1,0:T(8,128)(2,1)} async-done(((bf16[320,1280]{1,0:T(8,128)(2,1)}), bf16[2560,1280]{1,0:T(8,128)(2,1)}) %all-gather.7.cloned.1.call-update) | async-done | bytes 6553616 | tf_op jit(solution)/shard_map/all_gather | solution.py:138
  124.8 36.6 %all-gather.15.cloned.1.call-done = bf16[8,320,276]{1,2,0:T(8,128)(2,1)} async-done(((bf16[1,320,276]{1,2,0:T(8,128)(2,1)}), bf16[8,320,276]{1,2,0:T(8,128)(2,1)}) %all-gather.15.cloned.1.call-update) | async-done | bytes 1413136 | tf_op jit(solution)/shard_map/all_gather | solution.py:139
  165.4 4.7 fusion.140
  179.7 11.3 fusion.138
  191.1 7.6 fusion.106
  198.7 6.0 copy.201
  204.7 7.6 reshape.478
  212.3 5.8 copy.204
  218.1 46.7 %all-gather.9.cloned.1.call-done = bf16[2560,1280]{1,0:T(8,128)(2,1)} async-done(((bf16[320,1280]{1,0:T(8,128)(2,1)}), bf16[2560,1280]{1,0:T(8,128)(2,1)}) %all-gather.9.cloned.1.call-update) | async-done | bytes 6553616 | tf_op jit(solution)/shard_map/all_gather | solution.py:143
  268.4 212.4 %while.46 = (s32[]{:T(128)}, f32[20,64,128]{2,1,0:T(8,128)S(1)}, s32[]{:T(128)}, f32[4,256,20,64]{1,0,3,2:T(4,128)}, f32[4,20,64,128]{3,2,1,0:T(8,128)}, /*index...) while((s32[]{:T(128)}, f32[20,64,128]{2,1,0:T(8,128)S(1)}, ...), condition=%wide.region_4.5_spmd.clone, body=%wide.region_1.4_spmd.clone.sunk | while | flops 2123158656 | bytes 16843172 | solution.py:89
  277.4 7.5 fusion.231
  292.0 29.0 %dynamic_update_slice.88 = f32[4,256,20,64]{1,0,3,2:T(4,128)} dynamic-update-slice(f32[4,256,20,64]{1,0,3,2:T(4,128)} %get-tuple-element.1290, f32[1,256,20,64]{1,0,3,2:T(1,128)S(1)} %copy.320, s32[]{:T(128)S(6)} %copy.347, s32[]{:T(128)} %constant.141.clone.1..sunk, s32[]{:T(128)} %constant.141.clone.1..sunk, s32[]{:T(128)} %constant.141.clone.1..sunk) | dynamic-update-slice | bytes 2621444 | tf_op jit(solution)/shard_map/jvp()/while/body/jit(dynamic_update_index_in_dim)/dynamic_update_slice | solution.py:89
  330.4 7.5 fusion.231
  345.0 29.1 %dynamic_update_slice.88 = f32[4,256,20,64]{1,0,3,2:T(4,128)} dynamic-update-slice(f32[4,256,20,64]{1,0,3,2:T(4,128)} %get-tuple-element.1290, f32[1,256,20,64]{1,0,3,2:T(1,128)S(1)} %copy.320, s32[]{:T(128)S(6)} %copy.347, s32[]{:T(128)} %constant.141.clone.1..sunk, s32[]{:T(128)} %constant.141.clone.1..sunk, s32[]{:T(128)} %constant.141.clone.1..sunk) | dynamic-update-slice | bytes 2621444 | tf_op jit(solution)/shard_map/jvp()/while/body/jit(dynamic_update_index_in_dim)/dynamic_update_slice | solution.py:89
  383.5 7.5 fusion.231
  398.1 29.0 %dynamic_update_slice.88 = f32[4,256,20,64]{1,0,3,2:T(4,128)} dynamic-update-slice(f32[4,256,20,64]{1,0,3,2:T(4,128)} %get-tuple-element.1290, f32[1,256,20,64]{1,0,3,2:T(1,128)S(1)} %copy.320, s32[]{:T(128)S(6)} %copy.347, s32[]{:T(128)} %constant.141.clone.1..sunk, s32[]{:T(128)} %constant.141.clone.1..sunk, s32[]{:T(128)} %constant.141.clone.1..sunk) | dynamic-update-slice | bytes 2621444 | tf_op jit(solution)/shard_map/jvp()/while/body/jit(dynamic_update_index_in_dim)/dynamic_update_slice | solution.py:89
  436.5 7.5 fusion.231
  451.1 29.0 %dynamic_update_slice.88 = f32[4,256,20,64]{1,0,3,2:T(4,128)} dynamic-update-slice(f32[4,256,20,64]{1,0,3,2:T(4,128)} %get-tuple-element.1290, f32[1,256,20,64]{1,0,3,2:T(1,128)S(1)} %copy.320, s32[]{:T(128)S(6)} %copy.347, s32[]{:T(128)} %constant.141.clone.1..sunk, s32[]{:T(128)} %constant.141.clone.1..sunk, s32[]{:T(128)} %constant.141.clone.1..sunk) | dynamic-update-slice | bytes 2621444 | tf_op jit(solution)/shard_map/jvp()/while/body/jit(dynamic_update_index_in_dim)/dynamic_update_slice | solution.py:89
  480.8 6.0 copy.294
  486.8 5.9 copy.208
  492.7 18.5 %multiply_reduce_fusion.10 = (f32[1024]{0:T(1024)S(1)}, f32[1024,1280]{1,0:T(8,128)}, f32[1024,1280]{1,0:T(8,128)}) fusion(f32[1024,1280]{1,0:T(8,128)} %copy.208, f32[1024,1280]{1,0:T(8,128)} %get-tuple-element.975, f32[1280]{0:T(1024)S(1)} %mul.955, bf16[2560,1280]{1,0:T(8,128)(2,1)} %all-gather.9.cloned.1.call-done, bf16[1024,2560]{1,0:T(8,128)(2,1)} %param.21, ...), kind=kOutput, calls=%fused_computation.167 | convolution fusion | flops 6738410496 | bytes 32791552 | tf_op jit(solution)/shard_map/dot_general | solution.py:167
  511.2 6.2 psum.91
  517.5 13.8 multiply_reduce_fusion.4
  531.3 6.0 psum.92
  537.3 14.8 multiply_reduce_fusion.5
  552.1 5.9 copy.209
  558.0 7.6 reshape.482
  572.1 402.1 %while.47 = (s32[]{:T(128)}, f32[20,64,128]{2,1,0:T(8,128)}, f32[4,256,20,64]{1,0,3,2:T(4,128)}, f32[4,256,128]{2,1,0:T(8,128)}, f32[4,256,128]{2,1,0:T(8,128)},...) while((s32[]{:T(128)}, f32[20,64,128]{2,1,0:T(8,128)}, ...), condition=%wide.region_22.23_spmd.clone, body=%wide.region_10.22_spmd.clone.sunk | while | flops 4863421440 | bytes 49441304 | solution.py:89
  578.6 3.9 constant_dynamic-slice_fusion.7
  601.6 10.2 fusion.253
  617.4 4.8 fusion.257
  642.9 28.9 %dynamic_update_slice.92 = f32[4,256,20,64]{1,0,3,2:T(4,128)} dynamic-update-slice(f32[4,256,20,64]{1,0,3,2:T(4,128)} %get-tuple-element.1341, f32[1,256,20,64]{1,0,3,2:T(1,128)S(1)} %copy-done.2, s32[]{:T(128)S(6)} %sub.292, s32[]{:T(128)} %constant.141.clone.1..sunk.1, s32[]{:T(128)} %constant.141.clone.1..sunk.1, s32[]{:T(128)} %constant.141.clone.1..sunk.1) | dynamic-update-slice | bytes 2621444 | tf_op jit(solution)/shard_map/transpose(jvp())/while/body/jit(dynamic_update_index_in_dim)/dynamic_update_slice | solution.py:89
  702.3 10.2 fusion.253
  718.1 4.8 fusion.257
  743.5 28.9 %dynamic_update_slice.92 = f32[4,256,20,64]{1,0,3,2:T(4,128)} dynamic-update-slice(f32[4,256,20,64]{1,0,3,2:T(4,128)} %get-tuple-element.1341, f32[1,256,20,64]{1,0,3,2:T(1,128)S(1)} %copy-done.2, s32[]{:T(128)S(6)} %sub.292, s32[]{:T(128)} %constant.141.clone.1..sunk.1, s32[]{:T(128)} %constant.141.clone.1..sunk.1, s32[]{:T(128)} %constant.141.clone.1..sunk.1) | dynamic-update-slice | bytes 2621444 | tf_op jit(solution)/shard_map/transpose(jvp())/while/body/jit(dynamic_update_index_in_dim)/dynamic_update_slice | solution.py:89
  803.0 10.2 fusion.253
  818.7 4.8 fusion.257
  844.2 28.9 %dynamic_update_slice.92 = f32[4,256,20,64]{1,0,3,2:T(4,128)} dynamic-update-slice(f32[4,256,20,64]{1,0,3,2:T(4,128)} %get-tuple-element.1341, f32[1,256,20,64]{1,0,3,2:T(1,128)S(1)} %copy-done.2, s32[]{:T(128)S(6)} %sub.292, s32[]{:T(128)} %constant.141.clone.1..sunk.1, s32[]{:T(128)} %constant.141.clone.1..sunk.1, s32[]{:T(128)} %constant.141.clone.1..sunk.1) | dynamic-update-slice | bytes 2621444 | tf_op jit(solution)/shard_map/transpose(jvp())/while/body/jit(dynamic_update_index_in_dim)/dynamic_update_slice | solution.py:89
  903.7 10.2 fusion.253
  919.4 4.8 fusion.257
  944.9 28.9 %dynamic_update_slice.92 = f32[4,256,20,64]{1,0,3,2:T(4,128)} dynamic-update-slice(f32[4,256,20,64]{1,0,3,2:T(4,128)} %get-tuple-element.1341, f32[1,256,20,64]{1,0,3,2:T(1,128)S(1)} %copy-done.2, s32[]{:T(128)S(6)} %sub.292, s32[]{:T(128)} %constant.141.clone.1..sunk.1, s32[]{:T(128)} %constant.141.clone.1..sunk.1, s32[]{:T(128)} %constant.141.clone.1..sunk.1) | dynamic-update-slice | bytes 2621444 | tf_op jit(solution)/shard_map/transpose(jvp())/while/body/jit(dynamic_update_index_in_dim)/dynamic_update_slice | solution.py:89
  989.5 12.4 fusion.101
  1001.9 9.6 copy.236
  1011.5 42.6 %reduce-scatter.23.cloned.1.call-done = bf16[320,276]{1,0:T(8,128)(2,1)} async-done(((bf16[2560,276]{1,0:T(8,128)(2,1)}), bf16[320,276]{1,0:T(8,128)(2,1)}) %reduce-scatter.23.cloned.1.call-update) | async-done | bytes 176656
  1056.1 12.5 multiply_convert_fusion
  1068.6 8.0 copy.230
  1076.5 6.0 copy.295
  1082.6 5.9 copy.217
  1089.2 11.8 multiply_reduce_fusion.9
  1101.0 6.6 multiply_reduce_fusion.8
  1118.8 6.4 fusion.142
  1125.2 9.3 fusion.153
  1134.6 11.6 fusion.154
  1146.2 8.0 add_convert_fusion
  1154.2 8.0 copy.232
  1162.3 11.2 convolution_convert_fusion.2
  1175.3 10.9 convolution_convert_fusion.1
  1187.1 39.7 %all-reduce.26 = (f32[4,256]{1,0:T(4,128)}, f32[256]{0:T(256)}) all-reduce(f32[4,256]{1,0:T(4,128)S(1)} %pad_add_fusion.1, f32[256]{0:T(256)S(1)} %get-tuple-element.881), channel_id=1, replica_groups=mesh['gx'=8,'gy'=4] {'gx','gy'}, use_global_device_ids=true, to_apply=%region_43.44 | all-reduce | flops 1280 | bytes 10240 | tf_op jit(solution)/shard_map/psum | solution.py:220
  1232.9 34.9 %reduce-scatter.19.cloned.1.call-done = bf16[640,1024]{1,0:T(8,128)(2,1)} async-done(((bf16[2560,1024]{1,0:T(8,128)(2,1)}), bf16[640,1024]{1,0:T(8,128)(2,1)}) %reduce-scatter.19.cloned.1.call-update) | async-done | bytes 1310736
  1270.2 51.4 %reduce-scatter.21.cloned.1.call-done = bf16[640,1024]{1,0:T(8,128)(2,1)} async-done(((bf16[2560,1024]{1,0:T(8,128)(2,1)}), bf16[640,1024]{1,0:T(8,128)(2,1)}) %reduce-scatter.21.cloned.1.call-update) | async-done | bytes 1310736
  1325.9 40.4 %all-reduce.27 = (f32[640]{0:T(1024)}, f32[4,1280]{1,0:T(4,128)}, f32[1280]{0:T(1024)}, f32[20]{0:T(128)}, f32[20]{0:T(128)}, /*index=5*/f32[20]{0:T(128)}, f32[1280]{0:T(1024)}) all-reduce(f32[640]{0:T(1024)S(1)} %get-tuple-element.877, f32[4,1280]{1,0:T(4,128)S(1)} %pad_add_fusion, ...), channel_id=1, replica_groups=mesh['gx'=8,'gy'=4] {'gx'}, use_global_device_ids=true, to_apply=%region_27.28 | all-reduce | flops 8380 | bytes 67040 | tf_op jit(solution)/shard_map/psum | solution.py:222
  1366.3 6.0 psum.93
  1376.2 72.1 %reduce-scatter.15.cloned.1.call-done = bf16[320,1280]{1,0:T(8,128)(2,1)} async-done(((bf16[2560,1280]{1,0:T(8,128)(2,1)}), bf16[320,1280]{1,0:T(8,128)(2,1)}) %reduce-scatter.15.cloned.1.call-update) | async-done | bytes 819216 | tf_op jit(solution)/shard_map/reduce_scatter | solution.py:109
  1450.7 121.9 %reduce-scatter.17.cloned.1.call-done = bf16[320,1280]{1,0:T(8,128)(2,1)} async-done(((bf16[2560,1280]{1,0:T(8,128)(2,1)}), bf16[320,1280]{1,0:T(8,128)(2,1)}) %reduce-scatter.17.cloned.1.call-update) | async-done | bytes 819216 | tf_op jit(solution)/shard_map/reduce_scatter | solution.py:109
  (673 shorter events, 365.4 us)
Async XLA Ops:
  7.2 117.5 %copy-start.30 = (s32[1024]{0:T(1024)S(1)}, s32[1024]{0:T(1024)}, u32[]{:S(2)}) copy-start(s32[1024]{0:T(1024)} %param.36) | copy-start | bytes 12292
  7.2 108.0 %all-gather.7.cloned.1.call-start = ((), (), s32[]{:S(2)}) async-start(), calls=%async_computation.6 | async-start | bytes 7372800 | tf_op jit(solution)/shard_map/all_gather | solution.py:138
  7.9 153.5 %all-gather.15.cloned.1.call-start = ((), (), s32[]{:S(2)}) async-start(), calls=%async_computation.13 | async-start | bytes 1935360 | tf_op jit(solution)/shard_map/all_gather | solution.py:139
  10.5 254.3 %all-gather.9.cloned.1.call-start = ((), (), s32[]{:S(2)}) async-start(), calls=%async_computation.7 | async-start | bytes 7372800 | tf_op jit(solution)/shard_map/all_gather | solution.py:143
  115.2 402.2 %all-gather.13.cloned.1.call-start = ((), (), s32[]{:S(2)}) async-start(), calls=%async_computation.9 | async-start | bytes 6553600 | tf_op jit(solution)/shard_map/all_gather | solution.py:146
  115.8 401.6 %all-gather.11.cloned.1.call-start = ((), (), s32[]{:S(2)}) async-start(), calls=%async_computation.8 | async-start | bytes 7372800 | tf_op jit(solution)/shard_map/all_gather | solution.py:145
  118.0 419.4 %copy-start.43 = (f32[1280]{0:T(1024)}, f32[1280]{0:T(1024)S(1)}, u32[]{:S(2)}) copy-start(f32[1280]{0:T(1024)S(1)} %mul.955) | copy-start | bytes 15364
  118.9 72.1 %copy-start.37 = (f32[1280]{0:T(1024)}, f32[1280]{0:T(1024)S(1)}, u32[]{:S(2)}) copy-start(f32[1280]{0:T(1024)S(1)} %get-tuple-element.884) | copy-start | bytes 15364
  118.9 72.1 %copy-start.39 = (f32[1280]{0:T(1024)}, f32[1280]{0:T(1024)S(1)}, u32[]{:S(2)}) copy-start(f32[1280]{0:T(1024)S(1)} %get-tuple-element.886) | copy-start | bytes 15364
  118.9 72.1 %copy-start.41 = (f32[1280]{0:T(1024)}, f32[1280]{0:T(1024)S(1)}, u32[]{:S(2)}) copy-start(f32[1280]{0:T(1024)S(1)} %get-tuple-element.885) | copy-start | bytes 15364
  118.9 72.1 %copy-start.45 = (f32[1280]{0:T(1024)}, f32[1280]{0:T(1024)S(1)}, u32[]{:S(2)}) copy-start(f32[1280]{0:T(1024)S(1)} %get-tuple-element.883) | copy-start | bytes 15364
  119.6 52.8 %copy-start.69 = (f32[20]{0:T(128)}, f32[20]{0:T(128)S(1)}, u32[]{:S(2)}) copy-start(f32[20]{0:T(128)S(1)} %exponential_negate_fusion) | copy-start | bytes 244
  120.5 53.5 %copy-start.54 = (f32[1,256]{1,0:T(1,128)}, f32[1,256]{1,0:T(1,128)S(1)}, u32[]{:S(2)}) copy-start(f32[1,256]{1,0:T(1,128)S(1)} %get-tuple-element.1015) | copy-start | bytes 3076
  120.5 53.5 %copy-start.56 = (f32[1,256]{1,0:T(1,128)}, f32[1,256]{1,0:T(1,128)S(1)}, u32[]{:S(2)}) copy-start(f32[1,256]{1,0:T(1,128)S(1)} %get-tuple-element.1017) | copy-start | bytes 3076
  120.5 53.5 %copy-start.58 = (f32[1,256]{1,0:T(1,128)}, f32[1,256]{1,0:T(1,128)S(1)}, u32[]{:S(2)}) copy-start(f32[1,256]{1,0:T(1,128)S(1)} %get-tuple-element.1016) | copy-start | bytes 3076
  120.5 53.5 %copy-start.60 = (f32[1,256]{1,0:T(1,128)}, f32[1,256]{1,0:T(1,128)S(1)}, u32[]{:S(2)}) copy-start(f32[1,256]{1,0:T(1,128)S(1)} %get-tuple-element.1018) | copy-start | bytes 3076
  120.5 44.9 %copy-start.72 = (f32[2560]{0:T(1024)S(1)}, f32[2560]{0:T(1024)}, u32[]{:S(2)}) copy-start(f32[2560]{0:T(1024)} %param.22) | copy-start | bytes 30724
  124.7 368.0 %copy-start.48 = (f32[1024]{0:T(1024)}, f32[1024]{0:T(1024)S(1)}, u32[]{:S(2)}) copy-start(f32[1024]{0:T(1024)S(1)} %get-tuple-element.1014) | copy-start | bytes 12292
  124.8 66.3 %copy-start.31 = (f32[1024]{0:T(1024)}, f32[1024]{0:T(1024)S(1)}, u32[]{:S(2)}) copy-start(f32[1024]{0:T(1024)S(1)} %get-tuple-element.1019) | copy-start | bytes 12292
  124.8 66.3 %copy-start.33 = (f32[1024]{0:T(1024)}, f32[1024]{0:T(1024)S(1)}, u32[]{:S(2)}) copy-start(f32[1024]{0:T(1024)S(1)} %get-tuple-element.1020) | copy-start | bytes 12292
  124.8 66.3 %copy-start.35 = (f32[1024]{0:T(1024)}, f32[1024]{0:T(1024)S(1)}, u32[]{:S(2)}) copy-start(f32[1024]{0:T(1024)S(1)} %get-tuple-element.1021) | copy-start | bytes 12292
  179.7 11.4 copy-start.62
  191.0 7.7 copy-start
  264.9 789.3 %reduce-scatter.23.cloned.1.call-start = ((), (), s32[]{:S(2)}) async-start(), calls=%async_computation.16 | async-start | bytes 2211840
  492.7 24.7 %copy-start.63 = (f32[1280]{0:T(1024)S(1)}, f32[1280]{0:T(1024)}, u32[]{:S(2)}) copy-start(f32[1280]{0:T(1024)} %param.34) | copy-start | bytes 15364
  517.4 19.9 %copy-start.52 = (f32[1024]{0:T(1024)}, f32[1024]{0:T(1024)S(1)}, u32[]{:S(2)}) copy-start(f32[1024]{0:T(1024)S(1)} %add_rsqrt_fusion) | copy-start | bytes 12292
  597.7 15.4 copy-start.27
  601.6 11.5 copy-start.9
  601.6 11.5 copy-start.14
  601.6 11.5 copy-start.26
  617.4 8.0 copy-start.1
  628.3 14.6 copy-start.2
  698.4 15.4 copy-start.27
  702.3 11.5 copy-start.9
  702.3 11.5 copy-start.14
  702.3 11.5 copy-start.26
  718.0 8.0 copy-start.1
  728.9 14.6 copy-start.2
  799.0 15.4 copy-start.27
  803.0 11.5 copy-start.9
  803.0 11.5 copy-start.14
  803.0 11.5 copy-start.26
  818.7 8.0 copy-start.1
  829.6 14.6 copy-start.2
  899.7 15.4 copy-start.27
  903.6 11.5 copy-start.9
  903.6 11.5 copy-start.14
  903.6 11.5 copy-start.26
  919.4 8.0 copy-start.1
  930.3 14.6 copy-start.2
  989.4 237.5 %reduce-scatter.25.cloned.1.call-start = ((), (), s32[]{:S(2)}) async-start(), calls=%async_computation.17 | async-start | bytes 7372800
  1011.5 219.6 %all-reduce.30.cloned.1.call-start = ((), (), s32[]{:S(2)}) async-start(), calls=%async_computation.12 | async-start | bytes 786432 | tf_op jit(solution)/shard_map/psum | solution.py:221
  1056.0 211.8 %reduce-scatter.19.cloned.1.call-start = ((), (), s32[]{:S(2)}) async-start(), calls=%async_computation.14 | async-start | bytes 6553600
  1088.5 233.1 %reduce-scatter.21.cloned.1.call-start = ((), (), s32[]{:S(2)}) async-start(), calls=%async_computation.15 | async-start | bytes 6553600
  1125.2 9.3 copy-start.18
  1134.6 11.6 copy-start.11
  1162.2 286.1 %reduce-scatter.15.cloned.1.call-start = ((), (), s32[]{:S(2)}) async-start(), calls=%async_computation.10 | async-start | bytes 7372800 | tf_op jit(solution)/shard_map/reduce_scatter | solution.py:109
  1173.5 399.1 %reduce-scatter.17.cloned.1.call-start = ((), (), s32[]{:S(2)}) async-start(), calls=%async_computation.11 | async-start | bytes 7372800 | tf_op jit(solution)/shard_map/reduce_scatter | solution.py:109
  1186.2 40.6 %copy-start.75 = (f32[20]{0:T(128)S(1)}, f32[20]{0:T(128)}, u32[]{:S(2)}) copy-start(f32[20]{0:T(128)} %param.32) | copy-start | bytes 244
  1186.2 44.1 %copy-start.21 = (bf16[320,276]{1,0:T(8,128)(2,1)S(1)}, bf16[320,276]{1,0:T(8,128)(2,1)}, u32[]{:S(2)}) copy-start(bf16[320,276]{1,0:T(8,128)(2,1)} %reduce-scatter.23.cloned.1.call-done) | copy-start | bytes 529924
  1230.3 95.5 %copy-start.65 = (f32[1280]{0:T(1024)S(1)}, f32[1280]{0:T(1024)}, u32[]{:S(2)}) copy-start(f32[1280]{0:T(1024)} %get-tuple-element.875) | copy-start | bytes 15364
  1230.3 95.6 %copy-start.71 = (f32[20]{0:T(128)S(1)}, f32[20]{0:T(128)}, u32[]{:S(2)}) copy-start(f32[20]{0:T(128)} %get-tuple-element.961) | copy-start | bytes 244
  1230.3 142.0 %copy-start.16 = (bf16[1024,640]{1,0:T(8,128)(2,1)S(1)}, bf16[1024,640]{1,0:T(8,128)(2,1)}, u32[]{:S(2)}) copy-start(bf16[1024,640]{1,0:T(8,128)(2,1)} %param.37) | copy-start | bytes 3932164
  1230.3 142.0 %copy-start.51 = (f32[1024]{0:T(1024)S(1)}, f32[1024]{0:T(1024)}, u32[]{:S(2)}) copy-start(f32[1024]{0:T(1024)} %get-tuple-element.1013) | copy-start | bytes 12292
  (78 other events, 416.2 us)
Sparse Core Ops, SparseCore 0:
  10.2 104.9 all-gather.6
  118.0 43.4 all-gather.14
  163.6 101.1 all-gather.8
  266.3 38.5 all-gather.12
  306.9 102.1 all-gather.10
  989.5 64.5 reduce-scatter.22
  1058.2 120.5 reduce-scatter.24
  1181.7 31.9 all-reduce.29
  1216.4 51.3 reduce-scatter.18
  1270.2 51.3 reduce-scatter.20
  1325.7 122.5 reduce-scatter.14
  1451.8 120.7 reduce-scatter.16

commit v2 on v1

v2 whole, which is shorter than its diff:
```python
import functools

import jax
import jax.numpy as jnp
from jax import lax
from jax.experimental import pallas as pl
from jax.experimental.pallas import tpu as pltpu
from jax.sharding import PartitionSpec as P

INNER = 5120
SPAN = 128
LANES = 128
HALF = 64
LOG2E = 1.4426950408889634
VMEM_BYTES = 56 * 1024 * 1024

epsilon = 1e-05
highest = lax.Precision.HIGHEST
low = jnp.bfloat16
wide = jnp.float32


def dot(left, right, precision=None):
    return jnp.dot(left, right, preferred_element_type=wide, precision=precision)


def contract_rows(left, right, precision=None):
    return lax.dot_general(
        left, right, (((0,), (0,)), ((), ())), preferred_element_type=wide, precision=precision
    )


def contract_cols(left, right, precision=None):
    return lax.dot_general(
        left, right, (((1,), (1,)), ((), ())), preferred_element_type=wide, precision=precision
    )


def sigmoid(v):
    return 1.0 / (1.0 + jnp.exp(-v))


def softplus(v):
    return jnp.maximum(v, 0.0) + jnp.log1p(jnp.exp(-jnp.abs(v)))


def conv_in(v, taps, bias, masks):
    total = bias + taps[0:1] * v
    for k in range(1, 4):
        total = total + taps[k : k + 1] * (pltpu.roll(v, k, 0) * masks[k - 1])
    return total


def conv_back(grad, v, taps, masks):
    rows = grad.shape[0]
    back = taps[0:1] * grad
    sums = [jnp.sum(grad * v, axis=0, keepdims=True)]
    for k in range(1, 4):
        kept = grad * masks[k - 1]
        sums.append(jnp.sum(kept * pltpu.roll(v, k, 0), axis=0, keepdims=True))
        back = back + taps[k : k + 1] * pltpu.roll(kept, rows - k, 0)
    sums.append(jnp.sum(grad, axis=0, keepdims=True))
    return back, sums


def visible_block(seg_col, seg_row, row_is_query):
    shape = (SPAN, SPAN)
    first = lax.broadcasted_iota(jnp.int32, shape, 0)
    second = lax.broadcasted_iota(jnp.int32, shape, 1)
    ordered = (first >= second) if row_is_query else (first <= second)
    return ordered & (seg_col == seg_row)


def lower_triangle():
    shape = (SPAN, SPAN)
    return (
        lax.broadcasted_iota(jnp.int32, shape, 0) >= lax.broadcasted_iota(jnp.int32, shape, 1)
    ).astype(wide)


def prep_kernel(
    state_ref, step_ref, taps_ref, bias_ref, step_bias_ref, rate_ref, masks_ref, seg_col_ref,
    seg_row_ref, b_ref, c_ref, bt_ref, ct_ref, g_ref, gt_ref, dtx_ref, cumx_ref, cumt_ref,
):
    rows, states = b_ref.shape
    masks = [masks_ref[k] for k in range(3)]
    for part, (out, out_t) in enumerate(((b_ref, bt_ref), (c_ref, ct_ref))):
        cols = slice(part * states, (part + 1) * states)
        pre = conv_in(state_ref[:, cols], taps_ref[:, cols], bias_ref[:, cols], masks)
        act = pre * sigmoid(pre)
        out[...] = act.astype(low)
        out_t[...] = act.T.astype(low)
    step = softplus(step_ref[...] + step_bias_ref[...])
    triangle = lower_triangle()
    heads = lax.broadcasted_iota(jnp.int32, (LANES, dtx_ref.shape[1]), 0)
    channels = lax.broadcasted_iota(jnp.int32, (LANES, dtx_ref.shape[1]), 1)
    expand = (channels // HALF == heads).astype(wide)
    rate = step * (rate_ref[...] * LOG2E)
    for c in range(rows // SPAN):
        at = slice(c * SPAN, (c + 1) * SPAN)
        grams = dot(c_ref[at], bt_ref[:, at])
        g_ref[at] = jnp.where(visible_block(seg_col_ref[at], seg_row_ref[:, at], True), grams, 0.0)
        grams_t = dot(b_ref[at], ct_ref[:, at])
        gt_ref[at] = jnp.where(
            visible_block(seg_col_ref[at], seg_row_ref[:, at], False), grams_t, 0.0
        )
        total = dot(triangle, rate[at], highest)
        cumx_ref[at] = dot(total, expand, highest)
        dtx_ref[at] = dot(step[at], expand, highest)
        cumt_ref[:, at] = total.T


def decays(cumx_ref, cumt_ref, at, head, row_is_query):
    lane = head * HALF
    column = cumx_ref[at, lane : lane + 1]
    row = cumt_ref[0, head : head + 1, at]
    gap = (column - row) if row_is_query else (row - column)
    return jnp.exp2(jnp.minimum(gap, 0.0))


def split_heads(block):
    left = lax.broadcasted_iota(jnp.int32, block.shape, 1) < HALF
    zero = jnp.zeros_like(block)
    return jnp.concatenate([jnp.where(left, block, zero), jnp.where(left, zero, block)], 0)


def fwd_kernel(
    value_ref, taps_ref, bias_ref, skip_ref, dtx_ref, cumx_ref, cumt_ref, masks_ref, c_ref, bt_ref,
    g_ref, out_ref, x_scr,
):
    rows = value_ref.shape[0]
    masks = [masks_ref[k] for k in range(3)]
    pre = conv_in(value_ref[...], taps_ref[...], bias_ref[...], masks)
    x_scr[...] = pre * sigmoid(pre)
    state = jnp.zeros((c_ref.shape[1], LANES), wide)
    for c in range(rows // SPAN):
        at = slice(c * SPAN, (c + 1) * SPAN)
        x = x_scr[at]
        cum = cumx_ref[at]
        stepped = x * dtx_ref[at]
        mixing = jnp.concatenate(
            [decays(cumx_ref, cumt_ref, at, head, True) * g_ref[at] for head in (0, 1)], 1
        ).astype(low)
        y = dot(mixing, split_heads(stepped.astype(low)))
        if c > 0:
            y = y + dot(c_ref[at], state.astype(low)) * (jnp.exp2(cum) * masks_ref[3, at])
        out_ref[at] = y + skip_ref[...] * x
        if c + 1 < rows // SPAN:
            end = slice((c + 1) * SPAN - 1, (c + 1) * SPAN)
            last = cum[SPAN - 1 : SPAN]
            tail = jnp.exp2(last - cum) * masks_ref[4, at]
            fresh = dot(bt_ref[:, at], (stepped.astype(low) * tail).astype(low))
            state = (masks_ref[3, end] * jnp.exp2(last)) * state + fresh


def bwd_kernel(
    value_ref, mixed_ref, grad_ref, taps_ref, bias_ref, skip_ref, dtx_ref, cumx_ref, cumt_ref,
    masks_ref, b_ref, c_ref, bt_ref, ct_ref, gt_ref,
    value_out, sums_out, db_ref, dc_ref, dg_ref, z_ref, dt_ref,
    pre_scr, x_scr, dpre_scr, state_scr,
):
    rows = value_ref.shape[0]
    blocks = rows // SPAN
    pair = pl.program_id(0)
    masks = [masks_ref[k] for k in range(3)]

    @pl.when(pair == 0)
    def _():
        for ref in (db_ref, dc_ref, dg_ref, z_ref, dt_ref):
            ref[...] = jnp.zeros_like(ref)

    pre = conv_in(value_ref[...], taps_ref[...], bias_ref[...], masks)
    pre_scr[...] = pre
    x_scr[...] = pre * sigmoid(pre)
    state = jnp.zeros((c_ref.shape[1], LANES), wide)
    for c in range(blocks):
        at = slice(c * SPAN, (c + 1) * SPAN)
        state_scr[c] = state
        if c + 1 < blocks:
            end = slice((c + 1) * SPAN - 1, (c + 1) * SPAN)
            cum = cumx_ref[at]
            last = cum[SPAN - 1 : SPAN]
            tail = jnp.exp2(last - cum) * masks_ref[4, at]
            stepped = (x_scr[at] * dtx_ref[at]).astype(low)
            fresh = dot(bt_ref[:, at], (stepped * tail).astype(low))
            state = (masks_ref[3, end] * jnp.exp2(last)) * state + fresh

    lanes = lax.broadcasted_iota(jnp.int32, (LANES, LANES), 0)
    heads = lax.broadcasted_iota(jnp.int32, (LANES, LANES), 1)
    gather = (lanes // HALF + 2 * pair == heads).astype(low)
    row_number = lax.broadcasted_iota(jnp.int32, (SPAN, LANES), 0)
    grad_skip = jnp.zeros((1, LANES), wide)
    grad_state = jnp.zeros((c_ref.shape[1], LANES), wide)
    for c in reversed(range(blocks)):
        at = slice(c * SPAN, (c + 1) * SPAN)
        end = slice((c + 1) * SPAN - 1, (c + 1) * SPAN)
        x = x_scr[at]
        dtx = dtx_ref[at]
        cum = cumx_ref[at]
        grad = grad_ref[at]
        grad_low = grad.astype(low)
        stepped = (x * dtx).astype(low)
        y = mixed_ref[at] - skip_ref[...] * x
        grad_mix = contract_cols(split_heads(stepped), grad_low)
        mixing = []
        grams = dg_ref[at]
        for head in (0, 1):
            decay = decays(cumx_ref, cumt_ref, at, head, False)
            mixing.append((decay * gt_ref[at]).astype(low))
            grams = grams + decay * grad_mix[head * SPAN : (head + 1) * SPAN]
        dg_ref[at] = grams
        grad_stepped = dot(jnp.concatenate(mixing, 1), split_heads(grad_low))
        last = cum[SPAN - 1 : SPAN]
        at_end = jnp.zeros((1, LANES), wide)
        carry = masks_ref[3, end] * jnp.exp2(last)
        if c + 1 < blocks:
            tail = jnp.exp2(last - cum) * masks_ref[4, at]
            grad_state_low = grad_state.astype(low)
            from_tail = dot(b_ref[at], grad_state_low) * tail
            grad_stepped = grad_stepped + from_tail
            db_ref[at] += contract_cols((stepped * tail).astype(low), grad_state_low)
            at_end = jnp.sum(stepped.astype(wide) * from_tail, axis=0, keepdims=True)
            at_end = at_end + carry * jnp.sum(state_scr[c] * grad_state, axis=0, keepdims=True)
        if c > 0:
            reach = (grad * (jnp.exp2(cum) * masks_ref[3, at])).astype(low)
            dc_ref[at] += contract_cols(reach, state_scr[c].astype(low))
            grad_state = carry * grad_state + dot(ct_ref[:, at], reach)
        z = grad_low.astype(wide) * y - stepped.astype(wide) * grad_stepped
        z = z + jnp.where(row_number == SPAN - 1, at_end, 0.0)
        z_high = z.astype(low)
        z_low = (z - z_high.astype(wide)).astype(low)
        z_ref[at] += dot(z_high, gather) + dot(z_low, gather)
        dt_ref[at] += dot((x * grad_stepped).astype(low), gather)
        grad_skip = grad_skip + jnp.sum(grad * x, axis=0, keepdims=True)
        pre_c = pre_scr[at]
        opened = sigmoid(pre_c)
        grad_x = grad_stepped * dtx + skip_ref[...] * grad
        dpre_scr[at] = grad_x * opened * (1.0 + pre_c * (1.0 - opened))

    back, sums = conv_back(dpre_scr[...], value_ref[...], taps_ref[...], masks)
    value_out[...] = back.astype(low)
    sums_out[...] = jnp.concatenate(sums + [grad_skip, jnp.zeros((2, LANES), wide)], 0)


def post_kernel(
    state_ref, step_ref, taps_ref, bias_ref, step_bias_ref, rate_ref, masks_ref, seg_col_ref,
    seg_row_ref, b_ref, c_ref, db_ref, dc_ref, dg_ref, z_ref, dt_ref,
    state_out, step_out, state_sums, step_sums, act_scr,
):
    rows, states = b_ref.shape
    masks = [masks_ref[k] for k in range(3)]
    triangle = lower_triangle()
    for c in range(rows // SPAN):
        at = slice(c * SPAN, (c + 1) * SPAN)
        seen = visible_block(seg_col_ref[at], seg_row_ref[:, at], False)
        grams = jnp.where(seen, dg_ref[at], 0.0)
        act_scr[0, at] = db_ref[at] + dot(grams.astype(low), c_ref[at])
        act_scr[1, at] = dc_ref[at] + dot(grams.T.astype(low), b_ref[at])
    for part in (0, 1):
        cols = slice(part * states, (part + 1) * states)
        v = state_ref[:, cols]
        pre = conv_in(v, taps_ref[:, cols], bias_ref[:, cols], masks)
        opened = sigmoid(pre)
        grad = act_scr[part] * opened * (1.0 + pre * (1.0 - opened))
        back, sums = conv_back(grad, v, taps_ref[:, cols], masks)
        state_out[:, cols] = back.astype(low)
        state_sums[:, cols] = jnp.concatenate(sums + [jnp.zeros((3, states), wide)], 0)
    pre = step_ref[...] + step_bias_ref[...]
    step = softplus(pre)
    rate_sum = jnp.zeros((1, LANES), wide)
    bias_sum = jnp.zeros((1, LANES), wide)
    for c in range(rows // SPAN):
        at = slice(c * SPAN, (c + 1) * SPAN)
        grad_rate = contract_rows(triangle, z_ref[at], highest)
        grad_step = (dt_ref[at] + rate_ref[...] * grad_rate) * sigmoid(pre[at])
        step_out[at] = grad_step.astype(low)
        rate_sum = rate_sum + jnp.sum(
            grad_rate * (rate_ref[...] * step[at]), axis=0, keepdims=True
        )
        bias_sum = bias_sum + jnp.sum(grad_step, axis=0, keepdims=True)
    step_sums[...] = jnp.concatenate([bias_sum, rate_sum, jnp.zeros((6, LANES), wide)], 0)


def call(kernel, outs, operands, grid=None, in_specs=None, out_specs=None, scratch=(), flops=0):
    shapes = tuple(jax.ShapeDtypeStruct(shape, kind) for shape, kind in outs)
    moved = sum(a.size * a.dtype.itemsize for a in operands)
    moved += sum(s.size * s.dtype.itemsize for s in shapes)
    extra = {} if grid is None else dict(grid=grid, in_specs=in_specs, out_specs=out_specs)
    return pl.pallas_call(
        kernel,
        out_shape=shapes,
        scratch_shapes=list(scratch),
        compiler_params=pltpu.CompilerParams(vmem_limit_bytes=VMEM_BYTES),
        cost_estimate=pl.CostEstimate(flops=flops, bytes_accessed=moved, transcendentals=0),
        **extra,
    )(*operands)


def column_block(rows):
    return pl.BlockSpec((rows, LANES), lambda i: (0, i))


def whole_block(shape):
    return pl.BlockSpec(shape, lambda i: (0,) * len(shape))


def lane_pad(v):
    return jnp.pad(v, ((0, 0), (0, LANES - v.shape[1])))


class Mixer:
    def __init__(
        self, state_in, step_in, conv_state, conv_state_bias, step_bias, decay_log, segments
    ):
        rows = state_in.shape[0]
        self.rows = rows
        self.head_count = step_bias.shape[0]
        self.pairs = (self.head_count + 1) // 2
        self.width = self.pairs * LANES
        self.states = conv_state.shape[1] // 2
        self.blocks = rows // SPAN
        before = [
            jnp.concatenate([jnp.full((k,), -1, jnp.int32), segments[: rows - k]]) == segments
            for k in (1, 2, 3)
        ]
        ends = segments.reshape(self.blocks, SPAN)[:, SPAN - 1]
        previous = jnp.concatenate([jnp.full((1,), -1, jnp.int32), ends[:-1]])
        carried = jnp.repeat(previous, SPAN) == segments
        tail = jnp.repeat(ends, SPAN) == segments
        flags = jnp.stack(before + [carried, tail]).astype(wide)
        self.masks = jnp.broadcast_to(flags[:, :, None], (5, rows, LANES))
        self.shared = (
            state_in,
            lane_pad(step_in),
            conv_state,
            conv_state_bias[None],
            lane_pad(step_bias[None]),
            lane_pad(-jnp.exp(decay_log)[None]),
            self.masks,
            segments[:, None],
            segments[None],
        )
        (
            self.b, self.c, self.bt, self.ct, self.g, self.gt, self.dtx, self.cumx, cumt,
        ) = call(
            prep_kernel,
            [((rows, self.states), low)] * 2
            + [((self.states, rows), low)] * 2
            + [((rows, SPAN), wide)] * 2
            + [((rows, self.width), wide)] * 2
            + [((LANES, rows), wide)],
            self.shared,
            flops=12 * rows * LANES * self.width,
        )
        self.cumt = cumt[: 2 * self.pairs].reshape(self.pairs, 2, rows)

    def widen(self, v):
        return jnp.pad(v, ((0, 0), (0, self.width - v.shape[1])))

    def forward(self, value_in, conv_value, conv_value_bias, skip_scale):
        rows, states = self.rows, self.states
        self.inner = value_in.shape[1]
        self.value = (
            self.widen(value_in),
            self.widen(conv_value),
            self.widen(conv_value_bias[None]),
            self.widen(jnp.repeat(skip_scale, HALF)[None]),
        )
        (mixed,) = call(
            fwd_kernel,
            [((rows, self.width), wide)],
            self.value + (self.dtx, self.cumx, self.cumt, self.masks, self.c, self.bt, self.g),
            grid=(self.pairs,),
            in_specs=[
                column_block(rows),
                column_block(4),
                column_block(1),
                column_block(1),
                column_block(rows),
                column_block(rows),
                pl.BlockSpec((1, 2, rows), lambda i: (i, 0, 0)),
                whole_block((5, rows, LANES)),
                whole_block((rows, states)),
                whole_block((states, rows)),
                whole_block((rows, SPAN)),
            ],
            out_specs=[column_block(rows)],
            scratch=[pltpu.VMEM((rows, LANES), wide)],
            flops=20 * rows * LANES * self.width,
        )
        self.mixed = mixed
        return mixed[:, : self.inner]

    def backward(self, grad_mixed):
        rows, states = self.rows, self.states
        value_grad, sums, db, dc, dg, z, dt = call(
            bwd_kernel,
            [((rows, self.width), low), ((8, self.width), wide)]
            + [((rows, LANES), wide)] * 5,
            (self.value[0], self.mixed, self.widen(grad_mixed))
            + self.value[1:]
            + (self.dtx, self.cumx, self.cumt, self.masks, self.b, self.c, self.bt, self.ct)
            + (self.gt,),
            grid=(self.pairs,),
            in_specs=[
                column_block(rows),
                column_block(rows),
                column_block(rows),
                column_block(4),
                column_block(1),
                column_block(1),
                column_block(rows),
                column_block(rows),
                pl.BlockSpec((1, 2, rows), lambda i: (i, 0, 0)),
                whole_block((5, rows, LANES)),
                whole_block((rows, states)),
                whole_block((rows, states)),
                whole_block((states, rows)),
                whole_block((states, rows)),
                whole_block((rows, SPAN)),
            ],
            out_specs=[column_block(rows), column_block(8)] + [whole_block((rows, LANES))] * 5,
            scratch=[pltpu.VMEM((rows, LANES), wide)] * 3
            + [pltpu.VMEM((self.blocks, states, LANES), wide)],
            flops=60 * rows * LANES * self.width,
        )
        state_grad, step_grad, state_sums, step_sums = call(
            post_kernel,
            [
                ((rows, 2 * states), low),
                ((rows, LANES), low),
                ((8, 2 * states), wide),
                ((8, LANES), wide),
            ],
            self.shared + (self.b, self.c, db, dc, dg, z, dt),
            scratch=[pltpu.VMEM((2, rows, states), wide)],
            flops=12 * rows * LANES * self.width,
        )
        heads = self.head_count
        skip_grad = sums[5, : self.inner].reshape(heads, HALF).sum(axis=1)
        return (
            value_grad[:, : self.inner],
            state_grad,
            step_grad[:, :heads],
            sums[:4, : self.inner],
            sums[4, : self.inner],
            state_sums[:4],
            state_sums[4],
            step_sums[0, :heads],
            step_sums[1, :heads],
            skip_grad,
        )


def scatter_rows(partial):
    return lax.psum_scatter(
        partial.astype(jnp.bfloat16), "gx", scatter_dimension=0, tiled=True
    ).astype(jnp.float32)


def on_device(
    layer_input,
    norm_gain,
    gate_weight,
    value_weight,
    state_weight,
    step_weight,
    conv_value,
    conv_value_bias,
    conv_state,
    conv_state_bias,
    step_bias,
    decay_log,
    skip_scale,
    gated_gain,
    out_weight,
    segment_ids,
    cotangent,
):
    model_width = layer_input.shape[1]
    col_width = cotangent.shape[1]
    state_cols = state_weight.shape[1]
    col_start = lax.axis_index("gy") * col_width

    full_value = lax.all_gather(value_weight, "gx", axis=0, tiled=True)
    full_state = lax.all_gather(
        jnp.concatenate([state_weight, step_weight], 1), "gx", axis=0, tiled=True
    )
    gate_weight, full_value = lax.optimization_barrier((gate_weight, full_value))
    full_gate = lax.all_gather(gate_weight, "gx", axis=0, tiled=True)
    out_rows, full_gate = lax.optimization_barrier((out_weight.T, full_gate))
    full_out = lax.all_gather(out_rows, "gx", axis=0, tiled=True)
    upstream = lax.all_gather(cotangent, "gy", axis=1, tiled=True)

    tokens = layer_input.astype(jnp.float32)
    scale_in = lax.rsqrt(jnp.mean(tokens * tokens, axis=1, keepdims=True) + epsilon)
    normed = (tokens * scale_in * norm_gain).astype(jnp.bfloat16)

    value_in = jnp.dot(normed, full_value, preferred_element_type=jnp.float32)
    state_step = jnp.dot(normed, full_state, preferred_element_type=jnp.float32)
    mixer = Mixer(
        state_step[:, :state_cols],
        state_step[:, state_cols:],
        conv_state,
        conv_state_bias,
        step_bias,
        decay_log,
        segment_ids,
    )
    mixed = mixer.forward(value_in, conv_value, conv_value_bias, skip_scale)
    gate_in = jnp.dot(normed, full_gate, preferred_element_type=jnp.float32)
    gate_open = jax.nn.sigmoid(gate_in)
    gate_act = gate_in * gate_open
    gated = mixed * gate_act
    squares = lax.psum(jnp.sum(gated * gated, axis=1), "gy")
    scale_out = lax.rsqrt(squares / INNER + epsilon)[:, None]
    scaled = (gated * gated_gain).astype(jnp.bfloat16)

    scaled_out = (gated * gated_gain * scale_out).astype(jnp.bfloat16)
    grad_out = scatter_rows(contract_rows(upstream, scaled_out))

    up_back = jnp.dot(upstream, full_out, preferred_element_type=jnp.float32)
    grad_scale = lax.psum(jnp.sum(gated * gated_gain * up_back, axis=1), "gy")[:, None]
    grad_scaled = scale_out * up_back
    grad_gated = grad_scaled * gated_gain - grad_scale * scale_out**3 * gated / INNER
    gate_gain_part = jnp.sum(grad_scaled * gated, axis=0)
    grad_gate_in = (
        grad_gated * mixed * gate_open * (1.0 + gate_in * (1.0 - gate_open))
    ).astype(jnp.bfloat16)
    grad_gate = scatter_rows(contract_rows(normed, grad_gate_in))

    pulled = mixer.backward(grad_gated * gate_act)
    grad_value_in = pulled[0]
    grad_state_in = jnp.concatenate([pulled[1], pulled[2]], 1)
    grad_state_step = scatter_rows(contract_rows(normed, grad_state_in))
    grad_value = scatter_rows(contract_rows(normed, grad_value_in))

    product = lax.psum_scatter(
        (contract_cols(scaled, full_out) * scale_out).astype(jnp.bfloat16),
        "gy",
        scatter_dimension=1,
        tiled=True,
    )
    token_cols = lax.dynamic_slice_in_dim(layer_input, col_start, col_width, 1).astype(jnp.float32)
    layer_output = (token_cols + product.astype(jnp.float32)).astype(jnp.bfloat16)

    grad_normed_part = (
        contract_cols(grad_gate_in, full_gate)
        + contract_cols(grad_value_in, full_value)
        + contract_cols(grad_state_in, full_state)
    )
    grad_normed = lax.psum_scatter(
        grad_normed_part.astype(jnp.bfloat16), "gy", scatter_dimension=1, tiled=True
    ).astype(jnp.float32)
    gain_cols = lax.dynamic_slice_in_dim(norm_gain, col_start, col_width, 0)
    weighted = grad_normed * gain_cols
    inner_dot = lax.psum(jnp.sum(weighted * token_cols, axis=1), "gy")[:, None]
    grad_input = (
        cotangent.astype(jnp.float32)
        + scale_in * weighted
        - token_cols * scale_in**3 * inner_dot / model_width
    )
    norm_gain_part = jnp.sum(grad_normed * token_cols * scale_in, axis=0)
    conv_state_sum, conv_bias_sum = lax.psum((pulled[5], pulled[6]), ("gx", "gy"))
    grad_state = lax.psum(grad_state_step[:, :state_cols], "gy")
    small_sums = lax.psum(
        (norm_gain_part, gate_gain_part, pulled[3], pulled[4], pulled[7], pulled[8], pulled[9]),
        "gx",
    )
    return (
        layer_output,
        grad_input,
        small_sums[0],
        grad_gate,
        grad_value,
        grad_state,
        grad_state_step[:, state_cols:],
        small_sums[2],
        small_sums[3],
        conv_state_sum,
        conv_bias_sum,
        small_sums[4],
        small_sums[5],
        small_sums[6],
        small_sums[1],
        grad_out.T,
    )


def solution(mesh):
    return jax.shard_map(
        on_device,
        mesh=mesh,
        in_specs=(
            P("gx", None),
            P(),
            P("gx", "gy"),
            P("gx", "gy"),
            P("gx", None),
            P("gx", "gy"),
            P(None, "gy"),
            P("gy"),
            P(),
            P(),
            P("gy"),
            P("gy"),
            P("gy"),
            P("gy"),
            P("gy", "gx"),
            P("gx"),
            P("gx", "gy"),
        ),
        out_specs=(
            P("gx", "gy"),
            P("gx", "gy"),
            P("gy"),
            P("gx", "gy"),
            P("gx", "gy"),
            P("gx", None),
            P("gx", "gy"),
            P(None, "gy"),
            P("gy"),
            P(),
            P(),
            P("gy"),
            P("gy"),
            P("gy"),
            P("gy"),
            P("gy", "gx"),
        ),
        check_vma=False,
    )
```

time: 1600 us -> 1090 us (0.68)
  local copies, waits for them, and re-layouts: 484 us -> 63.5 us
  matrix products: 310 us -> 126 us
  waiting for transfers between devices: 512 us -> 669 us
  other arithmetic: 149 us -> 30.6 us
  Pallas kernels: 0 us -> 78.3 us
    dynamic_update_slice x36 -> x0, local copies, waits for them, and re-layouts: 268 us -> none  [ssm_mixer(): finished, outputs = lax.scan(jax.checkpoint(group_step), initial, inputs)]
    dot_general x56 -> x0, matrix products: 184 us -> none  [the longest x12 89.6 us: group_step(): within = jnp.einsum('hts,shp->thp', mixing, x_block, precision=highest)]
    pallas_call x0 -> x4, Pallas kernels: none -> 78.3 us  [call(): pl.pallas_call(kernel, out_shape=shapes, scratch_shapes=list(scratch), co...]
    all_gather x1, waiting for transfers between devices: 0.02 us -> 62.1 us  [on_device(): full_out = lax.all_gather(out_rows, 'gx', axis=0, tiled=True)]
    all_gather x1, waiting for transfers between devices: 46.7 us -> 99.4 us  [on_device(): full_gate = lax.all_gather(gate_weight, 'gx', axis=0, tiled=True)]
    reduce_sum x13 -> x1, other arithmetic: 49.9 us -> 0.12 us  [backward(): skip_grad = sums[5, :self.inner].reshape(heads, HALF).sum(axis=1)]
    another operation x70 -> x8, local copies, waits for them, and re-layouts: 31.7 us -> 0.83 us  [the longest x1 0.67 us: forward(): jnp.repeat(skip_scale, HALF)[None]]
    reshape x17 -> x1, local copies, waits for them, and re-layouts: 31.3 us -> 0.67 us  [__init__(): self.cumt = cumt[:2 * self.pairs].reshape(self.pairs, 2, rows)]
  transfers between devices with their start and end apart: 12 -> 12, of which waited for: 8 -> 10; matrix products, arithmetic and copies ran while one was open for 30% -> 17% of each run, Pallas kernels for 0% -> 3%
where the time goes in v2:
time: 1090 us; the launch traced here: 1080 us
  waiting for transfers between devices  669 us (61%)
  matrix products  126 us (12%)
  blocking collectives  102 us (9%)
  Pallas kernels  78.3 us (7%)
  local copies, waits for them, and re-layouts  63.5 us (6%)
  other arithmetic  30.6 us (3%)
  between operations  14.7 us (1%)
    reduce_scatter x2, waiting for transfers between devices, scatter_rows(): lax.psum_scatter(partial.astype(jnp.bfloat16), 'gx', scatter_dimension=0,...  194 us
    unnamed x16, waiting for transfers between devices  148 us
    all_gather x1, waiting for transfers between devices, on_device(): full_value = lax.all_gather(value_weight, 'gx', axis=0, tiled=True)  107 us
    all_gather x1, waiting for transfers between devices, on_device(): full_gate = lax.all_gather(gate_weight, 'gx', axis=0, tiled=True)  99.4 us
    pallas_call x4, Pallas kernels, call(): pl.pallas_call(kernel, out_shape=shapes, scratch_shapes=list(scratch), co...  78.3 us
    all_gather x1, waiting for transfers between devices, on_device(): full_out = lax.all_gather(out_rows, 'gx', axis=0, tiled=True)  62.1 us
    unnamed x45, local copies, waits for them, and re-layouts  46.6 us
    psum x1, blocking collectives, on_device(): lax.psum((pulled[5], pulled[6]), ('gx', 'gy'))  42.7 us
  transfers between devices with their start and end apart: 12, of which 10 were waited for; matrix products, arithmetic and copies ran while one was open for 17% of the time, Pallas kernels for 3%

profile of v2, /device:TPU:0, one launch (start us, length us, event | category | flops | bytes accessed | tf_op | source)
XLA Modules:
  0.0 1084.2 jit_solution(7903561246538166984)
XLA Ops:
  8.0 107.2 %all-gather.7.cloned.1.call-done = bf16[2560,1280]{1,0:T(8,128)(2,1)} async-done(((bf16[320,1280]{1,0:T(8,128)(2,1)}), bf16[2560,1280]{1,0:T(8,128)(2,1)}) %all-gather.7.cloned.1.call-update) | async-done | bytes 6553616 | tf_op jit(solution)/shard_map/all_gather | solution.py:485
  115.3 1.1 copy.63
  116.3 1.4 maximum_bitcast_fusion
  118.4 99.4 %all-gather.9.cloned.1.call-done = bf16[2560,1280]{1,0:T(8,128)(2,1)} async-done(((bf16[320,1280]{1,0:T(8,128)(2,1)}), bf16[2560,1280]{1,0:T(8,128)(2,1)}) %all-gather.9.cloned.1.call-update) | async-done | bytes 6553616 | tf_op jit(solution)/shard_map/all_gather | solution.py:490
  217.9 1.2 pad.14.step_bias_ref
  220.2 0.9 slice_reduce_fusion.3
  221.2 0.9 slice_reduce_fusion.2
  222.1 0.9 bitcast_compare_fusion
  223.0 1.3 broadcast_in_dim.18.bias_ref
  225.8 1.7 copy.67.seg_col_ref
  227.5 3.6 fusion
  231.7 32.3 %all-gather.15.cloned.1.call-done = bf16[8,320,276]{1,2,0:T(8,128)(2,1)} async-done(((bf16[1,320,276]{1,2,0:T(8,128)(2,1)}), bf16[8,320,276]{1,2,0:T(8,128)(2,1)}) %all-gather.15.cloned.1.call-update) | async-done | bytes 1413136 | tf_op jit(solution)/shard_map/all_gather | solution.py:486
  264.0 1.7 copy.64
  265.7 1.2 reshape.115
  267.0 5.2 fusion.28
  272.2 1.1 slice.77.state_ref
  273.3 0.8 pad.13.step_ref
  274.1 1.9 broadcast_in_dim.47.masks_ref
  276.0 17.6 %shard_map.288 = (bf16[1024,128]{1,0:T(8,128)(2,1)}, bf16[1024,128]{1,0:T(8,128)(2,1)}, bf16[128,1024]{1,0:T(8,128)(2,1)}, bf16[128,1024]{1,0:T(8,128)(2,1)}, f3...) custom-call(f32[1024,256]{1,0:T(8,128)} %slice.77.state_ref, ...), custom_call_target="tpu_custom_call" | custom-call | flops 2013265920 | bytes 17315840 | tf_op jit(solution)/shard_map/pallas_call | solution.py:289
  293.6 0.9 slice.66
  295.1 12.9 %fusion.30.value_ref = f32[1024,1280]{1,0:T(8,128)} fusion(bf16[2560,1280]{1,0:T(8,128)(2,1)} %all-gather.7.cloned.1.call-done, bf16[1024,2560]{1,0:T(8,128)(2,1)} %param.17, f32[2560]{0:T(1024)S(1)} %copy-done.10, f32[1024]{0:T(1024)S(1)} %get-tuple-element.168), kind=kOutput, calls=%fused_computation.67 | convolution fusion | flops 6721372160 | bytes 17053696 | tf_op jit(solution)/shard_map/dot_general | solution.py:499
  308.0 18.3 %shard_map.289.mixed_ref = f32[1024,1280]{1,0:T(8,128)} custom-call(f32[1024,1280]{1,0:T(8,128)} %fusion.30.value_ref, f32[4,1280]{1,0:T(4,128)} %taps_ref.6, f32[1,1280]{1,0:T(1,128)} %broadcast_in_dim.18.bias_ref, f32[1,1280]{1,0:T(1,128)} %broadcast_in_dim_reshape.3.skip_ref, f32[1024,1280]{1,0:T(8,128)} %get-tuple-element.41.dtx_ref, ...), custom_call_target="tpu_custom_call" | custom-call | flops 3355443200 | bytes 24754176 | tf_op jit(solution)/shard_map/pallas_call | solution.py:289
  326.4 14.2 %multiply_reduce_fusion.1 = (f32[1024]{0:T(1024)S(1)}, f32[1024,1280]{1,0:T(8,128)}, f32[1024,1280]{1,0:T(8,128)}) fusion(f32[1024,1280]{1,0:T(8,128)} %shard_map.289.mixed_ref, bf16[2560,1280]{1,0:T(8,128)(2,1)} %all-gather.9.cloned.1.call-done, bf16[1024,2560]{1,0:T(8,128)(2,1)S(1)} %bitcast.65, f32[2560]{0:T(1024)S(1)} %copy-done.10, ...), kind=kOutput, calls=%fused_computation.18 | convolution fusion | flops 6730546176 | bytes 27543552 | tf_op jit(solution)/shard_map/dot_general | solution.py:511
  340.6 6.4 psum.91
  347.0 62.1 %all-gather.11.cloned.1.call-done = bf16[2560,1280]{1,0:T(8,128)(2,1)} async-done(((bf16[320,1280]{1,0:T(8,128)(2,1)}), bf16[2560,1280]{1,0:T(8,128)(2,1)}) %all-gather.11.cloned.1.call-update) | async-done | bytes 6553616 | tf_op jit(solution)/shard_map/all_gather | solution.py:492
  409.2 13.3 %multiply_reduce_fusion = (f32[1280]{0:T(1024)S(1)}, f32[1024]{0:T(1024)S(1)}, f32[1280,1024]{0,1:T(8,128)}) fusion(f32[1024,1280]{1,0:T(8,128)} %get-tuple-element.160, f32[1024]{0:T(1024)S(1)} %add_rsqrt_fusion, f32[1280]{0:T(1024)S(1)} %copy-done.8, bf16[1024,2560]{1,0:T(8,128)(2,1)} %all-gather.13.cloned.1.call-done, ...), kind=kOutput, calls=%fused_computation.15 | convolution fusion | flops 6718748672 | bytes 22300672 | tf_op jit(solution)/shard_map/dot_general | solution.py:522
  422.5 6.1 psum.92
  428.6 11.9 %fusion.15 = (f32[1024,1280]{1,0:T(8,128)}, bf16[1024,1280]{1,0:T(8,128)(2,1)}) fusion(f32[1024,1280]{1,0:T(8,128)} %get-tuple-element.160, f32[1024]{0:T(1024)S(1)} %fusion.20, f32[1280,1024]{0,1:T(8,128)} %get-tuple-element.175, f32[1024]{0:T(1024)S(1)} %add_rsqrt_fusion, f32[1280]{0:T(1024)S(1)} %copy-done.8, f32[1024,1280]{1,0:T(8,128)} %get-tuple-element.174, ...), kind=kLoop, calls=%fused_computation.37 | loop fusion | flops 22282240 | bytes 28849152 | tf_op jit(solution)/shard_map/mul | solution.py:532
  440.5 35.3 %shard_map.290 = (bf16[1024,1280]{1,0:T(8,128)(2,1)}, f32[8,1280]{1,0:T(8,128)}, f32[1024,128]{1,0:T(8,128)}, f32[1024,128]{1,0:T(8,128)}, f32[1024,128]{1,0:T(8...) custom-call(f32[1024,1280]{1,0:T(8,128)} %fusion.30.value_ref, f32[1024,1280]{1,0:T(8,128)} %shard_map.289.mixed_ref, ...), custom_call_target="tpu_custom_call" | custom-call | flops 10066329600 | bytes 35805184 | tf_op jit(solution)/shard_map/pallas_call | solution.py:289
  475.8 7.1 shard_map.291
  482.9 4.2 convolution_convert_fusion.3
  487.1 3.7 copy.78
  490.9 12.6 %fusion.3 = bf16[2560,1280]{0,1:T(8,128)(2,1)} fusion(bf16[1024,2560]{1,0:T(8,128)(2,1)} %all-gather.13.cloned.1.call-done, f32[1024,1280]{1,0:T(8,128)} %get-tuple-element.160, f32[1024]{0:T(1024)S(1)} %add_rsqrt_fusion, f32[1280]{0:T(1024)S(1)} %copy-done.8), kind=kOutput, calls=%fused_computation.10 | convolution fusion | flops 6718095360 | bytes 17048576 | tf_op jit(solution)/shard_map/dot_general | solution.py:28
  503.5 9.5 copy.80
  513.2 42.6 %reduce-scatter.23.cloned.1.call-done = bf16[320,276]{1,0:T(8,128)(2,1)} async-done(((bf16[2560,276]{1,0:T(8,128)(2,1)}), bf16[320,276]{1,0:T(8,128)(2,1)}) %reduce-scatter.23.cloned.1.call-update) | async-done | bytes 176656
  555.7 0.9 slice.79
  556.7 0.9 copy.82
  557.7 12.4 %multiply_convert_fusion = bf16[1024,2560]{1,0:T(8,128)(2,1)} fusion(bf16[2560,1280]{1,0:T(8,128)(2,1)} %all-gather.11.cloned.1.call-done, f32[1024]{0:T(1024)S(1)} %add_rsqrt_fusion, f32[1024,1280]{1,0:T(8,128)} %get-tuple-element.160, f32[1280]{0:T(1024)S(1)} %copy-done.8), kind=kOutput, calls=%fused_computation.9 | convolution fusion | flops 6718750720 | bytes 17048576 | tf_op jit(solution)/shard_map/dot_general | solution.py:34
  570.1 7.9 copy.74
  578.1 10.1 fusion.34
  588.3 11.6 %fusion.33 = f32[1024,2560]{1,0:T(8,128)} fusion(bf16[1024,1280]{1,0:T(8,128)(2,1)S(1)} %copy-done.1, bf16[2560,1280]{1,0:T(8,128)(2,1)} %all-gather.9.cloned.1.call-done), kind=kOutput, calls=%fused_computation.68 | convolution fusion | flops 6710886400 | bytes 19660800 | tf_op jit(solution)/shard_map/dot_general | solution.py:34
  599.8 7.6 add_convert_fusion
  607.4 8.0 copy.76
  615.5 1.8 copy-done.11
  617.3 11.2 %convolution_convert_fusion.1 = bf16[2560,1280]{1,0:T(8,128)(2,1)} fusion(bf16[1024,1280]{1,0:T(8,128)(2,1)S(1)} %copy-done.11, bf16[1024,2560]{1,0:T(8,128)(2,1)} %param.17, f32[2560]{0:T(1024)S(1)} %copy-done.10, f32[1024]{0:T(1024)S(1)} %get-tuple-element.168), kind=kOutput, calls=%fused_computation.3 | convolution fusion | flops 6724648960 | bytes 14432256 | tf_op jit(solution)/shard_map/dot_general | solution.py:28
  628.6 1.7 copy-done.2
  630.3 11.0 %convolution_convert_fusion.2 = bf16[2560,1280]{1,0:T(8,128)(2,1)} fusion(bf16[1024,1280]{1,0:T(8,128)(2,1)S(1)} %copy-done.2, bf16[1024,2560]{1,0:T(8,128)(2,1)} %param.17, f32[2560]{0:T(1024)S(1)} %copy-done.10, f32[1024]{0:T(1024)S(1)} %get-tuple-element.168), kind=kOutput, calls=%fused_computation.4 | convolution fusion | flops 6724648960 | bytes 14432256 | tf_op jit(solution)/shard_map/dot_general | solution.py:28
  642.3 42.7 %all-reduce.5 = (f32[4,256]{1,0:T(4,128)}, f32[256]{0:T(256)}) all-reduce(f32[4,256]{1,0:T(4,128)S(1)} %slice.72, f32[256]{0:T(256)S(1)} %bitcast.81), channel_id=1, replica_groups=mesh['gx'=8,'gy'=4] {'gx','gy'}, use_global_device_ids=true, to_apply=%region_17.18 | all-reduce | flops 1280 | bytes 10240 | tf_op jit(solution)/shard_map/psum | solution.py:564
  685.8 1.5 copy.81
  687.5 1.7 copy.71
  689.9 26.3 %all-reduce.9.cloned.1.call-done = f32[320,256]{0,1:T(8,128)} async-done(((f32[320,256]{0,1:T(8,128)}), f32[320,256]{0,1:T(8,128)}) %all-reduce.9.cloned.1.call-update) | async-done | bytes 327696 | tf_op jit(solution)/shard_map/psum | solution.py:565
  716.2 1.9 copy.70
  718.1 52.3 %reduce-scatter.19.cloned.1.call-done = bf16[640,1024]{1,0:T(8,128)(2,1)} async-done(((bf16[2560,1024]{1,0:T(8,128)(2,1)}), bf16[640,1024]{1,0:T(8,128)(2,1)}) %reduce-scatter.19.cloned.1.call-update) | async-done | bytes 1310736
  770.3 2.4 copy.75
  772.7 51.4 %reduce-scatter.21.cloned.1.call-done = bf16[640,1024]{1,0:T(8,128)(2,1)} async-done(((bf16[2560,1024]{1,0:T(8,128)(2,1)}), bf16[640,1024]{1,0:T(8,128)(2,1)}) %reduce-scatter.21.cloned.1.call-update) | async-done | bytes 1310736
  824.1 1.7 copy.77
  825.9 2.5 fusion.14
  828.4 40.4 %all-reduce.6 = (f32[640]{0:T(1024)}, f32[4,1280]{1,0:T(4,128)}, f32[1280]{0:T(1024)}, f32[20]{0:T(128)}, f32[20]{0:T(128)}, /*index=5*/f32[20]{0:T(128)}, f32[1280]{0:T(1024)}) all-reduce(f32[640]{0:T(1024)S(1)} %get-tuple-element.146, f32[4,1280]{1,0:T(4,128)S(1)} %slice.70, ...), channel_id=1, replica_groups=mesh['gx'=8,'gy'=4] {'gx'}, use_global_device_ids=true, to_apply=%region_10.11 | all-reduce | flops 8380 | bytes 67040 | tf_op jit(solution)/shard_map/psum | solution.py:566
  868.8 6.1 psum.93
  874.8 3.8 fusion.8
  878.7 71.7 %reduce-scatter.17.cloned.1.call-done = bf16[320,1280]{1,0:T(8,128)(2,1)} async-done(((bf16[2560,1280]{1,0:T(8,128)(2,1)}), bf16[320,1280]{1,0:T(8,128)(2,1)}) %reduce-scatter.17.cloned.1.call-update) | async-done | bytes 819216 | tf_op jit(solution)/shard_map/reduce_scatter | solution.py:456
  950.4 2.4 convert_element_type.88
  952.8 121.9 %reduce-scatter.15.cloned.1.call-done = bf16[320,1280]{1,0:T(8,128)(2,1)} async-done(((bf16[2560,1280]{1,0:T(8,128)(2,1)}), bf16[320,1280]{1,0:T(8,128)(2,1)}) %reduce-scatter.15.cloned.1.call-update) | async-done | bytes 819216 | tf_op jit(solution)/shard_map/reduce_scatter | solution.py:456
  1074.7 2.4 convert_element_type.86
  (86 shorter events, 8.6 us)
Async XLA Ops:
  7.2 108.0 %all-gather.7.cloned.1.call-start = ((), (), s32[]{:S(2)}) async-start(), calls=%async_computation.6 | async-start | bytes 7372800 | tf_op jit(solution)/shard_map/all_gather | solution.py:485
  7.9 209.9 %all-gather.9.cloned.1.call-start = ((), (), s32[]{:S(2)}) async-start(), calls=%async_computation.7 | async-start | bytes 7372800 | tf_op jit(solution)/shard_map/all_gather | solution.py:490
  115.2 148.8 %all-gather.15.cloned.1.call-start = ((), (), s32[]{:S(2)}) async-start(), calls=%async_computation.13 | async-start | bytes 1935360 | tf_op jit(solution)/shard_map/all_gather | solution.py:486
  117.8 229.2 %all-gather.13.cloned.1.call-start = ((), (), s32[]{:S(2)}) async-start(), calls=%async_computation.9 | async-start | bytes 6553600 | tf_op jit(solution)/shard_map/all_gather | solution.py:493
  118.4 290.8 %all-gather.11.cloned.1.call-start = ((), (), s32[]{:S(2)}) async-start(), calls=%async_computation.8 | async-start | bytes 7372800 | tf_op jit(solution)/shard_map/all_gather | solution.py:492
  217.8 337.9 %reduce-scatter.23.cloned.1.call-start = ((), (), s32[]{:S(2)}) async-start(), calls=%async_computation.16 | async-start | bytes 2211840
  227.5 39.4 %copy-start.10 = (f32[2560]{0:T(1024)S(1)}, f32[2560]{0:T(1024)}, u32[]{:S(2)}) copy-start(f32[2560]{0:T(1024)} %param.18) | copy-start | bytes 30724
  276.0 50.4 %slice-start = ((s8[5242880]{0:T(1024)(128)(4,1)}), s8[1048576]{0:T(1024)(128)(4,1)S(1)}, s32[]{:S(2)}) async-start(s8[5242880]{0:T(1024)(128)(4,1)} %bitcast.64), calls=%async_computation.18 | async-start | bytes 2097152
  295.1 31.2 %slice-start.1 = ((s8[5242880]{0:T(1024)(128)(4,1)}), s8[4194304]{0:T(1024)(128)(4,1)S(1)}, s32[]{:S(2)}) async-start(s8[5242880]{0:T(1024)(128)(4,1)} %bitcast.64), calls=%async_computation.19 | async-start | bytes 8388608
  326.4 82.8 %copy-start.8 = (f32[1280]{0:T(1024)S(1)}, f32[1280]{0:T(1024)}, u32[]{:S(2)}) copy-start(f32[1280]{0:T(1024)} %param.30) | copy-start | bytes 15364
  440.5 42.4 %slice-start.2 = ((s8[5242880]{0:T(1024)(128)(4,1)}), s8[4194304]{0:T(1024)(128)(4,1)S(1)}, s32[]{:S(2)}) async-start(s8[5242880]{0:T(1024)(128)(4,1)} %bitcast.66), calls=%async_computation.20 | async-start | bytes 8388608
  440.5 42.4 %slice-start.3 = ((s8[5242880]{0:T(1024)(128)(4,1)}), s8[1048576]{0:T(1024)(128)(4,1)S(1)}, s32[]{:S(2)}) async-start(s8[5242880]{0:T(1024)(128)(4,1)} %bitcast.66), calls=%async_computation.21 | async-start | bytes 2097152
  490.9 194.9 %reduce-scatter.25.cloned.1.call-start = ((), (), s32[]{:S(2)}) async-start(), calls=%async_computation.17 | async-start | bytes 7372800
  513.1 203.1 %all-reduce.9.cloned.1.call-start = ((), (), s32[]{:S(2)}) async-start(), calls=%async_computation.12 | async-start | bytes 786432 | tf_op jit(solution)/shard_map/psum | solution.py:565
  557.6 212.7 %reduce-scatter.19.cloned.1.call-start = ((), (), s32[]{:S(2)}) async-start(), calls=%async_computation.14 | async-start | bytes 6553600
  578.0 246.1 %reduce-scatter.21.cloned.1.call-start = ((), (), s32[]{:S(2)}) async-start(), calls=%async_computation.15 | async-start | bytes 6553600
  578.1 10.1 copy-start.1
  588.2 11.6 %copy-start.4 = (bf16[1024,256]{1,0:T(8,128)(2,1)S(1)}, bf16[1024,256]{1,0:T(8,128)(2,1)}, u32[]{:S(2)}) copy-start(bf16[1024,256]{1,0:T(8,128)(2,1)} %get-tuple-element.59) | copy-start | bytes 1572868
  588.3 11.6 %copy-start.5 = (bf16[1024,128]{1,0:T(8,128)(2,1)S(1)}, bf16[1024,128]{1,0:T(8,128)(2,1)}, u32[]{:S(2)}) copy-start(bf16[1024,128]{1,0:T(8,128)(2,1)} %get-tuple-element.60) | copy-start | bytes 786436
  615.5 1.8 copy-start.11
  615.5 334.9 %reduce-scatter.17.cloned.1.call-start = ((), (), s32[]{:S(2)}) async-start(), calls=%async_computation.11 | async-start | bytes 7372800 | tf_op jit(solution)/shard_map/reduce_scatter | solution.py:456
  628.5 1.8 copy-start.2
  628.5 446.2 %reduce-scatter.15.cloned.1.call-start = ((), (), s32[]{:S(2)}) async-start(), calls=%async_computation.10 | async-start | bytes 7372800 | tf_op jit(solution)/shard_map/reduce_scatter | solution.py:456
  641.3 0.7 copy-start.9
  641.3 0.8 copy-start.6
  641.3 47.8 %copy-start.3 = (bf16[320,276]{1,0:T(8,128)(2,1)S(1)}, bf16[320,276]{1,0:T(8,128)(2,1)}, u32[]{:S(2)}) copy-start(bf16[320,276]{1,0:T(8,128)(2,1)} %reduce-scatter.23.cloned.1.call-done) | copy-start | bytes 529924
  689.2 185.7 %copy-start = (bf16[1024,640]{1,0:T(8,128)(2,1)S(1)}, bf16[1024,640]{1,0:T(8,128)(2,1)}, u32[]{:S(2)}) copy-start(bf16[1024,640]{1,0:T(8,128)(2,1)} %param.33) | copy-start | bytes 3932164
  689.2 185.7 %copy-start.7 = (f32[1024]{0:T(1024)S(1)}, f32[1024]{0:T(1024)}, u32[]{:S(2)}) copy-start(f32[1024]{0:T(1024)} %get-tuple-element.167) | copy-start | bytes 12292
Sparse Core Ops, SparseCore 0:
  10.2 104.9 all-gather.6
  117.4 100.3 all-gather.8
  220.6 43.4 all-gather.14
  265.5 39.3 all-gather.12
  306.9 102.2 all-gather.10
  491.0 64.7 reduce-scatter.22
  559.8 121.6 reduce-scatter.24
  684.4 31.7 all-reduce.8
  718.9 51.3 reduce-scatter.18
  772.7 51.3 reduce-scatter.20
  828.2 122.1 reduce-scatter.16
  953.9 120.7 reduce-scatter.14

commit v3 on v2

--- a/solution.py
+++ b/solution.py
@@ -452,10 +452,71 @@
         )
 
 
-def scatter_rows(partial):
-    return lax.psum_scatter(
-        partial.astype(jnp.bfloat16), "gx", scatter_dimension=0, tiled=True
-    ).astype(jnp.float32)
+def ring_place(index, count):
+    return jnp.where(index % 2 == 0, index // 2, count - 1 - index // 2)
+
+
+def ring_index(place, count):
+    place = place % count
+    return jnp.where(place < (count + 1) // 2, 2 * place, 2 * (count - 1 - place) + 1)
+
+
+def ring_moves(count):
+    order = list(range(0, count, 2)) + list(range(1, count, 2))[::-1]
+    ahead = [(order[k], order[(k + 1) % count]) for k in range(count)]
+    return ahead, [(target, source) for source, target in ahead]
+
+
+def ring_gather(shard, splits):
+    count = lax.axis_size("gx")
+    ahead, behind = ring_moves(count)
+    me = lax.axis_index("gx")
+    place = ring_place(me, count)
+    rows, width = shard.shape
+    half = rows // 2
+    edges = [0] + splits + [width]
+    fulls = [jnp.zeros((count * rows, hi - lo), shard.dtype) for lo, hi in zip(edges, edges[1:])]
+
+    def put(fulls, piece, start):
+        return [
+            lax.dynamic_update_slice(full, piece[:, lo:hi], (start, 0))
+            for full, lo, hi in zip(fulls, edges, edges[1:])
+        ]
+
+    fulls = put(fulls, shard, me * rows)
+    up, down = shard[:half], shard[half:]
+    for step in range(1, count):
+        up = lax.ppermute(up, "gx", ahead)
+        down = lax.ppermute(down, "gx", behind)
+        fulls = put(fulls, up, ring_index(place - step, count) * rows)
+        fulls = put(fulls, down, ring_index(place + step, count) * rows + half)
+    return fulls, (up, down)
+
+
+def ring_scatter(partial):
+    count = lax.axis_size("gx")
+    ahead, behind = ring_moves(count)
+    place = ring_place(lax.axis_index("gx"), count)
+    rows = partial.shape[0] // count
+    half = rows // 2
+
+    def part(target, offset):
+        start = ring_index(target, count) * rows + offset
+        return lax.dynamic_slice_in_dim(partial, start, half, 0)
+
+    up, down = part(place - 1, 0), part(place + 1, half)
+    for step in range(1, count):
+        up = lax.ppermute(up, "gx", ahead).astype(wide)
+        down = lax.ppermute(down, "gx", behind).astype(wide)
+        up = up + part(place - 1 - step, 0).astype(wide)
+        down = down + part(place + 1 + step, half).astype(wide)
+        if step < count - 1:
+            up, down = up.astype(low), down.astype(low)
+    return jnp.concatenate([up, down], 0)
+
+
+def after(value, *others):
+    return lax.optimization_barrier((value,) + others)[0]
 
 
 def on_device(
@@ -482,22 +543,18 @@
     state_cols = state_weight.shape[1]
     col_start = lax.axis_index("gy") * col_width
 
-    full_value = lax.all_gather(value_weight, "gx", axis=0, tiled=True)
-    full_state = lax.all_gather(
-        jnp.concatenate([state_weight, step_weight], 1), "gx", axis=0, tiled=True
-    )
-    gate_weight, full_value = lax.optimization_barrier((gate_weight, full_value))
-    full_gate = lax.all_gather(gate_weight, "gx", axis=0, tiled=True)
-    out_rows, full_gate = lax.optimization_barrier((out_weight.T, full_gate))
-    full_out = lax.all_gather(out_rows, "gx", axis=0, tiled=True)
+    state_step_weight = jnp.concatenate([state_weight, step_weight], 1)
+    (full_state,), moved = ring_gather(state_step_weight, [])
+    (full_value,), moved = ring_gather(after(value_weight, *moved), [])
+    (full_gate,), moved = ring_gather(after(gate_weight, *moved), [])
+    (full_out,), moved = ring_gather(after(out_weight.T, *moved), [])
     upstream = lax.all_gather(cotangent, "gy", axis=1, tiled=True)
 
-    tokens = layer_input.astype(jnp.float32)
+    tokens = layer_input.astype(wide)
     scale_in = lax.rsqrt(jnp.mean(tokens * tokens, axis=1, keepdims=True) + epsilon)
-    normed = (tokens * scale_in * norm_gain).astype(jnp.bfloat16)
-
-    value_in = jnp.dot(normed, full_value, preferred_element_type=jnp.float32)
-    state_step = jnp.dot(normed, full_state, preferred_element_type=jnp.float32)
+    normed = (tokens * scale_in * norm_gain).astype(low)
+
+    state_step = dot(normed, full_state)
     mixer = Mixer(
         state_step[:, :state_cols],
         state_step[:, state_cols:],
@@ -507,82 +564,88 @@
         decay_log,
         segment_ids,
     )
+    value_in = dot(normed, full_value)
     mixed = mixer.forward(value_in, conv_value, conv_value_bias, skip_scale)
-    gate_in = jnp.dot(normed, full_gate, preferred_element_type=jnp.float32)
+    gate_in = dot(normed, full_gate)
     gate_open = jax.nn.sigmoid(gate_in)
     gate_act = gate_in * gate_open
     gated = mixed * gate_act
     squares = lax.psum(jnp.sum(gated * gated, axis=1), "gy")
     scale_out = lax.rsqrt(squares / INNER + epsilon)[:, None]
-    scaled = (gated * gated_gain).astype(jnp.bfloat16)
-
-    scaled_out = (gated * gated_gain * scale_out).astype(jnp.bfloat16)
-    grad_out = scatter_rows(contract_rows(upstream, scaled_out))
-
-    up_back = jnp.dot(upstream, full_out, preferred_element_type=jnp.float32)
+    scaled = (gated * gated_gain).astype(low)
+
+    scaled_out = (gated * gated_gain * scale_out).astype(low)
+    grad_out = ring_scatter(contract_rows(upstream, scaled_out).astype(low))
+
+    up_back = dot(upstream, full_out)
     grad_scale = lax.psum(jnp.sum(gated * gated_gain * up_back, axis=1), "gy")[:, None]
     grad_scaled = scale_out * up_back
     grad_gated = grad_scaled * gated_gain - grad_scale * scale_out**3 * gated / INNER
     gate_gain_part = jnp.sum(grad_scaled * gated, axis=0)
     grad_gate_in = (
         grad_gated * mixed * gate_open * (1.0 + gate_in * (1.0 - gate_open))
-    ).astype(jnp.bfloat16)
-    grad_gate = scatter_rows(contract_rows(normed, grad_gate_in))
+    ).astype(low)
+    grad_gate = ring_scatter(contract_rows(normed, grad_gate_in).astype(low))
 
     pulled = mixer.backward(grad_gated * gate_act)
     grad_value_in = pulled[0]
     grad_state_in = jnp.concatenate([pulled[1], pulled[2]], 1)
-    grad_state_step = scatter_rows(contract_rows(normed, grad_state_in))
-    grad_value = scatter_rows(contract_rows(normed, grad_value_in))
+    grad_state_step = ring_scatter(contract_rows(normed, grad_state_in).astype(low))
+    grad_value = ring_scatter(contract_rows(normed, grad_value_in).astype(low))
 
     product = lax.psum_scatter(
-        (contract_cols(scaled, full_out) * scale_out).astype(jnp.bfloat16),
+        (contract_cols(full_out, scaled) * scale_out[:, 0]).astype(low),
         "gy",
-        scatter_dimension=1,
+        scatter_dimension=0,
         tiled=True,
-    )
-    token_cols = lax.dynamic_slice_in_dim(layer_input, col_start, col_width, 1).astype(jnp.float32)
-    layer_output = (token_cols + product.astype(jnp.float32)).astype(jnp.bfloat16)
+    ).T
+    token_cols = lax.dynamic_slice_in_dim(layer_input, col_start, col_width, 1).astype(wide)
+    layer_output = (token_cols + product.astype(wide)).astype(low)
 
     grad_normed_part = (
-        contract_cols(grad_gate_in, full_gate)
-        + contract_cols(grad_value_in, full_value)
-        + contract_cols(grad_state_in, full_state)
+        contract_cols(full_gate, grad_gate_in)
+        + contract_cols(full_value, grad_value_in)
+        + contract_cols(full_state, grad_state_in)
     )
     grad_normed = lax.psum_scatter(
-        grad_normed_part.astype(jnp.bfloat16), "gy", scatter_dimension=1, tiled=True
-    ).astype(jnp.float32)
+        grad_normed_part.astype(low), "gy", scatter_dimension=0, tiled=True
+    ).T.astype(wide)
     gain_cols = lax.dynamic_slice_in_dim(norm_gain, col_start, col_width, 0)
     weighted = grad_normed * gain_cols
     inner_dot = lax.psum(jnp.sum(weighted * token_cols, axis=1), "gy")[:, None]
     grad_input = (
-        cotangent.astype(jnp.float32)
+        cotangent.astype(wide)
         + scale_in * weighted
         - token_cols * scale_in**3 * inner_dot / model_width
     )
-    norm_gain_part = jnp.sum(grad_normed * token_cols * scale_in, axis=0)
-    conv_state_sum, conv_bias_sum = lax.psum((pulled[5], pulled[6]), ("gx", "gy"))
-    grad_state = lax.psum(grad_state_step[:, :state_cols], "gy")
-    small_sums = lax.psum(
-        (norm_gain_part, gate_gain_part, pulled[3], pulled[4], pulled[7], pulled[8], pulled[9]),
-        "gx",
-    )
+    grad_norm_gain = lax.psum(jnp.sum(grad_normed * token_cols * scale_in, axis=0), "gx")
+
+    small = (gate_gain_part,) + pulled[3:]
+    packed = lax.psum(jnp.concatenate([v.reshape(-1) for v in small]), "gx")
+    sums, start = [], 0
+    for v in small:
+        sums.append(packed[start : start + v.size].reshape(v.shape))
+        start += v.size
+    state_sums = lax.psum(
+        jnp.concatenate([grad_state_step[:, :state_cols], sums[3], sums[4][None]], 0), "gy"
+    )
+    state_rows = state_weight.shape[0]
     return (
         layer_output,
         grad_input,
-        small_sums[0],
+        grad_norm_gain,
         grad_gate,
         grad_value,
-        grad_state,
+        state_sums[:state_rows],
         grad_state_step[:, state_cols:],
-        small_sums[2],
-        small_sums[3],
-        conv_state_sum,
-        conv_bias_sum,
-        small_sums[4],
-        small_sums[5],
-        small_sums[6],
-        small_sums[1],
+        sums[1],
+        sums[2],
+        state_sums[state_rows:-1],
+        state_sums[-1],
+        sums[5],
+        sums[6],
+        sums[7],
+        sums[0],
         grad_out.T,
     )
 

time: 1090 us -> 818 us (0.75)
  waiting for transfers between devices: 669 us -> 284 us
  starting transfers between devices: 0.48 us -> 130 us
  blocking collectives: 102 us -> 54.3 us
  other arithmetic: 30.6 us -> 52.8 us
  local copies, waits for them, and re-layouts: 63.5 us -> 74.6 us
    all_gather x4 -> x0, waiting for transfers between devices: 301 us -> none  [the longest x1 107 us: on_device(): full_value = lax.all_gather(value_weight, 'gx', axis=0, tiled=True)]
    ppermute x0 -> x112, waiting for transfers between devices: none -> 263 us  [the longest x28 135 us: ring_gather(): up = lax.ppermute(up, 'gx', ahead)]
    reduce_scatter x2, waiting for transfers between devices: 194 us -> 0.02 us  [the longest x1 0.02 us: on_device(): lax.psum_scatter((contract_cols(full_out, scaled) * scale_out[:, 0]).asty...]
    unnamed x16 -> x4, waiting for transfers between devices: 148 us -> 0.07 us
    ppermute x0 -> x112, starting transfers between devices: none -> 130 us  [the longest x28 48.1 us: ring_scatter(): up = lax.ppermute(up, 'gx', ahead).astype(wide)]
    psum x2 -> x1, blocking collectives: 83.1 us -> 36.6 us  [on_device(): lax.psum(jnp.sum(grad_normed * token_cols * scale_in, axis=0), 'gx')]
    unnamed x45 -> x93, local copies, waits for them, and re-layouts: 46.6 us -> 10.5 us
    dynamic_update_slice x0 -> x59, local copies, waits for them, and re-layouts: none -> 32 us  [put(): lax.dynamic_update_slice(full, piece[:, lo:hi], (start, 0))]
  transfers between devices with their start and end apart: 12 -> 116, of which waited for: 10 -> 58; matrix products, arithmetic and copies ran while one was open for 17% -> 30% of each run, Pallas kernels for 3% -> 10%
where the time goes in v3:
time: 818 us; the launch traced here: 812 us
  waiting for transfers between devices  284 us (35%)
  starting transfers between devices  130 us (16%)
  matrix products  122 us (15%)
  Pallas kernels  78.7 us (10%)
  local copies, waits for them, and re-layouts  74.6 us (9%)
  blocking collectives  54.3 us (7%)
  other arithmetic  52.8 us (6%)
  between operations  15.7 us (2%)
    ppermute x28, waiting for transfers between devices, ring_gather(): up = lax.ppermute(up, 'gx', ahead)  135 us
    ppermute x28, waiting for transfers between devices, ring_scatter(): down = lax.ppermute(down, 'gx', behind).astype(wide)  81.3 us
    pallas_call x4, Pallas kernels, call(): pl.pallas_call(kernel, out_shape=shapes, scratch_shapes=list(scratch), co...  78.7 us
    ppermute x28, starting transfers between devices, ring_scatter(): up = lax.ppermute(up, 'gx', ahead).astype(wide)  48.1 us
    dot_general x4, matrix products, contract_cols(): lax.dot_general(left, right, (((1,), (1,)), ((), ())), preferred_element_...  47.4 us
    ppermute x28, starting transfers between devices, ring_gather(): up = lax.ppermute(up, 'gx', ahead)  46.6 us
    ppermute x28, waiting for transfers between devices, ring_scatter(): up = lax.ppermute(up, 'gx', ahead).astype(wide)  40.3 us
    dot_general x4, matrix products, dot(): jnp.dot(left, right, preferred_element_type=wide, precision=precision)  40.2 us
  transfers between devices with their start and end apart: 116, of which 58 were waited for; matrix products, arithmetic and copies ran while one was open for 30% of the time, Pallas kernels for 10%

profile of v3, /device:TPU:0, one launch (start us, length us, event | category | flops | bytes accessed | tf_op | source)
XLA Modules:
  0.0 812.3 jit_solution(10386376643523923975)
XLA Ops:
  9.1 3.1 collective-permute-start
  14.5 3.6 fusion
  40.1 3.3 collective-permute-done.4
  46.2 3.4 collective-permute-done.5
  56.3 5.1 fusion.44
  68.6 17.5 %shard_map.288 = (bf16[1024,128]{1,0:T(8,128)(2,1)}, bf16[1024,128]{1,0:T(8,128)(2,1)}, bf16[128,1024]{1,0:T(8,128)(2,1)}, bf16[128,1024]{1,0:T(8,128)(2,1)}, f3...) custom-call(f32[1024,256]{1,0:T(8,128)} %slice.157.state_ref, ...), custom_call_target="tpu_custom_call" | custom-call | flops 2013265920 | bytes 17315840 | tf_op jit(solution)/shard_map/pallas_call | solution.py:289
  92.4 8.2 %collective-permute-done.15 = bf16[160,1280]{1,0:T(8,128)(2,1)S(1)} collective-permute-done((bf16[160,1280]{1,0:T(8,128)(2,1)}, bf16[160,1280]{1,0:T(8,128)(2,1)S(1)}, u32[]{:S(2)}, u32[]{:S(2)}) %collective-permute-start.15) | collective-permute-done | bytes 409632 | tf_op jit(solution)/shard_map/ppermute | solution.py:489
  102.7 9.2 %collective-permute-done.16 = bf16[160,1280]{1,0:T(8,128)(2,1)S(1)} collective-permute-done((bf16[160,1280]{1,0:T(8,128)(2,1)S(1)}, bf16[160,1280]{1,0:T(8,128)(2,1)S(1)}, u32[]{:S(2)}, u32[]{:S(2)}) %collective-permute-start.16) | collective-permute-done | bytes 409632 | tf_op jit(solution)/shard_map/ppermute | solution.py:489
  114.0 8.3 %collective-permute-done.17 = bf16[160,1280]{1,0:T(8,128)(2,1)S(1)} collective-permute-done((bf16[160,1280]{1,0:T(8,128)(2,1)S(1)}, bf16[160,1280]{1,0:T(8,128)(2,1)S(1)}, u32[]{:S(2)}, u32[]{:S(2)}) %collective-permute-start.17) | collective-permute-done | bytes 409632 | tf_op jit(solution)/shard_map/ppermute | solution.py:489
  124.3 7.5 collective-permute-done.18
  133.9 6.5 collective-permute-done.19
  142.8 5.7 collective-permute-done.20
  150.3 8.9 %fusion.46.value_ref = f32[1024,1280]{1,0:T(8,128)} fusion(bf16[2560,1280]{1,0:T(8,128)(2,1)S(1)} %constant_dynamic-update-slice_fusion.29, bf16[1024,2560]{1,0:T(8,128)(2,1)S(1)} %bitcast.125, f32[2560]{0:T(1024)S(1)} %copy-done.22, f32[1024]{0:T(1024)S(1)} %get-tuple-element.236), kind=kOutput, calls=%fused_computation.219 | convolution fusion | flops 6721372160 | bytes 17053696 | tf_op jit(solution)/shard_map/dot_general | solution.py:24
  162.2 3.2 broadcast.69.clone
  166.3 18.1 %shard_map.289.mixed_ref = f32[1024,1280]{1,0:T(8,128)} custom-call(f32[1024,1280]{1,0:T(8,128)} %fusion.46.value_ref, f32[4,1280]{1,0:T(4,128)} %taps_ref.6, f32[1,1280]{1,0:T(1,128)} %broadcast_in_dim.22.bias_ref, f32[1,1280]{1,0:T(1,128)} %broadcast_in_dim_reshape.3.skip_ref, f32[1024,1280]{1,0:T(8,128)} %get-tuple-element.42.dtx_ref, ...), custom_call_target="tpu_custom_call" | custom-call | flops 3355443200 | bytes 24754176 | tf_op jit(solution)/shard_map/pallas_call | solution.py:289
  190.1 6.7 collective-permute-done.29
  200.4 7.6 collective-permute-done.30
  211.6 6.7 collective-permute-done.31
  222.0 6.0 collective-permute-done.32
  231.6 6.9 collective-permute-done.33
  242.1 4.4 collective-permute-done.34
  252.5 13.6 %multiply_reduce_fusion.1 = (f32[1024]{0:T(1024)S(1)}, f32[1024,1280]{1,0:T(8,128)}, f32[1024,1280]{1,0:T(8,128)}) fusion(f32[1024,1280]{1,0:T(8,128)S(1)} %copy-done, bf16[2560,1280]{1,0:T(8,128)(2,1)} %constant_dynamic-update-slice_fusion, bf16[1024,2560]{1,0:T(8,128)(2,1)S(1)} %bitcast.125, f32[2560]{0:T(1024)S(1)} %copy-done.22, ...), kind=kOutput, calls=%fused_computation.17 | convolution fusion | flops 6730546176 | bytes 27543552 | tf_op jit(solution)/shard_map/dot_general | solution.py:24
  266.1 5.6 psum.42
  271.7 3.1 broadcast.69.clone.2
  281.4 5.8 collective-permute-done.44
  290.9 6.8 collective-permute-done.46
  302.5 11.6 %convolution_convert_fusion = bf16[1280,2560]{0,1:T(8,128)(2,1)S(1)} fusion(bf16[1024,2560]{1,0:T(8,128)(2,1)} %all-gather.2.cloned.1.call-done, f32[1024,1280]{1,0:T(8,128)} %get-tuple-element.151, f32[1024]{0:T(1024)S(1)} %add_rsqrt_fusion, f32[1280]{0:T(1024)S(1)} %copy-done.18), kind=kOutput, calls=%fused_computation.2 | convolution fusion | flops 6718095360 | bytes 17048576 | tf_op jit(solution)/shard_map/dot_general | solution.py:28
  320.0 6.7 collective-permute-done.105
  330.4 5.6 collective-permute-done.50
  339.7 11.2 %collective-permute-done.52 = bf16[160,1280]{1,0:T(8,128)(2,1)S(1)} collective-permute-done((bf16[160,1280]{1,0:T(8,128)(2,1)S(1)}, bf16[160,1280]{1,0:T(8,128)(2,1)S(1)}, u32[]{:S(2)}, u32[]{:S(2)}) %collective-permute-start.52) | collective-permute-done | bytes 409632 | tf_op jit(solution)/shard_map/ppermute | solution.py:489
  354.5 4.3 collective-permute-done.54
  361.1 12.6 %multiply_reduce_fusion = (f32[1280]{0:T(1024)}, f32[1024]{0:T(1024)S(1)}, f32[1280,1024]{0,1:T(8,128)}) fusion(f32[1024,1280]{1,0:T(8,128)S(1)} %bitcast.133, f32[1024]{0:T(1024)S(1)} %add_rsqrt_fusion, f32[1280]{0:T(1024)S(1)} %copy-done.18, bf16[1024,2560]{1,0:T(8,128)(2,1)S(1)} %bitcast.155, bf16[2560,1280]{1,0:T(8,128)(2,1)} %constant_dynamic-update-slice_fusion.44), kind=kOutput, calls=%fused_computation.14 | convolution fusion | flops 6718748672 | bytes 22300672 | tf_op jit(solution)/shard_map/dot_general | solution.py:24
  373.6 6.0 psum.43
  379.7 11.1 %fusion.14 = (f32[1024,1280]{1,0:T(8,128)}, bf16[1024,1280]{1,0:T(8,128)(2,1)S(1)}) fusion(f32[1024,1280]{1,0:T(8,128)} %get-tuple-element.151, f32[1024]{0:T(1024)S(1)} %fusion.36, f32[1280,1024]{0,1:T(8,128)} %get-tuple-element.243, f32[1024]{0:T(1024)S(1)} %add_rsqrt_fusion, f32[1280]{0:T(1024)S(1)} %copy-done.18, f32[1024,1280]{1,0:T(8,128)} %get-tuple-element.242, ...), kind=kLoop, calls=%fused_computation.36 | loop fusion | flops 22282240 | bytes 28849152 | tf_op jit(solution)/shard_map/mul | solution.py:590
  390.8 36.1 %shard_map.290 = (bf16[1024,1280]{1,0:T(8,128)(2,1)}, f32[8,1280]{1,0:T(8,128)}, f32[1024,128]{1,0:T(8,128)}, f32[1024,128]{1,0:T(8,128)}, f32[1024,128]{1,0:T(8...) custom-call(f32[1024,1280]{1,0:T(8,128)} %fusion.46.value_ref, f32[1024,1280]{1,0:T(8,128)} %shard_map.289.mixed_ref, ...), custom_call_target="tpu_custom_call" | custom-call | flops 10066329600 | bytes 35805184 | tf_op jit(solution)/shard_map/pallas_call | solution.py:289
  426.9 12.8 %fusion.55 = f32[2560,1024]{1,0:T(8,128)} fusion(bf16[2560,1280]{1,0:T(8,128)(2,1)} %copy-done.3, bf16[1024,1280]{1,0:T(8,128)(2,1)} %get-tuple-element.51), kind=kOutput, calls=%fused_computation.226 | convolution fusion | flops 6710886400 | bytes 19660800 | tf_op jit(solution)/shard_map/dot_general | solution.py:34
  439.7 11.6 %fusion.54 = f32[2560,1024]{1,0:T(8,128)} fusion(bf16[2560,1280]{1,0:T(8,128)(2,1)} %constant_dynamic-update-slice_fusion, bf16[1024,1280]{1,0:T(8,128)(2,1)S(1)} %get-tuple-element.153), kind=kOutput, calls=%fused_computation.225 | convolution fusion | flops 6710886400 | bytes 19660800 | tf_op jit(solution)/shard_map/dot_general | solution.py:34
  451.3 7.0 shard_map.291
  458.3 11.3 %add_convert_fusion = bf16[2560,1024]{1,0:T(8,128)(2,1)} fusion(f32[2560,1024]{1,0:T(8,128)} %fusion.54, f32[2560,1024]{1,0:T(8,128)} %fusion.55, bf16[2560,276]{1,0:T(8,128)(2,1)S(1)} %constant_dynamic-update-slice_fusion.15, bf16[1024,20]{1,0:T(8,128)(2,1)} %bitcast.147, bf16[1024,256]{1,0:T(8,128)(2,1)} %get-tuple-element.57), kind=kOutput, calls=%fused_computation.8 | convolution fusion | flops 1456029696 | bytes 28192768 | tf_op jit(solution)/shard_map/dot_general | solution.py:34
  478.5 5.1 collective-permute-done.100
  489.4 5.7 convolution_convert_fusion.3
  497.4 7.9 convolution_convert_fusion.1
  506.2 9.4 %convolution_convert_fusion.2 = bf16[2560,1280]{1,0:T(8,128)(2,1)} fusion(bf16[1024,1280]{1,0:T(8,128)(2,1)S(1)} %copy-done.11, bf16[1024,2560]{1,0:T(8,128)(2,1)S(1)} %bitcast.127, f32[2560]{0:T(1024)S(1)} %copy-done.23, f32[1024]{0:T(1024)S(1)} %get-tuple-element.236), kind=kOutput, calls=%fused_computation.4 | convolution fusion | flops 6724648960 | bytes 14432256 | tf_op jit(solution)/shard_map/dot_general | solution.py:28
  515.7 11.7 %multiply_convert_fusion = bf16[2560,1024]{1,0:T(8,128)(2,1)} fusion(bf16[2560,1280]{1,0:T(8,128)(2,1)} %constant_dynamic-update-slice_fusion.44, f32[1024]{0:T(1024)S(1)} %add_rsqrt_fusion, f32[1024,1280]{1,0:T(8,128)S(1)} %bitcast.135, f32[1280]{0:T(1024)S(1)} %copy-done.18), kind=kOutput, calls=%fused_computation.9 | convolution fusion | flops 6718750720 | bytes 17048576 | tf_op jit(solution)/shard_map/dot_general | solution.py:34
  561.3 8.8 %collective-permute-done.88 = bf16[160,276]{0,1:T(8,128)(2,1)S(1)} collective-permute-done((bf16[160,276]{0,1:T(8,128)(2,1)S(1)}, bf16[160,276]{0,1:T(8,128)(2,1)S(1)}, u32[]{:S(2)}, u32[]{:S(2)}) %collective-permute-start.88) | collective-permute-done | bytes 88352 | tf_op jit(solution)/shard_map/ppermute | solution.py:509
  577.2 7.0 collective-permute-done.89
  591.7 9.8 %collective-permute-done.90 = bf16[160,276]{0,1:T(8,128)(2,1)S(1)} collective-permute-done((bf16[160,276]{0,1:T(8,128)(2,1)S(1)}, bf16[160,276]{0,1:T(8,128)(2,1)S(1)}, u32[]{:S(2)}, u32[]{:S(2)}) %collective-permute-start.90) | collective-permute-done | bytes 88352 | tf_op jit(solution)/shard_map/ppermute | solution.py:509
  610.4 3.5 collective-permute-done.78
  618.3 4.4 collective-permute-done.64
  627.0 4.4 collective-permute-done.110
  635.8 4.4 collective-permute-done.79
  644.6 4.4 collective-permute-done.65
  651.4 6.4 collective-permute-done.111
  660.4 6.2 collective-permute-done.80
  668.9 6.5 collective-permute-done.66
  677.7 6.5 collective-permute-done.81
  686.5 6.5 collective-permute-done.67
  695.3 6.5 collective-permute-done.82
  704.0 5.1 collective-permute-done.68
  724.3 36.6 %all-reduce.5 = (f32[640]{0:T(1024)}, f32[9020]{0:T(1024)S(1)}) all-reduce(f32[640]{0:T(1024)S(1)} %get-tuple-element.144, f32[9020]{0:T(1024)S(1)} %concatenate.49), channel_id=1, replica_groups=mesh['gx'=8,'gy'=4] {'gx'}, use_global_device_ids=true, to_apply=%region_10.11 | all-reduce | flops 9660 | bytes 77280 | tf_op jit(solution)/shard_map/psum | solution.py:621
  761.8 6.0 psum.44
  769.4 5.1 fusion.8
  774.5 3.3 copy.129
  779.8 20.2 %all-reduce.8.cloned.1.call-done = f32[325,256]{0,1:T(8,128)} async-done(((f32[325,256]{0,1:T(8,128)}), f32[325,256]{0,1:T(8,128)}) %all-reduce.8.cloned.1.call-update) | async-done | bytes 332816 | tf_op jit(solution)/shard_map/psum | solution.py:629
  (450 shorter events, 262.2 us)
Async XLA Ops:
  7.2 295.2 %all-gather.2.cloned.1.call-start = ((), (), s32[]{:S(2)}) async-start(), calls=%async_computation.3 | async-start | bytes 6553600 | tf_op jit(solution)/shard_map/all_gather | solution.py:551
  9.1 13.5 %collective-permute-start = (bf16[160,276]{1,0:T(8,128)(2,1)S(1)}, bf16[160,276]{1,0:T(8,128)(2,1)S(1)}, u32[]{:S(2)}, u32[]{:S(2)}) collective-permute-start(bf16[160,276]{1,0:T(8,128)(2,1)S(1)} %get-tuple-element.227), channel_id=1, source_target_pairs={{0,8},{8,16},{16,24},{24,28},{28,20},{20,12},{12,4},{4,0},{1,9},{9... | collective-permute-start | bytes 264968 | tf_op jit(solution)/shard_map/ppermute | solution.py:489
  12.2 12.5 %collective-permute-start.7 = (bf16[160,276]{1,0:T(8,128)(2,1)S(1)}, bf16[160,276]{1,0:T(8,128)(2,1)S(1)}, u32[]{:S(2)}, u32[]{:S(2)}) collective-permute-start(bf16[160,276]{1,0:T(8,128)(2,1)S(1)} %get-tuple-element.226), channel_id=1, source_target_pairs={{8,0},{16,8},{24,16},{28,24},{20,28},{12,20},{4,12},{0,4},{9,1},{1... | collective-permute-start | bytes 264968 | tf_op jit(solution)/shard_map/ppermute | solution.py:490
  12.2 709.4 %reduce-scatter.5.cloned.1.call-start = ((), (), s32[]{:S(2)}) async-start(), calls=%async_computation.4 | async-start | bytes 6553600 | tf_op jit(solution)/shard_map/reduce_scatter | solution.py:610
  64.2 24.0 %collective-permute-start.14 = (bf16[160,1280]{1,0:T(8,128)(2,1)}, bf16[160,1280]{1,0:T(8,128)(2,1)}, u32[]{:S(2)}, u32[]{:S(2)}) collective-permute-start(bf16[160,1280]{1,0:T(8,128)(2,1)} %get-tuple-element.225), channel_id=1, source_target_pairs={{0,8},{8,16},{16,24},{24,28},{28,20},{20,12},{12,4},{4,0},{1,9},{9... | collective-permute-start | bytes 1228808 | tf_op jit(solution)/shard_map/ppermute | solution.py:489
  65.8 24.1 %collective-permute-start.21 = (bf16[160,1280]{1,0:T(8,128)(2,1)S(1)}, bf16[160,1280]{1,0:T(8,128)(2,1)}, u32[]{:S(2)}, u32[]{:S(2)}) collective-permute-start(bf16[160,1280]{1,0:T(8,128)(2,1)S(1)} %get-tuple-element.224), channel_id=1, source_target_pairs={{8,0},{16,8},{24,16},{28,24},{20,28},{12,20},{4,12},{0,4},{9,1},{1... | collective-permute-start | bytes 1228808 | tf_op jit(solution)/shard_map/ppermute | solution.py:490
  88.2 12.4 %collective-permute-start.15 = (bf16[160,1280]{1,0:T(8,128)(2,1)}, bf16[160,1280]{1,0:T(8,128)(2,1)S(1)}, u32[]{:S(2)}, u32[]{:S(2)}) collective-permute-start(bf16[160,1280]{1,0:T(8,128)(2,1)} %collective-permute-done.14), channel_id=1, source_target_pairs={{0,8},{8,16},{16,24},{24,28},{28,20},{20,12},{12,4},{4,0},{1,9},{9... | collective-permute-start | bytes 1228808 | tf_op jit(solution)/shard_map/ppermute | solution.py:489
  89.8 12.3 %collective-permute-start.22 = (bf16[160,1280]{1,0:T(8,128)(2,1)}, bf16[160,1280]{1,0:T(8,128)(2,1)S(1)}, u32[]{:S(2)}, u32[]{:S(2)}) collective-permute-start(bf16[160,1280]{1,0:T(8,128)(2,1)} %collective-permute-done.21), channel_id=1, source_target_pairs={{8,0},{16,8},{24,16},{28,24},{20,28},{12,20},{4,12},{0,4},{9,1},{1... | collective-permute-start | bytes 1228808 | tf_op jit(solution)/shard_map/ppermute | solution.py:490
  160.1 24.3 %collective-permute-start.28 = (bf16[160,1280]{1,0:T(8,128)(2,1)}, bf16[160,1280]{1,0:T(8,128)(2,1)}, u32[]{:S(2)}, u32[]{:S(2)}) collective-permute-start(bf16[160,1280]{1,0:T(8,128)(2,1)} %get-tuple-element.223), channel_id=1, source_target_pairs={{0,8},{8,16},{16,24},{24,28},{28,20},{20,12},{12,4},{4,0},{1,9},{9... | collective-permute-start | bytes 1228808 | tf_op jit(solution)/shard_map/ppermute | solution.py:489
  161.6 24.4 %collective-permute-start.35 = (bf16[160,1280]{1,0:T(8,128)(2,1)}, bf16[160,1280]{1,0:T(8,128)(2,1)}, u32[]{:S(2)}, u32[]{:S(2)}) collective-permute-start(bf16[160,1280]{1,0:T(8,128)(2,1)} %get-tuple-element.222), channel_id=1, source_target_pairs={{8,0},{16,8},{24,16},{28,24},{20,28},{12,20},{4,12},{0,4},{9,1},{1... | collective-permute-start | bytes 1228808 | tf_op jit(solution)/shard_map/ppermute | solution.py:490
  184.4 12.3 %collective-permute-start.29 = (bf16[160,1280]{1,0:T(8,128)(2,1)}, bf16[160,1280]{1,0:T(8,128)(2,1)S(1)}, u32[]{:S(2)}, u32[]{:S(2)}) collective-permute-start(bf16[160,1280]{1,0:T(8,128)(2,1)} %collective-permute-done.28), channel_id=1, source_target_pairs={{0,8},{8,16},{16,24},{24,28},{28,20},{20,12},{12,4},{4,0},{1,9},{9... | collective-permute-start | bytes 1228808 | tf_op jit(solution)/shard_map/ppermute | solution.py:489
  186.0 12.2 %collective-permute-start.36 = (bf16[160,1280]{1,0:T(8,128)(2,1)}, bf16[160,1280]{1,0:T(8,128)(2,1)S(1)}, u32[]{:S(2)}, u32[]{:S(2)}) collective-permute-start(bf16[160,1280]{1,0:T(8,128)(2,1)} %collective-permute-done.35), channel_id=1, source_target_pairs={{8,0},{16,8},{24,16},{28,24},{20,28},{12,20},{4,12},{0,4},{9,1},{1... | collective-permute-start | bytes 1228808 | tf_op jit(solution)/shard_map/ppermute | solution.py:490
  248.9 26.9 %collective-permute-start.42 = (bf16[160,1280]{1,0:T(8,128)(2,1)}, bf16[160,1280]{1,0:T(8,128)(2,1)}, u32[]{:S(2)}, u32[]{:S(2)}) collective-permute-start(bf16[160,1280]{1,0:T(8,128)(2,1)} %get-tuple-element.221), channel_id=1, source_target_pairs={{0,8},{8,16},{16,24},{24,28},{28,20},{20,12},{12,4},{4,0},{1,9},{9... | collective-permute-start | bytes 1228808 | tf_op jit(solution)/shard_map/ppermute | solution.py:489
  250.4 26.9 %collective-permute-start.43 = (bf16[160,1280]{1,0:T(8,128)(2,1)}, bf16[160,1280]{1,0:T(8,128)(2,1)}, u32[]{:S(2)}, u32[]{:S(2)}) collective-permute-start(bf16[160,1280]{1,0:T(8,128)(2,1)} %get-tuple-element.220), channel_id=1, source_target_pairs={{8,0},{16,8},{24,16},{28,24},{20,28},{12,20},{4,12},{0,4},{9,1},{1... | collective-permute-start | bytes 1228808 | tf_op jit(solution)/shard_map/ppermute | solution.py:490
  275.8 11.4 %collective-permute-start.44 = (bf16[160,1280]{1,0:T(8,128)(2,1)}, bf16[160,1280]{1,0:T(8,128)(2,1)S(1)}, u32[]{:S(2)}, u32[]{:S(2)}) collective-permute-start(bf16[160,1280]{1,0:T(8,128)(2,1)} %collective-permute-done.42), channel_id=1, source_target_pairs={{0,8},{8,16},{16,24},{24,28},{28,20},{20,12},{12,4},{4,0},{1,9},{9... | collective-permute-start | bytes 1228808 | tf_op jit(solution)/shard_map/ppermute | solution.py:489
  277.3 11.4 %collective-permute-start.45 = (bf16[160,1280]{1,0:T(8,128)(2,1)}, bf16[160,1280]{1,0:T(8,128)(2,1)S(1)}, u32[]{:S(2)}, u32[]{:S(2)}) collective-permute-start(bf16[160,1280]{1,0:T(8,128)(2,1)} %collective-permute-done.43), channel_id=1, source_target_pairs={{8,0},{16,8},{24,16},{28,24},{20,28},{12,20},{4,12},{0,4},{9,1},{1... | collective-permute-start | bytes 1228808 | tf_op jit(solution)/shard_map/ppermute | solution.py:490
  297.6 18.7 %collective-permute-start.48 = (bf16[160,1280]{1,0:T(8,128)(2,1)S(1)}, bf16[160,1280]{1,0:T(8,128)(2,1)S(1)}, u32[]{:S(2)}, u32[]{:S(2)}) collective-permute-start(bf16[160,1280]{1,0:T(8,128)(2,1)S(1)} %collective-permute-done.46), channel_id=1, source_target_pairs={{0,8},{8,16},{16,24},{24,28},{28,20},{20,12},{12,4},{4,0},{1,9},{9... | collective-permute-start | bytes 1228808 | tf_op jit(solution)/shard_map/ppermute | solution.py:489
  299.1 18.7 %collective-permute-start.49 = (bf16[160,1280]{1,0:T(8,128)(2,1)}, bf16[160,1280]{1,0:T(8,128)(2,1)S(1)}, u32[]{:S(2)}, u32[]{:S(2)}) collective-permute-start(bf16[160,1280]{1,0:T(8,128)(2,1)} %collective-permute-done.47), channel_id=1, source_target_pairs={{8,0},{16,8},{24,16},{28,24},{20,28},{12,20},{4,12},{0,4},{9,1},{1... | collective-permute-start | bytes 1228808 | tf_op jit(solution)/shard_map/ppermute | solution.py:490
  314.2 12.5 %collective-permute-start.105 = (bf16[160,1280]{1,0:T(8,128)(2,1)S(1)}, bf16[160,1280]{1,0:T(8,128)(2,1)S(1)}, u32[]{:S(2)}, u32[]{:S(2)}) collective-permute-start(bf16[160,1280]{1,0:T(8,128)(2,1)S(1)} %get-tuple-element.169), channel_id=1, source_target_pairs={{8,0},{16,8},{24,16},{28,24},{20,28},{12,20},{4,12},{0,4},{9,1},{1... | collective-permute-start | bytes 1228808 | tf_op jit(solution)/shard_map/ppermute | solution.py:510
  314.9 12.4 %collective-permute-start.98 = (bf16[160,1280]{1,0:T(8,128)(2,1)S(1)}, bf16[160,1280]{1,0:T(8,128)(2,1)S(1)}, u32[]{:S(2)}, u32[]{:S(2)}) collective-permute-start(bf16[160,1280]{1,0:T(8,128)(2,1)S(1)} %get-tuple-element.168), channel_id=1, source_target_pairs={{0,8},{8,16},{16,24},{24,28},{28,20},{20,12},{12,4},{4,0},{1,9},{9... | collective-permute-start | bytes 1228808 | tf_op jit(solution)/shard_map/ppermute | solution.py:509
  316.3 19.8 %collective-permute-start.50 = (bf16[160,1280]{1,0:T(8,128)(2,1)S(1)}, bf16[160,1280]{1,0:T(8,128)(2,1)S(1)}, u32[]{:S(2)}, u32[]{:S(2)}) collective-permute-start(bf16[160,1280]{1,0:T(8,128)(2,1)S(1)} %collective-permute-done.48), channel_id=1, source_target_pairs={{0,8},{8,16},{16,24},{24,28},{28,20},{20,12},{12,4},{4,0},{1,9},{9... | collective-permute-start | bytes 1228808 | tf_op jit(solution)/shard_map/ppermute | solution.py:489
  317.8 19.7 %collective-permute-start.51 = (bf16[160,1280]{1,0:T(8,128)(2,1)S(1)}, bf16[160,1280]{1,0:T(8,128)(2,1)S(1)}, u32[]{:S(2)}, u32[]{:S(2)}) collective-permute-start(bf16[160,1280]{1,0:T(8,128)(2,1)S(1)} %collective-permute-done.49), channel_id=1, source_target_pairs={{8,0},{16,8},{24,16},{28,24},{20,28},{12,20},{4,12},{0,4},{9,1},{1... | collective-permute-start | bytes 1228808 | tf_op jit(solution)/shard_map/ppermute | solution.py:490
  328.4 141.2 %collective-permute-start.106 = (bf16[160,1280]{1,0:T(8,128)(2,1)}, bf16[160,1280]{1,0:T(8,128)(2,1)S(1)}, u32[]{:S(2)}, u32[]{:S(2)}) collective-permute-start(bf16[160,1280]{1,0:T(8,128)(2,1)} %get-tuple-element.167), channel_id=1, source_target_pairs={{8,0},{16,8},{24,16},{28,24},{20,28},{12,20},{4,12},{0,4},{9,1},{1... | collective-permute-start | bytes 1228808 | tf_op jit(solution)/shard_map/ppermute | solution.py:510
  329.9 139.7 %collective-permute-start.99 = (bf16[160,1280]{1,0:T(8,128)(2,1)}, bf16[160,1280]{1,0:T(8,128)(2,1)}, u32[]{:S(2)}, u32[]{:S(2)}) collective-permute-start(bf16[160,1280]{1,0:T(8,128)(2,1)} %get-tuple-element.166), channel_id=1, source_target_pairs={{0,8},{8,16},{16,24},{24,28},{28,20},{20,12},{12,4},{4,0},{1,9},{9... | collective-permute-start | bytes 1228808 | tf_op jit(solution)/shard_map/ppermute | solution.py:509
  336.1 14.8 %collective-permute-start.52 = (bf16[160,1280]{1,0:T(8,128)(2,1)S(1)}, bf16[160,1280]{1,0:T(8,128)(2,1)S(1)}, u32[]{:S(2)}, u32[]{:S(2)}) collective-permute-start(bf16[160,1280]{1,0:T(8,128)(2,1)S(1)} %collective-permute-done.50), channel_id=1, source_target_pairs={{0,8},{8,16},{16,24},{24,28},{28,20},{20,12},{12,4},{4,0},{1,9},{9... | collective-permute-start | bytes 1228808 | tf_op jit(solution)/shard_map/ppermute | solution.py:489
  337.5 14.8 %collective-permute-start.53 = (bf16[160,1280]{1,0:T(8,128)(2,1)S(1)}, bf16[160,1280]{1,0:T(8,128)(2,1)S(1)}, u32[]{:S(2)}, u32[]{:S(2)}) collective-permute-start(bf16[160,1280]{1,0:T(8,128)(2,1)S(1)} %collective-permute-done.51), channel_id=1, source_target_pairs={{8,0},{16,8},{24,16},{28,24},{20,28},{12,20},{4,12},{0,4},{9,1},{1... | collective-permute-start | bytes 1228808 | tf_op jit(solution)/shard_map/ppermute | solution.py:490
  469.6 299.8 %reduce-scatter.3.cloned.1.call-start = ((), (), s32[]{:S(2)}) async-start(), calls=%async_computation.2 | async-start | bytes 6553600 | tf_op jit(solution)/shard_map/reduce_scatter | solution.py:596
  472.1 11.5 %collective-permute-start.100 = (bf16[160,1280]{1,0:T(8,128)(2,1)}, bf16[160,1280]{1,0:T(8,128)(2,1)}, u32[]{:S(2)}, u32[]{:S(2)}) collective-permute-start(bf16[160,1280]{1,0:T(8,128)(2,1)} %get-tuple-element.164), channel_id=1, source_target_pairs={{0,8},{8,16},{16,24},{24,28},{28,20},{20,12},{12,4},{4,0},{1,9},{9... | collective-permute-start | bytes 1228808 | tf_op jit(solution)/shard_map/ppermute | solution.py:509
  473.5 11.3 %collective-permute-start.107 = (bf16[160,1280]{1,0:T(8,128)(2,1)}, bf16[160,1280]{1,0:T(8,128)(2,1)}, u32[]{:S(2)}, u32[]{:S(2)}) collective-permute-start(bf16[160,1280]{1,0:T(8,128)(2,1)} %get-tuple-element.165), channel_id=1, source_target_pairs={{8,0},{16,8},{24,16},{28,24},{20,28},{12,20},{4,12},{0,4},{9,1},{1... | collective-permute-start | bytes 1228808 | tf_op jit(solution)/shard_map/ppermute | solution.py:510
  487.3 69.8 %collective-permute-start.101 = (bf16[160,1280]{1,0:T(8,128)(2,1)}, bf16[160,1280]{1,0:T(8,128)(2,1)}, u32[]{:S(2)}, u32[]{:S(2)}) collective-permute-start(bf16[160,1280]{1,0:T(8,128)(2,1)} %get-tuple-element.162), channel_id=1, source_target_pairs={{0,8},{8,16},{16,24},{24,28},{28,20},{20,12},{12,4},{4,0},{1,9},{9... | collective-permute-start | bytes 1228808 | tf_op jit(solution)/shard_map/ppermute | solution.py:509
  488.1 70.1 %collective-permute-start.108 = (bf16[160,1280]{1,0:T(8,128)(2,1)}, bf16[160,1280]{1,0:T(8,128)(2,1)}, u32[]{:S(2)}, u32[]{:S(2)}) collective-permute-start(bf16[160,1280]{1,0:T(8,128)(2,1)} %get-tuple-element.163), channel_id=1, source_target_pairs={{8,0},{16,8},{24,16},{28,24},{20,28},{12,20},{4,12},{0,4},{9,1},{1... | collective-permute-start | bytes 1228808 | tf_op jit(solution)/shard_map/ppermute | solution.py:510
  495.2 34.1 %collective-permute-start.84 = (bf16[160,276]{0,1:T(8,128)(2,1)S(1)}, bf16[160,276]{0,1:T(8,128)(2,1)}, u32[]{:S(2)}, u32[]{:S(2)}) collective-permute-start(bf16[160,276]{0,1:T(8,128)(2,1)S(1)} %get-tuple-element.217), channel_id=1, source_target_pairs={{0,8},{8,16},{16,24},{24,28},{28,20},{20,12},{12,4},{4,0},{1,9},{9... | collective-permute-start | bytes 264968 | tf_op jit(solution)/shard_map/ppermute | solution.py:509
  496.0 33.3 %collective-permute-start.91 = (bf16[160,276]{0,1:T(8,128)(2,1)S(1)}, bf16[160,276]{0,1:T(8,128)(2,1)}, u32[]{:S(2)}, u32[]{:S(2)}) collective-permute-start(bf16[160,276]{0,1:T(8,128)(2,1)S(1)} %get-tuple-element.216), channel_id=1, source_target_pairs={{8,0},{16,8},{24,16},{28,24},{20,28},{12,20},{4,12},{0,4},{9,1},{1... | collective-permute-start | bytes 264968 | tf_op jit(solution)/shard_map/ppermute | solution.py:510
  550.2 22.8 %collective-permute-start.70 = (bf16[160,1280]{1,0:T(8,128)(2,1)}, bf16[160,1280]{1,0:T(8,128)(2,1)}, u32[]{:S(2)}, u32[]{:S(2)}) collective-permute-start(bf16[160,1280]{1,0:T(8,128)(2,1)} %get-tuple-element.184), channel_id=1, source_target_pairs={{0,8},{8,16},{16,24},{24,28},{28,20},{20,12},{12,4},{4,0},{1,9},{9... | collective-permute-start | bytes 1228808 | tf_op jit(solution)/shard_map/ppermute | solution.py:509
  552.3 247.8 %all-reduce.8.cloned.1.call-start = ((), (), s32[]{:S(2)}) async-start(), calls=%async_computation.5 | async-start | bytes 786432 | tf_op jit(solution)/shard_map/psum | solution.py:629
  553.4 22.2 %collective-permute-start.77 = (bf16[160,1280]{1,0:T(8,128)(2,1)}, bf16[160,1280]{1,0:T(8,128)(2,1)S(1)}, u32[]{:S(2)}, u32[]{:S(2)}) collective-permute-start(bf16[160,1280]{1,0:T(8,128)(2,1)} %get-tuple-element.185), channel_id=1, source_target_pairs={{8,0},{16,8},{24,16},{28,24},{20,28},{12,20},{4,12},{0,4},{9,1},{1... | collective-permute-start | bytes 1228808 | tf_op jit(solution)/shard_map/ppermute | solution.py:510
  554.6 33.3 %collective-permute-start.56 = (bf16[160,1280]{1,0:T(8,128)(2,1)}, bf16[160,1280]{1,0:T(8,128)(2,1)S(1)}, u32[]{:S(2)}, u32[]{:S(2)}) collective-permute-start(bf16[160,1280]{1,0:T(8,128)(2,1)} %get-tuple-element.200), channel_id=1, source_target_pairs={{0,8},{8,16},{16,24},{24,28},{28,20},{20,12},{12,4},{4,0},{1,9},{9... | collective-permute-start | bytes 1228808 | tf_op jit(solution)/shard_map/ppermute | solution.py:509
  557.1 13.0 %collective-permute-start.88 = (bf16[160,276]{0,1:T(8,128)(2,1)S(1)}, bf16[160,276]{0,1:T(8,128)(2,1)S(1)}, u32[]{:S(2)}, u32[]{:S(2)}) collective-permute-start(bf16[160,276]{0,1:T(8,128)(2,1)S(1)} %get-tuple-element.209), channel_id=1, source_target_pairs={{0,8},{8,16},{16,24},{24,28},{28,20},{20,12},{12,4},{4,0},{1,9},{9... | collective-permute-start | bytes 264968 | tf_op jit(solution)/shard_map/ppermute | solution.py:509
  558.2 12.4 %collective-permute-start.95 = (bf16[160,276]{0,1:T(8,128)(2,1)S(1)}, bf16[160,276]{0,1:T(8,128)(2,1)S(1)}, u32[]{:S(2)}, u32[]{:S(2)}) collective-permute-start(bf16[160,276]{0,1:T(8,128)(2,1)S(1)} %get-tuple-element.208), channel_id=1, source_target_pairs={{8,0},{16,8},{24,16},{28,24},{20,28},{12,20},{4,12},{0,4},{9,1},{1... | collective-permute-start | bytes 264968 | tf_op jit(solution)/shard_map/ppermute | solution.py:510
  570.1 20.4 %collective-permute-start.63 = (bf16[160,1280]{1,0:T(8,128)(2,1)S(1)}, bf16[160,1280]{1,0:T(8,128)(2,1)S(1)}, u32[]{:S(2)}, u32[]{:S(2)}) collective-permute-start(bf16[160,1280]{1,0:T(8,128)(2,1)S(1)} %get-tuple-element.201), channel_id=1, source_target_pairs={{8,0},{16,8},{24,16},{28,24},{20,28},{12,20},{4,12},{0,4},{9,1},{1... | collective-permute-start | bytes 1228808 | tf_op jit(solution)/shard_map/ppermute | solution.py:510
  570.6 34.0 %collective-permute-start.102 = (bf16[160,1280]{1,0:T(8,128)(2,1)S(1)}, bf16[160,1280]{1,0:T(8,128)(2,1)S(1)}, u32[]{:S(2)}, u32[]{:S(2)}) collective-permute-start(bf16[160,1280]{1,0:T(8,128)(2,1)S(1)} %get-tuple-element.160), channel_id=1, source_target_pairs={{0,8},{8,16},{16,24},{24,28},{28,20},{20,12},{12,4},{4,0},{1,9},{9... | collective-permute-start | bytes 1228808 | tf_op jit(solution)/shard_map/ppermute | solution.py:509
  584.3 22.4 %collective-permute-start.109 = (bf16[160,1280]{1,0:T(8,128)(2,1)S(1)}, bf16[160,1280]{1,0:T(8,128)(2,1)S(1)}, u32[]{:S(2)}, u32[]{:S(2)}) collective-permute-start(bf16[160,1280]{1,0:T(8,128)(2,1)S(1)} %get-tuple-element.161), channel_id=1, source_target_pairs={{8,0},{16,8},{24,16},{28,24},{20,28},{12,20},{4,12},{0,4},{9,1},{1... | collective-permute-start | bytes 1228808 | tf_op jit(solution)/shard_map/ppermute | solution.py:510
  586.7 21.8 %collective-permute-start.71 = (bf16[160,1280]{1,0:T(8,128)(2,1)S(1)}, bf16[160,1280]{1,0:T(8,128)(2,1)S(1)}, u32[]{:S(2)}, u32[]{:S(2)}) collective-permute-start(bf16[160,1280]{1,0:T(8,128)(2,1)S(1)} %get-tuple-element.182), channel_id=1, source_target_pairs={{0,8},{8,16},{16,24},{24,28},{28,20},{20,12},{12,4},{4,0},{1,9},{9... | collective-permute-start | bytes 1228808 | tf_op jit(solution)/shard_map/ppermute | solution.py:509
  587.9 13.7 %collective-permute-start.90 = (bf16[160,276]{0,1:T(8,128)(2,1)S(1)}, bf16[160,276]{0,1:T(8,128)(2,1)S(1)}, u32[]{:S(2)}, u32[]{:S(2)}) collective-permute-start(bf16[160,276]{0,1:T(8,128)(2,1)S(1)} %get-tuple-element.205), channel_id=1, source_target_pairs={{0,8},{8,16},{16,24},{24,28},{28,20},{20,12},{12,4},{4,0},{1,9},{9... | collective-permute-start | bytes 264968 | tf_op jit(solution)/shard_map/ppermute | solution.py:509
  590.4 12.5 %collective-permute-start.97 = (bf16[160,276]{0,1:T(8,128)(2,1)S(1)}, bf16[160,276]{0,1:T(8,128)(2,1)S(1)}, u32[]{:S(2)}, u32[]{:S(2)}) collective-permute-start(bf16[160,276]{0,1:T(8,128)(2,1)S(1)} %get-tuple-element.204), channel_id=1, source_target_pairs={{8,0},{16,8},{24,16},{28,24},{20,28},{12,20},{4,12},{0,4},{9,1},{1... | collective-permute-start | bytes 264968 | tf_op jit(solution)/shard_map/ppermute | solution.py:510
  601.5 12.4 %collective-permute-start.78 = (bf16[160,1280]{1,0:T(8,128)(2,1)S(1)}, bf16[160,1280]{1,0:T(8,128)(2,1)S(1)}, u32[]{:S(2)}, u32[]{:S(2)}) collective-permute-start(bf16[160,1280]{1,0:T(8,128)(2,1)S(1)} %get-tuple-element.183), channel_id=1, source_target_pairs={{8,0},{16,8},{24,16},{28,24},{20,28},{12,20},{4,12},{0,4},{9,1},{1... | collective-permute-start | bytes 1228808 | tf_op jit(solution)/shard_map/ppermute | solution.py:510
  602.9 14.4 %collective-permute-start.57 = (bf16[160,1280]{1,0:T(8,128)(2,1)S(1)}, bf16[160,1280]{1,0:T(8,128)(2,1)S(1)}, u32[]{:S(2)}, u32[]{:S(2)}) collective-permute-start(bf16[160,1280]{1,0:T(8,128)(2,1)S(1)} %get-tuple-element.198), channel_id=1, source_target_pairs={{0,8},{8,16},{16,24},{24,28},{28,20},{20,12},{12,4},{4,0},{1,9},{9... | collective-permute-start | bytes 1228808 | tf_op jit(solution)/shard_map/ppermute | solution.py:509
  604.6 18.1 %collective-permute-start.64 = (bf16[160,1280]{1,0:T(8,128)(2,1)S(1)}, bf16[160,1280]{1,0:T(8,128)(2,1)S(1)}, u32[]{:S(2)}, u32[]{:S(2)}) collective-permute-start(bf16[160,1280]{1,0:T(8,128)(2,1)S(1)} %get-tuple-element.199), channel_id=1, source_target_pairs={{8,0},{16,8},{24,16},{28,24},{20,28},{12,20},{4,12},{0,4},{9,1},{1... | collective-permute-start | bytes 1228808 | tf_op jit(solution)/shard_map/ppermute | solution.py:510
  608.0 17.0 %collective-permute-start.103 = (bf16[160,1280]{1,0:T(8,128)(2,1)S(1)}, bf16[160,1280]{1,0:T(8,128)(2,1)S(1)}, u32[]{:S(2)}, u32[]{:S(2)}) collective-permute-start(bf16[160,1280]{1,0:T(8,128)(2,1)S(1)} %get-tuple-element.158), channel_id=1, source_target_pairs={{0,8},{8,16},{16,24},{24,28},{28,20},{20,12},{12,4},{4,0},{1,9},{9... | collective-permute-start | bytes 1228808 | tf_op jit(solution)/shard_map/ppermute | solution.py:509
  608.5 22.9 %collective-permute-start.110 = (bf16[160,1280]{1,0:T(8,128)(2,1)S(1)}, bf16[160,1280]{1,0:T(8,128)(2,1)S(1)}, u32[]{:S(2)}, u32[]{:S(2)}) collective-permute-start(bf16[160,1280]{1,0:T(8,128)(2,1)S(1)} %get-tuple-element.159), channel_id=1, source_target_pairs={{8,0},{16,8},{24,16},{28,24},{20,28},{12,20},{4,12},{0,4},{9,1},{1... | collective-permute-start | bytes 1228808 | tf_op jit(solution)/shard_map/ppermute | solution.py:510
  615.3 19.7 %collective-permute-start.72 = (bf16[160,1280]{1,0:T(8,128)(2,1)S(1)}, bf16[160,1280]{1,0:T(8,128)(2,1)S(1)}, u32[]{:S(2)}, u32[]{:S(2)}) collective-permute-start(bf16[160,1280]{1,0:T(8,128)(2,1)S(1)} %get-tuple-element.180), channel_id=1, source_target_pairs={{0,8},{8,16},{16,24},{24,28},{28,20},{20,12},{12,4},{4,0},{1,9},{9... | collective-permute-start | bytes 1228808 | tf_op jit(solution)/shard_map/ppermute | solution.py:509
  617.4 22.9 %collective-permute-start.79 = (bf16[160,1280]{1,0:T(8,128)(2,1)S(1)}, bf16[160,1280]{1,0:T(8,128)(2,1)S(1)}, u32[]{:S(2)}, u32[]{:S(2)}) collective-permute-start(bf16[160,1280]{1,0:T(8,128)(2,1)S(1)} %get-tuple-element.181), channel_id=1, source_target_pairs={{8,0},{16,8},{24,16},{28,24},{20,28},{12,20},{4,12},{0,4},{9,1},{1... | collective-permute-start | bytes 1228808 | tf_op jit(solution)/shard_map/ppermute | solution.py:510
  622.9 19.7 %collective-permute-start.58 = (bf16[160,1280]{1,0:T(8,128)(2,1)S(1)}, bf16[160,1280]{1,0:T(8,128)(2,1)S(1)}, u32[]{:S(2)}, u32[]{:S(2)}) collective-permute-start(bf16[160,1280]{1,0:T(8,128)(2,1)S(1)} %get-tuple-element.196), channel_id=1, source_target_pairs={{0,8},{8,16},{16,24},{24,28},{28,20},{20,12},{12,4},{4,0},{1,9},{9... | collective-permute-start | bytes 1228808 | tf_op jit(solution)/shard_map/ppermute | solution.py:509
  625.0 24.0 %collective-permute-start.65 = (bf16[160,1280]{1,0:T(8,128)(2,1)S(1)}, bf16[160,1280]{1,0:T(8,128)(2,1)S(1)}, u32[]{:S(2)}, u32[]{:S(2)}) collective-permute-start(bf16[160,1280]{1,0:T(8,128)(2,1)S(1)} %get-tuple-element.197), channel_id=1, source_target_pairs={{8,0},{16,8},{24,16},{28,24},{20,28},{12,20},{4,12},{0,4},{9,1},{1... | collective-permute-start | bytes 1228808 | tf_op jit(solution)/shard_map/ppermute | solution.py:510
  632.8 18.5 %collective-permute-start.104 = (bf16[160,1280]{1,0:T(8,128)(2,1)S(1)}, bf16[160,1280]{1,0:T(8,128)(2,1)S(1)}, u32[]{:S(2)}, u32[]{:S(2)}) collective-permute-start(bf16[160,1280]{1,0:T(8,128)(2,1)S(1)} %get-tuple-element.156), channel_id=1, source_target_pairs={{0,8},{8,16},{16,24},{24,28},{28,20},{20,12},{12,4},{4,0},{1,9},{9... | collective-permute-start | bytes 1228808 | tf_op jit(solution)/shard_map/ppermute | solution.py:509
  634.9 22.9 %collective-permute-start.111 = (bf16[160,1280]{1,0:T(8,128)(2,1)S(1)}, bf16[160,1280]{1,0:T(8,128)(2,1)S(1)}, u32[]{:S(2)}, u32[]{:S(2)}) collective-permute-start(bf16[160,1280]{1,0:T(8,128)(2,1)S(1)} %get-tuple-element.157), channel_id=1, source_target_pairs={{8,0},{16,8},{24,16},{28,24},{20,28},{12,20},{4,12},{0,4},{9,1},{1... | collective-permute-start | bytes 1228808 | tf_op jit(solution)/shard_map/ppermute | solution.py:510
  640.5 19.9 %collective-permute-start.73 = (bf16[160,1280]{1,0:T(8,128)(2,1)S(1)}, bf16[160,1280]{1,0:T(8,128)(2,1)S(1)}, u32[]{:S(2)}, u32[]{:S(2)}) collective-permute-start(bf16[160,1280]{1,0:T(8,128)(2,1)S(1)} %get-tuple-element.178), channel_id=1, source_target_pairs={{0,8},{8,16},{16,24},{24,28},{28,20},{20,12},{12,4},{4,0},{1,9},{9... | collective-permute-start | bytes 1228808 | tf_op jit(solution)/shard_map/ppermute | solution.py:509
  642.6 24.0 %collective-permute-start.80 = (bf16[160,1280]{1,0:T(8,128)(2,1)S(1)}, bf16[160,1280]{1,0:T(8,128)(2,1)S(1)}, u32[]{:S(2)}, u32[]{:S(2)}) collective-permute-start(bf16[160,1280]{1,0:T(8,128)(2,1)S(1)} %get-tuple-element.179), channel_id=1, source_target_pairs={{8,0},{16,8},{24,16},{28,24},{20,28},{12,20},{4,12},{0,4},{9,1},{1... | collective-permute-start | bytes 1228808 | tf_op jit(solution)/shard_map/ppermute | solution.py:510
  649.3 19.6 %collective-permute-start.59 = (bf16[160,1280]{1,0:T(8,128)(2,1)S(1)}, bf16[160,1280]{1,0:T(8,128)(2,1)S(1)}, u32[]{:S(2)}, u32[]{:S(2)}) collective-permute-start(bf16[160,1280]{1,0:T(8,128)(2,1)S(1)} %get-tuple-element.194), channel_id=1, source_target_pairs={{0,8},{8,16},{16,24},{24,28},{28,20},{20,12},{12,4},{4,0},{1,9},{9... | collective-permute-start | bytes 1228808 | tf_op jit(solution)/shard_map/ppermute | solution.py:509
  651.4 24.0 %collective-permute-start.66 = (bf16[160,1280]{1,0:T(8,128)(2,1)S(1)}, bf16[160,1280]{1,0:T(8,128)(2,1)S(1)}, u32[]{:S(2)}, u32[]{:S(2)}) collective-permute-start(bf16[160,1280]{1,0:T(8,128)(2,1)S(1)} %get-tuple-element.195), channel_id=1, source_target_pairs={{8,0},{16,8},{24,16},{28,24},{20,28},{12,20},{4,12},{0,4},{9,1},{1... | collective-permute-start | bytes 1228808 | tf_op jit(solution)/shard_map/ppermute | solution.py:510
  668.9 15.2 %collective-permute-start.81 = (bf16[160,1280]{1,0:T(8,128)(2,1)S(1)}, bf16[160,1280]{1,0:T(8,128)(2,1)S(1)}, u32[]{:S(2)}, u32[]{:S(2)}) collective-permute-start(bf16[160,1280]{1,0:T(8,128)(2,1)S(1)} %get-tuple-element.177), channel_id=1, source_target_pairs={{8,0},{16,8},{24,16},{28,24},{20,28},{12,20},{4,12},{0,4},{9,1},{1... | collective-permute-start | bytes 1228808 | tf_op jit(solution)/shard_map/ppermute | solution.py:510
  677.7 15.3 %collective-permute-start.67 = (bf16[160,1280]{1,0:T(8,128)(2,1)S(1)}, bf16[160,1280]{1,0:T(8,128)(2,1)S(1)}, u32[]{:S(2)}, u32[]{:S(2)}) collective-permute-start(bf16[160,1280]{1,0:T(8,128)(2,1)S(1)} %get-tuple-element.193), channel_id=1, source_target_pairs={{8,0},{16,8},{24,16},{28,24},{20,28},{12,20},{4,12},{0,4},{9,1},{1... | collective-permute-start | bytes 1228808 | tf_op jit(solution)/shard_map/ppermute | solution.py:510
  686.5 15.3 %collective-permute-start.82 = (bf16[160,1280]{1,0:T(8,128)(2,1)S(1)}, bf16[160,1280]{1,0:T(8,128)(2,1)S(1)}, u32[]{:S(2)}, u32[]{:S(2)}) collective-permute-start(bf16[160,1280]{1,0:T(8,128)(2,1)S(1)} %get-tuple-element.175), channel_id=1, source_target_pairs={{8,0},{16,8},{24,16},{28,24},{20,28},{12,20},{4,12},{0,4},{9,1},{1... | collective-permute-start | bytes 1228808 | tf_op jit(solution)/shard_map/ppermute | solution.py:510
  695.2 13.9 %collective-permute-start.68 = (bf16[160,1280]{1,0:T(8,128)(2,1)S(1)}, bf16[160,1280]{1,0:T(8,128)(2,1)S(1)}, u32[]{:S(2)}, u32[]{:S(2)}) collective-permute-start(bf16[160,1280]{1,0:T(8,128)(2,1)S(1)} %get-tuple-element.191), channel_id=1, source_target_pairs={{8,0},{16,8},{24,16},{28,24},{20,28},{12,20},{4,12},{0,4},{9,1},{1... | collective-permute-start | bytes 1228808 | tf_op jit(solution)/shard_map/ppermute | solution.py:510
  (94 other events, 1643.2 us)
Sparse Core Ops, SparseCore 0:
  12.4 42.0 all-gather.1
  469.7 51.3 reduce-scatter.4
  552.4 50.1 reduce-scatter.2
  769.5 30.5 all-reduce.7

commit v4 on v3

--- a/solution.py
+++ b/solution.py
@@ -4,6 +4,7 @@
 import jax.numpy as jnp
 from jax import lax
 from jax.experimental import pallas as pl
+from jax.experimental.layout import Layout, with_layout_constraint
 from jax.experimental.pallas import tpu as pltpu
 from jax.sharding import PartitionSpec as P
 
@@ -154,20 +155,21 @@
 
 
 def bwd_kernel(
-    value_ref, mixed_ref, grad_ref, taps_ref, bias_ref, skip_ref, dtx_ref, cumx_ref, cumt_ref,
-    masks_ref, b_ref, c_ref, bt_ref, ct_ref, gt_ref,
-    value_out, sums_out, db_ref, dc_ref, dg_ref, z_ref, dt_ref,
-    pre_scr, x_scr, dpre_scr, state_scr,
+    first, resumed, value_ref, mixed_ref, grad_ref, taps_ref, bias_ref, skip_ref, dtx_ref, cumx_ref, cumt_ref,
+    masks_ref, b_ref, c_ref, bt_ref, ct_ref, gt_ref, *more,
 ):
+    earlier, more = more[: 7 * resumed], more[7 * resumed :]
+    value_out, sums_out, *totals, pre_scr, x_scr, dpre_scr, state_scr = more
+    db_ref, dc_ref, dg_ref, z_ref, dt_ref = totals
     rows = value_ref.shape[0]
     blocks = rows // SPAN
-    pair = pl.program_id(0)
+    pair = pl.program_id(0) + first
     masks = [masks_ref[k] for k in range(3)]
 
-    @pl.when(pair == 0)
+    @pl.when(pl.program_id(0) == 0)
     def _():
-        for ref in (db_ref, dc_ref, dg_ref, z_ref, dt_ref):
-            ref[...] = jnp.zeros_like(ref)
+        for place, ref in enumerate(totals):
+            ref[...] = earlier[2 + place][...] if resumed else jnp.zeros_like(ref)
 
     pre = conv_in(value_ref[...], taps_ref[...], bias_ref[...], masks)
     pre_scr[...] = pre
@@ -281,7 +283,9 @@
     step_sums[...] = jnp.concatenate([bias_sum, rate_sum, jnp.zeros((6, LANES), wide)], 0)
 
 
-def call(kernel, outs, operands, grid=None, in_specs=None, out_specs=None, scratch=(), flops=0):
+def call(
+    kernel, outs, operands, grid=None, in_specs=None, out_specs=None, scratch=(), flops=0, aliases={}
+):
     shapes = tuple(jax.ShapeDtypeStruct(shape, kind) for shape, kind in outs)
     moved = sum(a.size * a.dtype.itemsize for a in operands)
     moved += sum(s.size * s.dtype.itemsize for s in shapes)
@@ -291,13 +295,14 @@
         out_shape=shapes,
         scratch_shapes=list(scratch),
         compiler_params=pltpu.CompilerParams(vmem_limit_bytes=VMEM_BYTES),
+        input_output_aliases=dict(aliases),
         cost_estimate=pl.CostEstimate(flops=flops, bytes_accessed=moved, transcendentals=0),
         **extra,
     )(*operands)
 
 
-def column_block(rows):
-    return pl.BlockSpec((rows, LANES), lambda i: (0, i))
+def column_block(rows, first=0):
+    return pl.BlockSpec((rows, LANES), lambda i: (0, i + first))
 
 
 def whole_block(shape):
@@ -391,40 +396,50 @@
         self.mixed = mixed
         return mixed[:, : self.inner]
 
-    def backward(self, grad_mixed):
+    def backward_part(self, grad_mixed, first, last, earlier=()):
         rows, states = self.rows, self.states
-        value_grad, sums, db, dc, dg, z, dt = call(
-            bwd_kernel,
-            [((rows, self.width), low), ((8, self.width), wide)]
-            + [((rows, LANES), wide)] * 5,
+        operands = (
             (self.value[0], self.mixed, self.widen(grad_mixed))
             + self.value[1:]
             + (self.dtx, self.cumx, self.cumt, self.masks, self.b, self.c, self.bt, self.ct)
-            + (self.gt,),
-            grid=(self.pairs,),
+            + (self.gt,)
+        )
+        totals = [whole_block((rows, LANES))] * 5
+        resumed = bool(earlier)
+        return call(
+            functools.partial(bwd_kernel, first, resumed),
+            [((rows, self.width), low), ((8, self.width), wide)]
+            + [((rows, LANES), wide)] * 5,
+            operands + tuple(earlier),
+            grid=(last - first,),
             in_specs=[
-                column_block(rows),
-                column_block(rows),
-                column_block(rows),
-                column_block(4),
-                column_block(1),
-                column_block(1),
-                column_block(rows),
-                column_block(rows),
-                pl.BlockSpec((1, 2, rows), lambda i: (i, 0, 0)),
+                column_block(rows, first),
+                column_block(rows, first),
+                column_block(rows, first),
+                column_block(4, first),
+                column_block(1, first),
+                column_block(1, first),
+                column_block(rows, first),
+                column_block(rows, first),
+                pl.BlockSpec((1, 2, rows), lambda i: (i + first, 0, 0)),
                 whole_block((5, rows, LANES)),
                 whole_block((rows, states)),
                 whole_block((rows, states)),
                 whole_block((states, rows)),
                 whole_block((states, rows)),
                 whole_block((rows, SPAN)),
-            ],
-            out_specs=[column_block(rows), column_block(8)] + [whole_block((rows, LANES))] * 5,
+            ]
+            + ([pl.BlockSpec(memory_space=pl.ANY)] * 2 + totals if resumed else []),
+            out_specs=[column_block(rows, first), column_block(8, first)] + totals,
             scratch=[pltpu.VMEM((rows, LANES), wide)] * 3
             + [pltpu.VMEM((self.blocks, states, LANES), wide)],
-            flops=60 * rows * LANES * self.width,
-        )
-        state_grad, step_grad, state_sums, step_sums = call(
+            flops=60 * rows * LANES * (last - first) * LANES,
+            aliases={len(operands): 0, len(operands) + 1: 1} if resumed else {},
+        )
+
+    def backward_end(self, db, dc, dg, z, dt):
+        rows, states = self.rows, self.states
+        return call(
             post_kernel,
             [
                 ((rows, 2 * states), low),
@@ -436,6 +451,14 @@
             scratch=[pltpu.VMEM((2, rows, states), wide)],
             flops=12 * rows * LANES * self.width,
         )
+
+    def backward(self, grad_mixed):
+        half = (self.pairs + 1) // 2
+        part = self.backward_part(grad_mixed, 0, half)
+        value_grad, sums, *totals = self.backward_part(grad_mixed, half, self.pairs, part)
+        return self.gradients(value_grad, sums, *self.backward_end(*totals))
+
+    def gradients(self, value_grad, sums, state_grad, step_grad, state_sums, step_sums):
         heads = self.head_count
         skip_grad = sums[5, : self.inner].reshape(heads, HALF).sum(axis=1)
         return (
@@ -493,26 +516,74 @@
     return fulls, (up, down)
 
 
-def ring_scatter(partial):
-    count = lax.axis_size("gx")
-    ahead, behind = ring_moves(count)
-    place = ring_place(lax.axis_index("gx"), count)
-    rows = partial.shape[0] // count
-    half = rows // 2
-
-    def part(target, offset):
-        start = ring_index(target, count) * rows + offset
-        return lax.dynamic_slice_in_dim(partial, start, half, 0)
-
-    up, down = part(place - 1, 0), part(place + 1, half)
-    for step in range(1, count):
-        up = lax.ppermute(up, "gx", ahead).astype(wide)
-        down = lax.ppermute(down, "gx", behind).astype(wide)
-        up = up + part(place - 1 - step, 0).astype(wide)
-        down = down + part(place + 1 + step, half).astype(wide)
-        if step < count - 1:
-            up, down = up.astype(low), down.astype(low)
-    return jnp.concatenate([up, down], 0)
+class RingSum:
+    def __init__(self, partial):
+        self.count = lax.axis_size("gx")
+        self.moves = ring_moves(self.count)
+        self.place = ring_place(lax.axis_index("gx"), self.count)
+        self.rows = partial.shape[0] // self.count
+        self.half = self.rows // 2
+        self.partial = partial
+        self.taken = 0
+        self.held = (self.part(-1, 0), self.part(1, self.half))
+
+    def part(self, target, offset):
+        start = ring_index(self.place + target, self.count) * self.rows + offset
+        return lax.dynamic_slice_in_dim(self.partial, start, self.half, 0)
+
+    def step(self, times=1):
+        for _ in range(min(times, self.count - 1 - self.taken)):
+            self.taken += 1
+            up, down = (
+                lax.ppermute(held, "gx", move).astype(wide)
+                for held, move in zip(self.held, self.moves)
+            )
+            up = up + self.part(-1 - self.taken, 0).astype(wide)
+            down = down + self.part(1 + self.taken, self.half).astype(wide)
+            if self.taken < self.count - 1:
+                up, down = up.astype(low), down.astype(low)
+            self.held = (up, down)
+        return self.held
+
+    def finish(self):
+        return jnp.concatenate(self.step(self.count), 0)
+
+
+def flips(count, bit):
+    return [(k, k ^ bit) for k in range(count)]
+
+
+def halving_sum(partial, axis):
+    count = lax.axis_size(axis)
+    me = lax.axis_index(axis)
+    held = partial.reshape(count, partial.shape[0] // count, partial.shape[1])
+    bit = 1
+    while bit < count:
+        pairs = held.reshape(held.shape[0] // 2, 2, *held.shape[1:])
+        mine = (me // bit) % 2
+        kept = lax.dynamic_index_in_dim(pairs, mine, 1, keepdims=False)
+        given = lax.dynamic_index_in_dim(pairs, 1 - mine, 1, keepdims=False)
+        got = lax.ppermute(given, axis, flips(count, bit))
+        held = (kept.astype(wide) + got.astype(wide)).astype(partial.dtype)
+        bit *= 2
+    return held[0]
+
+
+def butterfly_sum(v, axis):
+    count = lax.axis_size(axis)
+    bit = 1
+    while bit < count:
+        v = v + lax.ppermute(v, axis, flips(count, bit))
+        bit *= 2
+    return v
+
+
+def scatter_rows(partial):
+    return lax.psum_scatter(partial, "gx", scatter_dimension=0, tiled=True)
+
+
+def row_major(v):
+    return with_layout_constraint(v, Layout((0, 1)))
 
 
 def after(value, *others):
@@ -544,11 +615,11 @@
     col_start = lax.axis_index("gy") * col_width
 
     state_step_weight = jnp.concatenate([state_weight, step_weight], 1)
-    (full_state,), moved = ring_gather(state_step_weight, [])
-    (full_value,), moved = ring_gather(after(value_weight, *moved), [])
+    full_state = lax.all_gather(state_step_weight, "gx", axis=0, tiled=True)
+    upstream = lax.all_gather(cotangent, "gy", axis=1, tiled=True)
+    full_out = lax.all_gather(out_weight.T, "gx", axis=0, tiled=True)
+    (full_value,), moved = ring_gather(value_weight, [])
     (full_gate,), moved = ring_gather(after(gate_weight, *moved), [])
-    (full_out,), moved = ring_gather(after(out_weight.T, *moved), [])
-    upstream = lax.all_gather(cotangent, "gy", axis=1, tiled=True)
 
     tokens = layer_input.astype(wide)
     scale_in = lax.rsqrt(jnp.mean(tokens * tokens, axis=1, keepdims=True) + epsilon)
@@ -566,50 +637,69 @@
     )
     value_in = dot(normed, full_value)
     mixed = mixer.forward(value_in, conv_value, conv_value_bias, skip_scale)
+    full_value_state = jnp.concatenate([full_value, full_state], 1)
+    up_back = dot(upstream, full_out)
     gate_in = dot(normed, full_gate)
     gate_open = jax.nn.sigmoid(gate_in)
     gate_act = gate_in * gate_open
     gated = mixed * gate_act
-    squares = lax.psum(jnp.sum(gated * gated, axis=1), "gy")
-    scale_out = lax.rsqrt(squares / INNER + epsilon)[:, None]
+
+    sums_out = lax.psum(
+        jnp.stack(
+            [jnp.sum(gated * gated, axis=1), jnp.sum(gated * gated_gain * up_back, axis=1)]
+        ),
+        "gy",
+    )
+    scale_out = lax.rsqrt(sums_out[0] / INNER + epsilon)[:, None]
+    grad_scale = sums_out[1][:, None]
     scaled = (gated * gated_gain).astype(low)
 
     scaled_out = (gated * gated_gain * scale_out).astype(low)
-    grad_out = ring_scatter(contract_rows(upstream, scaled_out).astype(low))
-
-    up_back = dot(upstream, full_out)
-    grad_scale = lax.psum(jnp.sum(gated * gated_gain * up_back, axis=1), "gy")[:, None]
-    grad_scaled = scale_out * up_back
+    out_ring = RingSum(row_major(contract_rows(upstream, scaled_out).astype(low)))
+
+    grad_scaled = scale_out * after(up_back, *out_ring.held)
     grad_gated = grad_scaled * gated_gain - grad_scale * scale_out**3 * gated / INNER
     gate_gain_part = jnp.sum(grad_scaled * gated, axis=0)
     grad_gate_in = (
         grad_gated * mixed * gate_open * (1.0 + gate_in * (1.0 - gate_open))
     ).astype(low)
-    grad_gate = ring_scatter(contract_rows(normed, grad_gate_in).astype(low))
-
-    pulled = mixer.backward(grad_gated * gate_act)
-    grad_value_in = pulled[0]
+    grad_mixed = grad_gated * gate_act
+    gate_partial = contract_rows(after(normed, *out_ring.step()), grad_gate_in)
+    gate_ring = RingSum(row_major(gate_partial.astype(low)))
+
+    half = (mixer.pairs + 1) // 2
+    part = mixer.backward_part(after(grad_mixed, *out_ring.step(), *gate_ring.held), 0, half)
+    grad_mixed = after(grad_mixed, *out_ring.step(), *gate_ring.step(), part[0])
+    value_grad, value_sums, *totals = mixer.backward_part(grad_mixed, half, mixer.pairs, part)
+    grad_value_in = value_grad[:, : gate_weight.shape[1]]
+    value_partial = contract_rows(
+        after(normed, *out_ring.step(), *gate_ring.step()), grad_value_in
+    )
+    value_ring = RingSum(row_major(value_partial.astype(low)))
+    ends = mixer.backward_end(
+        after(totals[0], *out_ring.step(), *gate_ring.step(), *value_ring.held), *totals[1:]
+    )
+    pulled = mixer.gradients(value_grad, value_sums, *ends)
     grad_state_in = jnp.concatenate([pulled[1], pulled[2]], 1)
-    grad_state_step = ring_scatter(contract_rows(normed, grad_state_in).astype(low))
-    grad_value = ring_scatter(contract_rows(normed, grad_value_in).astype(low))
-
-    product = lax.psum_scatter(
-        (contract_cols(full_out, scaled) * scale_out[:, 0]).astype(low),
-        "gy",
-        scatter_dimension=0,
-        tiled=True,
-    ).T
+    state_partial = row_major(contract_rows(normed, grad_state_in).astype(low))
+    grad_state_step = scatter_rows(state_partial).astype(wide)
+
+    held = out_ring.step() + gate_ring.step() + value_ring.step()
+    grad_normed_part = contract_cols(full_gate, after(grad_gate_in, state_partial, *held))
+    grad_value_state_in = jnp.concatenate([grad_value_in, grad_state_in], 1)
+    held = out_ring.step() + gate_ring.step() + value_ring.step()
+    grad_value_state_in = after(grad_value_state_in, *held)
+    grad_normed_part = grad_normed_part + contract_cols(full_value_state, grad_value_state_in)
+    grad_normed_part = grad_normed_part.astype(low)
+    held = gate_ring.step() + value_ring.step()
+    product_part = contract_cols(full_out, after(scaled, grad_normed_part, *held))
+    product_part = (product_part * scale_out[:, 0]).astype(low)
+    grad_out = out_ring.finish()
+    grad_gate = gate_ring.finish()
+    grad_value = value_ring.finish()
+
+    grad_normed = halving_sum(grad_normed_part, "gy").T.astype(wide)
     token_cols = lax.dynamic_slice_in_dim(layer_input, col_start, col_width, 1).astype(wide)
-    layer_output = (token_cols + product.astype(wide)).astype(low)
-
-    grad_normed_part = (
-        contract_cols(full_gate, grad_gate_in)
-        + contract_cols(full_value, grad_value_in)
-        + contract_cols(full_state, grad_state_in)
-    )
-    grad_normed = lax.psum_scatter(
-        grad_normed_part.astype(low), "gy", scatter_dimension=0, tiled=True
-    ).T.astype(wide)
     gain_cols = lax.dynamic_slice_in_dim(norm_gain, col_start, col_width, 0)
     weighted = grad_normed * gain_cols
     inner_dot = lax.psum(jnp.sum(weighted * token_cols, axis=1), "gy")[:, None]
@@ -618,15 +708,18 @@
         + scale_in * weighted
         - token_cols * scale_in**3 * inner_dot / model_width
     )
-    grad_norm_gain = lax.psum(jnp.sum(grad_normed * token_cols * scale_in, axis=0), "gx")
+    grad_norm_gain = butterfly_sum(jnp.sum(grad_normed * token_cols * scale_in, axis=0), "gx")
+    product = halving_sum(product_part, "gy").T
+    layer_output = (token_cols + product.astype(wide)).astype(low)
 
     small = (gate_gain_part,) + pulled[3:]
-    packed = lax.psum(jnp.concatenate([v.reshape(-1) for v in small]), "gx")
+    packed = jnp.concatenate([v.reshape(-1) for v in small])
+    packed = butterfly_sum(after(packed, product_part), "gx")
     sums, start = [], 0
     for v in small:
         sums.append(packed[start : start + v.size].reshape(v.shape))
         start += v.size
-    state_sums = lax.psum(
+    state_sums = butterfly_sum(
         jnp.concatenate([grad_state_step[:, :state_cols], sums[3], sums[4][None]], 0), "gy"
     )
     state_rows = state_weight.shape[0]

time: 818 us -> 734 us (0.90)
  waiting for transfers between devices: 284 us -> 204 us
  blocking collectives: 54.3 us -> 11.4 us
  other arithmetic: 52.8 us -> 80.9 us
  local copies, waits for them, and re-layouts: 74.6 us -> 97.4 us
  starting transfers between devices: 130 us -> 115 us
    psum x3 -> x1, blocking collectives: 48.2 us -> 5.77 us  [on_device(): lax.psum(jnp.stack([jnp.sum(gated * gated, axis=1), jnp.sum(gated * gated...]
    ppermute x28 -> x14, waiting for transfers between devices: 135 us -> 95.2 us  [ring_gather(): up = lax.ppermute(up, 'gx', ahead)]
    ppermute x56 -> x54, waiting for transfers between devices: 122 us -> 93 us  [the longest x42 55.5 us: step(): lax.ppermute(held, 'gx', move).astype(wide)]
    convert_element_type x24 -> x22, other arithmetic: 21.1 us -> 48.1 us  [the longest x18 26.7 us: step(): up, down = (up.astype(low), down.astype(low))]
    psum x1 -> x0, waiting for transfers between devices: 20.2 us -> none  [on_device(): lax.psum(jnp.concatenate([grad_state_step[:, :state_cols], sums[3], sums[...]
    dynamic_slice x5 -> x7, local copies, waits for them, and re-layouts: 4.6 us -> 20.1 us  [the longest x2 15.3 us: halving_sum(): kept = lax.dynamic_index_in_dim(pairs, mine, 1, keepdims=False)]
    dynamic_update_slice x59 -> x30, local copies, waits for them, and re-layouts: 32 us -> 18.7 us  [put(): lax.dynamic_update_slice(full, piece[:, lo:hi], (start, 0))]
    ppermute x56 -> x54, starting transfers between devices: 70.8 us -> 58.9 us  [the longest x42 47.2 us: step(): lax.ppermute(held, 'gx', move).astype(wide)]
  transfers between devices with their start and end apart: 116 -> 86, of which waited for: 58 -> 33; matrix products, arithmetic and copies ran while one was open for 30% -> 35% of each run, Pallas kernels for 10% -> 12%
where the time goes in v4:
time: 734 us; the launch traced here: 726 us
  waiting for transfers between devices  204 us (28%)
  matrix products  117 us (16%)
  starting transfers between devices  115 us (16%)
  local copies, waits for them, and re-layouts  97.4 us (13%)
  Pallas kernels  84.6 us (12%)
  other arithmetic  80.9 us (11%)
  between operations  15.5 us (2%)
  blocking collectives  11.4 us (2%)
    ppermute x14, waiting for transfers between devices, ring_gather(): up = lax.ppermute(up, 'gx', ahead)  95.2 us
    pallas_call x5, Pallas kernels, call(): pl.pallas_call(kernel, out_shape=shapes, scratch_shapes=list(scratch), co...  84.6 us
    ppermute x42, waiting for transfers between devices, step(): lax.ppermute(held, 'gx', move).astype(wide)  55.5 us
    ppermute x14, starting transfers between devices, ring_gather(): up = lax.ppermute(up, 'gx', ahead)  49.4 us
    ppermute x42, starting transfers between devices, step(): lax.ppermute(held, 'gx', move).astype(wide)  47.2 us
    dot_general x4, matrix products, dot(): jnp.dot(left, right, preferred_element_type=wide, precision=precision)  43.2 us
    dot_general x4, matrix products, contract_rows(): lax.dot_general(left, right, (((0,), (0,)), ((), ())), preferred_element_...  37.2 us
    dot_general x3, matrix products, contract_cols(): lax.dot_general(left, right, (((1,), (1,)), ((), ())), preferred_element_...  36.7 us
  transfers between devices with their start and end apart: 86, of which 33 were waited for; matrix products, arithmetic and copies ran while one was open for 35% of the time, Pallas kernels for 12%

profile of v4, /device:TPU:0, one launch (start us, length us, event | category | flops | bytes accessed | tf_op | source)
XLA Modules:
  0.0 725.8 jit_solution(14732686749973108896)
XLA Ops:
  11.8 3.1 collective-permute-start
  15.8 3.6 fusion
  22.0 6.0 fusion.2
  31.1 3.1 broadcast.85.clone
  38.8 13.5 %collective-permute-done.2 = bf16[160,1280]{1,0:T(8,128)(2,1)S(1)} collective-permute-done((bf16[160,1280]{1,0:T(8,128)(2,1)S(1)}, bf16[160,1280]{1,0:T(8,128)(2,1)S(1)}, u32[]{:S(2)}, u32[]{:S(2)}) %collective-permute-start.2) | collective-permute-done | bytes 409632 | tf_op jit(solution)/shard_map/ppermute | solution.py:512
  52.3 5.0 collective-permute-start.4
  57.2 4.5 collective-permute-done.3
  63.3 6.9 collective-permute-done.4
  70.2 2.5 collective-permute-start.6
  74.2 7.2 collective-permute-done.6
  81.4 2.5 collective-permute-start.8
  85.5 7.9 %collective-permute-done.8 = bf16[160,1280]{1,0:T(8,128)(2,1)S(1)} collective-permute-done((bf16[160,1280]{1,0:T(8,128)(2,1)S(1)}, bf16[160,1280]{1,0:T(8,128)(2,1)S(1)}, u32[]{:S(2)}, u32[]{:S(2)}) %collective-permute-start.8) | collective-permute-done | bytes 409632 | tf_op jit(solution)/shard_map/ppermute | solution.py:512
  93.5 2.5 collective-permute-start.10
  97.5 8.2 %collective-permute-done.10 = bf16[160,1280]{1,0:T(8,128)(2,1)} collective-permute-done((bf16[160,1280]{1,0:T(8,128)(2,1)S(1)}, bf16[160,1280]{1,0:T(8,128)(2,1)}, u32[]{:S(2)}, u32[]{:S(2)}) %collective-permute-start.10) | collective-permute-done | bytes 409632 | tf_op jit(solution)/shard_map/ppermute | solution.py:512
  114.8 5.3 fusion.45
  126.4 17.6 %shard_map.288 = (bf16[1024,128]{1,0:T(8,128)(2,1)}, bf16[1024,128]{1,0:T(8,128)(2,1)}, bf16[128,1024]{1,0:T(8,128)(2,1)}, bf16[128,1024]{1,0:T(8,128)(2,1)}, f3...) custom-call(f32[1024,256]{1,0:T(8,128)} %slice.145.state_ref, ...), custom_call_target="tpu_custom_call" | custom-call | flops 2013265920 | bytes 17315840 | tf_op jit(solution)/shard_map/pallas_call | solution.py:293
  152.1 12.4 %fusion.44.value_ref = f32[1024,1280]{1,0:T(8,128)} fusion(bf16[1024,2560]{1,0:T(8,128)(2,1)} %fusion.2, bf16[2560,1280]{1,0:T(8,128)(2,1)} %constant_dynamic-update-slice_fusion.15), kind=kOutput, calls=%fused_computation.179 | convolution fusion | flops 6710886400 | bytes 17039360 | tf_op jit(solution)/shard_map/dot_general | solution.py:25
  165.0 18.9 %shard_map.289.mixed_ref = f32[1024,1280]{1,0:T(8,128)} custom-call(f32[1024,1280]{1,0:T(8,128)} %fusion.44.value_ref, f32[4,1280]{1,0:T(4,128)} %taps_ref.8, f32[1,1280]{1,0:T(1,128)} %broadcast_in_dim.20.bias_ref, f32[1,1280]{1,0:T(1,128)} %broadcast_in_dim_reshape.3.skip_ref, f32[1024,1280]{1,0:T(8,128)} %get-tuple-element.54.dtx_ref, ...), custom_call_target="tpu_custom_call" | custom-call | flops 3355443200 | bytes 24754176 | tf_op jit(solution)/shard_map/pallas_call | solution.py:293
  188.3 13.9 %collective-permute-done.16 = bf16[160,1280]{1,0:T(8,128)(2,1)S(1)} collective-permute-done((bf16[160,1280]{1,0:T(8,128)(2,1)}, bf16[160,1280]{1,0:T(8,128)(2,1)S(1)}, u32[]{:S(2)}, u32[]{:S(2)}) %collective-permute-start.16) | collective-permute-done | bytes 409632 | tf_op jit(solution)/shard_map/ppermute | solution.py:512
  202.2 8.7 %collective-permute-start.18 = (bf16[160,1280]{1,0:T(8,128)(2,1)S(1)}, bf16[160,1280]{1,0:T(8,128)(2,1)S(1)}, u32[]{:S(2)}, u32[]{:S(2)}) collective-permute-start(bf16[160,1280]{1,0:T(8,128)(2,1)S(1)} %collective-permute-done.16), channel_id=1, source_target_pairs={{0,8},{8,16},{16,24},{24,28},{28,20},{20,12},{12,4},{4,0},{1,9},{9... | collective-permute-start | bytes 1228808 | tf_op jit(solution)/shard_map/ppermute | solution.py:512
  210.9 4.9 collective-permute-done.17
  215.8 4.8 collective-permute-done.18
  220.7 16.2 %collective-permute-start.20 = (bf16[160,1280]{1,0:T(8,128)(2,1)S(1)}, bf16[160,1280]{1,0:T(8,128)(2,1)S(1)}, u32[]{:S(2)}, u32[]{:S(2)}) collective-permute-start(bf16[160,1280]{1,0:T(8,128)(2,1)S(1)} %collective-permute-done.18), channel_id=1, source_target_pairs={{0,8},{8,16},{16,24},{24,28},{28,20},{20,12},{12,4},{4,0},{1,9},{9... | collective-permute-start | bytes 1228808 | tf_op jit(solution)/shard_map/ppermute | solution.py:512
  236.8 3.0 collective-permute-done.19
  241.3 8.6 %collective-permute-done.20 = bf16[160,1280]{1,0:T(8,128)(2,1)S(1)} collective-permute-done((bf16[160,1280]{1,0:T(8,128)(2,1)S(1)}, bf16[160,1280]{1,0:T(8,128)(2,1)S(1)}, u32[]{:S(2)}, u32[]{:S(2)}) %collective-permute-start.20) | collective-permute-done | bytes 409632 | tf_op jit(solution)/shard_map/ppermute | solution.py:512
  252.3 9.1 %collective-permute-done.22 = bf16[160,1280]{1,0:T(8,128)(2,1)S(1)} collective-permute-done((bf16[160,1280]{1,0:T(8,128)(2,1)S(1)}, bf16[160,1280]{1,0:T(8,128)(2,1)S(1)}, u32[]{:S(2)}, u32[]{:S(2)}) %collective-permute-start.22) | collective-permute-done | bytes 409632 | tf_op jit(solution)/shard_map/ppermute | solution.py:512
  264.4 9.3 %collective-permute-done.24 = bf16[160,1280]{1,0:T(8,128)(2,1)S(1)} collective-permute-done((bf16[160,1280]{1,0:T(8,128)(2,1)S(1)}, bf16[160,1280]{1,0:T(8,128)(2,1)S(1)}, u32[]{:S(2)}, u32[]{:S(2)}) %collective-permute-start.24) | collective-permute-done | bytes 409632 | tf_op jit(solution)/shard_map/ppermute | solution.py:512
  275.9 5.8 collective-permute-done.26
  282.5 2.8 copy-done.7
  285.2 12.1 %multiply_convert_fusion.3 = (bf16[1024,1280]{1,0:T(8,128)(2,1)}, f32[1024,1280]{1,0:T(8,128)}, f32[1024,1280]{1,0:T(8,128)}) fusion(f32[1280]{0:T(1024)S(1)} %copy-done.29, f32[1024,1280]{1,0:T(8,128)S(1)} %copy-done, bf16[1024,2560]{1,0:T(8,128)(2,1)} %fusion.2, bf16[2560,1280]{1,0:T(8,128)(2,1)S(1)} %constant_dynamic-update-slice_fusion), kind=kOutput, calls=%fused_computation.28 | convolution fusion | flops 6720061440 | bytes 30151680 | tf_op jit(solution)/shard_map/dot_general | solution.py:25
  297.4 13.3 %multiply_reduce_fusion.2 = (f32[1024]{0:T(1024)S(1)}, f32[1024]{0:T(1024)S(1)}, f32[1024,1280]{1,0:T(8,128)}) fusion(f32[1024,1280]{1,0:T(8,128)} %get-tuple-element.180, f32[1280]{0:T(1024)S(1)} %copy-done.29, bf16[1024,2560]{1,0:T(8,128)(2,1)} %all-gather.5.cloned.1.call-done, bf16[2560,1280]{1,0:T(8,128)(2,1)} %all-gather.7.cloned.1.call-done), kind=kOutput, calls=%fused_computation.24 | convolution fusion | flops 6717437952 | bytes 22295552 | tf_op jit(solution)/shard_map/dot_general | solution.py:25
  310.7 5.8 psum.14
  316.5 11.4 %fusion.3 = bf16[2560,1280]{1,0:T(8,128)(2,1)S(1)} fusion(bf16[1024,2560]{1,0:T(8,128)(2,1)} %all-gather.5.cloned.1.call-done, f32[1024,1280]{1,0:T(8,128)} %get-tuple-element.180, f32[1024]{0:T(1024)S(1)} %bitcast.118, f32[1280]{0:T(1024)S(1)} %copy-done.29), kind=kOutput, calls=%fused_computation.10 | convolution fusion | flops 6718095360 | bytes 17048576 | tf_op jit(solution)/shard_map/dot_general | solution.py:29
  330.1 9.0 %multiply_convert_fusion.1 = (bf16[1024,1280]{1,0:T(8,128)(2,1)S(1)}, f32[1024,1280]{1,0:T(8,128)}, f32[1280]{0:T(1024)}) fusion(f32[1024,1280]{1,0:T(8,128)} %get-tuple-element.254, f32[1024,1280]{1,0:T(8,128)S(1)} %bitcast.102, f32[1024,1280]{1,0:T(8,128)S(1)} %copy-done.8, f32[1024]{0:T(1024)S(1)} %fusion.31, f32[1024,1280]{1,0:T(8,128)} %get-tuple-element.61, ...), kind=kLoop, calls=%fused_computation.20 | loop fusion | flops 24902400 | bytes 28854272 | tf_op jit(solution)/shard_map/convert_element_type | solution.py:665
  343.6 9.0 %convolution_convert_fusion.1 = bf16[2560,1280]{1,0:T(8,128)(2,1)S(1)} fusion(bf16[1024,2560]{1,0:T(8,128)(2,1)} %fusion.2, bf16[1024,1280]{1,0:T(8,128)(2,1)S(1)} %get-tuple-element.85), kind=kOutput, calls=%fused_computation.3 | convolution fusion | flops 6714163200 | bytes 14417920 | tf_op jit(solution)/shard_map/dot_general | solution.py:29
  357.8 7.3 %collective-permute-done.34 = bf16[160,1280]{1,0:T(8,128)(2,1)S(1)} collective-permute-done((bf16[160,1280]{1,0:T(8,128)(2,1)S(1)}, bf16[160,1280]{1,0:T(8,128)(2,1)S(1)}, u32[]{:S(2)}, u32[]{:S(2)}) %collective-permute-start.34) | collective-permute-done | bytes 409632 | tf_op jit(solution)/shard_map/ppermute | solution.py:538
  367.0 20.4 %shard_map.290 = (bf16[1024,1280]{1,0:T(8,128)(2,1)}, f32[8,1280]{1,0:T(8,128)}, f32[1024,128]{1,0:T(8,128)}, f32[1024,128]{1,0:T(8,128)}, f32[1024,128]{1,0:T(8...) custom-call(f32[1024,1280]{1,0:T(8,128)} %fusion.44.value_ref, f32[1024,1280]{1,0:T(8,128)} %shard_map.289.mixed_ref, ...), custom_call_target="tpu_custom_call" | custom-call | flops 5033164800 | bytes 35805184 | tf_op jit(solution)/shard_map/pallas_call | solution.py:293
  395.1 20.7 %shard_map.291 = (bf16[1024,1280]{1,0:T(8,128)(2,1)}, f32[8,1280]{1,0:T(8,128)}, f32[1024,128]{1,0:T(8,128)}, f32[1024,128]{1,0:T(8,128)}, f32[1024,128]{1,0:T(8...) custom-call(f32[1024,1280]{1,0:T(8,128)} %fusion.44.value_ref, ...), custom_call_target="tpu_custom_call", output_to_operand_aliasing={{0}: (15, {}), {1}: (16, {})} | custom-call | flops 5033164800 | bytes 41089024 | tf_op jit(solution)/shard_map/pallas_call | solution.py:293
  426.3 9.8 %convolution_convert_fusion = bf16[2560,1280]{1,0:T(8,128)(2,1)S(1)} fusion(bf16[1024,2560]{1,0:T(8,128)(2,1)} %fusion.2, bf16[1024,1280]{1,0:T(8,128)(2,1)} %get-tuple-element.77), kind=kOutput, calls=%fused_computation.2 | convolution fusion | flops 6714163200 | bytes 14417920 | tf_op jit(solution)/shard_map/dot_general | solution.py:29
  445.3 7.0 shard_map.292
  458.7 7.0 convolution_convert_fusion.3
  467.2 2.8 pad_maximum_fusion
  477.7 10.8 %collective-permute-done.52 = bf16[160,1280]{1,0:T(8,128)(2,1)S(1)} collective-permute-done((bf16[160,1280]{1,0:T(8,128)(2,1)S(1)}, bf16[160,1280]{1,0:T(8,128)(2,1)S(1)}, u32[]{:S(2)}, u32[]{:S(2)}) %collective-permute-start.52) | collective-permute-done | bytes 409632 | tf_op jit(solution)/shard_map/ppermute | solution.py:538
  490.0 3.1 collective-permute-start.53
  493.1 13.7 %collective-permute-done.55 = bf16[160,1280]{1,0:T(8,128)(2,1)S(1)} collective-permute-done((bf16[160,1280]{1,0:T(8,128)(2,1)S(1)}, bf16[160,1280]{1,0:T(8,128)(2,1)S(1)}, u32[]{:S(2)}, u32[]{:S(2)}) %collective-permute-start.55) | collective-permute-done | bytes 409632 | tf_op jit(solution)/shard_map/ppermute | solution.py:538
  506.8 6.1 collective-permute-done.58
  514.3 3.2 collective-permute-start.59
  517.5 4.2 collective-permute-done.56
  524.1 3.2 collective-permute-start.57
  528.8 14.5 %fusion.4 = f32[2560,1024]{1,0:T(8,128)} fusion(bf16[1024,1556]{1,0:T(8,128)(2,1)S(1)} %copy-done.9, bf16[2560,276]{1,0:T(8,128)(2,1)} %copy.79, bf16[2560,1280]{1,0:T(8,128)(2,1)} %constant_dynamic-update-slice_fusion.15), kind=kOutput, calls=%fused_computation.11 | convolution fusion | flops 8173854720 | bytes 21639168 | tf_op jit(solution)/shard_map/dot_general | solution.py:35
  543.3 10.5 %add_convert_fusion = bf16[2560,1024]{1,0:T(8,128)(2,1)S(1)} fusion(f32[2560,1024]{1,0:T(8,128)} %fusion.4, bf16[2560,1280]{1,0:T(8,128)(2,1)S(1)} %bitcast.104, bf16[1024,1280]{1,0:T(8,128)(2,1)} %copy-done.14), kind=kOutput, calls=%fused_computation.9 | convolution fusion | flops 6716129280 | bytes 24903680 | tf_op jit(solution)/shard_map/dot_general | solution.py:35
  553.9 2.5 add_convert_fusion.8
  558.7 11.6 %fusion.11 = bf16[2560,1024]{0,1:T(8,128)(2,1)} fusion(f32[1024]{0:T(1024)S(1)} %bitcast.121, bf16[1024,1280]{1,0:T(8,128)(2,1)S(1)} %copy-done.33, bf16[2560,1280]{1,0:T(8,128)(2,1)} %all-gather.7.cloned.1.call-done), kind=kOutput, calls=%fused_computation.27 | convolution fusion | flops 6716129280 | bytes 14422016 | tf_op jit(solution)/shard_map/dot_general | solution.py:35
  577.7 2.6 copy.83
  580.3 3.1 copy.87
  586.4 11.6 %reshape_reshape.6 = bf16[2,2,640,1024]{2,1,0,3:T(2,128)(2,1)} reshape(bf16[2560,1024]{0,1:T(8,128)(2,1)} %fusion.11) | data formatting | bytes 10485760 | tf_op jit(solution)/shard_map/reshape;reshape | solution.py:562
  599.6 13.2 %constant_dynamic-slice_fusion.5 = (bf16[2,1,640,1024]{2,1,0,3:T(2,128)(2,1)}, bf16[2,1,640,1024]{2,1,0,3:T(2,128)(2,1)S(1)}) fusion(bf16[2,2,640,1024]{2,1,0,3:T(2,128)(2,1)} %reshape_reshape.6, s32[]{:T(128)S(6)} %select_n.533, s32[]{:T(128)S(6)} %select_n.534), kind=kLoop, calls=%fused_computation.112 | loop fusion | bytes 10485768 | tf_op jit(solution)/shard_map/jit(dynamic_index_in_dim)/dynamic_slice | solution.py:564
  622.8 7.4 %collective-permute-done.71 = bf16[160,1280]{1,0:T(8,128)(2,1)S(1)} collective-permute-done((bf16[160,1280]{1,0:T(8,128)(2,1)S(1)}, bf16[160,1280]{1,0:T(8,128)(2,1)S(1)}, u32[]{:S(2)}, u32[]{:S(2)}) %collective-permute-start.71) | collective-permute-done | bytes 409632 | tf_op jit(solution)/shard_map/ppermute | solution.py:538
  651.2 4.0 fusion.9
  659.5 12.0 %collective-permute-done.63 = bf16[1,640,1024]{1,2,0:T(8,128)(2,1)} collective-permute-done((bf16[1,640,1024]{1,2,0:T(8,128)(2,1)}, bf16[1,640,1024]{1,2,0:T(8,128)(2,1)}, u32[]{:S(2)}, u32[]{:S(2)}) %collective-permute-start.63) | collective-permute-done | bytes 1310752 | tf_op jit(solution)/shard_map/ppermute | solution.py:566
  671.6 4.0 fusion.18
  681.5 23.1 %collective-permute-done.81 = f32[325,256]{1,0:T(8,128)S(1)} collective-permute-done((f32[325,256]{1,0:T(8,128)S(1)}, f32[325,256]{1,0:T(8,128)S(1)}, u32[]{:S(2)}, u32[]{:S(2)}) %collective-permute-start.81) | collective-permute-done | bytes 332832 | tf_op jit(solution)/shard_map/ppermute | solution.py:576
  708.1 5.6 psum.15
  714.4 4.5 fusion.15
  (353 shorter events, 182.3 us)
Async XLA Ops:
  7.2 104.7 %all-gather.9.cloned.1.call-start = ((), (), s32[]{:S(2)}) async-start(), calls=%async_computation.4 | async-start | bytes 1935360 | tf_op jit(solution)/shard_map/all_gather | solution.py:618
  9.8 287.6 %all-gather.5.cloned.1.call-start = ((), (), s32[]{:S(2)}) async-start(), calls=%async_computation.1 | async-start | bytes 6553600 | tf_op jit(solution)/shard_map/all_gather | solution.py:619
  10.5 286.8 %all-gather.7.cloned.1.call-start = ((), (), s32[]{:S(2)}) async-start(), calls=%async_computation.2 | async-start | bytes 7372800 | tf_op jit(solution)/shard_map/all_gather | solution.py:620
  11.8 23.4 %collective-permute-start = (bf16[160,1280]{1,0:T(8,128)(2,1)S(1)}, bf16[160,1280]{1,0:T(8,128)(2,1)S(1)}, u32[]{:S(2)}, u32[]{:S(2)}) collective-permute-start(bf16[160,1280]{1,0:T(8,128)(2,1)S(1)} %get-tuple-element.237), channel_id=1, source_target_pairs={{0,8},{8,16},{16,24},{24,28},{28,20},{20,12},{12,4},{4,0},{1,9},{9... | collective-permute-start | bytes 1228808 | tf_op jit(solution)/shard_map/ppermute | solution.py:512
  14.9 22.3 %collective-permute-start.1 = (bf16[160,1280]{1,0:T(8,128)(2,1)S(1)}, bf16[160,1280]{1,0:T(8,128)(2,1)S(1)}, u32[]{:S(2)}, u32[]{:S(2)}) collective-permute-start(bf16[160,1280]{1,0:T(8,128)(2,1)S(1)} %get-tuple-element.236), channel_id=1, source_target_pairs={{8,0},{16,8},{24,16},{28,24},{20,28},{12,20},{4,12},{0,4},{9,1},{1... | collective-permute-start | bytes 1228808 | tf_op jit(solution)/shard_map/ppermute | solution.py:513
  14.9 632.2 %reduce-scatter.2.cloned.1.call-start = ((), (), s32[]{:S(2)}) async-start(), calls=%async_computation.3 | async-start | bytes 2211840 | tf_op jit(solution)/shard_map/reduce_scatter | solution.py:582
  35.1 17.1 %collective-permute-start.2 = (bf16[160,1280]{1,0:T(8,128)(2,1)S(1)}, bf16[160,1280]{1,0:T(8,128)(2,1)S(1)}, u32[]{:S(2)}, u32[]{:S(2)}) collective-permute-start(bf16[160,1280]{1,0:T(8,128)(2,1)S(1)} %collective-permute-done), channel_id=1, source_target_pairs={{0,8},{8,16},{16,24},{24,28},{28,20},{20,12},{12,4},{4,0},{1,9},{9... | collective-permute-start | bytes 1228808 | tf_op jit(solution)/shard_map/ppermute | solution.py:512
  37.2 24.6 %collective-permute-start.3 = (bf16[160,1280]{1,0:T(8,128)(2,1)S(1)}, bf16[160,1280]{1,0:T(8,128)(2,1)S(1)}, u32[]{:S(2)}, u32[]{:S(2)}) collective-permute-start(bf16[160,1280]{1,0:T(8,128)(2,1)S(1)} %collective-permute-done.1), channel_id=1, source_target_pairs={{8,0},{16,8},{24,16},{28,24},{20,28},{12,20},{4,12},{0,4},{9,1},{1... | collective-permute-start | bytes 1228808 | tf_op jit(solution)/shard_map/ppermute | solution.py:513
  52.3 17.9 %collective-permute-start.4 = (bf16[160,1280]{1,0:T(8,128)(2,1)S(1)}, bf16[160,1280]{1,0:T(8,128)(2,1)S(1)}, u32[]{:S(2)}, u32[]{:S(2)}) collective-permute-start(bf16[160,1280]{1,0:T(8,128)(2,1)S(1)} %collective-permute-done.2), channel_id=1, source_target_pairs={{0,8},{8,16},{16,24},{24,28},{28,20},{20,12},{12,4},{4,0},{1,9},{9... | collective-permute-start | bytes 1228808 | tf_op jit(solution)/shard_map/ppermute | solution.py:512
  93.5 12.2 %collective-permute-start.10 = (bf16[160,1280]{1,0:T(8,128)(2,1)S(1)}, bf16[160,1280]{1,0:T(8,128)(2,1)}, u32[]{:S(2)}, u32[]{:S(2)}) collective-permute-start(bf16[160,1280]{1,0:T(8,128)(2,1)S(1)} %collective-permute-done.8), channel_id=1, source_target_pairs={{0,8},{8,16},{16,24},{24,28},{28,20},{20,12},{12,4},{4,0},{1,9},{9... | collective-permute-start | bytes 1228808 | tf_op jit(solution)/shard_map/ppermute | solution.py:512
  95.9 12.2 %collective-permute-start.11 = (bf16[160,1280]{1,0:T(8,128)(2,1)S(1)}, bf16[160,1280]{1,0:T(8,128)(2,1)}, u32[]{:S(2)}, u32[]{:S(2)}) collective-permute-start(bf16[160,1280]{1,0:T(8,128)(2,1)S(1)} %collective-permute-done.9), channel_id=1, source_target_pairs={{8,0},{16,8},{24,16},{28,24},{20,28},{12,20},{4,12},{0,4},{9,1},{1... | collective-permute-start | bytes 1228808 | tf_op jit(solution)/shard_map/ppermute | solution.py:513
  105.7 39.9 %collective-permute-start.12 = (bf16[160,1280]{1,0:T(8,128)(2,1)}, bf16[160,1280]{1,0:T(8,128)(2,1)S(1)}, u32[]{:S(2)}, u32[]{:S(2)}) collective-permute-start(bf16[160,1280]{1,0:T(8,128)(2,1)} %collective-permute-done.10), channel_id=1, source_target_pairs={{0,8},{8,16},{16,24},{24,28},{28,20},{20,12},{12,4},{4,0},{1,9},{9... | collective-permute-start | bytes 1228808 | tf_op jit(solution)/shard_map/ppermute | solution.py:512
  108.2 38.2 %collective-permute-start.13 = (bf16[160,1280]{1,0:T(8,128)(2,1)}, bf16[160,1280]{1,0:T(8,128)(2,1)}, u32[]{:S(2)}, u32[]{:S(2)}) collective-permute-start(bf16[160,1280]{1,0:T(8,128)(2,1)} %collective-permute-done.11), channel_id=1, source_target_pairs={{8,0},{16,8},{24,16},{28,24},{20,28},{12,20},{4,12},{0,4},{9,1},{1... | collective-permute-start | bytes 1228808 | tf_op jit(solution)/shard_map/ppermute | solution.py:513
  146.4 37.5 %collective-permute-start.14 = (bf16[160,1280]{1,0:T(8,128)(2,1)S(1)}, bf16[160,1280]{1,0:T(8,128)(2,1)}, u32[]{:S(2)}, u32[]{:S(2)}) collective-permute-start(bf16[160,1280]{1,0:T(8,128)(2,1)S(1)} %get-tuple-element.235), channel_id=1, source_target_pairs={{0,8},{8,16},{16,24},{24,28},{28,20},{20,12},{12,4},{4,0},{1,9},{9... | collective-permute-start | bytes 1228808 | tf_op jit(solution)/shard_map/ppermute | solution.py:512
  148.4 37.5 %collective-permute-start.15 = (bf16[160,1280]{1,0:T(8,128)(2,1)S(1)}, bf16[160,1280]{1,0:T(8,128)(2,1)}, u32[]{:S(2)}, u32[]{:S(2)}) collective-permute-start(bf16[160,1280]{1,0:T(8,128)(2,1)S(1)} %get-tuple-element.234), channel_id=1, source_target_pairs={{8,0},{16,8},{24,16},{28,24},{20,28},{12,20},{4,12},{0,4},{9,1},{1... | collective-permute-start | bytes 1228808 | tf_op jit(solution)/shard_map/ppermute | solution.py:513
  183.9 18.3 %collective-permute-start.16 = (bf16[160,1280]{1,0:T(8,128)(2,1)}, bf16[160,1280]{1,0:T(8,128)(2,1)S(1)}, u32[]{:S(2)}, u32[]{:S(2)}) collective-permute-start(bf16[160,1280]{1,0:T(8,128)(2,1)} %collective-permute-done.14), channel_id=1, source_target_pairs={{0,8},{8,16},{16,24},{24,28},{28,20},{20,12},{12,4},{4,0},{1,9},{9... | collective-permute-start | bytes 1228808 | tf_op jit(solution)/shard_map/ppermute | solution.py:512
  185.9 29.9 %collective-permute-start.17 = (bf16[160,1280]{1,0:T(8,128)(2,1)}, bf16[160,1280]{1,0:T(8,128)(2,1)S(1)}, u32[]{:S(2)}, u32[]{:S(2)}) collective-permute-start(bf16[160,1280]{1,0:T(8,128)(2,1)} %collective-permute-done.15), channel_id=1, source_target_pairs={{8,0},{16,8},{24,16},{28,24},{20,28},{12,20},{4,12},{0,4},{9,1},{1... | collective-permute-start | bytes 1228808 | tf_op jit(solution)/shard_map/ppermute | solution.py:513
  202.2 18.5 %collective-permute-start.18 = (bf16[160,1280]{1,0:T(8,128)(2,1)S(1)}, bf16[160,1280]{1,0:T(8,128)(2,1)S(1)}, u32[]{:S(2)}, u32[]{:S(2)}) collective-permute-start(bf16[160,1280]{1,0:T(8,128)(2,1)S(1)} %collective-permute-done.16), channel_id=1, source_target_pairs={{0,8},{8,16},{16,24},{24,28},{28,20},{20,12},{12,4},{4,0},{1,9},{9... | collective-permute-start | bytes 1228808 | tf_op jit(solution)/shard_map/ppermute | solution.py:512
  215.7 24.1 %collective-permute-start.19 = (bf16[160,1280]{1,0:T(8,128)(2,1)S(1)}, bf16[160,1280]{1,0:T(8,128)(2,1)S(1)}, u32[]{:S(2)}, u32[]{:S(2)}) collective-permute-start(bf16[160,1280]{1,0:T(8,128)(2,1)S(1)} %collective-permute-done.17), channel_id=1, source_target_pairs={{8,0},{16,8},{24,16},{28,24},{20,28},{12,20},{4,12},{0,4},{9,1},{1... | collective-permute-start | bytes 1228808 | tf_op jit(solution)/shard_map/ppermute | solution.py:513
  220.7 29.2 %collective-permute-start.20 = (bf16[160,1280]{1,0:T(8,128)(2,1)S(1)}, bf16[160,1280]{1,0:T(8,128)(2,1)S(1)}, u32[]{:S(2)}, u32[]{:S(2)}) collective-permute-start(bf16[160,1280]{1,0:T(8,128)(2,1)S(1)} %collective-permute-done.18), channel_id=1, source_target_pairs={{0,8},{8,16},{16,24},{24,28},{28,20},{20,12},{12,4},{4,0},{1,9},{9... | collective-permute-start | bytes 1228808 | tf_op jit(solution)/shard_map/ppermute | solution.py:512
  261.4 12.3 %collective-permute-start.24 = (bf16[160,1280]{1,0:T(8,128)(2,1)S(1)}, bf16[160,1280]{1,0:T(8,128)(2,1)S(1)}, u32[]{:S(2)}, u32[]{:S(2)}) collective-permute-start(bf16[160,1280]{1,0:T(8,128)(2,1)S(1)} %collective-permute-done.22), channel_id=1, source_target_pairs={{0,8},{8,16},{16,24},{24,28},{28,20},{20,12},{12,4},{4,0},{1,9},{9... | collective-permute-start | bytes 1228808 | tf_op jit(solution)/shard_map/ppermute | solution.py:512
  341.5 13.2 %collective-permute-start.29 = (bf16[160,1280]{1,0:T(8,128)(2,1)S(1)}, bf16[160,1280]{1,0:T(8,128)(2,1)S(1)}, u32[]{:S(2)}, u32[]{:S(2)}) collective-permute-start(bf16[160,1280]{1,0:T(8,128)(2,1)S(1)} %get-tuple-element.225), channel_id=1, source_target_pairs={{0,8},{8,16},{16,24},{24,28},{28,20},{20,12},{12,4},{4,0},{1,9},{9... | collective-permute-start | bytes 1228808 | tf_op jit(solution)/shard_map/ppermute | solution.py:538
  352.6 12.5 %collective-permute-start.34 = (bf16[160,1280]{1,0:T(8,128)(2,1)S(1)}, bf16[160,1280]{1,0:T(8,128)(2,1)S(1)}, u32[]{:S(2)}, u32[]{:S(2)}) collective-permute-start(bf16[160,1280]{1,0:T(8,128)(2,1)S(1)} %get-tuple-element.219), channel_id=1, source_target_pairs={{0,8},{8,16},{16,24},{24,28},{28,20},{20,12},{12,4},{4,0},{1,9},{9... | collective-permute-start | bytes 1228808 | tf_op jit(solution)/shard_map/ppermute | solution.py:538
  354.4 37.3 %collective-permute-start.35 = (bf16[160,1280]{1,0:T(8,128)(2,1)S(1)}, bf16[160,1280]{1,0:T(8,128)(2,1)}, u32[]{:S(2)}, u32[]{:S(2)}) collective-permute-start(bf16[160,1280]{1,0:T(8,128)(2,1)S(1)} %get-tuple-element.218), channel_id=1, source_target_pairs={{8,0},{16,8},{24,16},{28,24},{20,28},{12,20},{4,12},{0,4},{9,1},{1... | collective-permute-start | bytes 1228808 | tf_op jit(solution)/shard_map/ppermute | solution.py:538
  355.7 31.7 %collective-permute-start.30 = (bf16[160,1280]{1,0:T(8,128)(2,1)}, bf16[160,1280]{1,0:T(8,128)(2,1)S(1)}, u32[]{:S(2)}, u32[]{:S(2)}) collective-permute-start(bf16[160,1280]{1,0:T(8,128)(2,1)} %get-tuple-element.223), channel_id=1, source_target_pairs={{0,8},{8,16},{16,24},{24,28},{28,20},{20,12},{12,4},{4,0},{1,9},{9... | collective-permute-start | bytes 1228808 | tf_op jit(solution)/shard_map/ppermute | solution.py:538
  357.5 30.0 %collective-permute-start.33 = (bf16[160,1280]{1,0:T(8,128)(2,1)S(1)}, bf16[160,1280]{1,0:T(8,128)(2,1)}, u32[]{:S(2)}, u32[]{:S(2)}) collective-permute-start(bf16[160,1280]{1,0:T(8,128)(2,1)S(1)} %get-tuple-element.222), channel_id=1, source_target_pairs={{8,0},{16,8},{24,16},{28,24},{20,28},{12,20},{4,12},{0,4},{9,1},{1... | collective-permute-start | bytes 1228808 | tf_op jit(solution)/shard_map/ppermute | solution.py:538
  365.2 26.5 %collective-permute-start.40 = (bf16[160,1280]{1,0:T(8,128)(2,1)S(1)}, bf16[160,1280]{1,0:T(8,128)(2,1)}, u32[]{:S(2)}, u32[]{:S(2)}) collective-permute-start(bf16[160,1280]{1,0:T(8,128)(2,1)S(1)} %add_convert_fusion.32), channel_id=1, source_target_pairs={{0,8},{8,16},{16,24},{24,28},{28,20},{20,12},{12,4},{4,0},{1,9},{9... | collective-permute-start | bytes 1228808 | tf_op jit(solution)/shard_map/ppermute | solution.py:538
  389.7 29.7 %collective-permute-start.36 = (bf16[160,1280]{1,0:T(8,128)(2,1)}, bf16[160,1280]{1,0:T(8,128)(2,1)S(1)}, u32[]{:S(2)}, u32[]{:S(2)}) collective-permute-start(bf16[160,1280]{1,0:T(8,128)(2,1)} %get-tuple-element.221), channel_id=1, source_target_pairs={{0,8},{8,16},{16,24},{24,28},{28,20},{20,12},{12,4},{4,0},{1,9},{9... | collective-permute-start | bytes 1228808 | tf_op jit(solution)/shard_map/ppermute | solution.py:538
  390.0 29.4 %collective-permute-start.38 = (bf16[160,1280]{1,0:T(8,128)(2,1)S(1)}, bf16[160,1280]{1,0:T(8,128)(2,1)}, u32[]{:S(2)}, u32[]{:S(2)}) collective-permute-start(bf16[160,1280]{1,0:T(8,128)(2,1)S(1)} %get-tuple-element.220), channel_id=1, source_target_pairs={{8,0},{16,8},{24,16},{28,24},{20,28},{12,20},{4,12},{0,4},{9,1},{1... | collective-permute-start | bytes 1228808 | tf_op jit(solution)/shard_map/ppermute | solution.py:538
  393.0 29.9 %collective-permute-start.41 = (bf16[160,1280]{1,0:T(8,128)(2,1)S(1)}, bf16[160,1280]{1,0:T(8,128)(2,1)S(1)}, u32[]{:S(2)}, u32[]{:S(2)}) collective-permute-start(bf16[160,1280]{1,0:T(8,128)(2,1)S(1)} %get-tuple-element.212), channel_id=1, source_target_pairs={{0,8},{8,16},{16,24},{24,28},{28,20},{20,12},{12,4},{4,0},{1,9},{9... | collective-permute-start | bytes 1228808 | tf_op jit(solution)/shard_map/ppermute | solution.py:538
  393.4 29.5 %collective-permute-start.42 = (bf16[160,1280]{1,0:T(8,128)(2,1)S(1)}, bf16[160,1280]{1,0:T(8,128)(2,1)S(1)}, u32[]{:S(2)}, u32[]{:S(2)}) collective-permute-start(bf16[160,1280]{1,0:T(8,128)(2,1)S(1)} %get-tuple-element.213), channel_id=1, source_target_pairs={{8,0},{16,8},{24,16},{28,24},{20,28},{12,20},{4,12},{0,4},{9,1},{1... | collective-permute-start | bytes 1228808 | tf_op jit(solution)/shard_map/ppermute | solution.py:538
  420.8 15.8 %collective-permute-start.37 = (bf16[160,1280]{1,0:T(8,128)(2,1)S(1)}, bf16[160,1280]{1,0:T(8,128)(2,1)S(1)}, u32[]{:S(2)}, u32[]{:S(2)}) collective-permute-start(bf16[160,1280]{1,0:T(8,128)(2,1)S(1)} %get-tuple-element.217), channel_id=1, source_target_pairs={{0,8},{8,16},{16,24},{24,28},{28,20},{20,12},{12,4},{4,0},{1,9},{9... | collective-permute-start | bytes 1228808 | tf_op jit(solution)/shard_map/ppermute | solution.py:538
  421.2 17.2 %collective-permute-start.39 = (bf16[160,1280]{1,0:T(8,128)(2,1)S(1)}, bf16[160,1280]{1,0:T(8,128)(2,1)S(1)}, u32[]{:S(2)}, u32[]{:S(2)}) collective-permute-start(bf16[160,1280]{1,0:T(8,128)(2,1)S(1)} %get-tuple-element.216), channel_id=1, source_target_pairs={{8,0},{16,8},{24,16},{28,24},{20,28},{12,20},{4,12},{0,4},{9,1},{1... | collective-permute-start | bytes 1228808 | tf_op jit(solution)/shard_map/ppermute | solution.py:538
  424.2 16.8 %collective-permute-start.43 = (bf16[160,1280]{1,0:T(8,128)(2,1)S(1)}, bf16[160,1280]{1,0:T(8,128)(2,1)S(1)}, u32[]{:S(2)}, u32[]{:S(2)}) collective-permute-start(bf16[160,1280]{1,0:T(8,128)(2,1)S(1)} %get-tuple-element.210), channel_id=1, source_target_pairs={{8,0},{16,8},{24,16},{28,24},{20,28},{12,20},{4,12},{0,4},{9,1},{1... | collective-permute-start | bytes 1228808 | tf_op jit(solution)/shard_map/ppermute | solution.py:538
  424.6 18.1 %collective-permute-start.46 = (bf16[160,1280]{1,0:T(8,128)(2,1)S(1)}, bf16[160,1280]{1,0:T(8,128)(2,1)S(1)}, u32[]{:S(2)}, u32[]{:S(2)}) collective-permute-start(bf16[160,1280]{1,0:T(8,128)(2,1)S(1)} %get-tuple-element.211), channel_id=1, source_target_pairs={{0,8},{8,16},{16,24},{24,28},{28,20},{20,12},{12,4},{4,0},{1,9},{9... | collective-permute-start | bytes 1228808 | tf_op jit(solution)/shard_map/ppermute | solution.py:538
  436.2 19.9 %collective-permute-start.48 = (bf16[160,1280]{1,0:T(8,128)(2,1)S(1)}, bf16[160,1280]{1,0:T(8,128)(2,1)S(1)}, u32[]{:S(2)}, u32[]{:S(2)}) collective-permute-start(bf16[160,1280]{1,0:T(8,128)(2,1)S(1)} %get-tuple-element.209), channel_id=1, source_target_pairs={{0,8},{8,16},{16,24},{24,28},{28,20},{20,12},{12,4},{4,0},{1,9},{9... | collective-permute-start | bytes 1228808 | tf_op jit(solution)/shard_map/ppermute | solution.py:538
  436.6 36.3 %collective-permute-start.49 = (bf16[160,1280]{1,0:T(8,128)(2,1)S(1)}, bf16[160,1280]{1,0:T(8,128)(2,1)}, u32[]{:S(2)}, u32[]{:S(2)}) collective-permute-start(bf16[160,1280]{1,0:T(8,128)(2,1)S(1)} %get-tuple-element.208), channel_id=1, source_target_pairs={{8,0},{16,8},{24,16},{28,24},{20,28},{12,20},{4,12},{0,4},{9,1},{1... | collective-permute-start | bytes 1228808 | tf_op jit(solution)/shard_map/ppermute | solution.py:538
  440.7 29.4 %collective-permute-start.44 = (bf16[160,1280]{1,0:T(8,128)(2,1)}, bf16[160,1280]{1,0:T(8,128)(2,1)}, u32[]{:S(2)}, u32[]{:S(2)}) collective-permute-start(bf16[160,1280]{1,0:T(8,128)(2,1)} %get-tuple-element.215), channel_id=1, source_target_pairs={{0,8},{8,16},{16,24},{24,28},{28,20},{20,12},{12,4},{4,0},{1,9},{9... | collective-permute-start | bytes 1228808 | tf_op jit(solution)/shard_map/ppermute | solution.py:538
  441.0 29.4 %collective-permute-start.45 = (bf16[160,1280]{1,0:T(8,128)(2,1)}, bf16[160,1280]{1,0:T(8,128)(2,1)}, u32[]{:S(2)}, u32[]{:S(2)}) collective-permute-start(bf16[160,1280]{1,0:T(8,128)(2,1)} %get-tuple-element.214), channel_id=1, source_target_pairs={{8,0},{16,8},{24,16},{28,24},{20,28},{12,20},{4,12},{0,4},{9,1},{1... | collective-permute-start | bytes 1228808 | tf_op jit(solution)/shard_map/ppermute | solution.py:538
  445.0 32.4 %collective-permute-start.47 = (bf16[160,1280]{1,0:T(8,128)(2,1)}, bf16[160,1280]{1,0:T(8,128)(2,1)}, u32[]{:S(2)}, u32[]{:S(2)}) collective-permute-start(bf16[160,1280]{1,0:T(8,128)(2,1)} %get-tuple-element.203), channel_id=1, source_target_pairs={{8,0},{16,8},{24,16},{28,24},{20,28},{12,20},{4,12},{0,4},{9,1},{1... | collective-permute-start | bytes 1228808 | tf_op jit(solution)/shard_map/ppermute | solution.py:538
  457.0 17.1 %collective-permute-start.54 = (bf16[160,1280]{1,0:T(8,128)(2,1)}, bf16[160,1280]{1,0:T(8,128)(2,1)}, u32[]{:S(2)}, u32[]{:S(2)}) collective-permute-start(bf16[160,1280]{1,0:T(8,128)(2,1)} %add_convert_fusion.18), channel_id=1, source_target_pairs={{0,8},{8,16},{16,24},{24,28},{28,20},{20,12},{12,4},{4,0},{1,9},{9... | collective-permute-start | bytes 1228808 | tf_op jit(solution)/shard_map/ppermute | solution.py:538
  470.1 18.4 %collective-permute-start.52 = (bf16[160,1280]{1,0:T(8,128)(2,1)S(1)}, bf16[160,1280]{1,0:T(8,128)(2,1)S(1)}, u32[]{:S(2)}, u32[]{:S(2)}) collective-permute-start(bf16[160,1280]{1,0:T(8,128)(2,1)S(1)} %copy-done.17), channel_id=1, source_target_pairs={{0,8},{8,16},{16,24},{24,28},{28,20},{20,12},{12,4},{4,0},{1,9},{9... | collective-permute-start | bytes 1228808 | tf_op jit(solution)/shard_map/ppermute | solution.py:538
  472.0 55.2 %collective-permute-start.50 = (bf16[160,1280]{1,0:T(8,128)(2,1)S(1)}, bf16[160,1280]{1,0:T(8,128)(2,1)S(1)}, u32[]{:S(2)}, u32[]{:S(2)}) collective-permute-start(bf16[160,1280]{1,0:T(8,128)(2,1)S(1)} %get-tuple-element.207), channel_id=1, source_target_pairs={{0,8},{8,16},{16,24},{24,28},{28,20},{20,12},{12,4},{4,0},{1,9},{9... | collective-permute-start | bytes 1228808 | tf_op jit(solution)/shard_map/ppermute | solution.py:538
  472.9 54.6 %collective-permute-start.51 = (bf16[160,1280]{1,0:T(8,128)(2,1)S(1)}, bf16[160,1280]{1,0:T(8,128)(2,1)S(1)}, u32[]{:S(2)}, u32[]{:S(2)}) collective-permute-start(bf16[160,1280]{1,0:T(8,128)(2,1)S(1)} %get-tuple-element.206), channel_id=1, source_target_pairs={{8,0},{16,8},{24,16},{28,24},{20,28},{12,20},{4,12},{0,4},{9,1},{1... | collective-permute-start | bytes 1228808 | tf_op jit(solution)/shard_map/ppermute | solution.py:538
  475.7 31.2 %collective-permute-start.55 = (bf16[160,1280]{1,0:T(8,128)(2,1)S(1)}, bf16[160,1280]{1,0:T(8,128)(2,1)S(1)}, u32[]{:S(2)}, u32[]{:S(2)}) collective-permute-start(bf16[160,1280]{1,0:T(8,128)(2,1)S(1)} %get-tuple-element.198), channel_id=1, source_target_pairs={{8,0},{16,8},{24,16},{28,24},{20,28},{12,20},{4,12},{0,4},{9,1},{1... | collective-permute-start | bytes 1228808 | tf_op jit(solution)/shard_map/ppermute | solution.py:538
  477.4 35.5 %collective-permute-start.58 = (bf16[160,1280]{1,0:T(8,128)(2,1)S(1)}, bf16[160,1280]{1,0:T(8,128)(2,1)S(1)}, u32[]{:S(2)}, u32[]{:S(2)}) collective-permute-start(bf16[160,1280]{1,0:T(8,128)(2,1)S(1)} %get-tuple-element.199), channel_id=1, source_target_pairs={{0,8},{8,16},{16,24},{24,28},{28,20},{20,12},{12,4},{4,0},{1,9},{9... | collective-permute-start | bytes 1228808 | tf_op jit(solution)/shard_map/ppermute | solution.py:538
  490.0 27.5 %collective-permute-start.53 = (bf16[160,1280]{1,0:T(8,128)(2,1)S(1)}, bf16[160,1280]{1,0:T(8,128)(2,1)S(1)}, u32[]{:S(2)}, u32[]{:S(2)}) collective-permute-start(bf16[160,1280]{1,0:T(8,128)(2,1)S(1)} %get-tuple-element.200), channel_id=1, source_target_pairs={{8,0},{16,8},{24,16},{28,24},{20,28},{12,20},{4,12},{0,4},{9,1},{1... | collective-permute-start | bytes 1228808 | tf_op jit(solution)/shard_map/ppermute | solution.py:538
  506.8 14.9 %collective-permute-start.56 = (bf16[160,1280]{1,0:T(8,128)(2,1)S(1)}, bf16[160,1280]{1,0:T(8,128)(2,1)S(1)}, u32[]{:S(2)}, u32[]{:S(2)}) collective-permute-start(bf16[160,1280]{1,0:T(8,128)(2,1)S(1)} %get-tuple-element.201), channel_id=1, source_target_pairs={{0,8},{8,16},{16,24},{24,28},{28,20},{20,12},{12,4},{4,0},{1,9},{9... | collective-permute-start | bytes 1228808 | tf_op jit(solution)/shard_map/ppermute | solution.py:538
  514.3 39.6 %collective-permute-start.59 = (bf16[160,1280]{1,0:T(8,128)(2,1)S(1)}, bf16[160,1280]{1,0:T(8,128)(2,1)S(1)}, u32[]{:S(2)}, u32[]{:S(2)}) collective-permute-start(bf16[160,1280]{1,0:T(8,128)(2,1)S(1)} %get-tuple-element.195), channel_id=1, source_target_pairs={{8,0},{16,8},{24,16},{28,24},{20,28},{12,20},{4,12},{0,4},{9,1},{1... | collective-permute-start | bytes 1228808 | tf_op jit(solution)/shard_map/ppermute | solution.py:538
  517.5 36.4 %collective-permute-start.69 = (bf16[160,1280]{1,0:T(8,128)(2,1)S(1)}, bf16[160,1280]{1,0:T(8,128)(2,1)}, u32[]{:S(2)}, u32[]{:S(2)}) collective-permute-start(bf16[160,1280]{1,0:T(8,128)(2,1)S(1)} %get-tuple-element.194), channel_id=1, source_target_pairs={{0,8},{8,16},{16,24},{24,28},{28,20},{20,12},{12,4},{4,0},{1,9},{9... | collective-permute-start | bytes 1228808 | tf_op jit(solution)/shard_map/ppermute | solution.py:538
  524.1 32.3 %collective-permute-start.57 = (bf16[160,1280]{1,0:T(8,128)(2,1)}, bf16[160,1280]{1,0:T(8,128)(2,1)}, u32[]{:S(2)}, u32[]{:S(2)}) collective-permute-start(bf16[160,1280]{1,0:T(8,128)(2,1)} %get-tuple-element.197), channel_id=1, source_target_pairs={{8,0},{16,8},{24,16},{28,24},{20,28},{12,20},{4,12},{0,4},{9,1},{1... | collective-permute-start | bytes 1228808 | tf_op jit(solution)/shard_map/ppermute | solution.py:538
  527.2 29.2 %collective-permute-start.67 = (bf16[160,1280]{1,0:T(8,128)(2,1)}, bf16[160,1280]{1,0:T(8,128)(2,1)}, u32[]{:S(2)}, u32[]{:S(2)}) collective-permute-start(bf16[160,1280]{1,0:T(8,128)(2,1)} %get-tuple-element.196), channel_id=1, source_target_pairs={{0,8},{8,16},{16,24},{24,28},{28,20},{20,12},{12,4},{4,0},{1,9},{9... | collective-permute-start | bytes 1228808 | tf_op jit(solution)/shard_map/ppermute | solution.py:538
  574.3 24.0 %collective-permute-start.78 = (f32[9020]{0:T(1024)S(1)}, f32[9020]{0:T(1024)S(1)}, u32[]{:S(2)}, u32[]{:S(2)}) collective-permute-start(f32[9020]{0:T(1024)S(1)} %add.882), channel_id=1, source_target_pairs={{0,8},{4,12},{8,0},{12,4},{16,24},{20,28},{24,16},{28,20},{1,9},{5... | collective-permute-start | bytes 108248 | tf_op jit(solution)/shard_map/ppermute | solution.py:576
  580.3 54.2 %collective-permute-start.62 = (bf16[2,640,1024]{1,2,0:T(8,128)(2,1)}, bf16[2,640,1024]{1,2,0:T(8,128)(2,1)}, u32[]{:S(2)}, u32[]{:S(2)}) collective-permute-start(bf16[2,640,1024]{1,2,0:T(8,128)(2,1)} %bitcast.106), channel_id=1, source_target_pairs={{0,1},{1,0},{2,3},{3,2},{4,5},{5,4},{6,7},{7,6},{8,9},{9,8},{10,11... | collective-permute-start | bytes 7864328 | tf_op jit(solution)/shard_map/ppermute | solution.py:566
  583.5 33.2 %collective-permute-start.73 = (bf16[160,1280]{1,0:T(8,128)(2,1)}, bf16[160,1280]{1,0:T(8,128)(2,1)}, u32[]{:S(2)}, u32[]{:S(2)}) collective-permute-start(bf16[160,1280]{1,0:T(8,128)(2,1)} %get-tuple-element.191), channel_id=1, source_target_pairs={{8,0},{16,8},{24,16},{28,24},{20,28},{12,20},{4,12},{0,4},{9,1},{1... | collective-permute-start | bytes 1228808 | tf_op jit(solution)/shard_map/ppermute | solution.py:538
  584.4 35.9 %collective-permute-start.68 = (bf16[160,1280]{1,0:T(8,128)(2,1)}, bf16[160,1280]{1,0:T(8,128)(2,1)}, u32[]{:S(2)}, u32[]{:S(2)}) collective-permute-start(bf16[160,1280]{1,0:T(8,128)(2,1)} %get-tuple-element.193), channel_id=1, source_target_pairs={{8,0},{16,8},{24,16},{28,24},{20,28},{12,20},{4,12},{0,4},{9,1},{1... | collective-permute-start | bytes 1228808 | tf_op jit(solution)/shard_map/ppermute | solution.py:538
  598.0 18.6 %collective-permute-start.70 = (bf16[160,1280]{1,0:T(8,128)(2,1)}, bf16[160,1280]{1,0:T(8,128)(2,1)}, u32[]{:S(2)}, u32[]{:S(2)}) collective-permute-start(bf16[160,1280]{1,0:T(8,128)(2,1)} %get-tuple-element.190), channel_id=1, source_target_pairs={{0,8},{8,16},{16,24},{24,28},{28,20},{20,12},{12,4},{4,0},{1,9},{9... | collective-permute-start | bytes 1228808 | tf_op jit(solution)/shard_map/ppermute | solution.py:538
  598.3 16.5 %collective-permute-start.79 = (f32[9020]{0:T(1024)S(1)}, f32[9020]{0:T(1024)S(1)}, u32[]{:S(2)}, u32[]{:S(2)}) collective-permute-start(f32[9020]{0:T(1024)S(1)} %add.883), channel_id=1, source_target_pairs={{0,16},{4,20},{8,24},{12,28},{16,0},{20,4},{24,8},{28,12},{1,17},{... | collective-permute-start | bytes 108248 | tf_op jit(solution)/shard_map/ppermute | solution.py:576
  614.8 36.4 %collective-permute-start.60 = (bf16[2,640,1024]{1,2,0:T(8,128)(2,1)}, bf16[2,640,1024]{1,2,0:T(8,128)(2,1)}, u32[]{:S(2)}, u32[]{:S(2)}) collective-permute-start(bf16[2,640,1024]{1,2,0:T(8,128)(2,1)} %bitcast.96), channel_id=1, source_target_pairs={{0,1},{1,0},{2,3},{3,2},{4,5},{5,4},{6,7},{7,6},{8,9},{9,8},{10,11... | collective-permute-start | bytes 7864328 | tf_op jit(solution)/shard_map/ppermute | solution.py:566
  639.6 32.0 %collective-permute-start.63 = (bf16[1,640,1024]{1,2,0:T(8,128)(2,1)}, bf16[1,640,1024]{1,2,0:T(8,128)(2,1)}, u32[]{:S(2)}, u32[]{:S(2)}) collective-permute-start(bf16[1,640,1024]{1,2,0:T(8,128)(2,1)} %constant_dynamic-slice_fusion), channel_id=1, source_target_pairs={{0,2},{1,3},{2,0},{3,1},{4,6},{5,7},{6,4},{7,5},{8,10},{9,11},{10,... | collective-permute-start | bytes 3932168 | tf_op jit(solution)/shard_map/ppermute | solution.py:566
  646.1 30.3 %collective-permute-start.76 = (bf16[160,1280]{1,0:T(8,128)(2,1)}, bf16[160,1280]{1,0:T(8,128)(2,1)}, u32[]{:S(2)}, u32[]{:S(2)}) collective-permute-start(bf16[160,1280]{1,0:T(8,128)(2,1)} %get-tuple-element.185), channel_id=1, source_target_pairs={{8,0},{16,8},{24,16},{28,24},{20,28},{12,20},{4,12},{0,4},{9,1},{1... | collective-permute-start | bytes 1228808 | tf_op jit(solution)/shard_map/ppermute | solution.py:538
  656.4 58.0 %collective-permute-start.61 = (bf16[1,640,1024]{1,2,0:T(8,128)(2,1)}, bf16[1,640,1024]{1,2,0:T(8,128)(2,1)}, u32[]{:S(2)}, u32[]{:S(2)}) collective-permute-start(bf16[1,640,1024]{1,2,0:T(8,128)(2,1)} %constant_dynamic-slice_fusion.3), channel_id=1, source_target_pairs={{0,2},{1,3},{2,0},{3,1},{4,6},{5,7},{6,4},{7,5},{8,10},{9,11},{10,... | collective-permute-start | bytes 3932168 | tf_op jit(solution)/shard_map/ppermute | solution.py:566
  659.0 45.5 %collective-permute-start.81 = (f32[325,256]{1,0:T(8,128)S(1)}, f32[325,256]{1,0:T(8,128)S(1)}, u32[]{:S(2)}, u32[]{:S(2)}) collective-permute-start(f32[325,256]{1,0:T(8,128)S(1)} %fusion.36), channel_id=1, source_target_pairs={{0,2},{1,3},{2,0},{3,1},{4,6},{5,7},{6,4},{7,5},{8,10},{9,11},{10,... | collective-permute-start | bytes 998408 | tf_op jit(solution)/shard_map/ppermute | solution.py:576
  679.2 27.4 %collective-permute-start.65 = (f32[640]{0:T(1024)S(1)}, f32[640]{0:T(1024)S(1)}, u32[]{:S(2)}, u32[]{:S(2)}) collective-permute-start(f32[640]{0:T(1024)S(1)} %add.869), channel_id=1, source_target_pairs={{0,8},{4,12},{8,0},{12,4},{16,24},{20,28},{24,16},{28,20},{1,9},{5... | collective-permute-start | bytes 7688 | tf_op jit(solution)/shard_map/ppermute | solution.py:576
  (60 other events, 931.0 us)
Sparse Core Ops, SparseCore 0:
  10.8 55.6 all-gather.8
  68.0 43.0 all-gather.4
  113.3 128.2 all-gather.6
  465.9 76.9 reduce-scatter.1

commit v5 on v4

--- a/solution.py
+++ b/solution.py
@@ -490,30 +490,37 @@
     return ahead, [(target, source) for source, target in ahead]
 
 
-def ring_gather(shard, splits):
-    count = lax.axis_size("gx")
-    ahead, behind = ring_moves(count)
-    me = lax.axis_index("gx")
-    place = ring_place(me, count)
-    rows, width = shard.shape
-    half = rows // 2
-    edges = [0] + splits + [width]
-    fulls = [jnp.zeros((count * rows, hi - lo), shard.dtype) for lo, hi in zip(edges, edges[1:])]
-
-    def put(fulls, piece, start):
-        return [
-            lax.dynamic_update_slice(full, piece[:, lo:hi], (start, 0))
-            for full, lo, hi in zip(fulls, edges, edges[1:])
-        ]
-
-    fulls = put(fulls, shard, me * rows)
-    up, down = shard[:half], shard[half:]
-    for step in range(1, count):
-        up = lax.ppermute(up, "gx", ahead)
-        down = lax.ppermute(down, "gx", behind)
-        fulls = put(fulls, up, ring_index(place - step, count) * rows)
-        fulls = put(fulls, down, ring_index(place + step, count) * rows + half)
-    return fulls, (up, down)
+class RingGather:
+    def __init__(self, shard):
+        self.count = lax.axis_size("gx")
+        self.moves = ring_moves(self.count)
+        me = lax.axis_index("gx")
+        self.place = ring_place(me, self.count)
+        self.rows, width = shard.shape
+        self.half = self.rows // 2
+        self.taken = 0
+        self.held = (shard[: self.half], shard[self.half :])
+        full = jnp.zeros((self.count * self.rows, width), shard.dtype)
+        self.full = lax.dynamic_update_slice(full, shard, (me * self.rows, 0))
+
+    def step(self, times=1):
+        for _ in range(min(times, self.count - 1 - self.taken)):
+            self.taken += 1
+            self.held = tuple(
+                lax.ppermute(held, "gx", move) for held, move in zip(self.held, self.moves)
+            )
+            for piece, sign, offset in zip(self.held, (-1, 1), (0, self.half)):
+                owner = ring_index(self.place + sign * self.taken, self.count)
+                start = owner * self.rows + offset
+                self.full = lax.dynamic_update_slice(self.full, piece, (start, 0))
+        return self.held
+
+    def wait_for(self, *others):
+        self.held = (after(self.held[0], *others), self.held[1])
+
+    def finish(self):
+        self.step(self.count)
+        return self.full
 
 
 class RingSum:
@@ -616,14 +623,17 @@
 
     state_step_weight = jnp.concatenate([state_weight, step_weight], 1)
     full_state = lax.all_gather(state_step_weight, "gx", axis=0, tiled=True)
+    full_gate = lax.all_gather(gate_weight, "gx", axis=0, tiled=True)
     upstream = lax.all_gather(cotangent, "gy", axis=1, tiled=True)
-    full_out = lax.all_gather(out_weight.T, "gx", axis=0, tiled=True)
-    (full_value,), moved = ring_gather(value_weight, [])
-    (full_gate,), moved = ring_gather(after(gate_weight, *moved), [])
-
-    tokens = layer_input.astype(wide)
+    value_gather = RingGather(value_weight)
+    value_gather.step()
+
+    tokens = after(layer_input, *value_gather.step()).astype(wide)
     scale_in = lax.rsqrt(jnp.mean(tokens * tokens, axis=1, keepdims=True) + epsilon)
     normed = (tokens * scale_in * norm_gain).astype(low)
+    value_gather.step()
+    value_gather.wait_for(normed)
+    value_gather.step()
 
     state_step = dot(normed, full_state)
     mixer = Mixer(
@@ -635,14 +645,22 @@
         decay_log,
         segment_ids,
     )
+    value_gather.step()
+    value_gather.wait_for(mixer.g)
+    full_value = value_gather.finish()
+    out_gather = RingGather(after(out_weight.T, *value_gather.held))
     value_in = dot(normed, full_value)
+    value_in = after(value_in, *out_gather.step())
     mixed = mixer.forward(value_in, conv_value, conv_value_bias, skip_scale)
+    out_gather.step(2)
+    out_gather.wait_for(mixed)
+    full_out = out_gather.finish()
     full_value_state = jnp.concatenate([full_value, full_state], 1)
-    up_back = dot(upstream, full_out)
     gate_in = dot(normed, full_gate)
     gate_open = jax.nn.sigmoid(gate_in)
     gate_act = gate_in * gate_open
     gated = mixed * gate_act
+    up_back = dot(upstream, full_out)
 
     sums_out = lax.psum(
         jnp.stack(
@@ -667,10 +685,13 @@
     gate_partial = contract_rows(after(normed, *out_ring.step()), grad_gate_in)
     gate_ring = RingSum(row_major(gate_partial.astype(low)))
 
-    half = (mixer.pairs + 1) // 2
-    part = mixer.backward_part(after(grad_mixed, *out_ring.step(), *gate_ring.held), 0, half)
+    first = (mixer.pairs + 2) // 3
+    second = (first + mixer.pairs + 1) // 2
+    part = mixer.backward_part(after(grad_mixed, *out_ring.step(), *gate_ring.held), 0, first)
     grad_mixed = after(grad_mixed, *out_ring.step(), *gate_ring.step(), part[0])
-    value_grad, value_sums, *totals = mixer.backward_part(grad_mixed, half, mixer.pairs, part)
+    part = mixer.backward_part(grad_mixed, first, second, part)
+    grad_mixed = after(grad_mixed, *out_ring.step(), *gate_ring.step(), part[0])
+    value_grad, value_sums, *totals = mixer.backward_part(grad_mixed, second, mixer.pairs, part)
     grad_value_in = value_grad[:, : gate_weight.shape[1]]
     value_partial = contract_rows(
         after(normed, *out_ring.step(), *gate_ring.step()), grad_value_in
@@ -684,16 +705,16 @@
     state_partial = row_major(contract_rows(normed, grad_state_in).astype(low))
     grad_state_step = scatter_rows(state_partial).astype(wide)
 
-    held = out_ring.step() + gate_ring.step() + value_ring.step()
+    held = value_ring.step()
     grad_normed_part = contract_cols(full_gate, after(grad_gate_in, state_partial, *held))
     grad_value_state_in = jnp.concatenate([grad_value_in, grad_state_in], 1)
-    held = out_ring.step() + gate_ring.step() + value_ring.step()
+    held = out_ring.step() + gate_ring.step()
     grad_value_state_in = after(grad_value_state_in, *held)
     grad_normed_part = grad_normed_part + contract_cols(full_value_state, grad_value_state_in)
-    grad_normed_part = grad_normed_part.astype(low)
-    held = gate_ring.step() + value_ring.step()
+    grad_normed_part = row_major(grad_normed_part.astype(low))
+    held = value_ring.step()
     product_part = contract_cols(full_out, after(scaled, grad_normed_part, *held))
-    product_part = (product_part * scale_out[:, 0]).astype(low)
+    product_part = row_major((product_part * scale_out[:, 0]).astype(low))
     grad_out = out_ring.finish()
     grad_gate = gate_ring.finish()
     grad_value = value_ring.finish()

time: 734 us -> 749 us (1.020)
    mul x0 -> x1, other arithmetic: none -> 9.9 us  [on_device(): grad_mixed = grad_gated * gate_act]
    convert_element_type x1 -> x0, other arithmetic: 9.04 us -> none  [on_device(): grad_gate_in = (grad_gated * mixed * gate_open * (1.0 + gate_in * (1.0 -...]
    dynamic_update_slice x30, local copies, waits for them, and re-layouts: 18.7 us -> 27.1 us  [the longest x28 25.2 us: step(): self.full = lax.dynamic_update_slice(self.full, piece, (start, 0))]
    another operation x3 -> x2, local copies, waits for them, and re-layouts: 15.1 us -> 6.73 us  [the longest x1 11.6 us: halving_sum(): pairs = held.reshape(held.shape[0] // 2, 2, *held.shape[1:])]
    unnamed x83 -> x88, local copies, waits for them, and re-layouts: 15.8 us -> 21.7 us
    pallas_call x5 -> x6, Pallas kernels: 84.6 us -> 88.8 us  [call(): pl.pallas_call(kernel, out_shape=shapes, scratch_shapes=list(scratch), co...]
  transfers between devices with their start and end apart: 86 -> 86, of which waited for: 33 -> 28; matrix products, arithmetic and copies ran while one was open for 35% -> 36% of each run, Pallas kernels for 12% -> 12%
where the time goes in v5:
time: 749 us; the launch traced here: 743 us
  waiting for transfers between devices  207 us (28%)
  matrix products  123 us (16%)
  starting transfers between devices  114 us (15%)
  local copies, waits for them, and re-layouts  102 us (14%)
  Pallas kernels  88.8 us (12%)
  other arithmetic  80.3 us (11%)
  between operations  15.3 us (2%)
  blocking collectives  11.6 us (2%)
    ppermute x28, waiting for transfers between devices, step(): lax.ppermute(held, 'gx', move)  113 us
    pallas_call x6, Pallas kernels, call(): pl.pallas_call(kernel, out_shape=shapes, scratch_shapes=list(scratch), co...  88.8 us
    ppermute x28, starting transfers between devices, step(): lax.ppermute(held, 'gx', move)  56.7 us
    ppermute x42, waiting for transfers between devices, step(): lax.ppermute(held, 'gx', move).astype(wide)  49.4 us
    ppermute x42, starting transfers between devices, step(): lax.ppermute(held, 'gx', move).astype(wide)  46.9 us
    dot_general x4, matrix products, dot(): jnp.dot(left, right, preferred_element_type=wide, precision=precision)  45.6 us
    dot_general x3, matrix products, contract_cols(): lax.dot_general(left, right, (((1,), (1,)), ((), ())), preferred_element_...  39.9 us
    dot_general x4, matrix products, contract_rows(): lax.dot_general(left, right, (((0,), (0,)), ((), ())), preferred_element_...  37.8 us
  transfers between devices with their start and end apart: 86, of which 28 were waited for; matrix products, arithmetic and copies ran while one was open for 36% of the time, Pallas kernels for 12%

profile of v5, /device:TPU:0, one launch (start us, length us, event | category | flops | bytes accessed | tf_op | source)
XLA Modules:
  0.0 742.6 jit_solution(14562336959346476414)
XLA Ops:
  11.9 3.0 collective-permute-start.3
  21.0 3.6 broadcast.84.clone
  30.1 11.1 %collective-permute-done.4 = bf16[160,1280]{1,0:T(8,128)(2,1)S(1)} collective-permute-done((bf16[160,1280]{1,0:T(8,128)(2,1)S(1)}, bf16[160,1280]{1,0:T(8,128)(2,1)S(1)}, u32[]{:S(2)}, u32[]{:S(2)}) %collective-permute-start.4) | collective-permute-done | bytes 409632 | tf_op jit(solution)/shard_map/ppermute | solution.py:510
  43.5 3.5 fusion.2
  47.1 2.7 collective-permute-start.9
  51.4 13.3 %collective-permute-done.2 = bf16[160,1280]{1,0:T(8,128)(2,1)S(1)} collective-permute-done((bf16[160,1280]{1,0:T(8,128)(2,1)S(1)}, bf16[160,1280]{1,0:T(8,128)(2,1)S(1)}, u32[]{:S(2)}, u32[]{:S(2)}) %collective-permute-start.2) | collective-permute-done | bytes 409632 | tf_op jit(solution)/shard_map/ppermute | solution.py:510
  64.7 2.5 collective-permute-start.5
  69.8 8.0 %collective-permute-done.10 = bf16[160,1280]{1,0:T(8,128)(2,1)S(1)} collective-permute-done((bf16[160,1280]{1,0:T(8,128)(2,1)S(1)}, bf16[160,1280]{1,0:T(8,128)(2,1)S(1)}, u32[]{:S(2)}, u32[]{:S(2)}) %collective-permute-start.10) | collective-permute-done | bytes 409632 | tf_op jit(solution)/shard_map/ppermute | solution.py:510
  81.5 26.3 %collective-permute-done.11 = bf16[160,1280]{1,0:T(8,128)(2,1)} collective-permute-done((bf16[160,1280]{1,0:T(8,128)(2,1)S(1)}, bf16[160,1280]{1,0:T(8,128)(2,1)}, u32[]{:S(2)}, u32[]{:S(2)}) %collective-permute-start.11) | collective-permute-done | bytes 409632 | tf_op jit(solution)/shard_map/ppermute | solution.py:510
  110.9 4.8 fusion.45
  119.6 17.6 %shard_map.288 = (bf16[1024,128]{1,0:T(8,128)(2,1)}, bf16[1024,128]{1,0:T(8,128)(2,1)}, bf16[128,1024]{1,0:T(8,128)(2,1)}, bf16[128,1024]{1,0:T(8,128)(2,1)}, f3...) custom-call(f32[1024,256]{1,0:T(8,128)} %slice.145.state_ref, ...), custom_call_target="tpu_custom_call" | custom-call | flops 2013265920 | bytes 17315840 | tf_op jit(solution)/shard_map/pallas_call | solution.py:293
  147.1 9.2 %collective-permute-done.7 = bf16[160,1280]{1,0:T(8,128)(2,1)S(1)} collective-permute-done((bf16[160,1280]{1,0:T(8,128)(2,1)}, bf16[160,1280]{1,0:T(8,128)(2,1)S(1)}, u32[]{:S(2)}, u32[]{:S(2)}) %collective-permute-start.7) | collective-permute-done | bytes 409632 | tf_op jit(solution)/shard_map/ppermute | solution.py:510
  156.3 7.7 %collective-permute-start.8 = (bf16[160,1280]{1,0:T(8,128)(2,1)S(1)}, bf16[160,1280]{1,0:T(8,128)(2,1)S(1)}, u32[]{:S(2)}, u32[]{:S(2)}) collective-permute-start(bf16[160,1280]{1,0:T(8,128)(2,1)S(1)} %collective-permute-done.7), channel_id=1, source_target_pairs={{0,8},{8,16},{16,24},{24,28},{28,20},{20,12},{12,4},{4,0},{1,9},{9... | collective-permute-start | bytes 1228808 | tf_op jit(solution)/shard_map/ppermute | solution.py:510
  166.5 3.9 collective-permute-done.13
  170.5 13.0 %collective-permute-done.8 = bf16[160,1280]{1,0:T(8,128)(2,1)S(1)} collective-permute-done((bf16[160,1280]{1,0:T(8,128)(2,1)S(1)}, bf16[160,1280]{1,0:T(8,128)(2,1)S(1)}, u32[]{:S(2)}, u32[]{:S(2)}) %collective-permute-start.8) | collective-permute-done | bytes 409632 | tf_op jit(solution)/shard_map/ppermute | solution.py:510
  183.6 15.1 %collective-permute-start.15 = (bf16[160,1280]{1,0:T(8,128)(2,1)S(1)}, bf16[160,1280]{1,0:T(8,128)(2,1)S(1)}, u32[]{:S(2)}, u32[]{:S(2)}) collective-permute-start(bf16[160,1280]{1,0:T(8,128)(2,1)S(1)} %get-tuple-element.260), channel_id=1, source_target_pairs={{8,0},{16,8},{24,16},{28,24},{20,28},{12,20},{4,12},{0,4},{9,1},{1... | collective-permute-start | bytes 1228808 | tf_op jit(solution)/shard_map/ppermute | solution.py:510
  200.2 12.3 %fusion.46.value_ref = f32[1024,1280]{1,0:T(8,128)} fusion(bf16[1024,2560]{1,0:T(8,128)(2,1)} %fusion.2, bf16[2560,1280]{1,0:T(8,128)(2,1)} %constant_dynamic-update-slice_fusion.8), kind=kOutput, calls=%fused_computation.178 | convolution fusion | flops 6710886400 | bytes 17039360 | tf_op jit(solution)/shard_map/dot_general | solution.py:25
  212.5 3.1 broadcast.84.clone.1
  216.6 4.6 collective-permute-start.17
  222.7 18.2 %shard_map.289.mixed_ref = f32[1024,1280]{1,0:T(8,128)} custom-call(f32[1024,1280]{1,0:T(8,128)} %fusion.46.value_ref, f32[4,1280]{1,0:T(4,128)} %taps_ref.10, f32[1,1280]{1,0:T(1,128)} %broadcast_in_dim.50.bias_ref, f32[1,1280]{1,0:T(1,128)} %broadcast_in_dim_reshape.3.skip_ref, f32[1024,1280]{1,0:T(8,128)} %get-tuple-element.73.dtx_ref, ...), custom_call_target="tpu_custom_call" | custom-call | flops 3355443200 | bytes 24754176 | tf_op jit(solution)/shard_map/pallas_call | solution.py:293
  244.6 9.2 %collective-permute-done.18 = bf16[160,1280]{1,0:T(8,128)(2,1)S(1)} collective-permute-done((bf16[160,1280]{1,0:T(8,128)(2,1)S(1)}, bf16[160,1280]{1,0:T(8,128)(2,1)S(1)}, u32[]{:S(2)}, u32[]{:S(2)}) %collective-permute-start.18) | collective-permute-done | bytes 409632 | tf_op jit(solution)/shard_map/ppermute | solution.py:510
  257.4 6.4 collective-permute-done.21
  267.4 4.4 collective-permute-done.23
  276.8 2.9 collective-permute-done.25
  285.2 4.8 collective-permute-done.26
  291.5 12.3 %fusion.47 = f32[1024,1280]{1,0:T(8,128)} fusion(bf16[1024,2560]{1,0:T(8,128)(2,1)} %fusion.2, bf16[2560,1280]{1,0:T(8,128)(2,1)} %all-gather.5.cloned.1.call-done), kind=kOutput, calls=%fused_computation.179 | convolution fusion | flops 6710886400 | bytes 17039360 | tf_op jit(solution)/shard_map/dot_general | solution.py:25
  303.8 16.2 %multiply_reduce_fusion.2 = (f32[1024]{0:T(1024)S(1)}, f32[1024]{0:T(1024)S(1)}, f32[1024,1280]{1,0:T(8,128)}, f32[1024,1280]{1,0:T(8,128)}) fusion(f32[1280]{0:T(1024)S(1)} %copy-done.32, f32[1024,1280]{1,0:T(8,128)} %shard_map.289.mixed_ref, f32[1024,1280]{1,0:T(8,128)} %fusion.47, bf16[1024,2560]{1,0:T(8,128)(2,1)} %all-gather.7.cloned.1.call-done, ...), kind=kOutput, calls=%fused_computation.25 | convolution fusion | flops 6723991552 | bytes 32781312 | tf_op jit(solution)/shard_map/dot_general | solution.py:25
  320.0 5.9 psum.14
  326.0 11.2 %fusion.4 = bf16[2560,1280]{1,0:T(8,128)(2,1)S(1)} fusion(bf16[1024,2560]{1,0:T(8,128)(2,1)} %all-gather.7.cloned.1.call-done, f32[1024,1280]{1,0:T(8,128)} %get-tuple-element.205, f32[1024]{0:T(1024)S(1)} %bitcast.121, f32[1280]{0:T(1024)S(1)} %copy-done.32), kind=kOutput, calls=%fused_computation.11 | convolution fusion | flops 6718095360 | bytes 17048576 | tf_op jit(solution)/shard_map/dot_general | solution.py:29
  339.5 9.9 %fusion.24 = (f32[1024,1280]{1,0:T(8,128)}, bf16[1024,1280]{1,0:T(8,128)(2,1)}, f32[1280]{0:T(1024)}, bf16[1024,1280]{1,0:T(8,128)(2,1)}) fusion(f32[1024,1280]{1,0:T(8,128)S(1)} %copy-done.10, f32[1024]{0:T(1024)S(1)} %fusion.33, f32[1024,1280]{1,0:T(8,128)S(1)} %copy-done.11, f32[1024]{0:T(1024)S(1)} %bitcast.122, f32[1280]{0:T(1024)S(1)} %copy-done.32, ...), kind=kLoop, calls=%fused_computation.50 | loop fusion | flops 27523840 | bytes 31475712 | tf_op jit(solution)/shard_map/mul | solution.py:684
  351.9 9.8 %convolution_convert_fusion.1 = bf16[2560,1280]{1,0:T(8,128)(2,1)S(1)} fusion(bf16[1024,2560]{1,0:T(8,128)(2,1)} %fusion.2, bf16[1024,1280]{1,0:T(8,128)(2,1)} %get-tuple-element.111), kind=kOutput, calls=%fused_computation.3 | convolution fusion | flops 6714163200 | bytes 14417920 | tf_op jit(solution)/shard_map/dot_general | solution.py:29
  367.0 7.8 %collective-permute-done.34 = bf16[160,1280]{1,0:T(8,128)(2,1)S(1)} collective-permute-done((bf16[160,1280]{1,0:T(8,128)(2,1)S(1)}, bf16[160,1280]{1,0:T(8,128)(2,1)S(1)}, u32[]{:S(2)}, u32[]{:S(2)}) %collective-permute-start.34) | collective-permute-done | bytes 409632 | tf_op jit(solution)/shard_map/ppermute | solution.py:545
  376.4 17.0 %shard_map.290 = (bf16[1024,1280]{1,0:T(8,128)(2,1)}, f32[8,1280]{1,0:T(8,128)}, f32[1024,128]{1,0:T(8,128)}, f32[1024,128]{1,0:T(8,128)}, f32[1024,128]{1,0:T(8...) custom-call(f32[1024,1280]{1,0:T(8,128)} %fusion.46.value_ref, f32[1024,1280]{1,0:T(8,128)} %shard_map.289.mixed_ref, ...), custom_call_target="tpu_custom_call" | custom-call | flops 4026531840 | bytes 35805184 | tf_op jit(solution)/shard_map/pallas_call | solution.py:293
  402.1 14.5 %shard_map.291 = (bf16[1024,1280]{1,0:T(8,128)(2,1)}, f32[8,1280]{1,0:T(8,128)}, f32[1024,128]{1,0:T(8,128)}, f32[1024,128]{1,0:T(8,128)}, f32[1024,128]{1,0:T(8...) custom-call(f32[1024,1280]{1,0:T(8,128)} %fusion.46.value_ref, ...), custom_call_target="tpu_custom_call", output_to_operand_aliasing={{0}: (15, {}), {1}: (16, {})} | custom-call | flops 3019898880 | bytes 41089024 | tf_op jit(solution)/shard_map/pallas_call | solution.py:293
  426.0 14.5 %shard_map.292 = (bf16[1024,1280]{1,0:T(8,128)(2,1)}, f32[8,1280]{1,0:T(8,128)}, f32[1024,128]{1,0:T(8,128)}, f32[1024,128]{1,0:T(8,128)}, f32[1024,128]{1,0:T(8...) custom-call(f32[1024,1280]{1,0:T(8,128)} %fusion.46.value_ref, ...), custom_call_target="tpu_custom_call", output_to_operand_aliasing={{0}: (15, {}), {1}: (16, {})} | custom-call | flops 3019898880 | bytes 41089024 | tf_op jit(solution)/shard_map/pallas_call | solution.py:293
  451.0 9.8 %convolution_convert_fusion = bf16[2560,1280]{1,0:T(8,128)(2,1)S(1)} fusion(bf16[1024,2560]{1,0:T(8,128)(2,1)} %fusion.2, bf16[1024,1280]{1,0:T(8,128)(2,1)} %get-tuple-element.103), kind=kOutput, calls=%fused_computation.2 | convolution fusion | flops 6714163200 | bytes 14417920 | tf_op jit(solution)/shard_map/dot_general | solution.py:29
  460.8 2.8 copy-done.7
  474.1 7.0 shard_map.293
  481.1 7.0 convolution_convert_fusion.3
  496.8 2.9 pad_maximum_fusion
  501.7 6.4 collective-permute-done.54
  510.7 13.9 %collective-permute-done.63 = bf16[160,1280]{1,0:T(8,128)(2,1)S(1)} collective-permute-done((bf16[160,1280]{1,0:T(8,128)(2,1)S(1)}, bf16[160,1280]{1,0:T(8,128)(2,1)S(1)}, u32[]{:S(2)}, u32[]{:S(2)}) %collective-permute-start.63) | collective-permute-done | bytes 409632 | tf_op jit(solution)/shard_map/ppermute | solution.py:545
  529.5 2.6 convert_add_fusion.7
  534.5 11.5 %fusion.48 = f32[1024,2560]{0,1:T(8,128)} fusion(bf16[1024,1280]{1,0:T(8,128)(2,1)S(1)} %copy-done.16, bf16[2560,1280]{1,0:T(8,128)(2,1)} %all-gather.5.cloned.1.call-done), kind=kOutput, calls=%fused_computation.180 | convolution fusion | flops 6710886400 | bytes 19660800 | tf_op jit(solution)/shard_map/dot_general | solution.py:35
  546.0 16.6 %fusion.3 = bf16[2560,1024]{1,0:T(8,128)(2,1)} fusion(f32[1024,2560]{0,1:T(8,128)} %fusion.48, bf16[1024,1556]{1,0:T(8,128)(2,1)S(1)} %copy-done.12, bf16[2560,276]{1,0:T(8,128)(2,1)} %copy.86, bf16[2560,1280]{1,0:T(8,128)(2,1)} %constant_dynamic-update-slice_fusion.8), kind=kOutput, calls=%fused_computation.9 | convolution fusion | flops 8179097600 | bytes 26882048 | tf_op jit(solution)/shard_map/dot_general | solution.py:35
  562.5 2.8 maximum_bitcast_fusion
  565.4 2.6 add_convert_fusion.9
  568.0 11.8 %multiply_convert_fusion = bf16[2560,1024]{1,0:T(8,128)(2,1)} fusion(bf16[2560,1280]{1,0:T(8,128)(2,1)} %constant_dynamic-update-slice_fusion, bf16[1024,1280]{1,0:T(8,128)(2,1)S(1)} %copy-done.15, f32[1024]{0:T(1024)S(1)} %bitcast.123), kind=kOutput, calls=%fused_computation.10 | convolution fusion | flops 6716129280 | bytes 14422016 | tf_op jit(solution)/shard_map/dot_general | solution.py:35
  579.9 2.9 constant_dynamic-slice_fusion.2
  582.9 3.1 copy.95
  586.0 4.6 copy.90
  599.0 4.9 collective-permute-done.78
  605.6 5.4 constant_dynamic-slice_fusion.5
  611.0 4.4 copy.94
  615.4 4.4 copy.88
  625.3 8.6 %collective-permute-done.69 = bf16[160,1280]{1,0:T(8,128)(2,1)S(1)} collective-permute-done((bf16[160,1280]{1,0:T(8,128)(2,1)S(1)}, bf16[160,1280]{1,0:T(8,128)(2,1)S(1)}, u32[]{:S(2)}, u32[]{:S(2)}) %collective-permute-start.69) | collective-permute-done | bytes 409632 | tf_op jit(solution)/shard_map/ppermute | solution.py:545
  640.9 6.3 collective-permute-done.70
  656.6 3.1 collective-permute-done.71
  667.9 2.5 fusion.12
  673.9 14.8 %collective-permute-done.59 = bf16[1,640,1024]{1,2,0:T(8,128)(2,1)} collective-permute-done((bf16[1,640,1024]{1,2,0:T(8,128)(2,1)}, bf16[1,640,1024]{1,2,0:T(8,128)(2,1)}, u32[]{:S(2)}, u32[]{:S(2)}) %collective-permute-start.59) | collective-permute-done | bytes 1310752 | tf_op jit(solution)/shard_map/ppermute | solution.py:573
  688.6 4.0 fusion.20
  699.3 21.8 %collective-permute-done.81 = f32[325,256]{1,0:T(8,128)S(1)} collective-permute-done((f32[325,256]{1,0:T(8,128)S(1)}, f32[325,256]{1,0:T(8,128)S(1)}, u32[]{:S(2)}, u32[]{:S(2)}) %collective-permute-start.81) | collective-permute-done | bytes 332832 | tf_op jit(solution)/shard_map/ppermute | solution.py:583
  725.0 5.7 psum.15
  731.3 4.5 fusion.17
  (358 shorter events, 198.3 us)
Async XLA Ops:
  7.2 100.7 %all-gather.9.cloned.1.call-start = ((), (), s32[]{:S(2)}) async-start(), calls=%async_computation.4 | async-start | bytes 1935360 | tf_op jit(solution)/shard_map/all_gather | solution.py:625
  9.8 281.7 %all-gather.5.cloned.1.call-start = ((), (), s32[]{:S(2)}) async-start(), calls=%async_computation.1 | async-start | bytes 7372800 | tf_op jit(solution)/shard_map/all_gather | solution.py:626
  10.6 293.2 %all-gather.7.cloned.1.call-start = ((), (), s32[]{:S(2)}) async-start(), calls=%async_computation.2 | async-start | bytes 6553600 | tf_op jit(solution)/shard_map/all_gather | solution.py:627
  11.9 14.0 %collective-permute-start.3 = (bf16[160,1280]{1,0:T(8,128)(2,1)S(1)}, bf16[160,1280]{1,0:T(8,128)(2,1)S(1)}, u32[]{:S(2)}, u32[]{:S(2)}) collective-permute-start(bf16[160,1280]{1,0:T(8,128)(2,1)S(1)} %get-tuple-element.262), channel_id=1, source_target_pairs={{8,0},{16,8},{24,16},{28,24},{20,28},{12,20},{4,12},{0,4},{9,1},{1... | collective-permute-start | bytes 1228808 | tf_op jit(solution)/shard_map/ppermute | solution.py:510
  14.9 13.5 %collective-permute-start = (bf16[160,1280]{1,0:T(8,128)(2,1)S(1)}, bf16[160,1280]{1,0:T(8,128)(2,1)S(1)}, u32[]{:S(2)}, u32[]{:S(2)}) collective-permute-start(bf16[160,1280]{1,0:T(8,128)(2,1)S(1)} %get-tuple-element.263), channel_id=1, source_target_pairs={{0,8},{8,16},{16,24},{24,28},{28,20},{20,12},{12,4},{4,0},{1,9},{9... | collective-permute-start | bytes 1228808 | tf_op jit(solution)/shard_map/ppermute | solution.py:510
  15.1 648.5 %reduce-scatter.2.cloned.1.call-start = ((), (), s32[]{:S(2)}) async-start(), calls=%async_computation.3 | async-start | bytes 2211840 | tf_op jit(solution)/shard_map/reduce_scatter | solution.py:589
  25.9 15.3 %collective-permute-start.4 = (bf16[160,1280]{1,0:T(8,128)(2,1)S(1)}, bf16[160,1280]{1,0:T(8,128)(2,1)S(1)}, u32[]{:S(2)}, u32[]{:S(2)}) collective-permute-start(bf16[160,1280]{1,0:T(8,128)(2,1)S(1)} %collective-permute-done.3), channel_id=1, source_target_pairs={{8,0},{16,8},{24,16},{28,24},{20,28},{12,20},{4,12},{0,4},{9,1},{1... | collective-permute-start | bytes 1228808 | tf_op jit(solution)/shard_map/ppermute | solution.py:510
  28.4 12.8 %collective-permute-start.1 = (bf16[160,1280]{1,0:T(8,128)(2,1)S(1)}, bf16[160,1280]{1,0:T(8,128)(2,1)S(1)}, u32[]{:S(2)}, u32[]{:S(2)}) collective-permute-start(bf16[160,1280]{1,0:T(8,128)(2,1)S(1)} %collective-permute-done), channel_id=1, source_target_pairs={{0,8},{8,16},{16,24},{24,28},{28,20},{20,12},{12,4},{4,0},{1,9},{9... | collective-permute-start | bytes 1228808 | tf_op jit(solution)/shard_map/ppermute | solution.py:510
  47.1 20.1 %collective-permute-start.9 = (bf16[160,1280]{1,0:T(8,128)(2,1)S(1)}, bf16[160,1280]{1,0:T(8,128)(2,1)S(1)}, u32[]{:S(2)}, u32[]{:S(2)}) collective-permute-start(bf16[160,1280]{1,0:T(8,128)(2,1)S(1)} %collective-permute-done.4), channel_id=1, source_target_pairs={{8,0},{16,8},{24,16},{28,24},{20,28},{12,20},{4,12},{0,4},{9,1},{1... | collective-permute-start | bytes 1228808 | tf_op jit(solution)/shard_map/ppermute | solution.py:510
  49.8 14.9 %collective-permute-start.2 = (bf16[160,1280]{1,0:T(8,128)(2,1)S(1)}, bf16[160,1280]{1,0:T(8,128)(2,1)S(1)}, u32[]{:S(2)}, u32[]{:S(2)}) collective-permute-start(bf16[160,1280]{1,0:T(8,128)(2,1)S(1)} %collective-permute-done.1), channel_id=1, source_target_pairs={{0,8},{8,16},{16,24},{24,28},{28,20},{20,12},{12,4},{4,0},{1,9},{9... | collective-permute-start | bytes 1228808 | tf_op jit(solution)/shard_map/ppermute | solution.py:510
  64.7 14.5 %collective-permute-start.5 = (bf16[160,1280]{1,0:T(8,128)(2,1)S(1)}, bf16[160,1280]{1,0:T(8,128)(2,1)S(1)}, u32[]{:S(2)}, u32[]{:S(2)}) collective-permute-start(bf16[160,1280]{1,0:T(8,128)(2,1)S(1)} %collective-permute-done.2), channel_id=1, source_target_pairs={{0,8},{8,16},{16,24},{24,28},{28,20},{20,12},{12,4},{4,0},{1,9},{9... | collective-permute-start | bytes 1228808 | tf_op jit(solution)/shard_map/ppermute | solution.py:510
  77.9 29.9 %collective-permute-start.11 = (bf16[160,1280]{1,0:T(8,128)(2,1)S(1)}, bf16[160,1280]{1,0:T(8,128)(2,1)}, u32[]{:S(2)}, u32[]{:S(2)}) collective-permute-start(bf16[160,1280]{1,0:T(8,128)(2,1)S(1)} %collective-permute-done.10), channel_id=1, source_target_pairs={{8,0},{16,8},{24,16},{28,24},{20,28},{12,20},{4,12},{0,4},{9,1},{1... | collective-permute-start | bytes 1228808 | tf_op jit(solution)/shard_map/ppermute | solution.py:510
  79.2 57.9 %collective-permute-start.6 = (bf16[160,1280]{1,0:T(8,128)(2,1)S(1)}, bf16[160,1280]{1,0:T(8,128)(2,1)}, u32[]{:S(2)}, u32[]{:S(2)}) collective-permute-start(bf16[160,1280]{1,0:T(8,128)(2,1)S(1)} %collective-permute-done.5), channel_id=1, source_target_pairs={{0,8},{8,16},{16,24},{24,28},{28,20},{20,12},{12,4},{4,0},{1,9},{9... | collective-permute-start | bytes 1228808 | tf_op jit(solution)/shard_map/ppermute | solution.py:510
  107.8 35.0 %collective-permute-start.12 = (bf16[160,1280]{1,0:T(8,128)(2,1)}, bf16[160,1280]{1,0:T(8,128)(2,1)}, u32[]{:S(2)}, u32[]{:S(2)}) collective-permute-start(bf16[160,1280]{1,0:T(8,128)(2,1)} %collective-permute-done.11), channel_id=1, source_target_pairs={{8,0},{16,8},{24,16},{28,24},{20,28},{12,20},{4,12},{0,4},{9,1},{1... | collective-permute-start | bytes 1228808 | tf_op jit(solution)/shard_map/ppermute | solution.py:510
  137.2 19.1 %collective-permute-start.7 = (bf16[160,1280]{1,0:T(8,128)(2,1)}, bf16[160,1280]{1,0:T(8,128)(2,1)S(1)}, u32[]{:S(2)}, u32[]{:S(2)}) collective-permute-start(bf16[160,1280]{1,0:T(8,128)(2,1)} %collective-permute-done.6), channel_id=1, source_target_pairs={{0,8},{8,16},{16,24},{24,28},{28,20},{20,12},{12,4},{4,0},{1,9},{9... | collective-permute-start | bytes 1228808 | tf_op jit(solution)/shard_map/ppermute | solution.py:510
  142.8 27.7 %collective-permute-start.13 = (bf16[160,1280]{1,0:T(8,128)(2,1)}, bf16[160,1280]{1,0:T(8,128)(2,1)S(1)}, u32[]{:S(2)}, u32[]{:S(2)}) collective-permute-start(bf16[160,1280]{1,0:T(8,128)(2,1)} %collective-permute-done.12), channel_id=1, source_target_pairs={{8,0},{16,8},{24,16},{28,24},{20,28},{12,20},{4,12},{0,4},{9,1},{1... | collective-permute-start | bytes 1228808 | tf_op jit(solution)/shard_map/ppermute | solution.py:510
  156.3 27.2 %collective-permute-start.8 = (bf16[160,1280]{1,0:T(8,128)(2,1)S(1)}, bf16[160,1280]{1,0:T(8,128)(2,1)S(1)}, u32[]{:S(2)}, u32[]{:S(2)}) collective-permute-start(bf16[160,1280]{1,0:T(8,128)(2,1)S(1)} %collective-permute-done.7), channel_id=1, source_target_pairs={{0,8},{8,16},{16,24},{24,28},{28,20},{20,12},{12,4},{4,0},{1,9},{9... | collective-permute-start | bytes 1228808 | tf_op jit(solution)/shard_map/ppermute | solution.py:510
  183.6 33.0 %collective-permute-start.15 = (bf16[160,1280]{1,0:T(8,128)(2,1)S(1)}, bf16[160,1280]{1,0:T(8,128)(2,1)S(1)}, u32[]{:S(2)}, u32[]{:S(2)}) collective-permute-start(bf16[160,1280]{1,0:T(8,128)(2,1)S(1)} %get-tuple-element.260), channel_id=1, source_target_pairs={{8,0},{16,8},{24,16},{28,24},{20,28},{12,20},{4,12},{0,4},{9,1},{1... | collective-permute-start | bytes 1228808 | tf_op jit(solution)/shard_map/ppermute | solution.py:510
  198.6 22.5 %collective-permute-start.14 = (bf16[160,1280]{1,0:T(8,128)(2,1)S(1)}, bf16[160,1280]{1,0:T(8,128)(2,1)S(1)}, u32[]{:S(2)}, u32[]{:S(2)}) collective-permute-start(bf16[160,1280]{1,0:T(8,128)(2,1)S(1)} %get-tuple-element.261), channel_id=1, source_target_pairs={{0,8},{8,16},{16,24},{24,28},{28,20},{20,12},{12,4},{4,0},{1,9},{9... | collective-permute-start | bytes 1228808 | tf_op jit(solution)/shard_map/ppermute | solution.py:510
  216.6 24.4 %collective-permute-start.17 = (bf16[160,1280]{1,0:T(8,128)(2,1)S(1)}, bf16[160,1280]{1,0:T(8,128)(2,1)S(1)}, u32[]{:S(2)}, u32[]{:S(2)}) collective-permute-start(bf16[160,1280]{1,0:T(8,128)(2,1)S(1)} %collective-permute-done.15), channel_id=1, source_target_pairs={{8,0},{16,8},{24,16},{28,24},{20,28},{12,20},{4,12},{0,4},{9,1},{1... | collective-permute-start | bytes 1228808 | tf_op jit(solution)/shard_map/ppermute | solution.py:510
  221.1 21.8 %collective-permute-start.16 = (bf16[160,1280]{1,0:T(8,128)(2,1)S(1)}, bf16[160,1280]{1,0:T(8,128)(2,1)S(1)}, u32[]{:S(2)}, u32[]{:S(2)}) collective-permute-start(bf16[160,1280]{1,0:T(8,128)(2,1)S(1)} %collective-permute-done.14), channel_id=1, source_target_pairs={{0,8},{8,16},{16,24},{24,28},{28,20},{20,12},{12,4},{4,0},{1,9},{9... | collective-permute-start | bytes 1228808 | tf_op jit(solution)/shard_map/ppermute | solution.py:510
  240.9 13.2 %collective-permute-start.19 = (bf16[160,1280]{1,0:T(8,128)(2,1)S(1)}, bf16[160,1280]{1,0:T(8,128)(2,1)S(1)}, u32[]{:S(2)}, u32[]{:S(2)}) collective-permute-start(bf16[160,1280]{1,0:T(8,128)(2,1)S(1)} %collective-permute-done.17), channel_id=1, source_target_pairs={{8,0},{16,8},{24,16},{28,24},{20,28},{12,20},{4,12},{0,4},{9,1},{1... | collective-permute-start | bytes 1228808 | tf_op jit(solution)/shard_map/ppermute | solution.py:510
  349.6 14.2 %collective-permute-start.32 = (bf16[160,1280]{1,0:T(8,128)(2,1)S(1)}, bf16[160,1280]{1,0:T(8,128)(2,1)S(1)}, u32[]{:S(2)}, u32[]{:S(2)}) collective-permute-start(bf16[160,1280]{1,0:T(8,128)(2,1)S(1)} %get-tuple-element.249), channel_id=1, source_target_pairs={{8,0},{16,8},{24,16},{28,24},{20,28},{12,20},{4,12},{0,4},{9,1},{1... | collective-permute-start | bytes 1228808 | tf_op jit(solution)/shard_map/ppermute | solution.py:545
  350.5 13.4 %collective-permute-start.29 = (bf16[160,1280]{1,0:T(8,128)(2,1)S(1)}, bf16[160,1280]{1,0:T(8,128)(2,1)S(1)}, u32[]{:S(2)}, u32[]{:S(2)}) collective-permute-start(bf16[160,1280]{1,0:T(8,128)(2,1)S(1)} %get-tuple-element.250), channel_id=1, source_target_pairs={{0,8},{8,16},{16,24},{24,28},{28,20},{20,12},{12,4},{4,0},{1,9},{9... | collective-permute-start | bytes 1228808 | tf_op jit(solution)/shard_map/ppermute | solution.py:545
  361.7 36.1 %collective-permute-start.35 = (bf16[160,1280]{1,0:T(8,128)(2,1)S(1)}, bf16[160,1280]{1,0:T(8,128)(2,1)S(1)}, u32[]{:S(2)}, u32[]{:S(2)}) collective-permute-start(bf16[160,1280]{1,0:T(8,128)(2,1)S(1)} %get-tuple-element.243), channel_id=1, source_target_pairs={{8,0},{16,8},{24,16},{28,24},{20,28},{12,20},{4,12},{0,4},{9,1},{1... | collective-permute-start | bytes 1228808 | tf_op jit(solution)/shard_map/ppermute | solution.py:545
  362.4 12.4 %collective-permute-start.34 = (bf16[160,1280]{1,0:T(8,128)(2,1)S(1)}, bf16[160,1280]{1,0:T(8,128)(2,1)S(1)}, u32[]{:S(2)}, u32[]{:S(2)}) collective-permute-start(bf16[160,1280]{1,0:T(8,128)(2,1)S(1)} %get-tuple-element.244), channel_id=1, source_target_pairs={{0,8},{8,16},{16,24},{24,28},{28,20},{20,12},{12,4},{4,0},{1,9},{9... | collective-permute-start | bytes 1228808 | tf_op jit(solution)/shard_map/ppermute | solution.py:545
  364.9 28.4 %collective-permute-start.33 = (bf16[160,1280]{1,0:T(8,128)(2,1)}, bf16[160,1280]{1,0:T(8,128)(2,1)S(1)}, u32[]{:S(2)}, u32[]{:S(2)}) collective-permute-start(bf16[160,1280]{1,0:T(8,128)(2,1)} %get-tuple-element.247), channel_id=1, source_target_pairs={{8,0},{16,8},{24,16},{28,24},{20,28},{12,20},{4,12},{0,4},{9,1},{1... | collective-permute-start | bytes 1228808 | tf_op jit(solution)/shard_map/ppermute | solution.py:545
  365.6 27.8 %collective-permute-start.30 = (bf16[160,1280]{1,0:T(8,128)(2,1)}, bf16[160,1280]{1,0:T(8,128)(2,1)}, u32[]{:S(2)}, u32[]{:S(2)}) collective-permute-start(bf16[160,1280]{1,0:T(8,128)(2,1)} %get-tuple-element.248), channel_id=1, source_target_pairs={{0,8},{8,16},{16,24},{24,28},{28,20},{20,12},{12,4},{4,0},{1,9},{9... | collective-permute-start | bytes 1228808 | tf_op jit(solution)/shard_map/ppermute | solution.py:545
  374.9 22.9 %collective-permute-start.38 = (bf16[160,1280]{1,0:T(8,128)(2,1)S(1)}, bf16[160,1280]{1,0:T(8,128)(2,1)}, u32[]{:S(2)}, u32[]{:S(2)}) collective-permute-start(bf16[160,1280]{1,0:T(8,128)(2,1)S(1)} %add_convert_fusion.31), channel_id=1, source_target_pairs={{0,8},{8,16},{16,24},{24,28},{28,20},{20,12},{12,4},{4,0},{1,9},{9... | collective-permute-start | bytes 1228808 | tf_op jit(solution)/shard_map/ppermute | solution.py:545
  395.8 20.9 %collective-permute-start.37 = (bf16[160,1280]{1,0:T(8,128)(2,1)}, bf16[160,1280]{1,0:T(8,128)(2,1)S(1)}, u32[]{:S(2)}, u32[]{:S(2)}) collective-permute-start(bf16[160,1280]{1,0:T(8,128)(2,1)} %get-tuple-element.245), channel_id=1, source_target_pairs={{8,0},{16,8},{24,16},{28,24},{20,28},{12,20},{4,12},{0,4},{9,1},{1... | collective-permute-start | bytes 1228808 | tf_op jit(solution)/shard_map/ppermute | solution.py:545
  396.4 21.0 %collective-permute-start.36 = (bf16[160,1280]{1,0:T(8,128)(2,1)}, bf16[160,1280]{1,0:T(8,128)(2,1)}, u32[]{:S(2)}, u32[]{:S(2)}) collective-permute-start(bf16[160,1280]{1,0:T(8,128)(2,1)} %get-tuple-element.246), channel_id=1, source_target_pairs={{0,8},{8,16},{16,24},{24,28},{28,20},{20,12},{12,4},{4,0},{1,9},{9... | collective-permute-start | bytes 1228808 | tf_op jit(solution)/shard_map/ppermute | solution.py:545
  399.9 21.2 %collective-permute-start.44 = (bf16[160,1280]{1,0:T(8,128)(2,1)}, bf16[160,1280]{1,0:T(8,128)(2,1)S(1)}, u32[]{:S(2)}, u32[]{:S(2)}) collective-permute-start(bf16[160,1280]{1,0:T(8,128)(2,1)} %get-tuple-element.239), channel_id=1, source_target_pairs={{0,8},{8,16},{16,24},{24,28},{28,20},{20,12},{12,4},{4,0},{1,9},{9... | collective-permute-start | bytes 1228808 | tf_op jit(solution)/shard_map/ppermute | solution.py:545
  401.9 20.0 %collective-permute-start.39 = (bf16[160,1280]{1,0:T(8,128)(2,1)}, bf16[160,1280]{1,0:T(8,128)(2,1)}, u32[]{:S(2)}, u32[]{:S(2)}) collective-permute-start(bf16[160,1280]{1,0:T(8,128)(2,1)} %get-tuple-element.240), channel_id=1, source_target_pairs={{8,0},{16,8},{24,16},{28,24},{20,28},{12,20},{4,12},{0,4},{9,1},{1... | collective-permute-start | bytes 1228808 | tf_op jit(solution)/shard_map/ppermute | solution.py:545
  419.0 25.1 %collective-permute-start.42 = (bf16[160,1280]{1,0:T(8,128)(2,1)S(1)}, bf16[160,1280]{1,0:T(8,128)(2,1)S(1)}, u32[]{:S(2)}, u32[]{:S(2)}) collective-permute-start(bf16[160,1280]{1,0:T(8,128)(2,1)S(1)} %get-tuple-element.241), channel_id=1, source_target_pairs={{8,0},{16,8},{24,16},{28,24},{20,28},{12,20},{4,12},{0,4},{9,1},{1... | collective-permute-start | bytes 1228808 | tf_op jit(solution)/shard_map/ppermute | solution.py:545
  419.7 24.4 %collective-permute-start.40 = (bf16[160,1280]{1,0:T(8,128)(2,1)S(1)}, bf16[160,1280]{1,0:T(8,128)(2,1)}, u32[]{:S(2)}, u32[]{:S(2)}) collective-permute-start(bf16[160,1280]{1,0:T(8,128)(2,1)S(1)} %get-tuple-element.242), channel_id=1, source_target_pairs={{0,8},{8,16},{16,24},{24,28},{28,20},{20,12},{12,4},{4,0},{1,9},{9... | collective-permute-start | bytes 1228808 | tf_op jit(solution)/shard_map/ppermute | solution.py:545
  423.9 23.7 %collective-permute-start.45 = (bf16[160,1280]{1,0:T(8,128)(2,1)}, bf16[160,1280]{1,0:T(8,128)(2,1)S(1)}, u32[]{:S(2)}, u32[]{:S(2)}) collective-permute-start(bf16[160,1280]{1,0:T(8,128)(2,1)} %get-tuple-element.233), channel_id=1, source_target_pairs={{0,8},{8,16},{16,24},{24,28},{28,20},{20,12},{12,4},{4,0},{1,9},{9... | collective-permute-start | bytes 1228808 | tf_op jit(solution)/shard_map/ppermute | solution.py:545
  425.9 21.7 %collective-permute-start.46 = (bf16[160,1280]{1,0:T(8,128)(2,1)S(1)}, bf16[160,1280]{1,0:T(8,128)(2,1)S(1)}, u32[]{:S(2)}, u32[]{:S(2)}) collective-permute-start(bf16[160,1280]{1,0:T(8,128)(2,1)S(1)} %get-tuple-element.234), channel_id=1, source_target_pairs={{8,0},{16,8},{24,16},{28,24},{20,28},{12,20},{4,12},{0,4},{9,1},{1... | collective-permute-start | bytes 1228808 | tf_op jit(solution)/shard_map/ppermute | solution.py:545
  445.5 19.6 %collective-permute-start.43 = (bf16[160,1280]{1,0:T(8,128)(2,1)S(1)}, bf16[160,1280]{1,0:T(8,128)(2,1)S(1)}, u32[]{:S(2)}, u32[]{:S(2)}) collective-permute-start(bf16[160,1280]{1,0:T(8,128)(2,1)S(1)} %get-tuple-element.237), channel_id=1, source_target_pairs={{8,0},{16,8},{24,16},{28,24},{20,28},{12,20},{4,12},{0,4},{9,1},{1... | collective-permute-start | bytes 1228808 | tf_op jit(solution)/shard_map/ppermute | solution.py:545
  446.2 20.7 %collective-permute-start.41 = (bf16[160,1280]{1,0:T(8,128)(2,1)S(1)}, bf16[160,1280]{1,0:T(8,128)(2,1)S(1)}, u32[]{:S(2)}, u32[]{:S(2)}) collective-permute-start(bf16[160,1280]{1,0:T(8,128)(2,1)S(1)} %get-tuple-element.238), channel_id=1, source_target_pairs={{0,8},{8,16},{16,24},{24,28},{28,20},{20,12},{12,4},{4,0},{1,9},{9... | collective-permute-start | bytes 1228808 | tf_op jit(solution)/shard_map/ppermute | solution.py:545
  448.9 20.9 %collective-permute-start.47 = (bf16[160,1280]{1,0:T(8,128)(2,1)S(1)}, bf16[160,1280]{1,0:T(8,128)(2,1)S(1)}, u32[]{:S(2)}, u32[]{:S(2)}) collective-permute-start(bf16[160,1280]{1,0:T(8,128)(2,1)S(1)} %get-tuple-element.231), channel_id=1, source_target_pairs={{8,0},{16,8},{24,16},{28,24},{20,28},{12,20},{4,12},{0,4},{9,1},{1... | collective-permute-start | bytes 1228808 | tf_op jit(solution)/shard_map/ppermute | solution.py:545
  449.6 21.6 %collective-permute-start.52 = (bf16[160,1280]{1,0:T(8,128)(2,1)S(1)}, bf16[160,1280]{1,0:T(8,128)(2,1)S(1)}, u32[]{:S(2)}, u32[]{:S(2)}) collective-permute-start(bf16[160,1280]{1,0:T(8,128)(2,1)S(1)} %get-tuple-element.232), channel_id=1, source_target_pairs={{0,8},{8,16},{16,24},{24,28},{28,20},{20,12},{12,4},{4,0},{1,9},{9... | collective-permute-start | bytes 1228808 | tf_op jit(solution)/shard_map/ppermute | solution.py:545
  464.5 35.2 %collective-permute-start.49 = (bf16[160,1280]{1,0:T(8,128)(2,1)}, bf16[160,1280]{1,0:T(8,128)(2,1)}, u32[]{:S(2)}, u32[]{:S(2)}) collective-permute-start(bf16[160,1280]{1,0:T(8,128)(2,1)} %get-tuple-element.229), channel_id=1, source_target_pairs={{8,0},{16,8},{24,16},{28,24},{20,28},{12,20},{4,12},{0,4},{9,1},{1... | collective-permute-start | bytes 1228808 | tf_op jit(solution)/shard_map/ppermute | solution.py:545
  465.1 23.7 %collective-permute-start.48 = (bf16[160,1280]{1,0:T(8,128)(2,1)}, bf16[160,1280]{1,0:T(8,128)(2,1)}, u32[]{:S(2)}, u32[]{:S(2)}) collective-permute-start(bf16[160,1280]{1,0:T(8,128)(2,1)} %get-tuple-element.230), channel_id=1, source_target_pairs={{0,8},{8,16},{16,24},{24,28},{28,20},{20,12},{12,4},{4,0},{1,9},{9... | collective-permute-start | bytes 1228808 | tf_op jit(solution)/shard_map/ppermute | solution.py:545
  469.2 60.3 %collective-permute-start.51 = (bf16[160,1280]{1,0:T(8,128)(2,1)}, bf16[160,1280]{1,0:T(8,128)(2,1)S(1)}, u32[]{:S(2)}, u32[]{:S(2)}) collective-permute-start(bf16[160,1280]{1,0:T(8,128)(2,1)} %get-tuple-element.235), channel_id=1, source_target_pairs={{8,0},{16,8},{24,16},{28,24},{20,28},{12,20},{4,12},{0,4},{9,1},{1... | collective-permute-start | bytes 1228808 | tf_op jit(solution)/shard_map/ppermute | solution.py:545
  469.8 59.7 %collective-permute-start.50 = (bf16[160,1280]{1,0:T(8,128)(2,1)}, bf16[160,1280]{1,0:T(8,128)(2,1)}, u32[]{:S(2)}, u32[]{:S(2)}) collective-permute-start(bf16[160,1280]{1,0:T(8,128)(2,1)} %get-tuple-element.236), channel_id=1, source_target_pairs={{0,8},{8,16},{16,24},{24,28},{28,20},{20,12},{12,4},{4,0},{1,9},{9... | collective-permute-start | bytes 1228808 | tf_op jit(solution)/shard_map/ppermute | solution.py:545
  473.5 51.2 %collective-permute-start.53 = (bf16[160,1280]{1,0:T(8,128)(2,1)}, bf16[160,1280]{1,0:T(8,128)(2,1)}, u32[]{:S(2)}, u32[]{:S(2)}) collective-permute-start(bf16[160,1280]{1,0:T(8,128)(2,1)} %get-tuple-element.226), channel_id=1, source_target_pairs={{8,0},{16,8},{24,16},{28,24},{20,28},{12,20},{4,12},{0,4},{9,1},{1... | collective-permute-start | bytes 1228808 | tf_op jit(solution)/shard_map/ppermute | solution.py:545
  490.8 17.2 %collective-permute-start.54 = (bf16[160,1280]{1,0:T(8,128)(2,1)}, bf16[160,1280]{1,0:T(8,128)(2,1)}, u32[]{:S(2)}, u32[]{:S(2)}) collective-permute-start(bf16[160,1280]{1,0:T(8,128)(2,1)} %add_convert_fusion.17), channel_id=1, source_target_pairs={{0,8},{8,16},{16,24},{24,28},{28,20},{20,12},{12,4},{4,0},{1,9},{9... | collective-permute-start | bytes 1228808 | tf_op jit(solution)/shard_map/ppermute | solution.py:545
  499.7 25.0 %collective-permute-start.63 = (bf16[160,1280]{1,0:T(8,128)(2,1)S(1)}, bf16[160,1280]{1,0:T(8,128)(2,1)S(1)}, u32[]{:S(2)}, u32[]{:S(2)}) collective-permute-start(bf16[160,1280]{1,0:T(8,128)(2,1)S(1)} %copy-done.18), channel_id=1, source_target_pairs={{0,8},{8,16},{16,24},{24,28},{28,20},{20,12},{12,4},{4,0},{1,9},{9... | collective-permute-start | bytes 1228808 | tf_op jit(solution)/shard_map/ppermute | solution.py:545
  510.5 54.9 %collective-permute-start.55 = (bf16[160,1280]{1,0:T(8,128)(2,1)}, bf16[160,1280]{1,0:T(8,128)(2,1)}, u32[]{:S(2)}, u32[]{:S(2)}) collective-permute-start(bf16[160,1280]{1,0:T(8,128)(2,1)} %get-tuple-element.224), channel_id=1, source_target_pairs={{8,0},{16,8},{24,16},{28,24},{20,28},{12,20},{4,12},{0,4},{9,1},{1... | collective-permute-start | bytes 1228808 | tf_op jit(solution)/shard_map/ppermute | solution.py:545
  527.0 65.6 %collective-permute-start.64 = (bf16[160,1280]{1,0:T(8,128)(2,1)}, bf16[160,1280]{1,0:T(8,128)(2,1)}, u32[]{:S(2)}, u32[]{:S(2)}) collective-permute-start(bf16[160,1280]{1,0:T(8,128)(2,1)} %get-tuple-element.221), channel_id=1, source_target_pairs={{0,8},{8,16},{16,24},{24,28},{28,20},{20,12},{12,4},{4,0},{1,9},{9... | collective-permute-start | bytes 1228808 | tf_op jit(solution)/shard_map/ppermute | solution.py:545
  529.5 65.2 %collective-permute-start.65 = (bf16[160,1280]{1,0:T(8,128)(2,1)}, bf16[160,1280]{1,0:T(8,128)(2,1)}, u32[]{:S(2)}, u32[]{:S(2)}) collective-permute-start(bf16[160,1280]{1,0:T(8,128)(2,1)} %get-tuple-element.222), channel_id=1, source_target_pairs={{8,0},{16,8},{24,16},{28,24},{20,28},{12,20},{4,12},{0,4},{9,1},{1... | collective-permute-start | bytes 1228808 | tf_op jit(solution)/shard_map/ppermute | solution.py:545
  532.1 33.2 %collective-permute-start.67 = (bf16[160,1280]{1,0:T(8,128)(2,1)}, bf16[160,1280]{1,0:T(8,128)(2,1)}, u32[]{:S(2)}, u32[]{:S(2)}) collective-permute-start(bf16[160,1280]{1,0:T(8,128)(2,1)} %get-tuple-element.223), channel_id=1, source_target_pairs={{0,8},{8,16},{16,24},{24,28},{28,20},{20,12},{12,4},{4,0},{1,9},{9... | collective-permute-start | bytes 1228808 | tf_op jit(solution)/shard_map/ppermute | solution.py:545
  579.9 12.7 %collective-permute-start.77 = (f32[9020]{0:T(1024)S(1)}, f32[9020]{0:T(1024)S(1)}, u32[]{:S(2)}, u32[]{:S(2)}) collective-permute-start(f32[9020]{0:T(1024)S(1)} %copy-done.22), channel_id=1, source_target_pairs={{0,4},{4,0},{8,12},{12,8},{16,20},{20,16},{24,28},{28,24},{1,5},{5... | collective-permute-start | bytes 108248 | tf_op jit(solution)/shard_map/ppermute | solution.py:583
  590.6 61.0 %collective-permute-start.58 = (bf16[2,640,1024]{1,2,0:T(8,128)(2,1)}, bf16[2,640,1024]{1,2,0:T(8,128)(2,1)}, u32[]{:S(2)}, u32[]{:S(2)}) collective-permute-start(bf16[2,640,1024]{1,2,0:T(8,128)(2,1)} %bitcast.108), channel_id=1, source_target_pairs={{0,1},{1,0},{2,3},{3,2},{4,5},{5,4},{6,7},{7,6},{8,9},{9,8},{10,11... | collective-permute-start | bytes 7864328 | tf_op jit(solution)/shard_map/ppermute | solution.py:573
  590.6 29.9 %collective-permute-start.72 = (bf16[160,1280]{1,0:T(8,128)(2,1)}, bf16[160,1280]{1,0:T(8,128)(2,1)}, u32[]{:S(2)}, u32[]{:S(2)}) collective-permute-start(bf16[160,1280]{1,0:T(8,128)(2,1)} %get-tuple-element.218), channel_id=1, source_target_pairs={{8,0},{16,8},{24,16},{28,24},{20,28},{12,20},{4,12},{0,4},{9,1},{1... | collective-permute-start | bytes 1228808 | tf_op jit(solution)/shard_map/ppermute | solution.py:545
  592.6 27.9 %collective-permute-start.68 = (bf16[160,1280]{1,0:T(8,128)(2,1)}, bf16[160,1280]{1,0:T(8,128)(2,1)}, u32[]{:S(2)}, u32[]{:S(2)}) collective-permute-start(bf16[160,1280]{1,0:T(8,128)(2,1)} %get-tuple-element.217), channel_id=1, source_target_pairs={{0,8},{8,16},{16,24},{24,28},{28,20},{20,12},{12,4},{4,0},{1,9},{9... | collective-permute-start | bytes 1228808 | tf_op jit(solution)/shard_map/ppermute | solution.py:545
  597.0 41.4 %collective-permute-start.66 = (bf16[160,1280]{1,0:T(8,128)(2,1)}, bf16[160,1280]{1,0:T(8,128)(2,1)}, u32[]{:S(2)}, u32[]{:S(2)}) collective-permute-start(bf16[160,1280]{1,0:T(8,128)(2,1)} %get-tuple-element.220), channel_id=1, source_target_pairs={{8,0},{16,8},{24,16},{28,24},{20,28},{12,20},{4,12},{0,4},{9,1},{1... | collective-permute-start | bytes 1228808 | tf_op jit(solution)/shard_map/ppermute | solution.py:545
  603.9 15.8 %collective-permute-start.79 = (f32[9020]{0:T(1024)S(1)}, f32[9020]{0:T(1024)S(1)}, u32[]{:S(2)}, u32[]{:S(2)}) collective-permute-start(f32[9020]{0:T(1024)S(1)} %add.911), channel_id=1, source_target_pairs={{0,16},{4,20},{8,24},{12,28},{16,0},{20,4},{24,8},{28,12},{1,17},{... | collective-permute-start | bytes 108248 | tf_op jit(solution)/shard_map/ppermute | solution.py:583
  619.8 48.1 %collective-permute-start.56 = (bf16[2,640,1024]{1,2,0:T(8,128)(2,1)}, bf16[2,640,1024]{1,2,0:T(8,128)(2,1)}, u32[]{:S(2)}, u32[]{:S(2)}) collective-permute-start(bf16[2,640,1024]{1,2,0:T(8,128)(2,1)} %bitcast.109), channel_id=1, source_target_pairs={{0,1},{1,0},{2,3},{3,2},{4,5},{5,4},{6,7},{7,6},{8,9},{9,8},{10,11... | collective-permute-start | bytes 7864328 | tf_op jit(solution)/shard_map/ppermute | solution.py:573
  656.6 32.0 %collective-permute-start.59 = (bf16[1,640,1024]{1,2,0:T(8,128)(2,1)}, bf16[1,640,1024]{1,2,0:T(8,128)(2,1)}, u32[]{:S(2)}, u32[]{:S(2)}) collective-permute-start(bf16[1,640,1024]{1,2,0:T(8,128)(2,1)} %constant_dynamic-slice_fusion), channel_id=1, source_target_pairs={{0,2},{1,3},{2,0},{3,1},{4,6},{5,7},{6,4},{7,5},{8,10},{9,11},{10,... | collective-permute-start | bytes 3932168 | tf_op jit(solution)/shard_map/ppermute | solution.py:573
  663.0 30.5 %collective-permute-start.76 = (bf16[160,1280]{1,0:T(8,128)(2,1)}, bf16[160,1280]{1,0:T(8,128)(2,1)}, u32[]{:S(2)}, u32[]{:S(2)}) collective-permute-start(bf16[160,1280]{1,0:T(8,128)(2,1)} %get-tuple-element.210), channel_id=1, source_target_pairs={{8,0},{16,8},{24,16},{28,24},{20,28},{12,20},{4,12},{0,4},{9,1},{1... | collective-permute-start | bytes 1228808 | tf_op jit(solution)/shard_map/ppermute | solution.py:545
  671.7 59.6 %collective-permute-start.57 = (bf16[1,640,1024]{1,2,0:T(8,128)(2,1)}, bf16[1,640,1024]{1,2,0:T(8,128)(2,1)}, u32[]{:S(2)}, u32[]{:S(2)}) collective-permute-start(bf16[1,640,1024]{1,2,0:T(8,128)(2,1)} %constant_dynamic-slice_fusion.3), channel_id=1, source_target_pairs={{0,2},{1,3},{2,0},{3,1},{4,6},{5,7},{6,4},{7,5},{8,10},{9,11},{10,... | collective-permute-start | bytes 3932168 | tf_op jit(solution)/shard_map/ppermute | solution.py:573
  671.8 49.3 %collective-permute-start.81 = (f32[325,256]{1,0:T(8,128)S(1)}, f32[325,256]{1,0:T(8,128)S(1)}, u32[]{:S(2)}, u32[]{:S(2)}) collective-permute-start(f32[325,256]{1,0:T(8,128)S(1)} %fusion.38), channel_id=1, source_target_pairs={{0,2},{1,3},{2,0},{3,1},{4,6},{5,7},{6,4},{7,5},{8,10},{9,11},{10,... | collective-permute-start | bytes 998408 | tf_op jit(solution)/shard_map/ppermute | solution.py:583
  696.2 26.8 %collective-permute-start.61 = (f32[640]{0:T(1024)S(1)}, f32[640]{0:T(1024)S(1)}, u32[]{:S(2)}, u32[]{:S(2)}) collective-permute-start(f32[640]{0:T(1024)S(1)} %add.893), channel_id=1, source_target_pairs={{0,8},{4,12},{8,0},{12,4},{16,24},{20,28},{24,16},{28,20},{1,9},{5... | collective-permute-start | bytes 7688 | tf_op jit(solution)/shard_map/ppermute | solution.py:583
  (62 other events, 866.1 us)
Sparse Core Ops, SparseCore 0:
  10.9 53.8 all-gather.8
  66.9 136.9 all-gather.4
  205.4 45.3 all-gather.6
  488.2 74.7 reduce-scatter.1

commit v6 on v5

--- a/solution.py
+++ b/solution.py
@@ -506,17 +506,15 @@
     def step(self, times=1):
         for _ in range(min(times, self.count - 1 - self.taken)):
             self.taken += 1
-            self.held = tuple(
+            arrived = tuple(
                 lax.ppermute(held, "gx", move) for held, move in zip(self.held, self.moves)
             )
+            self.held, self.full = lax.optimization_barrier((arrived, self.full))
             for piece, sign, offset in zip(self.held, (-1, 1), (0, self.half)):
                 owner = ring_index(self.place + sign * self.taken, self.count)
                 start = owner * self.rows + offset
                 self.full = lax.dynamic_update_slice(self.full, piece, (start, 0))
         return self.held
-
-    def wait_for(self, *others):
-        self.held = (after(self.held[0], *others), self.held[1])
 
     def finish(self):
         self.step(self.count)
@@ -560,22 +558,6 @@
     return [(k, k ^ bit) for k in range(count)]
 
 
-def halving_sum(partial, axis):
-    count = lax.axis_size(axis)
-    me = lax.axis_index(axis)
-    held = partial.reshape(count, partial.shape[0] // count, partial.shape[1])
-    bit = 1
-    while bit < count:
-        pairs = held.reshape(held.shape[0] // 2, 2, *held.shape[1:])
-        mine = (me // bit) % 2
-        kept = lax.dynamic_index_in_dim(pairs, mine, 1, keepdims=False)
-        given = lax.dynamic_index_in_dim(pairs, 1 - mine, 1, keepdims=False)
-        got = lax.ppermute(given, axis, flips(count, bit))
-        held = (kept.astype(wide) + got.astype(wide)).astype(partial.dtype)
-        bit *= 2
-    return held[0]
-
-
 def butterfly_sum(v, axis):
     count = lax.axis_size(axis)
     bit = 1
@@ -593,8 +575,15 @@
     return with_layout_constraint(v, Layout((0, 1)))
 
 
-def after(value, *others):
-    return lax.optimization_barrier((value,) + others)[0]
+def together(*values):
+    return lax.optimization_barrier(values)
+
+
+def tie(value, *rings):
+    value, held = lax.optimization_barrier((value, [ring.held for ring in rings]))
+    for ring, pieces in zip(rings, held):
+        ring.held = tuple(pieces)
+    return value
 
 
 def on_device(
@@ -623,18 +612,22 @@
 
     state_step_weight = jnp.concatenate([state_weight, step_weight], 1)
     full_state = lax.all_gather(state_step_weight, "gx", axis=0, tiled=True)
-    full_gate = lax.all_gather(gate_weight, "gx", axis=0, tiled=True)
     upstream = lax.all_gather(cotangent, "gy", axis=1, tiled=True)
     value_gather = RingGather(value_weight)
     value_gather.step()
-
-    tokens = after(layer_input, *value_gather.step()).astype(wide)
+    tokens = tie(layer_input, value_gather).astype(wide)
     scale_in = lax.rsqrt(jnp.mean(tokens * tokens, axis=1, keepdims=True) + epsilon)
     normed = (tokens * scale_in * norm_gain).astype(low)
     value_gather.step()
-    value_gather.wait_for(normed)
-    value_gather.step()
-
+    normed = tie(normed, value_gather)
+    value_gather.step(value_gather.count)
+    gate_shard = tie(gate_weight, value_gather)
+    full_gate = lax.all_gather(gate_shard, "gx", axis=0, tiled=True)
+    full_value = value_gather.finish()
+
+    out_gather = RingGather(tie(out_weight.T, value_gather))
+    out_gather.step()
+    normed = tie(normed, out_gather)
     state_step = dot(normed, full_state)
     mixer = Mixer(
         state_step[:, :state_cols],
@@ -645,15 +638,16 @@
         decay_log,
         segment_ids,
     )
-    value_gather.step()
-    value_gather.wait_for(mixer.g)
-    full_value = value_gather.finish()
-    out_gather = RingGather(after(out_weight.T, *value_gather.held))
+    out_gather.step()
+    normed, mixer.g = together(normed, mixer.g)
+    normed = tie(normed, out_gather)
     value_in = dot(normed, full_value)
-    value_in = after(value_in, *out_gather.step())
+    out_gather.step()
+    value_in = tie(value_in, out_gather)
     mixed = mixer.forward(value_in, conv_value, conv_value_bias, skip_scale)
-    out_gather.step(2)
-    out_gather.wait_for(mixed)
+    out_gather.step()
+    mixed = mixer.mixed = tie(mixer.mixed, out_gather)
+    mixed = mixed[:, : mixer.inner]
     full_out = out_gather.finish()
     full_value_state = jnp.concatenate([full_value, full_state], 1)
     gate_in = dot(normed, full_gate)
@@ -675,51 +669,63 @@
     scaled_out = (gated * gated_gain * scale_out).astype(low)
     out_ring = RingSum(row_major(contract_rows(upstream, scaled_out).astype(low)))
 
-    grad_scaled = scale_out * after(up_back, *out_ring.held)
+    scaled = tie(scaled, out_ring)
+    product_part = contract_cols(full_out, scaled)
+    product_part = row_major((product_part * scale_out[:, 0]).astype(low))
+    product = lax.psum_scatter(product_part, "gy", scatter_dimension=0, tiled=True)
+
+    out_ring.step()
+    up_back, product_part = together(up_back, product_part)
+    grad_scaled = scale_out * tie(up_back, out_ring)
     grad_gated = grad_scaled * gated_gain - grad_scale * scale_out**3 * gated / INNER
     gate_gain_part = jnp.sum(grad_scaled * gated, axis=0)
     grad_gate_in = (
         grad_gated * mixed * gate_open * (1.0 + gate_in * (1.0 - gate_open))
     ).astype(low)
     grad_mixed = grad_gated * gate_act
-    gate_partial = contract_rows(after(normed, *out_ring.step()), grad_gate_in)
-    gate_ring = RingSum(row_major(gate_partial.astype(low)))
-
-    first = (mixer.pairs + 2) // 3
-    second = (first + mixer.pairs + 1) // 2
-    part = mixer.backward_part(after(grad_mixed, *out_ring.step(), *gate_ring.held), 0, first)
-    grad_mixed = after(grad_mixed, *out_ring.step(), *gate_ring.step(), part[0])
-    part = mixer.backward_part(grad_mixed, first, second, part)
-    grad_mixed = after(grad_mixed, *out_ring.step(), *gate_ring.step(), part[0])
-    value_grad, value_sums, *totals = mixer.backward_part(grad_mixed, second, mixer.pairs, part)
+    out_ring.step()
+    normed = tie(normed, out_ring)
+    gate_ring = RingSum(row_major(contract_rows(normed, grad_gate_in).astype(low)))
+
+    half = (mixer.pairs + 1) // 2
+    out_ring.step()
+    grad_mixed = tie(grad_mixed, out_ring, gate_ring)
+    part = mixer.backward_part(grad_mixed, 0, half)
+    out_ring.step()
+    gate_ring.step()
+    grad_mixed = tie(grad_mixed, out_ring, gate_ring)
+    value_grad, value_sums, *totals = mixer.backward_part(grad_mixed, half, mixer.pairs, part)
     grad_value_in = value_grad[:, : gate_weight.shape[1]]
-    value_partial = contract_rows(
-        after(normed, *out_ring.step(), *gate_ring.step()), grad_value_in
-    )
-    value_ring = RingSum(row_major(value_partial.astype(low)))
-    ends = mixer.backward_end(
-        after(totals[0], *out_ring.step(), *gate_ring.step(), *value_ring.held), *totals[1:]
-    )
+    out_ring.step()
+    gate_ring.step()
+    normed = tie(normed, out_ring, gate_ring)
+    value_ring = RingSum(row_major(contract_rows(normed, grad_value_in).astype(low)))
+    out_ring.step()
+    gate_ring.step()
+    totals[0] = tie(totals[0], out_ring, gate_ring, value_ring)
+    ends = mixer.backward_end(*totals)
     pulled = mixer.gradients(value_grad, value_sums, *ends)
     grad_state_in = jnp.concatenate([pulled[1], pulled[2]], 1)
     state_partial = row_major(contract_rows(normed, grad_state_in).astype(low))
     grad_state_step = scatter_rows(state_partial).astype(wide)
 
-    held = value_ring.step()
-    grad_normed_part = contract_cols(full_gate, after(grad_gate_in, state_partial, *held))
+    value_ring.step()
+    grad_gate_in = tie(grad_gate_in, value_ring)
+    grad_normed_part = contract_cols(full_gate, grad_gate_in)
     grad_value_state_in = jnp.concatenate([grad_value_in, grad_state_in], 1)
-    held = out_ring.step() + gate_ring.step()
-    grad_value_state_in = after(grad_value_state_in, *held)
+    out_ring.step()
+    gate_ring.step()
+    grad_value_state_in = tie(grad_value_state_in, out_ring, gate_ring)
+    grad_value_state_in, product = together(grad_value_state_in, product)
     grad_normed_part = grad_normed_part + contract_cols(full_value_state, grad_value_state_in)
     grad_normed_part = row_major(grad_normed_part.astype(low))
-    held = value_ring.step()
-    product_part = contract_cols(full_out, after(scaled, grad_normed_part, *held))
-    product_part = row_major((product_part * scale_out[:, 0]).astype(low))
     grad_out = out_ring.finish()
     grad_gate = gate_ring.finish()
     grad_value = value_ring.finish()
 
-    grad_normed = halving_sum(grad_normed_part, "gy").T.astype(wide)
+    grad_normed = lax.psum_scatter(
+        grad_normed_part, "gy", scatter_dimension=0, tiled=True
+    ).T.astype(wide)
     token_cols = lax.dynamic_slice_in_dim(layer_input, col_start, col_width, 1).astype(wide)
     gain_cols = lax.dynamic_slice_in_dim(norm_gain, col_start, col_width, 0)
     weighted = grad_normed * gain_cols
@@ -730,12 +736,11 @@
         - token_cols * scale_in**3 * inner_dot / model_width
     )
     grad_norm_gain = butterfly_sum(jnp.sum(grad_normed * token_cols * scale_in, axis=0), "gx")
-    product = halving_sum(product_part, "gy").T
-    layer_output = (token_cols + product.astype(wide)).astype(low)
+    layer_output = (token_cols + product.T.astype(wide)).astype(low)
 
     small = (gate_gain_part,) + pulled[3:]
     packed = jnp.concatenate([v.reshape(-1) for v in small])
-    packed = butterfly_sum(after(packed, product_part), "gx")
+    packed = butterfly_sum(packed, "gx")
     sums, start = [], 0
     for v in small:
         sums.append(packed[start : start + v.size].reshape(v.shape))

time: 749 us -> 659 us (0.88)
  waiting for transfers between devices: 207 us -> 171 us
  local copies, waits for them, and re-layouts: 102 us -> 71.2 us
  starting transfers between devices: 114 us -> 92.4 us
    ppermute x28, starting transfers between devices: 56.7 us -> 30.6 us  [step(): lax.ppermute(held, 'gx', move)]
    ppermute x8, waiting for transfers between devices: 28.3 us -> 4.52 us  [butterfly_sum(): v = v + lax.ppermute(v, axis, flips(count, bit))]
    dynamic_slice x4 -> x1, local copies, waits for them, and re-layouts: 17.3 us -> 1.43 us  [on_device(): lax.dynamic_slice_in_dim(layer_input, col_start, col_width, 1).astype(wide)]
    ppermute x4 -> x0, waiting for transfers between devices: 14.8 us -> none  [halving_sum(): got = lax.ppermute(given, axis, flips(count, bit))]
    mul x1 -> x0, other arithmetic: 9.9 us -> none  [on_device(): grad_mixed = grad_gated * gate_act]
    convert_element_type x2 -> x1, other arithmetic: 4.89 us -> 14.6 us  [on_device(): grad_gate_in = (grad_gated * mixed * gate_open * (1.0 + gate_in * (1.0 -...]
    ppermute x28, waiting for transfers between devices: 113 us -> 123 us  [step(): lax.ppermute(held, 'gx', move)]
    pallas_call x6 -> x5, Pallas kernels: 88.8 us -> 83.4 us  [call(): pl.pallas_call(kernel, out_shape=shapes, scratch_shapes=list(scratch), co...]
  transfers between devices with their start and end apart: 86 -> 84, of which waited for: 28 -> 37; matrix products, arithmetic and copies ran while one was open for 36% -> 38% of each run, Pallas kernels for 12% -> 13%
where the time goes in v6:
time: 659 us; the launch traced here: 651 us
  waiting for transfers between devices  171 us (26%)
  matrix products  123 us (19%)
  starting transfers between devices  92.4 us (14%)
  Pallas kernels  83.4 us (13%)
  other arithmetic  82.9 us (13%)
  local copies, waits for them, and re-layouts  71.2 us (11%)
  between operations  15.8 us (2%)
  blocking collectives  11.4 us (2%)
    ppermute x28, waiting for transfers between devices, step(): lax.ppermute(held, 'gx', move)  123 us
    pallas_call x5, Pallas kernels, call(): pl.pallas_call(kernel, out_shape=shapes, scratch_shapes=list(scratch), co...  83.4 us
    ppermute x42, starting transfers between devices, step(): lax.ppermute(held, 'gx', move).astype(wide)  51 us
    dot_general x4, matrix products, dot(): jnp.dot(left, right, preferred_element_type=wide, precision=precision)  45.8 us
    ppermute x42, waiting for transfers between devices, step(): lax.ppermute(held, 'gx', move).astype(wide)  43.3 us
    dot_general x3, matrix products, contract_cols(): lax.dot_general(left, right, (((1,), (1,)), ((), ())), preferred_element_...  39.6 us
    dot_general x4, matrix products, contract_rows(): lax.dot_general(left, right, (((0,), (0,)), ((), ())), preferred_element_...  37.5 us
    convert_element_type x18, other arithmetic, step(): up, down = (up.astype(low), down.astype(low))  30.7 us
  transfers between devices with their start and end apart: 84, of which 37 were waited for; matrix products, arithmetic and copies ran while one was open for 38% of the time, Pallas kernels for 13%

profile of v6, /device:TPU:0, one launch (start us, length us, event | category | flops | bytes accessed | tf_op | source)
XLA Modules:
  0.0 650.9 jit_solution(210813567809907902)
XLA Ops:
  8.5 3.1 collective-permute-start
  14.6 3.6 broadcast.80.clone
  26.3 3.6 fusion.2
  32.5 6.1 collective-permute-done.2
  44.6 13.7 %collective-permute-done.8 = bf16[160,1280]{1,0:T(8,128)(2,1)S(1)} collective-permute-done((bf16[160,1280]{1,0:T(8,128)(2,1)S(1)}, bf16[160,1280]{1,0:T(8,128)(2,1)S(1)}, u32[]{:S(2)}, u32[]{:S(2)}) %collective-permute-start.8) | collective-permute-done | bytes 409632 | tf_op jit(solution)/shard_map/ppermute | solution.py:510
  58.3 8.5 %collective-permute-done.9 = bf16[160,1280]{1,0:T(8,128)(2,1)S(1)} collective-permute-done((bf16[160,1280]{1,0:T(8,128)(2,1)S(1)}, bf16[160,1280]{1,0:T(8,128)(2,1)S(1)}, u32[]{:S(2)}, u32[]{:S(2)}) %collective-permute-start.9) | collective-permute-done | bytes 409632 | tf_op jit(solution)/shard_map/ppermute | solution.py:510
  70.4 6.8 %collective-permute-done.10 = bf16[160,1280]{1,0:T(8,128)(2,1)S(1)} collective-permute-done((bf16[160,1280]{1,0:T(8,128)(2,1)S(1)}, bf16[160,1280]{1,0:T(8,128)(2,1)S(1)}, u32[]{:S(2)}, u32[]{:S(2)}) %collective-permute-start.10) | collective-permute-done | bytes 409632 | tf_op jit(solution)/shard_map/ppermute | solution.py:510
  81.0 8.0 %collective-permute-done.12 = bf16[160,1280]{1,0:T(8,128)(2,1)S(1)} collective-permute-done((bf16[160,1280]{1,0:T(8,128)(2,1)S(1)}, bf16[160,1280]{1,0:T(8,128)(2,1)S(1)}, u32[]{:S(2)}, u32[]{:S(2)}) %collective-permute-start.12) | collective-permute-done | bytes 409632 | tf_op jit(solution)/shard_map/ppermute | solution.py:510
  92.9 8.3 %collective-permute-done.14 = bf16[160,1280]{1,0:T(8,128)(2,1)S(1)} collective-permute-done((bf16[160,1280]{1,0:T(8,128)(2,1)S(1)}, bf16[160,1280]{1,0:T(8,128)(2,1)S(1)}, u32[]{:S(2)}, u32[]{:S(2)}) %collective-permute-start.14) | collective-permute-done | bytes 409632 | tf_op jit(solution)/shard_map/ppermute | solution.py:510
  106.6 8.4 %collective-permute-done.16 = bf16[160,1280]{1,0:T(8,128)(2,1)S(1)} collective-permute-done((bf16[160,1280]{1,0:T(8,128)(2,1)S(1)}, bf16[160,1280]{1,0:T(8,128)(2,1)S(1)}, u32[]{:S(2)}, u32[]{:S(2)}) %collective-permute-start.16) | collective-permute-done | bytes 409632 | tf_op jit(solution)/shard_map/ppermute | solution.py:510
  123.0 3.1 broadcast.80.clone.1
  129.3 2.5 collective-permute-start.7
  133.3 10.2 %collective-permute-done.6 = bf16[160,1280]{1,0:T(8,128)(2,1)S(1)} collective-permute-done((bf16[160,1280]{1,0:T(8,128)(2,1)S(1)}, bf16[160,1280]{1,0:T(8,128)(2,1)S(1)}, u32[]{:S(2)}, u32[]{:S(2)}) %collective-permute-start.6) | collective-permute-done | bytes 409632 | tf_op jit(solution)/shard_map/ppermute | solution.py:510
  143.5 11.5 %collective-permute-done.7 = bf16[160,1280]{1,0:T(8,128)(2,1)S(1)} collective-permute-done((bf16[160,1280]{1,0:T(8,128)(2,1)S(1)}, bf16[160,1280]{1,0:T(8,128)(2,1)S(1)}, u32[]{:S(2)}, u32[]{:S(2)}) %collective-permute-start.7) | collective-permute-done | bytes 409632 | tf_op jit(solution)/shard_map/ppermute | solution.py:510
  159.6 5.3 fusion.38
  171.2 17.5 %shard_map.288 = (bf16[1024,128]{1,0:T(8,128)(2,1)}, bf16[1024,128]{1,0:T(8,128)(2,1)}, bf16[128,1024]{1,0:T(8,128)(2,1)}, bf16[128,1024]{1,0:T(8,128)(2,1)}, f3...) custom-call(f32[1024,256]{1,0:T(8,128)} %slice.147.state_ref, ...), custom_call_target="tpu_custom_call" | custom-call | flops 2013265920 | bytes 17315840 | tf_op jit(solution)/shard_map/pallas_call | solution.py:293
  194.0 12.5 %fusion.39.value_ref = f32[1024,1280]{1,0:T(8,128)} fusion(bf16[1024,2560]{1,0:T(8,128)(2,1)} %fusion.2, bf16[2560,1280]{1,0:T(8,128)(2,1)} %constant_dynamic-update-slice_fusion.12), kind=kOutput, calls=%fused_computation.162 | convolution fusion | flops 6710886400 | bytes 17039360 | tf_op jit(solution)/shard_map/dot_general | solution.py:25
  206.5 13.2 %collective-permute-done.19 = bf16[160,1280]{1,0:T(8,128)(2,1)S(1)} collective-permute-done((bf16[160,1280]{1,0:T(8,128)(2,1)S(1)}, bf16[160,1280]{1,0:T(8,128)(2,1)S(1)}, u32[]{:S(2)}, u32[]{:S(2)}) %collective-permute-start.19) | collective-permute-done | bytes 409632 | tf_op jit(solution)/shard_map/ppermute | solution.py:510
  223.3 18.2 %shard_map.289.mixed_ref = f32[1024,1280]{1,0:T(8,128)} custom-call(f32[1024,1280]{1,0:T(8,128)} %fusion.39.value_ref, f32[4,1280]{1,0:T(4,128)} %taps_ref.8, f32[1,1280]{1,0:T(1,128)} %broadcast_in_dim.50.bias_ref, f32[1,1280]{1,0:T(1,128)} %broadcast_in_dim_reshape.3.skip_ref, f32[1024,1280]{1,0:T(8,128)} %get-tuple-element.192.dtx_ref, ...), custom_call_target="tpu_custom_call" | custom-call | flops 3355443200 | bytes 24754176 | tf_op jit(solution)/shard_map/pallas_call | solution.py:293
  245.3 6.2 collective-permute-done.22
  255.7 4.3 collective-permute-done.24
  265.3 4.3 collective-permute-done.26
  272.3 14.8 %multiply_convert_fusion.3 = (bf16[1024,1280]{1,0:T(8,128)(2,1)}, f32[1024,1280]{1,0:T(8,128)}, f32[1024,1280]{1,0:T(8,128)}) fusion(f32[1280]{0:T(1024)S(1)} %copy-done.32, f32[1024,1280]{1,0:T(8,128)} %shard_map.289.mixed_ref, bf16[1024,2560]{1,0:T(8,128)(2,1)} %fusion.2, bf16[2560,1280]{1,0:T(8,128)(2,1)} %all-gather.5.cloned.1.call-done), kind=kOutput, calls=%fused_computation.23 | convolution fusion | flops 6720061440 | bytes 30151680 | tf_op jit(solution)/shard_map/dot_general | solution.py:25
  287.1 13.2 %multiply_reduce_fusion.2 = (f32[1024]{0:T(1024)S(1)}, f32[1024]{0:T(1024)S(1)}, f32[1024,1280]{1,0:T(8,128)}) fusion(f32[1024,1280]{1,0:T(8,128)} %get-tuple-element.367, f32[1280]{0:T(1024)S(1)} %copy-done.32, bf16[1024,2560]{1,0:T(8,128)(2,1)} %all-gather.7.cloned.1.call-done, bf16[2560,1280]{1,0:T(8,128)(2,1)} %constant_dynamic-update-slice_fusion), kind=kOutput, calls=%fused_computation.20 | convolution fusion | flops 6717437952 | bytes 22295552 | tf_op jit(solution)/shard_map/dot_general | solution.py:25
  300.3 5.8 psum.14
  306.1 11.4 %fusion.3 = bf16[2560,1280]{1,0:T(8,128)(2,1)S(1)} fusion(bf16[1024,2560]{1,0:T(8,128)(2,1)} %all-gather.7.cloned.1.call-done, f32[1024,1280]{1,0:T(8,128)} %get-tuple-element.367, f32[1024]{0:T(1024)S(1)} %bitcast.86, f32[1280]{0:T(1024)S(1)} %copy-done.32), kind=kOutput, calls=%fused_computation.10 | convolution fusion | flops 6718095360 | bytes 17048576 | tf_op jit(solution)/shard_map/dot_general | solution.py:29
  317.5 2.8 copy-done.3
  322.4 11.7 %multiply_convert_fusion = bf16[2560,1024]{1,0:T(8,128)(2,1)} fusion(bf16[2560,1280]{1,0:T(8,128)(2,1)} %constant_dynamic-update-slice_fusion, bf16[1024,1280]{1,0:T(8,128)(2,1)S(1)} %copy-done.37, f32[1024]{0:T(1024)S(1)} %bitcast.87), kind=kOutput, calls=%fused_computation.9 | convolution fusion | flops 6716129280 | bytes 14422016 | tf_op jit(solution)/shard_map/dot_general | solution.py:35
  337.6 14.6 %multiply_convert_fusion.1 = (bf16[1024,1280]{1,0:T(8,128)(2,1)S(1)}, f32[1024,1280]{1,0:T(8,128)}, f32[1280]{0:T(1024)}) fusion(f32[1024,1280]{1,0:T(8,128)} %get-tuple-element.437, f32[1024,1280]{1,0:T(8,128)} %shard_map.289.mixed_ref, f32[1024,1280]{1,0:T(8,128)} %get-tuple-element.367, f32[1024]{0:T(1024)S(1)} %fusion.27, ...), kind=kLoop, calls=%fused_computation.16 | loop fusion | flops 24902400 | bytes 28854272 | tf_op jit(solution)/shard_map/convert_element_type | solution.py:684
  356.3 9.4 %convolution_convert_fusion.1 = bf16[2560,1280]{1,0:T(8,128)(2,1)S(1)} fusion(bf16[1024,2560]{1,0:T(8,128)(2,1)} %fusion.2, bf16[1024,1280]{1,0:T(8,128)(2,1)S(1)} %get-tuple-element.269), kind=kOutput, calls=%fused_computation.3 | convolution fusion | flops 6714163200 | bytes 14417920 | tf_op jit(solution)/shard_map/dot_general | solution.py:29
  365.8 2.7 add_convert_fusion.31
  372.6 20.1 %shard_map.290 = (bf16[1024,1280]{1,0:T(8,128)(2,1)}, f32[8,1280]{1,0:T(8,128)}, f32[1024,128]{1,0:T(8,128)}, f32[1024,128]{1,0:T(8,128)}, f32[1024,128]{1,0:T(8...) custom-call(f32[1024,1280]{1,0:T(8,128)} %fusion.39.value_ref, f32[1024,1280]{1,0:T(8,128)} %shard_map.289.mixed_ref, ...), custom_call_target="tpu_custom_call" | custom-call | flops 5033164800 | bytes 35805184 | tf_op jit(solution)/shard_map/pallas_call | solution.py:293
  400.5 20.6 %shard_map.291 = (bf16[1024,1280]{1,0:T(8,128)(2,1)}, f32[8,1280]{1,0:T(8,128)}, f32[1024,128]{1,0:T(8,128)}, f32[1024,128]{1,0:T(8,128)}, f32[1024,128]{1,0:T(8...) custom-call(f32[1024,1280]{1,0:T(8,128)} %fusion.39.value_ref, ...), custom_call_target="tpu_custom_call", output_to_operand_aliasing={{0}: (15, {}), {1}: (16, {})} | custom-call | flops 5033164800 | bytes 41089024 | tf_op jit(solution)/shard_map/pallas_call | solution.py:293
  428.3 9.8 %convolution_convert_fusion = bf16[2560,1280]{1,0:T(8,128)(2,1)S(1)} fusion(bf16[1024,2560]{1,0:T(8,128)(2,1)} %fusion.2, bf16[1024,1280]{1,0:T(8,128)(2,1)} %get-tuple-element.243), kind=kOutput, calls=%fused_computation.2 | convolution fusion | flops 6714163200 | bytes 14417920 | tf_op jit(solution)/shard_map/dot_general | solution.py:29
  449.4 7.0 %shard_map.292 = (bf16[1024,256]{1,0:T(8,128)(2,1)}, bf16[1024,128]{1,0:T(8,128)(2,1)}, f32[8,256]{1,0:T(8,128)}, f32[8,128]{1,0:T(8,128)}) custom-call(f32[1024,256]{1,0:T(8,128)} %slice.147.state_ref, f32[1024,128]{1,0:T(8,128)} %pad.13.step_ref, f32[4,256]{1,0:T(4,128)} %taps_ref.9, f32[1,256]{1,0:T(1,128)} %bitcast.98, f32[1,128]{1,0:T(1,128)} %pad.14.step_bias_ref, ...), custom_call_target="tpu_custom_call" | custom-call | flops 2013265920 | bytes 8153088 | tf_op jit(solution)/shard_map/pallas_call | solution.py:293
  456.4 7.0 %convolution_convert_fusion.3 = bf16[2560,276]{1,0:T(8,128)(2,1)} fusion(bf16[1024,2560]{1,0:T(8,128)(2,1)} %fusion.2, bf16[1024,20]{1,0:T(8,128)(2,1)} %bitcast.84, bf16[1024,256]{1,0:T(8,128)(2,1)} %get-tuple-element.259), kind=kOutput, calls=%fused_computation.29 | convolution fusion | flops 1448871936 | bytes 7221248 | tf_op jit(solution)/shard_map/dot_general | solution.py:29
  463.6 2.9 pad_maximum_fusion
  468.6 2.5 add_convert_fusion.15
  471.1 11.4 %fusion.40 = f32[2560,1024]{1,0:T(8,128)} fusion(bf16[2560,1280]{1,0:T(8,128)(2,1)} %all-gather.5.cloned.1.call-done, bf16[1024,1280]{1,0:T(8,128)(2,1)S(1)} %copy-done.12), kind=kOutput, calls=%fused_computation.163 | convolution fusion | flops 6710886400 | bytes 19660800 | tf_op jit(solution)/shard_map/dot_general | solution.py:35
  482.6 2.8 convert_add_fusion.5
  485.3 2.5 add_convert_fusion.17
  487.8 16.5 %add_convert_fusion = bf16[2560,1024]{1,0:T(8,128)(2,1)} fusion(f32[2560,1024]{1,0:T(8,128)} %fusion.40, bf16[1024,1556]{1,0:T(8,128)(2,1)S(1)} %copy-done.7, bf16[2560,276]{1,0:T(8,128)(2,1)} %copy.86, bf16[2560,1280]{1,0:T(8,128)(2,1)} %constant_dynamic-update-slice_fusion.12), kind=kOutput, calls=%fused_computation.8 | convolution fusion | flops 8179097600 | bytes 26882048 | tf_op jit(solution)/shard_map/dot_general | solution.py:35
  511.8 3.2 collective-permute-done.74
  515.0 2.5 collective-permute-start.75
  523.1 2.6 collective-permute-start.67
  532.1 5.5 collective-permute-done.67
  541.4 4.5 collective-permute-done.55
  549.4 5.1 collective-permute-done.63
  555.8 2.5 collective-permute-start.64
  558.8 4.5 collective-permute-done.56
  564.6 2.5 collective-permute-start.57
  567.6 4.5 collective-permute-done.64
  573.4 2.8 collective-permute-start.65
  576.6 3.9 collective-permute-done.57
  581.9 3.2 collective-permute-start.60
  585.1 3.2 collective-permute-done.70
  592.5 3.6 collective-permute-done.60
  599.0 2.6 collective-permute-done.71
  601.5 2.6 convert_add_fusion.2
  609.7 4.4 collective-permute-done.72
  615.3 2.6 fusion.17
  625.5 5.6 psum.15
  633.2 5.1 fusion.14
  638.3 3.3 copy.88
  (349 shorter events, 186.6 us)
Async XLA Ops:
  7.2 149.5 %all-gather.9.cloned.1.call-start = ((), (), s32[]{:S(2)}) async-start(), calls=%async_computation.8 | async-start | bytes 1935360 | tf_op jit(solution)/shard_map/all_gather | solution.py:614
  8.5 12.5 %collective-permute-start = (bf16[160,1280]{1,0:T(8,128)(2,1)S(1)}, bf16[160,1280]{1,0:T(8,128)(2,1)S(1)}, u32[]{:S(2)}, u32[]{:S(2)}) collective-permute-start(bf16[160,1280]{1,0:T(8,128)(2,1)S(1)} %get-tuple-element.420), channel_id=1, source_target_pairs={{0,8},{8,16},{16,24},{24,28},{28,20},{20,12},{12,4},{4,0},{1,9},{9... | collective-permute-start | bytes 1228808 | tf_op jit(solution)/shard_map/ppermute | solution.py:510
  14.1 258.1 %all-gather.5.cloned.1.call-start = ((), (), s32[]{:S(2)}) async-start(), calls=%async_computation.3 | async-start | bytes 7372800 | tf_op jit(solution)/shard_map/all_gather | solution.py:625
  22.6 16.0 %collective-permute-start.2 = (bf16[160,1280]{1,0:T(8,128)(2,1)S(1)}, bf16[160,1280]{1,0:T(8,128)(2,1)S(1)}, u32[]{:S(2)}, u32[]{:S(2)}) collective-permute-start(bf16[160,1280]{1,0:T(8,128)(2,1)S(1)} %collective-permute-done), channel_id=1, source_target_pairs={{0,8},{8,16},{16,24},{24,28},{28,20},{20,12},{12,4},{4,0},{1,9},{9... | collective-permute-start | bytes 1228808 | tf_op jit(solution)/shard_map/ppermute | solution.py:510
  24.2 16.9 %collective-permute-start.3 = (bf16[160,1280]{1,0:T(8,128)(2,1)}, bf16[160,1280]{1,0:T(8,128)(2,1)S(1)}, u32[]{:S(2)}, u32[]{:S(2)}) collective-permute-start(bf16[160,1280]{1,0:T(8,128)(2,1)} %collective-permute-done.1), channel_id=1, source_target_pairs={{8,0},{16,8},{24,16},{28,24},{20,28},{12,20},{4,12},{0,4},{9,1},{1... | collective-permute-start | bytes 1228808 | tf_op jit(solution)/shard_map/ppermute | solution.py:510
  41.0 17.3 %collective-permute-start.8 = (bf16[160,1280]{1,0:T(8,128)(2,1)S(1)}, bf16[160,1280]{1,0:T(8,128)(2,1)S(1)}, u32[]{:S(2)}, u32[]{:S(2)}) collective-permute-start(bf16[160,1280]{1,0:T(8,128)(2,1)S(1)} %collective-permute-done.2), channel_id=1, source_target_pairs={{0,8},{8,16},{16,24},{24,28},{28,20},{20,12},{12,4},{4,0},{1,9},{9... | collective-permute-start | bytes 1228808 | tf_op jit(solution)/shard_map/ppermute | solution.py:510
  42.6 24.2 %collective-permute-start.9 = (bf16[160,1280]{1,0:T(8,128)(2,1)S(1)}, bf16[160,1280]{1,0:T(8,128)(2,1)S(1)}, u32[]{:S(2)}, u32[]{:S(2)}) collective-permute-start(bf16[160,1280]{1,0:T(8,128)(2,1)S(1)} %collective-permute-done.3), channel_id=1, source_target_pairs={{8,0},{16,8},{24,16},{28,24},{20,28},{12,20},{4,12},{0,4},{9,1},{1... | collective-permute-start | bytes 1228808 | tf_op jit(solution)/shard_map/ppermute | solution.py:510
  77.2 11.8 %collective-permute-start.12 = (bf16[160,1280]{1,0:T(8,128)(2,1)S(1)}, bf16[160,1280]{1,0:T(8,128)(2,1)S(1)}, u32[]{:S(2)}, u32[]{:S(2)}) collective-permute-start(bf16[160,1280]{1,0:T(8,128)(2,1)S(1)} %collective-permute-done.10), channel_id=1, source_target_pairs={{0,8},{8,16},{16,24},{24,28},{28,20},{20,12},{12,4},{4,0},{1,9},{9... | collective-permute-start | bytes 1228808 | tf_op jit(solution)/shard_map/ppermute | solution.py:510
  77.2 11.8 %collective-permute-start.13 = (bf16[160,1280]{1,0:T(8,128)(2,1)S(1)}, bf16[160,1280]{1,0:T(8,128)(2,1)S(1)}, u32[]{:S(2)}, u32[]{:S(2)}) collective-permute-start(bf16[160,1280]{1,0:T(8,128)(2,1)S(1)} %collective-permute-done.11), channel_id=1, source_target_pairs={{8,0},{16,8},{24,16},{28,24},{20,28},{12,20},{4,12},{0,4},{9,1},{1... | collective-permute-start | bytes 1228808 | tf_op jit(solution)/shard_map/ppermute | solution.py:510
  89.0 12.3 %collective-permute-start.14 = (bf16[160,1280]{1,0:T(8,128)(2,1)S(1)}, bf16[160,1280]{1,0:T(8,128)(2,1)S(1)}, u32[]{:S(2)}, u32[]{:S(2)}) collective-permute-start(bf16[160,1280]{1,0:T(8,128)(2,1)S(1)} %collective-permute-done.12), channel_id=1, source_target_pairs={{0,8},{8,16},{16,24},{24,28},{28,20},{20,12},{12,4},{4,0},{1,9},{9... | collective-permute-start | bytes 1228808 | tf_op jit(solution)/shard_map/ppermute | solution.py:510
  91.1 11.8 %collective-permute-start.15 = (bf16[160,1280]{1,0:T(8,128)(2,1)S(1)}, bf16[160,1280]{1,0:T(8,128)(2,1)S(1)}, u32[]{:S(2)}, u32[]{:S(2)}) collective-permute-start(bf16[160,1280]{1,0:T(8,128)(2,1)S(1)} %collective-permute-done.13), channel_id=1, source_target_pairs={{8,0},{16,8},{24,16},{28,24},{20,28},{12,20},{4,12},{0,4},{9,1},{1... | collective-permute-start | bytes 1228808 | tf_op jit(solution)/shard_map/ppermute | solution.py:510
  103.0 12.0 %collective-permute-start.16 = (bf16[160,1280]{1,0:T(8,128)(2,1)S(1)}, bf16[160,1280]{1,0:T(8,128)(2,1)S(1)}, u32[]{:S(2)}, u32[]{:S(2)}) collective-permute-start(bf16[160,1280]{1,0:T(8,128)(2,1)S(1)} %collective-permute-done.14), channel_id=1, source_target_pairs={{0,8},{8,16},{16,24},{24,28},{28,20},{20,12},{12,4},{4,0},{1,9},{9... | collective-permute-start | bytes 1228808 | tf_op jit(solution)/shard_map/ppermute | solution.py:510
  103.3 11.9 %collective-permute-start.17 = (bf16[160,1280]{1,0:T(8,128)(2,1)S(1)}, bf16[160,1280]{1,0:T(8,128)(2,1)S(1)}, u32[]{:S(2)}, u32[]{:S(2)}) collective-permute-start(bf16[160,1280]{1,0:T(8,128)(2,1)S(1)} %collective-permute-done.15), channel_id=1, source_target_pairs={{8,0},{16,8},{24,16},{28,24},{20,28},{12,20},{4,12},{0,4},{9,1},{1... | collective-permute-start | bytes 1228808 | tf_op jit(solution)/shard_map/ppermute | solution.py:510
  115.2 171.9 %all-gather.7.cloned.1.call-start = ((), (), s32[]{:S(2)}) async-start(), calls=%async_computation.4 | async-start | bytes 6553600 | tf_op jit(solution)/shard_map/all_gather | solution.py:615
  116.0 11.1 %collective-permute-start.4 = (bf16[160,1280]{1,0:T(8,128)(2,1)S(1)}, bf16[160,1280]{1,0:T(8,128)(2,1)S(1)}, u32[]{:S(2)}, u32[]{:S(2)}) collective-permute-start(bf16[160,1280]{1,0:T(8,128)(2,1)S(1)} %get-tuple-element.418), channel_id=1, source_target_pairs={{0,8},{8,16},{16,24},{24,28},{28,20},{20,12},{12,4},{4,0},{1,9},{9... | collective-permute-start | bytes 1228808 | tf_op jit(solution)/shard_map/ppermute | solution.py:510
  116.5 12.8 %collective-permute-start.5 = (bf16[160,1280]{1,0:T(8,128)(2,1)S(1)}, bf16[160,1280]{1,0:T(8,128)(2,1)S(1)}, u32[]{:S(2)}, u32[]{:S(2)}) collective-permute-start(bf16[160,1280]{1,0:T(8,128)(2,1)S(1)} %get-tuple-element.417), channel_id=1, source_target_pairs={{8,0},{16,8},{24,16},{28,24},{20,28},{12,20},{4,12},{0,4},{9,1},{1... | collective-permute-start | bytes 1228808 | tf_op jit(solution)/shard_map/ppermute | solution.py:510
  118.1 369.7 %reduce-scatter.4.cloned.1.call-start = ((), (), s32[]{:S(2)}) async-start(), calls=%async_computation.5 | async-start | bytes 6553600 | tf_op jit(solution)/shard_map/reduce_scatter | solution.py:675
  129.3 14.2 %collective-permute-start.6 = (bf16[160,1280]{1,0:T(8,128)(2,1)S(1)}, bf16[160,1280]{1,0:T(8,128)(2,1)S(1)}, u32[]{:S(2)}, u32[]{:S(2)}) collective-permute-start(bf16[160,1280]{1,0:T(8,128)(2,1)S(1)} %collective-permute-done.4), channel_id=1, source_target_pairs={{0,8},{8,16},{16,24},{24,28},{28,20},{20,12},{12,4},{4,0},{1,9},{9... | collective-permute-start | bytes 1228808 | tf_op jit(solution)/shard_map/ppermute | solution.py:510
  129.3 25.7 %collective-permute-start.7 = (bf16[160,1280]{1,0:T(8,128)(2,1)S(1)}, bf16[160,1280]{1,0:T(8,128)(2,1)S(1)}, u32[]{:S(2)}, u32[]{:S(2)}) collective-permute-start(bf16[160,1280]{1,0:T(8,128)(2,1)S(1)} %collective-permute-done.5), channel_id=1, source_target_pairs={{8,0},{16,8},{24,16},{28,24},{20,28},{12,20},{4,12},{0,4},{9,1},{1... | collective-permute-start | bytes 1228808 | tf_op jit(solution)/shard_map/ppermute | solution.py:510
  188.8 17.7 %collective-permute-start.18 = (bf16[160,1280]{1,0:T(8,128)(2,1)S(1)}, bf16[160,1280]{1,0:T(8,128)(2,1)S(1)}, u32[]{:S(2)}, u32[]{:S(2)}) collective-permute-start(bf16[160,1280]{1,0:T(8,128)(2,1)S(1)} %copy-done.18), channel_id=1, source_target_pairs={{0,8},{8,16},{16,24},{24,28},{28,20},{20,12},{12,4},{4,0},{1,9},{9... | collective-permute-start | bytes 1228808 | tf_op jit(solution)/shard_map/ppermute | solution.py:510
  188.8 30.9 %collective-permute-start.19 = (bf16[160,1280]{1,0:T(8,128)(2,1)S(1)}, bf16[160,1280]{1,0:T(8,128)(2,1)S(1)}, u32[]{:S(2)}, u32[]{:S(2)}) collective-permute-start(bf16[160,1280]{1,0:T(8,128)(2,1)S(1)} %copy-done.20), channel_id=1, source_target_pairs={{8,0},{16,8},{24,16},{28,24},{20,28},{12,20},{4,12},{0,4},{9,1},{1... | collective-permute-start | bytes 1228808 | tf_op jit(solution)/shard_map/ppermute | solution.py:510
  219.7 21.8 %collective-permute-start.20 = (bf16[160,1280]{1,0:T(8,128)(2,1)S(1)}, bf16[160,1280]{1,0:T(8,128)(2,1)S(1)}, u32[]{:S(2)}, u32[]{:S(2)}) collective-permute-start(bf16[160,1280]{1,0:T(8,128)(2,1)S(1)} %collective-permute-done.18), channel_id=1, source_target_pairs={{0,8},{8,16},{16,24},{24,28},{28,20},{20,12},{12,4},{4,0},{1,9},{9... | collective-permute-start | bytes 1228808 | tf_op jit(solution)/shard_map/ppermute | solution.py:510
  219.7 21.8 %collective-permute-start.21 = (bf16[160,1280]{1,0:T(8,128)(2,1)S(1)}, bf16[160,1280]{1,0:T(8,128)(2,1)S(1)}, u32[]{:S(2)}, u32[]{:S(2)}) collective-permute-start(bf16[160,1280]{1,0:T(8,128)(2,1)S(1)} %collective-permute-done.19), channel_id=1, source_target_pairs={{8,0},{16,8},{24,16},{28,24},{20,28},{12,20},{4,12},{0,4},{9,1},{1... | collective-permute-start | bytes 1228808 | tf_op jit(solution)/shard_map/ppermute | solution.py:510
  320.3 13.8 %collective-permute-start.28 = (bf16[160,1280]{1,0:T(8,128)(2,1)S(1)}, bf16[160,1280]{1,0:T(8,128)(2,1)S(1)}, u32[]{:S(2)}, u32[]{:S(2)}) collective-permute-start(bf16[160,1280]{1,0:T(8,128)(2,1)S(1)} %get-tuple-element.219), channel_id=1, source_target_pairs={{0,8},{8,16},{16,24},{24,28},{28,20},{20,12},{12,4},{4,0},{1,9},{9... | collective-permute-start | bytes 1228808 | tf_op jit(solution)/shard_map/ppermute | solution.py:543
  322.2 12.0 %collective-permute-start.29 = (bf16[160,1280]{1,0:T(8,128)(2,1)S(1)}, bf16[160,1280]{1,0:T(8,128)(2,1)S(1)}, u32[]{:S(2)}, u32[]{:S(2)}) collective-permute-start(bf16[160,1280]{1,0:T(8,128)(2,1)S(1)} %get-tuple-element.220), channel_id=1, source_target_pairs={{8,0},{16,8},{24,16},{28,24},{20,28},{12,20},{4,12},{0,4},{9,1},{1... | collective-permute-start | bytes 1228808 | tf_op jit(solution)/shard_map/ppermute | solution.py:543
  334.1 263.1 %reduce-scatter.8.cloned.1.call-start = ((), (), s32[]{:S(2)}) async-start(), calls=%async_computation.7 | async-start | bytes 2211840 | tf_op jit(solution)/shard_map/reduce_scatter | solution.py:571
  335.5 16.7 %collective-permute-start.30 = (bf16[160,1280]{1,0:T(8,128)(2,1)S(1)}, bf16[160,1280]{1,0:T(8,128)(2,1)S(1)}, u32[]{:S(2)}, u32[]{:S(2)}) collective-permute-start(bf16[160,1280]{1,0:T(8,128)(2,1)S(1)} %get-tuple-element.222), channel_id=1, source_target_pairs={{0,8},{8,16},{16,24},{24,28},{28,20},{20,12},{12,4},{4,0},{1,9},{9... | collective-permute-start | bytes 1228808 | tf_op jit(solution)/shard_map/ppermute | solution.py:543
  337.3 14.9 %collective-permute-start.31 = (bf16[160,1280]{1,0:T(8,128)(2,1)S(1)}, bf16[160,1280]{1,0:T(8,128)(2,1)S(1)}, u32[]{:S(2)}, u32[]{:S(2)}) collective-permute-start(bf16[160,1280]{1,0:T(8,128)(2,1)S(1)} %get-tuple-element.223), channel_id=1, source_target_pairs={{8,0},{16,8},{24,16},{28,24},{20,28},{12,20},{4,12},{0,4},{9,1},{1... | collective-permute-start | bytes 1228808 | tf_op jit(solution)/shard_map/ppermute | solution.py:543
  354.2 11.5 %collective-permute-start.32 = (bf16[160,1280]{1,0:T(8,128)(2,1)S(1)}, bf16[160,1280]{1,0:T(8,128)(2,1)S(1)}, u32[]{:S(2)}, u32[]{:S(2)}) collective-permute-start(bf16[160,1280]{1,0:T(8,128)(2,1)S(1)} %get-tuple-element.224), channel_id=1, source_target_pairs={{0,8},{8,16},{16,24},{24,28},{28,20},{20,12},{12,4},{4,0},{1,9},{9... | collective-permute-start | bytes 1228808 | tf_op jit(solution)/shard_map/ppermute | solution.py:543
  368.5 24.1 %collective-permute-start.36 = (bf16[160,1280]{1,0:T(8,128)(2,1)S(1)}, bf16[160,1280]{1,0:T(8,128)(2,1)S(1)}, u32[]{:S(2)}, u32[]{:S(2)}) collective-permute-start(bf16[160,1280]{1,0:T(8,128)(2,1)S(1)} %get-tuple-element.230), channel_id=1, source_target_pairs={{0,8},{8,16},{16,24},{24,28},{28,20},{20,12},{12,4},{4,0},{1,9},{9... | collective-permute-start | bytes 1228808 | tf_op jit(solution)/shard_map/ppermute | solution.py:543
  370.4 23.1 %collective-permute-start.37 = (bf16[160,1280]{1,0:T(8,128)(2,1)S(1)}, bf16[160,1280]{1,0:T(8,128)(2,1)}, u32[]{:S(2)}, u32[]{:S(2)}) collective-permute-start(bf16[160,1280]{1,0:T(8,128)(2,1)S(1)} %get-tuple-element.231), channel_id=1, source_target_pairs={{8,0},{16,8},{24,16},{28,24},{20,28},{12,20},{4,12},{0,4},{9,1},{1... | collective-permute-start | bytes 1228808 | tf_op jit(solution)/shard_map/ppermute | solution.py:543
  370.6 24.2 %collective-permute-start.34 = (bf16[160,1280]{1,0:T(8,128)(2,1)}, bf16[160,1280]{1,0:T(8,128)(2,1)}, u32[]{:S(2)}, u32[]{:S(2)}) collective-permute-start(bf16[160,1280]{1,0:T(8,128)(2,1)} %get-tuple-element.228), channel_id=1, source_target_pairs={{0,8},{8,16},{16,24},{24,28},{28,20},{20,12},{12,4},{4,0},{1,9},{9... | collective-permute-start | bytes 1228808 | tf_op jit(solution)/shard_map/ppermute | solution.py:543
  372.4 22.4 %collective-permute-start.35 = (bf16[160,1280]{1,0:T(8,128)(2,1)S(1)}, bf16[160,1280]{1,0:T(8,128)(2,1)}, u32[]{:S(2)}, u32[]{:S(2)}) collective-permute-start(bf16[160,1280]{1,0:T(8,128)(2,1)S(1)} %get-tuple-element.229), channel_id=1, source_target_pairs={{8,0},{16,8},{24,16},{28,24},{20,28},{12,20},{4,12},{0,4},{9,1},{1... | collective-permute-start | bytes 1228808 | tf_op jit(solution)/shard_map/ppermute | solution.py:543
  396.4 24.7 %collective-permute-start.40 = (bf16[160,1280]{1,0:T(8,128)(2,1)S(1)}, bf16[160,1280]{1,0:T(8,128)(2,1)}, u32[]{:S(2)}, u32[]{:S(2)}) collective-permute-start(bf16[160,1280]{1,0:T(8,128)(2,1)S(1)} %get-tuple-element.247), channel_id=1, source_target_pairs={{0,8},{8,16},{16,24},{24,28},{28,20},{20,12},{12,4},{4,0},{1,9},{9... | collective-permute-start | bytes 1228808 | tf_op jit(solution)/shard_map/ppermute | solution.py:543
  398.2 22.8 %collective-permute-start.41 = (bf16[160,1280]{1,0:T(8,128)(2,1)S(1)}, bf16[160,1280]{1,0:T(8,128)(2,1)}, u32[]{:S(2)}, u32[]{:S(2)}) collective-permute-start(bf16[160,1280]{1,0:T(8,128)(2,1)S(1)} %get-tuple-element.248), channel_id=1, source_target_pairs={{8,0},{16,8},{24,16},{28,24},{20,28},{12,20},{4,12},{0,4},{9,1},{1... | collective-permute-start | bytes 1228808 | tf_op jit(solution)/shard_map/ppermute | solution.py:543
  398.4 24.0 %collective-permute-start.38 = (bf16[160,1280]{1,0:T(8,128)(2,1)S(1)}, bf16[160,1280]{1,0:T(8,128)(2,1)}, u32[]{:S(2)}, u32[]{:S(2)}) collective-permute-start(bf16[160,1280]{1,0:T(8,128)(2,1)S(1)} %get-tuple-element.245), channel_id=1, source_target_pairs={{0,8},{8,16},{16,24},{24,28},{28,20},{20,12},{12,4},{4,0},{1,9},{9... | collective-permute-start | bytes 1228808 | tf_op jit(solution)/shard_map/ppermute | solution.py:543
  400.3 22.1 %collective-permute-start.39 = (bf16[160,1280]{1,0:T(8,128)(2,1)S(1)}, bf16[160,1280]{1,0:T(8,128)(2,1)}, u32[]{:S(2)}, u32[]{:S(2)}) collective-permute-start(bf16[160,1280]{1,0:T(8,128)(2,1)S(1)} %get-tuple-element.246), channel_id=1, source_target_pairs={{8,0},{16,8},{24,16},{28,24},{20,28},{12,20},{4,12},{0,4},{9,1},{1... | collective-permute-start | bytes 1228808 | tf_op jit(solution)/shard_map/ppermute | solution.py:543
  424.0 14.9 %collective-permute-start.44 = (bf16[160,1280]{1,0:T(8,128)(2,1)S(1)}, bf16[160,1280]{1,0:T(8,128)(2,1)S(1)}, u32[]{:S(2)}, u32[]{:S(2)}) collective-permute-start(bf16[160,1280]{1,0:T(8,128)(2,1)S(1)} %get-tuple-element.251), channel_id=1, source_target_pairs={{0,8},{8,16},{16,24},{24,28},{28,20},{20,12},{12,4},{4,0},{1,9},{9... | collective-permute-start | bytes 1228808 | tf_op jit(solution)/shard_map/ppermute | solution.py:543
  425.9 13.0 %collective-permute-start.45 = (bf16[160,1280]{1,0:T(8,128)(2,1)S(1)}, bf16[160,1280]{1,0:T(8,128)(2,1)S(1)}, u32[]{:S(2)}, u32[]{:S(2)}) collective-permute-start(bf16[160,1280]{1,0:T(8,128)(2,1)S(1)} %get-tuple-element.252), channel_id=1, source_target_pairs={{8,0},{16,8},{24,16},{28,24},{20,28},{12,20},{4,12},{0,4},{9,1},{1... | collective-permute-start | bytes 1228808 | tf_op jit(solution)/shard_map/ppermute | solution.py:543
  426.2 15.0 %collective-permute-start.42 = (bf16[160,1280]{1,0:T(8,128)(2,1)S(1)}, bf16[160,1280]{1,0:T(8,128)(2,1)S(1)}, u32[]{:S(2)}, u32[]{:S(2)}) collective-permute-start(bf16[160,1280]{1,0:T(8,128)(2,1)S(1)} %get-tuple-element.249), channel_id=1, source_target_pairs={{0,8},{8,16},{16,24},{24,28},{28,20},{20,12},{12,4},{4,0},{1,9},{9... | collective-permute-start | bytes 1228808 | tf_op jit(solution)/shard_map/ppermute | solution.py:543
  428.1 13.6 %collective-permute-start.43 = (bf16[160,1280]{1,0:T(8,128)(2,1)S(1)}, bf16[160,1280]{1,0:T(8,128)(2,1)S(1)}, u32[]{:S(2)}, u32[]{:S(2)}) collective-permute-start(bf16[160,1280]{1,0:T(8,128)(2,1)S(1)} %get-tuple-element.250), channel_id=1, source_target_pairs={{8,0},{16,8},{24,16},{28,24},{20,28},{12,20},{4,12},{0,4},{9,1},{1... | collective-permute-start | bytes 1228808 | tf_op jit(solution)/shard_map/ppermute | solution.py:543
  443.9 41.4 %collective-permute-start.48 = (bf16[160,1280]{1,0:T(8,128)(2,1)}, bf16[160,1280]{1,0:T(8,128)(2,1)}, u32[]{:S(2)}, u32[]{:S(2)}) collective-permute-start(bf16[160,1280]{1,0:T(8,128)(2,1)} %get-tuple-element.263), channel_id=1, source_target_pairs={{0,8},{8,16},{16,24},{24,28},{28,20},{20,12},{12,4},{4,0},{1,9},{9... | collective-permute-start | bytes 1228808 | tf_op jit(solution)/shard_map/ppermute | solution.py:543
  445.4 40.0 %collective-permute-start.49 = (bf16[160,1280]{1,0:T(8,128)(2,1)}, bf16[160,1280]{1,0:T(8,128)(2,1)}, u32[]{:S(2)}, u32[]{:S(2)}) collective-permute-start(bf16[160,1280]{1,0:T(8,128)(2,1)} %get-tuple-element.264), channel_id=1, source_target_pairs={{8,0},{16,8},{24,16},{28,24},{20,28},{12,20},{4,12},{0,4},{9,1},{1... | collective-permute-start | bytes 1228808 | tf_op jit(solution)/shard_map/ppermute | solution.py:543
  445.9 36.6 %collective-permute-start.46 = (bf16[160,1280]{1,0:T(8,128)(2,1)}, bf16[160,1280]{1,0:T(8,128)(2,1)}, u32[]{:S(2)}, u32[]{:S(2)}) collective-permute-start(bf16[160,1280]{1,0:T(8,128)(2,1)} %get-tuple-element.261), channel_id=1, source_target_pairs={{0,8},{8,16},{16,24},{24,28},{28,20},{20,12},{12,4},{4,0},{1,9},{9... | collective-permute-start | bytes 1228808 | tf_op jit(solution)/shard_map/ppermute | solution.py:543
  447.4 20.2 %collective-permute-start.50 = (bf16[160,1280]{1,0:T(8,128)(2,1)}, bf16[160,1280]{1,0:T(8,128)(2,1)}, u32[]{:S(2)}, u32[]{:S(2)}) collective-permute-start(bf16[160,1280]{1,0:T(8,128)(2,1)} %get-tuple-element.267), channel_id=1, source_target_pairs={{0,8},{8,16},{16,24},{24,28},{28,20},{20,12},{12,4},{4,0},{1,9},{9... | collective-permute-start | bytes 1228808 | tf_op jit(solution)/shard_map/ppermute | solution.py:543
  447.8 20.8 %collective-permute-start.51 = (bf16[160,1280]{1,0:T(8,128)(2,1)S(1)}, bf16[160,1280]{1,0:T(8,128)(2,1)}, u32[]{:S(2)}, u32[]{:S(2)}) collective-permute-start(bf16[160,1280]{1,0:T(8,128)(2,1)S(1)} %get-tuple-element.268), channel_id=1, source_target_pairs={{8,0},{16,8},{24,16},{28,24},{20,28},{12,20},{4,12},{0,4},{9,1},{1... | collective-permute-start | bytes 1228808 | tf_op jit(solution)/shard_map/ppermute | solution.py:543
  463.5 151.8 %reduce-scatter.6.cloned.1.call-start = ((), (), s32[]{:S(2)}) async-start(), calls=%async_computation.6 | async-start | bytes 6553600 | tf_op jit(solution)/shard_map/reduce_scatter | solution.py:726
  467.7 14.9 %collective-permute-start.47 = (bf16[160,1280]{1,0:T(8,128)(2,1)S(1)}, bf16[160,1280]{1,0:T(8,128)(2,1)S(1)}, u32[]{:S(2)}, u32[]{:S(2)}) collective-permute-start(bf16[160,1280]{1,0:T(8,128)(2,1)S(1)} %copy-done.21), channel_id=1, source_target_pairs={{8,0},{16,8},{24,16},{28,24},{20,28},{12,20},{4,12},{0,4},{9,1},{1... | collective-permute-start | bytes 1228808 | tf_op jit(solution)/shard_map/ppermute | solution.py:543
  507.2 18.5 %collective-permute-start.61 = (bf16[160,1280]{1,0:T(8,128)(2,1)}, bf16[160,1280]{1,0:T(8,128)(2,1)}, u32[]{:S(2)}, u32[]{:S(2)}) collective-permute-start(bf16[160,1280]{1,0:T(8,128)(2,1)} %get-tuple-element.273), channel_id=1, source_target_pairs={{0,8},{8,16},{16,24},{24,28},{28,20},{20,12},{12,4},{4,0},{1,9},{9... | collective-permute-start | bytes 1228808 | tf_op jit(solution)/shard_map/ppermute | solution.py:543
  523.1 14.5 %collective-permute-start.67 = (bf16[160,1280]{1,0:T(8,128)(2,1)}, bf16[160,1280]{1,0:T(8,128)(2,1)S(1)}, u32[]{:S(2)}, u32[]{:S(2)}) collective-permute-start(bf16[160,1280]{1,0:T(8,128)(2,1)} %get-tuple-element.274), channel_id=1, source_target_pairs={{8,0},{16,8},{24,16},{28,24},{20,28},{12,20},{4,12},{0,4},{9,1},{1... | collective-permute-start | bytes 1228808 | tf_op jit(solution)/shard_map/ppermute | solution.py:543
  527.6 18.2 %collective-permute-start.55 = (bf16[160,1280]{1,0:T(8,128)(2,1)}, bf16[160,1280]{1,0:T(8,128)(2,1)S(1)}, u32[]{:S(2)}, u32[]{:S(2)}) collective-permute-start(bf16[160,1280]{1,0:T(8,128)(2,1)} %get-tuple-element.271), channel_id=1, source_target_pairs={{0,8},{8,16},{16,24},{24,28},{28,20},{20,12},{12,4},{4,0},{1,9},{9... | collective-permute-start | bytes 1228808 | tf_op jit(solution)/shard_map/ppermute | solution.py:543
  529.5 29.3 %collective-permute-start.58 = (bf16[160,1280]{1,0:T(8,128)(2,1)}, bf16[160,1280]{1,0:T(8,128)(2,1)S(1)}, u32[]{:S(2)}, u32[]{:S(2)}) collective-permute-start(bf16[160,1280]{1,0:T(8,128)(2,1)} %get-tuple-element.272), channel_id=1, source_target_pairs={{8,0},{16,8},{24,16},{28,24},{20,28},{12,20},{4,12},{0,4},{9,1},{1... | collective-permute-start | bytes 1228808 | tf_op jit(solution)/shard_map/ppermute | solution.py:543
  539.2 15.3 %collective-permute-start.63 = (bf16[160,1280]{1,0:T(8,128)(2,1)S(1)}, bf16[160,1280]{1,0:T(8,128)(2,1)S(1)}, u32[]{:S(2)}, u32[]{:S(2)}) collective-permute-start(bf16[160,1280]{1,0:T(8,128)(2,1)S(1)} %get-tuple-element.379), channel_id=1, source_target_pairs={{0,8},{8,16},{16,24},{24,28},{28,20},{20,12},{12,4},{4,0},{1,9},{9... | collective-permute-start | bytes 1228808 | tf_op jit(solution)/shard_map/ppermute | solution.py:543
  541.1 13.4 %collective-permute-start.68 = (bf16[160,1280]{1,0:T(8,128)(2,1)S(1)}, bf16[160,1280]{1,0:T(8,128)(2,1)S(1)}, u32[]{:S(2)}, u32[]{:S(2)}) collective-permute-start(bf16[160,1280]{1,0:T(8,128)(2,1)S(1)} %get-tuple-element.380), channel_id=1, source_target_pairs={{8,0},{16,8},{24,16},{28,24},{20,28},{12,20},{4,12},{0,4},{9,1},{1... | collective-permute-start | bytes 1228808 | tf_op jit(solution)/shard_map/ppermute | solution.py:543
  546.9 16.4 %collective-permute-start.56 = (bf16[160,1280]{1,0:T(8,128)(2,1)S(1)}, bf16[160,1280]{1,0:T(8,128)(2,1)S(1)}, u32[]{:S(2)}, u32[]{:S(2)}) collective-permute-start(bf16[160,1280]{1,0:T(8,128)(2,1)S(1)} %add_convert_fusion.14), channel_id=1, source_target_pairs={{0,8},{8,16},{16,24},{24,28},{28,20},{20,12},{12,4},{4,0},{1,9},{9... | collective-permute-start | bytes 1228808 | tf_op jit(solution)/shard_map/ppermute | solution.py:543
  555.8 16.2 %collective-permute-start.64 = (bf16[160,1280]{1,0:T(8,128)(2,1)S(1)}, bf16[160,1280]{1,0:T(8,128)(2,1)S(1)}, u32[]{:S(2)}, u32[]{:S(2)}) collective-permute-start(bf16[160,1280]{1,0:T(8,128)(2,1)S(1)} %get-tuple-element.377), channel_id=1, source_target_pairs={{0,8},{8,16},{16,24},{24,28},{28,20},{20,12},{12,4},{4,0},{1,9},{9... | collective-permute-start | bytes 1228808 | tf_op jit(solution)/shard_map/ppermute | solution.py:543
  558.4 13.7 %collective-permute-start.69 = (bf16[160,1280]{1,0:T(8,128)(2,1)S(1)}, bf16[160,1280]{1,0:T(8,128)(2,1)S(1)}, u32[]{:S(2)}, u32[]{:S(2)}) collective-permute-start(bf16[160,1280]{1,0:T(8,128)(2,1)S(1)} %get-tuple-element.378), channel_id=1, source_target_pairs={{8,0},{16,8},{24,16},{28,24},{20,28},{12,20},{4,12},{0,4},{9,1},{1... | collective-permute-start | bytes 1228808 | tf_op jit(solution)/shard_map/ppermute | solution.py:543
  564.6 16.0 %collective-permute-start.57 = (bf16[160,1280]{1,0:T(8,128)(2,1)S(1)}, bf16[160,1280]{1,0:T(8,128)(2,1)S(1)}, u32[]{:S(2)}, u32[]{:S(2)}) collective-permute-start(bf16[160,1280]{1,0:T(8,128)(2,1)S(1)} %get-tuple-element.383), channel_id=1, source_target_pairs={{0,8},{8,16},{16,24},{24,28},{28,20},{20,12},{12,4},{4,0},{1,9},{9... | collective-permute-start | bytes 1228808 | tf_op jit(solution)/shard_map/ppermute | solution.py:543
  567.1 13.4 %collective-permute-start.59 = (bf16[160,1280]{1,0:T(8,128)(2,1)S(1)}, bf16[160,1280]{1,0:T(8,128)(2,1)S(1)}, u32[]{:S(2)}, u32[]{:S(2)}) collective-permute-start(bf16[160,1280]{1,0:T(8,128)(2,1)S(1)} %get-tuple-element.384), channel_id=1, source_target_pairs={{8,0},{16,8},{24,16},{28,24},{20,28},{12,20},{4,12},{0,4},{9,1},{1... | collective-permute-start | bytes 1228808 | tf_op jit(solution)/shard_map/ppermute | solution.py:543
  573.4 11.7 %collective-permute-start.65 = (bf16[160,1280]{1,0:T(8,128)(2,1)S(1)}, bf16[160,1280]{1,0:T(8,128)(2,1)S(1)}, u32[]{:S(2)}, u32[]{:S(2)}) collective-permute-start(bf16[160,1280]{1,0:T(8,128)(2,1)S(1)} %get-tuple-element.375), channel_id=1, source_target_pairs={{0,8},{8,16},{16,24},{24,28},{28,20},{20,12},{12,4},{4,0},{1,9},{9... | collective-permute-start | bytes 1228808 | tf_op jit(solution)/shard_map/ppermute | solution.py:543
  576.2 12.1 %collective-permute-start.70 = (bf16[160,1280]{1,0:T(8,128)(2,1)S(1)}, bf16[160,1280]{1,0:T(8,128)(2,1)S(1)}, u32[]{:S(2)}, u32[]{:S(2)}) collective-permute-start(bf16[160,1280]{1,0:T(8,128)(2,1)S(1)} %get-tuple-element.376), channel_id=1, source_target_pairs={{8,0},{16,8},{24,16},{28,24},{20,28},{12,20},{4,12},{0,4},{9,1},{1... | collective-permute-start | bytes 1228808 | tf_op jit(solution)/shard_map/ppermute | solution.py:543
  581.9 14.2 %collective-permute-start.60 = (bf16[160,1280]{1,0:T(8,128)(2,1)S(1)}, bf16[160,1280]{1,0:T(8,128)(2,1)S(1)}, u32[]{:S(2)}, u32[]{:S(2)}) collective-permute-start(bf16[160,1280]{1,0:T(8,128)(2,1)S(1)} %get-tuple-element.382), channel_id=1, source_target_pairs={{8,0},{16,8},{24,16},{28,24},{20,28},{12,20},{4,12},{0,4},{9,1},{1... | collective-permute-start | bytes 1228808 | tf_op jit(solution)/shard_map/ppermute | solution.py:543
  608.3 12.7 %collective-permute-start.77 = (f32[325,256]{1,0:T(8,128)}, f32[325,256]{1,0:T(8,128)}, u32[]{:S(2)}, u32[]{:S(2)}) collective-permute-start(f32[325,256]{1,0:T(8,128)} %fusion.32), channel_id=1, source_target_pairs={{0,2},{1,3},{2,0},{3,1},{4,6},{5,7},{6,4},{7,5},{8,10},{9,11},{10,... | collective-permute-start | bytes 998408 | tf_op jit(solution)/shard_map/ppermute | solution.py:565
  631.2 11.9 %collective-permute-start.54 = (f32[640]{0:T(1024)S(1)}, f32[640]{0:T(1024)S(1)}, u32[]{:S(2)}, u32[]{:S(2)}) collective-permute-start(f32[640]{0:T(1024)S(1)} %add.842), channel_id=1, source_target_pairs={{0,16},{4,20},{8,24},{12,28},{16,0},{20,4},{24,8},{28,12},{1,17},{... | collective-permute-start | bytes 7688 | tf_op jit(solution)/shard_map/ppermute | solution.py:565
  (60 other events, 961.2 us)
Sparse Core Ops, SparseCore 0:
  14.2 55.6 all-gather.8
  115.3 118.9 all-gather.4
  235.9 42.6 all-gather.6
  334.2 50.2 reduce-scatter.3
  463.6 67.4 reduce-scatter.7
  533.4 50.7 reduce-scatter.5

commit v7 on v6

--- a/solution.py
+++ b/solution.py
@@ -558,6 +558,22 @@
     return [(k, k ^ bit) for k in range(count)]
 
 
+def halving_sum(partial, axis):
+    count = lax.axis_size(axis)
+    me = lax.axis_index(axis)
+    held = partial.reshape(count, partial.shape[0] // count, partial.shape[1])
+    bit = 1
+    while bit < count:
+        pairs = held.reshape(held.shape[0] // 2, 2, *held.shape[1:])
+        mine = (me // bit) % 2
+        kept = row_major(lax.dynamic_index_in_dim(pairs, mine, 1, keepdims=False))
+        given = row_major(lax.dynamic_index_in_dim(pairs, 1 - mine, 1, keepdims=False))
+        got = row_major(lax.ppermute(given, axis, flips(count, bit)))
+        held = row_major((kept.astype(wide) + got.astype(wide)).astype(partial.dtype))
+        bit *= 2
+    return held[0]
+
+
 def butterfly_sum(v, axis):
     count = lax.axis_size(axis)
     bit = 1
@@ -572,7 +588,7 @@
 
 
 def row_major(v):
-    return with_layout_constraint(v, Layout((0, 1)))
+    return with_layout_constraint(v, Layout(tuple(range(v.ndim))))
 
 
 def together(*values):
@@ -610,10 +626,9 @@
     state_cols = state_weight.shape[1]
     col_start = lax.axis_index("gy") * col_width
 
-    state_step_weight = jnp.concatenate([state_weight, step_weight], 1)
-    full_state = lax.all_gather(state_step_weight, "gx", axis=0, tiled=True)
+    inner = gate_weight.shape[1]
     upstream = lax.all_gather(cotangent, "gy", axis=1, tiled=True)
-    value_gather = RingGather(value_weight)
+    value_gather = RingGather(jnp.concatenate([value_weight, state_weight, step_weight], 1))
     value_gather.step()
     tokens = tie(layer_input, value_gather).astype(wide)
     scale_in = lax.rsqrt(jnp.mean(tokens * tokens, axis=1, keepdims=True) + epsilon)
@@ -622,13 +637,14 @@
     normed = tie(normed, value_gather)
     value_gather.step(value_gather.count)
     gate_shard = tie(gate_weight, value_gather)
+    gate_shard, upstream = together(gate_shard, upstream)
     full_gate = lax.all_gather(gate_shard, "gx", axis=0, tiled=True)
-    full_value = value_gather.finish()
+    full_value_state = value_gather.finish()
 
     out_gather = RingGather(tie(out_weight.T, value_gather))
     out_gather.step()
     normed = tie(normed, out_gather)
-    state_step = dot(normed, full_state)
+    state_step = dot(normed, full_value_state[:, inner:])
     mixer = Mixer(
         state_step[:, :state_cols],
         state_step[:, state_cols:],
@@ -641,7 +657,7 @@
     out_gather.step()
     normed, mixer.g = together(normed, mixer.g)
     normed = tie(normed, out_gather)
-    value_in = dot(normed, full_value)
+    value_in = dot(normed, full_value_state[:, :inner])
     out_gather.step()
     value_in = tie(value_in, out_gather)
     mixed = mixer.forward(value_in, conv_value, conv_value_bias, skip_scale)
@@ -649,7 +665,6 @@
     mixed = mixer.mixed = tie(mixer.mixed, out_gather)
     mixed = mixed[:, : mixer.inner]
     full_out = out_gather.finish()
-    full_value_state = jnp.concatenate([full_value, full_state], 1)
     gate_in = dot(normed, full_gate)
     gate_open = jax.nn.sigmoid(gate_in)
     gate_act = gate_in * gate_open
@@ -667,42 +682,40 @@
     scaled = (gated * gated_gain).astype(low)
 
     scaled_out = (gated * gated_gain * scale_out).astype(low)
-    out_ring = RingSum(row_major(contract_rows(upstream, scaled_out).astype(low)))
-
-    scaled = tie(scaled, out_ring)
-    product_part = contract_cols(full_out, scaled)
-    product_part = row_major((product_part * scale_out[:, 0]).astype(low))
-    product = lax.psum_scatter(product_part, "gy", scatter_dimension=0, tiled=True)
-
-    out_ring.step()
-    up_back, product_part = together(up_back, product_part)
-    grad_scaled = scale_out * tie(up_back, out_ring)
+    out_partial = row_major(contract_rows(upstream, scaled_out).astype(low))
+    up_back, out_partial = together(up_back, out_partial)
+    grad_out = scatter_rows(out_partial)
+
+    grad_scaled = scale_out * up_back
     grad_gated = grad_scaled * gated_gain - grad_scale * scale_out**3 * gated / INNER
     gate_gain_part = jnp.sum(grad_scaled * gated, axis=0)
     grad_gate_in = (
         grad_gated * mixed * gate_open * (1.0 + gate_in * (1.0 - gate_open))
     ).astype(low)
     grad_mixed = grad_gated * gate_act
-    out_ring.step()
-    normed = tie(normed, out_ring)
     gate_ring = RingSum(row_major(contract_rows(normed, grad_gate_in).astype(low)))
 
+    gate_ring.step()
+    scaled = tie(scaled, gate_ring)
+    product_part = contract_cols(full_out, scaled)
+    product_part = row_major((product_part * scale_out[:, 0]).astype(low))
+    grad_mixed, product_part = together(grad_mixed, product_part)
+    product = halving_sum(product_part, "gy")
+
     half = (mixer.pairs + 1) // 2
-    out_ring.step()
-    grad_mixed = tie(grad_mixed, out_ring, gate_ring)
+    gate_ring.step()
+    grad_mixed = tie(grad_mixed, gate_ring)
     part = mixer.backward_part(grad_mixed, 0, half)
-    out_ring.step()
     gate_ring.step()
-    grad_mixed = tie(grad_mixed, out_ring, gate_ring)
+    grad_mixed = tie(grad_mixed, gate_ring)
     value_grad, value_sums, *totals = mixer.backward_part(grad_mixed, half, mixer.pairs, part)
-    grad_value_in = value_grad[:, : gate_weight.shape[1]]
-    out_ring.step()
+    grad_value_in = value_grad[:, :inner]
     gate_ring.step()
-    normed = tie(normed, out_ring, gate_ring)
+    normed = tie(normed, gate_ring)
     value_ring = RingSum(row_major(contract_rows(normed, grad_value_in).astype(low)))
-    out_ring.step()
     gate_ring.step()
-    totals[0] = tie(totals[0], out_ring, gate_ring, value_ring)
+    totals[0] = tie(totals[0], gate_ring, value_ring)
+    totals[0], product = together(totals[0], product)
     ends = mixer.backward_end(*totals)
     pulled = mixer.gradients(value_grad, value_sums, *ends)
     grad_state_in = jnp.concatenate([pulled[1], pulled[2]], 1)
@@ -710,16 +723,17 @@
     grad_state_step = scatter_rows(state_partial).astype(wide)
 
     value_ring.step()
-    grad_gate_in = tie(grad_gate_in, value_ring)
+    gate_ring.step()
+    grad_gate_in = tie(grad_gate_in, gate_ring, value_ring)
     grad_normed_part = contract_cols(full_gate, grad_gate_in)
     grad_value_state_in = jnp.concatenate([grad_value_in, grad_state_in], 1)
-    out_ring.step()
+    value_ring.step()
     gate_ring.step()
-    grad_value_state_in = tie(grad_value_state_in, out_ring, gate_ring)
-    grad_value_state_in, product = together(grad_value_state_in, product)
+    grad_value_state_in = tie(grad_value_state_in, gate_ring, value_ring)
     grad_normed_part = grad_normed_part + contract_cols(full_value_state, grad_value_state_in)
     grad_normed_part = row_major(grad_normed_part.astype(low))
-    grad_out = out_ring.finish()
+    value_ring.step()
+    grad_out = tie(grad_out, value_ring)
     grad_gate = gate_ring.finish()
     grad_value = value_ring.finish()
 
@@ -765,7 +779,7 @@
         sums[6],
         sums[7],
         sums[0],
-        grad_out.T,
+        grad_out.T.astype(wide),
     )
 
 

time: 659 us -> 716 us (1.086)
  waiting for transfers between devices: 171 us -> 255 us
  other arithmetic: 82.9 us -> 65.4 us
  starting transfers between devices: 92.4 us -> 79 us
    ppermute x42 -> x28, waiting for transfers between devices: 43.3 us -> 90.1 us  [step(): lax.ppermute(held, 'gx', move).astype(wide)]
    reduce_scatter x1, waiting for transfers between devices: 0.02 us -> 18 us  [on_device(): lax.psum_scatter(grad_normed_part, 'gy', scatter_dimension=0, tiled=True)]
    convert_element_type x18 -> x12, other arithmetic: 30.7 us -> 14.3 us  [step(): up, down = (up.astype(low), down.astype(low))]
    ppermute x42 -> x28, starting transfers between devices: 51 us -> 34.8 us  [step(): lax.ppermute(held, 'gx', move).astype(wide)]
    reduce_scatter x1 -> x2, waiting for transfers between devices: 0.02 us -> 11.9 us  [scatter_rows(): return lax.psum_scatter(partial, 'gx', scatter_dimension=0, tiled=True)]
    ppermute x8, waiting for transfers between devices: 4.52 us -> 15.4 us  [butterfly_sum(): v = v + lax.ppermute(v, axis, flips(count, bit))]
    broadcast_in_dim x0 -> x2, local copies, waits for them, and re-layouts: none -> 7.53 us  [__init__(): full = jnp.zeros((self.count * self.rows, width), shard.dtype)]
    unnamed x90 -> x76, local copies, waits for them, and re-layouts: 18.2 us -> 18.8 us
  transfers between devices with their start and end apart: 84 -> 71, of which waited for: 37 -> 43; matrix products, arithmetic and copies ran while one was open for 38% -> 26% of each run, Pallas kernels for 13% -> 12%
where the time goes in v7:
time: 716 us; the launch traced here: 705 us
  waiting for transfers between devices  255 us (36%)
  matrix products  122 us (17%)
  Pallas kernels  83.5 us (12%)
  starting transfers between devices  79 us (11%)
  local copies, waits for them, and re-layouts  73.4 us (10%)
  other arithmetic  65.4 us (9%)
  between operations  14.6 us (2%)
  blocking collectives  12.1 us (2%)
    ppermute x28, waiting for transfers between devices, step(): lax.ppermute(held, 'gx', move)  119 us
    ppermute x28, waiting for transfers between devices, step(): lax.ppermute(held, 'gx', move).astype(wide)  90.1 us
    pallas_call x5, Pallas kernels, call(): pl.pallas_call(kernel, out_shape=shapes, scratch_shapes=list(scratch), co...  83.5 us
    dot_general x4, matrix products, dot(): jnp.dot(left, right, preferred_element_type=wide, precision=precision)  44.2 us
    dot_general x4, matrix products, contract_rows(): lax.dot_general(left, right, (((0,), (0,)), ((), ())), preferred_element_...  39.5 us
    dot_general x3, matrix products, contract_cols(): lax.dot_general(left, right, (((1,), (1,)), ((), ())), preferred_element_...  37.8 us
    ppermute x28, starting transfers between devices, step(): lax.ppermute(held, 'gx', move).astype(wide)  34.8 us
    ppermute x28, starting transfers between devices, step(): lax.ppermute(held, 'gx', move)  30.3 us
  transfers between devices with their start and end apart: 71, of which 43 were waited for; matrix products, arithmetic and copies ran while one was open for 26% of the time, Pallas kernels for 12%

profile of v7, /device:TPU:0, one launch (start us, length us, event | category | flops | bytes accessed | tf_op | source)
XLA Modules:
  0.0 705.1 jit_solution(4878960246312360542)
XLA Ops:
  8.8 3.8 broadcast_in_dim.24
  13.9 3.0 collective-permute-start
  17.0 12.0 %collective-permute-done = bf16[160,1556]{1,0:T(8,128)(2,1)S(1)} collective-permute-done((bf16[160,1556]{1,0:T(8,128)(2,1)S(1)}, bf16[160,1556]{1,0:T(8,128)(2,1)S(1)}, u32[]{:S(2)}, u32[]{:S(2)}) %collective-permute-start) | collective-permute-done | bytes 497952 | tf_op jit(solution)/shard_map/ppermute | solution.py:510
  32.5 3.6 fusion
  36.7 6.0 fusion.2
  48.3 8.5 %collective-permute-done.6 = bf16[160,1556]{1,0:T(8,128)(2,1)S(1)} collective-permute-done((bf16[160,1556]{1,0:T(8,128)(2,1)S(1)}, bf16[160,1556]{1,0:T(8,128)(2,1)S(1)}, u32[]{:S(2)}, u32[]{:S(2)}) %collective-permute-start.6) | collective-permute-done | bytes 497952 | tf_op jit(solution)/shard_map/ppermute | solution.py:510
  61.8 7.2 %collective-permute-done.8 = bf16[160,1556]{1,0:T(8,128)(2,1)S(1)} collective-permute-done((bf16[160,1556]{1,0:T(8,128)(2,1)S(1)}, bf16[160,1556]{1,0:T(8,128)(2,1)S(1)}, u32[]{:S(2)}, u32[]{:S(2)}) %collective-permute-start.8) | collective-permute-done | bytes 497952 | tf_op jit(solution)/shard_map/ppermute | solution.py:510
  76.0 6.4 collective-permute-done.10
  88.5 8.4 %collective-permute-done.12 = bf16[160,1556]{1,0:T(8,128)(2,1)S(1)} collective-permute-done((bf16[160,1556]{1,0:T(8,128)(2,1)S(1)}, bf16[160,1556]{1,0:T(8,128)(2,1)S(1)}, u32[]{:S(2)}, u32[]{:S(2)}) %collective-permute-start.12) | collective-permute-done | bytes 497952 | tf_op jit(solution)/shard_map/ppermute | solution.py:510
  101.6 8.6 %collective-permute-done.14 = bf16[160,1556]{1,0:T(8,128)(2,1)S(1)} collective-permute-done((bf16[160,1556]{1,0:T(8,128)(2,1)S(1)}, bf16[160,1556]{1,0:T(8,128)(2,1)S(1)}, u32[]{:S(2)}, u32[]{:S(2)}) %collective-permute-start.14) | collective-permute-done | bytes 497952 | tf_op jit(solution)/shard_map/ppermute | solution.py:510
  118.2 3.7 broadcast_in_dim.50
  122.8 4.7 collective-permute-done.4
  127.5 3.1 collective-permute-done.5
  130.6 2.5 collective-permute-start.17
  136.7 8.5 %collective-permute-done.16 = bf16[160,1280]{1,0:T(8,128)(2,1)S(1)} collective-permute-done((bf16[160,1280]{1,0:T(8,128)(2,1)}, bf16[160,1280]{1,0:T(8,128)(2,1)S(1)}, u32[]{:S(2)}, u32[]{:S(2)}) %collective-permute-start.16) | collective-permute-done | bytes 409632 | tf_op jit(solution)/shard_map/ppermute | solution.py:510
  145.1 9.6 %collective-permute-done.17 = bf16[160,1280]{1,0:T(8,128)(2,1)S(1)} collective-permute-done((bf16[160,1280]{1,0:T(8,128)(2,1)}, bf16[160,1280]{1,0:T(8,128)(2,1)S(1)}, u32[]{:S(2)}, u32[]{:S(2)}) %collective-permute-start.17) | collective-permute-done | bytes 409632 | tf_op jit(solution)/shard_map/ppermute | solution.py:510
  158.0 4.4 fusion.18
  166.2 17.5 %shard_map.288 = (bf16[1024,128]{1,0:T(8,128)(2,1)}, bf16[1024,128]{1,0:T(8,128)(2,1)}, bf16[128,1024]{1,0:T(8,128)(2,1)}, bf16[128,1024]{1,0:T(8,128)(2,1)}, f3...) custom-call(f32[1024,256]{1,0:T(8,128)} %slice.158.state_ref, ...), custom_call_target="tpu_custom_call" | custom-call | flops 2013265920 | bytes 17315840 | tf_op jit(solution)/shard_map/pallas_call | solution.py:293
  185.9 11.6 %fusion.3.value_ref = f32[1024,1280]{1,0:T(8,128)} fusion(bf16[1024,2560]{1,0:T(8,128)(2,1)S(1)} %bitcast.77, bf16[2560,1556]{1,0:T(8,128)(2,1)} %constant_dynamic-update-slice_fusion.14), kind=kOutput, calls=%fused_computation.10 | convolution fusion | flops 6710886400 | bytes 17039360 | tf_op jit(solution)/shard_map/dot_general | solution.py:25
  200.4 14.4 %collective-permute-done.19 = bf16[160,1280]{1,0:T(8,128)(2,1)S(1)} collective-permute-done((bf16[160,1280]{1,0:T(8,128)(2,1)S(1)}, bf16[160,1280]{1,0:T(8,128)(2,1)S(1)}, u32[]{:S(2)}, u32[]{:S(2)}) %collective-permute-start.19) | collective-permute-done | bytes 409632 | tf_op jit(solution)/shard_map/ppermute | solution.py:510
  218.4 18.2 %shard_map.289.mixed_ref = f32[1024,1280]{1,0:T(8,128)} custom-call(f32[1024,1280]{1,0:T(8,128)} %fusion.3.value_ref, f32[4,1280]{1,0:T(4,128)} %taps_ref.8, f32[1,1280]{1,0:T(1,128)} %broadcast_in_dim.58.bias_ref, f32[1,1280]{1,0:T(1,128)} %broadcast_in_dim_reshape.3.skip_ref, f32[1024,1280]{1,0:T(8,128)} %get-tuple-element.188.dtx_ref, ...), custom_call_target="tpu_custom_call" | custom-call | flops 3355443200 | bytes 24754176 | tf_op jit(solution)/shard_map/pallas_call | solution.py:293
  240.3 5.2 collective-permute-done.22
  249.4 4.3 collective-permute-done.24
  259.3 4.3 collective-permute-done.26
  267.2 13.9 %multiply_convert_fusion.3 = (bf16[1024,1280]{1,0:T(8,128)(2,1)}, f32[1024,1280]{1,0:T(8,128)S(1)}, f32[1024,1280]{1,0:T(8,128)}) fusion(f32[1280]{0:T(1024)S(1)} %copy-done.25, f32[1024,1280]{1,0:T(8,128)} %shard_map.289.mixed_ref, bf16[1024,2560]{1,0:T(8,128)(2,1)} %fusion.2, bf16[2560,1280]{1,0:T(8,128)(2,1)} %all-gather.5.cloned.1.call-done), kind=kOutput, calls=%fused_computation.21 | convolution fusion | flops 6720061440 | bytes 30151680 | tf_op jit(solution)/shard_map/dot_general | solution.py:25
  281.1 14.4 %multiply_reduce_fusion.2 = (f32[1024]{0:T(1024)S(1)}, f32[1024]{0:T(1024)S(1)}, f32[1024,1280]{1,0:T(8,128)}) fusion(f32[1024,1280]{1,0:T(8,128)S(1)} %get-tuple-element.327, f32[1280]{0:T(1024)S(1)} %copy-done.25, bf16[1024,2560]{1,0:T(8,128)(2,1)} %all-gather.3.cloned.1.call-done, bf16[2560,1280]{1,0:T(8,128)(2,1)} %constant_dynamic-update-slice_fusion), kind=kOutput, calls=%fused_computation.18 | convolution fusion | flops 6717437952 | bytes 22295552 | tf_op jit(solution)/shard_map/dot_general | solution.py:25
  295.5 6.1 psum.14
  301.6 12.6 %convolution_convert_fusion.2 = bf16[2560,1280]{1,0:T(8,128)(2,1)} fusion(bf16[1024,2560]{1,0:T(8,128)(2,1)} %all-gather.3.cloned.1.call-done, f32[1024,1280]{1,0:T(8,128)} %copy-done.7, f32[1024]{0:T(1024)S(1)} %bitcast.92, f32[1280]{0:T(1024)S(1)} %copy-done.25), kind=kOutput, calls=%fused_computation.4 | convolution fusion | flops 6718095360 | bytes 17048576 | tf_op jit(solution)/shard_map/dot_general | solution.py:29
  314.3 10.6 %multiply_convert_fusion.1 = (bf16[1024,1280]{1,0:T(8,128)(2,1)S(1)}, f32[1024,1280]{1,0:T(8,128)}, f32[1280]{0:T(1024)S(1)}) fusion(f32[1024,1280]{1,0:T(8,128)} %get-tuple-element.385, f32[1024,1280]{1,0:T(8,128)} %shard_map.289.mixed_ref, f32[1024,1280]{1,0:T(8,128)} %copy-done.7, f32[1024]{0:T(1024)S(1)} %fusion.25, f32[1024,1280]{1,0:T(8,128)} %get-tuple-element.215, ...), kind=kLoop, calls=%fused_computation.14 | loop fusion | flops 24902400 | bytes 28854272 | tf_op jit(solution)/shard_map/convert_element_type | solution.py:694
  324.8 10.1 %convolution_convert_fusion.1 = bf16[2560,1280]{1,0:T(8,128)(2,1)S(1)} fusion(bf16[1024,2560]{1,0:T(8,128)(2,1)} %fusion.2, bf16[1024,1280]{1,0:T(8,128)(2,1)S(1)} %get-tuple-element.248), kind=kOutput, calls=%fused_computation.3 | convolution fusion | flops 6714163200 | bytes 14417920 | tf_op jit(solution)/shard_map/dot_general | solution.py:29
  334.9 2.7 copy-done.2
  339.9 11.0 %collective-permute-done.28 = bf16[160,1280]{1,0:T(8,128)(2,1)S(1)} collective-permute-done((bf16[160,1280]{1,0:T(8,128)(2,1)S(1)}, bf16[160,1280]{1,0:T(8,128)(2,1)S(1)}, u32[]{:S(2)}, u32[]{:S(2)}) %collective-permute-start.28) | collective-permute-done | bytes 409632 | tf_op jit(solution)/shard_map/ppermute | solution.py:543
  350.9 4.6 collective-permute-done.29
  359.5 10.5 %multiply_convert_fusion = bf16[2560,1024]{1,0:T(8,128)(2,1)S(1)} fusion(bf16[2560,1280]{1,0:T(8,128)(2,1)} %constant_dynamic-update-slice_fusion, bf16[1024,1280]{1,0:T(8,128)(2,1)} %get-tuple-element.216, f32[1024]{0:T(1024)S(1)} %bitcast.95), kind=kOutput, calls=%fused_computation.9 | convolution fusion | flops 6716129280 | bytes 14422016 | tf_op jit(solution)/shard_map/dot_general | solution.py:35
  374.4 12.9 %collective-permute-done.31 = bf16[160,1280]{1,0:T(8,128)(2,1)S(1)} collective-permute-done((bf16[160,1280]{1,0:T(8,128)(2,1)S(1)}, bf16[160,1280]{1,0:T(8,128)(2,1)S(1)}, u32[]{:S(2)}, u32[]{:S(2)}) %collective-permute-start.31) | collective-permute-done | bytes 409632 | tf_op jit(solution)/shard_map/ppermute | solution.py:543
  389.5 20.0 %shard_map.290 = (bf16[1024,1280]{1,0:T(8,128)(2,1)}, f32[8,1280]{1,0:T(8,128)}, f32[1024,128]{1,0:T(8,128)}, f32[1024,128]{1,0:T(8,128)}, f32[1024,128]{1,0:T(8...) custom-call(f32[1024,1280]{1,0:T(8,128)} %fusion.3.value_ref, f32[1024,1280]{1,0:T(8,128)} %shard_map.289.mixed_ref, ...), custom_call_target="tpu_custom_call" | custom-call | flops 5033164800 | bytes 35805184 | tf_op jit(solution)/shard_map/pallas_call | solution.py:293
  409.6 7.2 %collective-permute-done.33 = bf16[160,1280]{1,0:T(8,128)(2,1)S(1)} collective-permute-done((bf16[160,1280]{1,0:T(8,128)(2,1)S(1)}, bf16[160,1280]{1,0:T(8,128)(2,1)S(1)}, u32[]{:S(2)}, u32[]{:S(2)}) %collective-permute-start.33) | collective-permute-done | bytes 409632 | tf_op jit(solution)/shard_map/ppermute | solution.py:543
  419.1 20.8 %shard_map.291 = (bf16[1024,1280]{1,0:T(8,128)(2,1)}, f32[8,1280]{1,0:T(8,128)}, f32[1024,128]{1,0:T(8,128)}, f32[1024,128]{1,0:T(8,128)}, f32[1024,128]{1,0:T(8...) custom-call(f32[1024,1280]{1,0:T(8,128)} %fusion.3.value_ref, ...), custom_call_target="tpu_custom_call", output_to_operand_aliasing={{0}: (15, {}), {1}: (16, {})} | custom-call | flops 5033164800 | bytes 41089024 | tf_op jit(solution)/shard_map/pallas_call | solution.py:293
  442.3 9.8 %convolution_convert_fusion = bf16[2560,1280]{1,0:T(8,128)(2,1)S(1)} fusion(bf16[1024,2560]{1,0:T(8,128)(2,1)} %fusion.2, bf16[1024,1280]{1,0:T(8,128)(2,1)} %get-tuple-element.240), kind=kOutput, calls=%fused_computation.2 | convolution fusion | flops 6714163200 | bytes 14417920 | tf_op jit(solution)/shard_map/dot_general | solution.py:29
  452.1 2.7 copy-done.1
  459.2 11.5 %collective-permute-done.42 = bf16[160,1280]{1,0:T(8,128)(2,1)S(1)} collective-permute-done((bf16[160,1280]{1,0:T(8,128)(2,1)S(1)}, bf16[160,1280]{1,0:T(8,128)(2,1)S(1)}, u32[]{:S(2)}, u32[]{:S(2)}) %collective-permute-start.42) | collective-permute-done | bytes 409632 | tf_op jit(solution)/shard_map/ppermute | solution.py:543
  472.1 11.7 %collective-permute-done.40 = bf16[160,1280]{1,0:T(8,128)(2,1)S(1)} collective-permute-done((bf16[160,1280]{1,0:T(8,128)(2,1)S(1)}, bf16[160,1280]{1,0:T(8,128)(2,1)S(1)}, u32[]{:S(2)}, u32[]{:S(2)}) %collective-permute-start.40) | collective-permute-done | bytes 409632 | tf_op jit(solution)/shard_map/ppermute | solution.py:543
  483.7 6.9 collective-permute-done.41
  492.0 5.1 collective-permute-start.46
  497.1 2.9 collective-permute-start.44
  500.0 3.8 add_convert_fusion.1
  503.9 4.2 collective-permute-start.39
  508.2 11.5 %fusion.35 = f32[2560,1024]{1,0:T(8,128)} fusion(bf16[2560,1280]{1,0:T(8,128)(2,1)} %all-gather.5.cloned.1.call-done, bf16[1024,1280]{1,0:T(8,128)(2,1)S(1)} %copy-done.10), kind=kOutput, calls=%fused_computation.147 | convolution fusion | flops 6710886400 | bytes 19660800 | tf_op jit(solution)/shard_map/dot_general | solution.py:35
  525.7 7.0 shard_map.292
  532.7 7.0 convolution_convert_fusion.3
  541.3 15.8 %add_convert_fusion = bf16[2560,1024]{1,0:T(8,128)(2,1)} fusion(f32[2560,1024]{1,0:T(8,128)} %fusion.35, bf16[2560,1556]{1,0:T(8,128)(2,1)} %constant_dynamic-update-slice_fusion.14, bf16[1024,1556]{1,0:T(8,128)(2,1)S(1)} %pad_maximum_fusion), kind=kOutput, calls=%fused_computation.8 | convolution fusion | flops 8163164160 | bytes 26882048 | tf_op jit(solution)/shard_map/dot_general | solution.py:35
  560.4 13.0 %collective-permute-done.51 = bf16[160,1280]{1,0:T(8,128)(2,1)S(1)} collective-permute-done((bf16[160,1280]{1,0:T(8,128)(2,1)S(1)}, bf16[160,1280]{1,0:T(8,128)(2,1)S(1)}, u32[]{:S(2)}, u32[]{:S(2)}) %collective-permute-start.51) | collective-permute-done | bytes 409632 | tf_op jit(solution)/shard_map/ppermute | solution.py:543
  576.4 2.9 collective-permute-start.53
  582.4 7.6 %collective-permute-done.61 = f32[9020]{0:T(1024)S(1)} collective-permute-done((f32[9020]{0:T(1024)S(1)}, f32[9020]{0:T(1024)S(1)}, u32[]{:S(2)}, u32[]{:S(2)}) %collective-permute-start.61) | collective-permute-done | bytes 36112 | tf_op jit(solution)/shard_map/ppermute | solution.py:581
  590.1 3.9 collective-permute-done.62
  599.8 11.9 %reduce-scatter.8.cloned.1.call-done = bf16[320,276]{1,0:T(8,128)(2,1)} async-done(((bf16[2560,276]{1,0:T(8,128)(2,1)}), bf16[320,276]{1,0:T(8,128)(2,1)}) %reduce-scatter.8.cloned.1.call-update) | async-done | bytes 176656 | tf_op jit(solution)/shard_map/reduce_scatter | solution.py:587
  620.2 4.7 collective-permute-done.57
  635.4 3.2 collective-permute-done.55
  646.5 18.0 %reduce-scatter.4.cloned.1.call-done = bf16[640,1024]{1,0:T(8,128)(2,1)} async-done(((bf16[2560,1024]{1,0:T(8,128)(2,1)}), bf16[640,1024]{1,0:T(8,128)(2,1)}) %reduce-scatter.4.cloned.1.call-update) | async-done | bytes 1310736 | tf_op jit(solution)/shard_map/reduce_scatter | solution.py:740
  664.4 2.6 fusion.12
  673.7 6.1 psum.15
  679.8 3.2 collective-permute-done.49
  685.4 5.1 fusion.9
  690.5 3.3 copy.67
  (302 shorter events, 168.2 us)
Async XLA Ops:
  7.2 103.9 %all-gather.3.cloned.1.call-start = ((), (), s32[]{:S(2)}) async-start(), calls=%async_computation.3 | async-start | bytes 6553600 | tf_op jit(solution)/shard_map/all_gather | solution.py:630
  7.9 259.3 %all-gather.5.cloned.1.call-start = ((), (), s32[]{:S(2)}) async-start(), calls=%async_computation.4 | async-start | bytes 7372800 | tf_op jit(solution)/shard_map/all_gather | solution.py:641
  13.9 15.1 %collective-permute-start = (bf16[160,1556]{1,0:T(8,128)(2,1)S(1)}, bf16[160,1556]{1,0:T(8,128)(2,1)S(1)}, u32[]{:S(2)}, u32[]{:S(2)}) collective-permute-start(bf16[160,1556]{1,0:T(8,128)(2,1)S(1)} %get-tuple-element.366), channel_id=1, source_target_pairs={{0,8},{8,16},{16,24},{24,28},{28,20},{20,12},{12,4},{4,0},{1,9},{9... | collective-permute-start | bytes 1493768 | tf_op jit(solution)/shard_map/ppermute | solution.py:510
  17.0 13.6 %collective-permute-start.1 = (bf16[160,1556]{1,0:T(8,128)(2,1)S(1)}, bf16[160,1556]{1,0:T(8,128)(2,1)S(1)}, u32[]{:S(2)}, u32[]{:S(2)}) collective-permute-start(bf16[160,1556]{1,0:T(8,128)(2,1)S(1)} %get-tuple-element.365), channel_id=1, source_target_pairs={{8,0},{16,8},{24,16},{28,24},{20,28},{12,20},{4,12},{0,4},{9,1},{1... | collective-permute-start | bytes 1493768 | tf_op jit(solution)/shard_map/ppermute | solution.py:510
  30.5 13.9 %collective-permute-start.2 = (bf16[160,1556]{1,0:T(8,128)(2,1)S(1)}, bf16[160,1556]{1,0:T(8,128)(2,1)S(1)}, u32[]{:S(2)}, u32[]{:S(2)}) collective-permute-start(bf16[160,1556]{1,0:T(8,128)(2,1)S(1)} %collective-permute-done), channel_id=1, source_target_pairs={{0,8},{8,16},{16,24},{24,28},{28,20},{20,12},{12,4},{4,0},{1,9},{9... | collective-permute-start | bytes 1493768 | tf_op jit(solution)/shard_map/ppermute | solution.py:510
  32.1 12.5 %collective-permute-start.3 = (bf16[160,1556]{1,0:T(8,128)(2,1)S(1)}, bf16[160,1556]{1,0:T(8,128)(2,1)S(1)}, u32[]{:S(2)}, u32[]{:S(2)}) collective-permute-start(bf16[160,1556]{1,0:T(8,128)(2,1)S(1)} %collective-permute-done.1), channel_id=1, source_target_pairs={{8,0},{16,8},{24,16},{28,24},{20,28},{12,20},{4,12},{0,4},{9,1},{1... | collective-permute-start | bytes 1493768 | tf_op jit(solution)/shard_map/ppermute | solution.py:510
  44.6 12.2 %collective-permute-start.6 = (bf16[160,1556]{1,0:T(8,128)(2,1)S(1)}, bf16[160,1556]{1,0:T(8,128)(2,1)S(1)}, u32[]{:S(2)}, u32[]{:S(2)}) collective-permute-start(bf16[160,1556]{1,0:T(8,128)(2,1)S(1)} %collective-permute-done.2), channel_id=1, source_target_pairs={{0,8},{8,16},{16,24},{24,28},{28,20},{20,12},{12,4},{4,0},{1,9},{9... | collective-permute-start | bytes 1493768 | tf_op jit(solution)/shard_map/ppermute | solution.py:510
  46.2 11.9 %collective-permute-start.7 = (bf16[160,1556]{1,0:T(8,128)(2,1)S(1)}, bf16[160,1556]{1,0:T(8,128)(2,1)S(1)}, u32[]{:S(2)}, u32[]{:S(2)}) collective-permute-start(bf16[160,1556]{1,0:T(8,128)(2,1)S(1)} %collective-permute-done.3), channel_id=1, source_target_pairs={{8,0},{16,8},{24,16},{28,24},{20,28},{12,20},{4,12},{0,4},{9,1},{1... | collective-permute-start | bytes 1493768 | tf_op jit(solution)/shard_map/ppermute | solution.py:510
  58.1 10.9 %collective-permute-start.8 = (bf16[160,1556]{1,0:T(8,128)(2,1)S(1)}, bf16[160,1556]{1,0:T(8,128)(2,1)S(1)}, u32[]{:S(2)}, u32[]{:S(2)}) collective-permute-start(bf16[160,1556]{1,0:T(8,128)(2,1)S(1)} %collective-permute-done.6), channel_id=1, source_target_pairs={{0,8},{8,16},{16,24},{24,28},{28,20},{20,12},{12,4},{4,0},{1,9},{9... | collective-permute-start | bytes 1493768 | tf_op jit(solution)/shard_map/ppermute | solution.py:510
  59.7 10.8 %collective-permute-start.9 = (bf16[160,1556]{1,0:T(8,128)(2,1)S(1)}, bf16[160,1556]{1,0:T(8,128)(2,1)S(1)}, u32[]{:S(2)}, u32[]{:S(2)}) collective-permute-start(bf16[160,1556]{1,0:T(8,128)(2,1)S(1)} %collective-permute-done.7), channel_id=1, source_target_pairs={{8,0},{16,8},{24,16},{28,24},{20,28},{12,20},{4,12},{0,4},{9,1},{1... | collective-permute-start | bytes 1493768 | tf_op jit(solution)/shard_map/ppermute | solution.py:510
  71.3 11.1 %collective-permute-start.10 = (bf16[160,1556]{1,0:T(8,128)(2,1)S(1)}, bf16[160,1556]{1,0:T(8,128)(2,1)S(1)}, u32[]{:S(2)}, u32[]{:S(2)}) collective-permute-start(bf16[160,1556]{1,0:T(8,128)(2,1)S(1)} %collective-permute-done.8), channel_id=1, source_target_pairs={{0,8},{8,16},{16,24},{24,28},{28,20},{20,12},{12,4},{4,0},{1,9},{9... | collective-permute-start | bytes 1493768 | tf_op jit(solution)/shard_map/ppermute | solution.py:510
  72.9 11.8 %collective-permute-start.11 = (bf16[160,1556]{1,0:T(8,128)(2,1)}, bf16[160,1556]{1,0:T(8,128)(2,1)S(1)}, u32[]{:S(2)}, u32[]{:S(2)}) collective-permute-start(bf16[160,1556]{1,0:T(8,128)(2,1)} %copy-done.13), channel_id=1, source_target_pairs={{8,0},{16,8},{24,16},{28,24},{20,28},{12,20},{4,12},{0,4},{9,1},{1... | collective-permute-start | bytes 1493768 | tf_op jit(solution)/shard_map/ppermute | solution.py:510
  84.7 12.1 %collective-permute-start.12 = (bf16[160,1556]{1,0:T(8,128)(2,1)S(1)}, bf16[160,1556]{1,0:T(8,128)(2,1)S(1)}, u32[]{:S(2)}, u32[]{:S(2)}) collective-permute-start(bf16[160,1556]{1,0:T(8,128)(2,1)S(1)} %collective-permute-done.10), channel_id=1, source_target_pairs={{0,8},{8,16},{16,24},{24,28},{28,20},{20,12},{12,4},{4,0},{1,9},{9... | collective-permute-start | bytes 1493768 | tf_op jit(solution)/shard_map/ppermute | solution.py:510
  85.5 12.4 %collective-permute-start.13 = (bf16[160,1556]{1,0:T(8,128)(2,1)S(1)}, bf16[160,1556]{1,0:T(8,128)(2,1)S(1)}, u32[]{:S(2)}, u32[]{:S(2)}) collective-permute-start(bf16[160,1556]{1,0:T(8,128)(2,1)S(1)} %collective-permute-done.11), channel_id=1, source_target_pairs={{8,0},{16,8},{24,16},{28,24},{20,28},{12,20},{4,12},{0,4},{9,1},{1... | collective-permute-start | bytes 1493768 | tf_op jit(solution)/shard_map/ppermute | solution.py:510
  97.9 12.4 %collective-permute-start.14 = (bf16[160,1556]{1,0:T(8,128)(2,1)S(1)}, bf16[160,1556]{1,0:T(8,128)(2,1)S(1)}, u32[]{:S(2)}, u32[]{:S(2)}) collective-permute-start(bf16[160,1556]{1,0:T(8,128)(2,1)S(1)} %collective-permute-done.12), channel_id=1, source_target_pairs={{0,8},{8,16},{16,24},{24,28},{28,20},{20,12},{12,4},{4,0},{1,9},{9... | collective-permute-start | bytes 1493768 | tf_op jit(solution)/shard_map/ppermute | solution.py:510
  98.3 12.8 %collective-permute-start.15 = (bf16[160,1556]{1,0:T(8,128)(2,1)S(1)}, bf16[160,1556]{1,0:T(8,128)(2,1)S(1)}, u32[]{:S(2)}, u32[]{:S(2)}) collective-permute-start(bf16[160,1556]{1,0:T(8,128)(2,1)S(1)} %collective-permute-done.13), channel_id=1, source_target_pairs={{8,0},{16,8},{24,16},{28,24},{20,28},{12,20},{4,12},{0,4},{9,1},{1... | collective-permute-start | bytes 1493768 | tf_op jit(solution)/shard_map/ppermute | solution.py:510
  111.2 465.2 %reduce-scatter.6.cloned.1.call-start = ((), (), s32[]{:S(2)}) async-start(), calls=%async_computation.6 | async-start | bytes 7372800 | tf_op jit(solution)/shard_map/reduce_scatter | solution.py:587
  112.0 15.4 %collective-permute-start.4 = (bf16[160,1280]{1,0:T(8,128)(2,1)}, bf16[160,1280]{1,0:T(8,128)(2,1)}, u32[]{:S(2)}, u32[]{:S(2)}) collective-permute-start(bf16[160,1280]{1,0:T(8,128)(2,1)} %get-tuple-element.368), channel_id=1, source_target_pairs={{0,8},{8,16},{16,24},{24,28},{28,20},{20,12},{12,4},{4,0},{1,9},{9... | collective-permute-start | bytes 1228808 | tf_op jit(solution)/shard_map/ppermute | solution.py:510
  112.3 18.3 %collective-permute-start.5 = (bf16[160,1280]{1,0:T(8,128)(2,1)S(1)}, bf16[160,1280]{1,0:T(8,128)(2,1)}, u32[]{:S(2)}, u32[]{:S(2)}) collective-permute-start(bf16[160,1280]{1,0:T(8,128)(2,1)S(1)} %get-tuple-element.367), channel_id=1, source_target_pairs={{8,0},{16,8},{24,16},{28,24},{20,28},{12,20},{4,12},{0,4},{9,1},{1... | collective-permute-start | bytes 1228808 | tf_op jit(solution)/shard_map/ppermute | solution.py:510
  130.6 14.5 %collective-permute-start.16 = (bf16[160,1280]{1,0:T(8,128)(2,1)}, bf16[160,1280]{1,0:T(8,128)(2,1)S(1)}, u32[]{:S(2)}, u32[]{:S(2)}) collective-permute-start(bf16[160,1280]{1,0:T(8,128)(2,1)} %collective-permute-done.4), channel_id=1, source_target_pairs={{0,8},{8,16},{16,24},{24,28},{28,20},{20,12},{12,4},{4,0},{1,9},{9... | collective-permute-start | bytes 1228808 | tf_op jit(solution)/shard_map/ppermute | solution.py:510
  130.6 24.1 %collective-permute-start.17 = (bf16[160,1280]{1,0:T(8,128)(2,1)}, bf16[160,1280]{1,0:T(8,128)(2,1)S(1)}, u32[]{:S(2)}, u32[]{:S(2)}) collective-permute-start(bf16[160,1280]{1,0:T(8,128)(2,1)} %collective-permute-done.5), channel_id=1, source_target_pairs={{8,0},{16,8},{24,16},{28,24},{20,28},{12,20},{4,12},{0,4},{9,1},{1... | collective-permute-start | bytes 1228808 | tf_op jit(solution)/shard_map/ppermute | solution.py:510
  183.7 16.7 %collective-permute-start.18 = (bf16[160,1280]{1,0:T(8,128)(2,1)S(1)}, bf16[160,1280]{1,0:T(8,128)(2,1)S(1)}, u32[]{:S(2)}, u32[]{:S(2)}) collective-permute-start(bf16[160,1280]{1,0:T(8,128)(2,1)S(1)} %collective-permute-done.16), channel_id=1, source_target_pairs={{0,8},{8,16},{16,24},{24,28},{28,20},{20,12},{12,4},{4,0},{1,9},{9... | collective-permute-start | bytes 1228808 | tf_op jit(solution)/shard_map/ppermute | solution.py:510
  184.0 30.8 %collective-permute-start.19 = (bf16[160,1280]{1,0:T(8,128)(2,1)S(1)}, bf16[160,1280]{1,0:T(8,128)(2,1)S(1)}, u32[]{:S(2)}, u32[]{:S(2)}) collective-permute-start(bf16[160,1280]{1,0:T(8,128)(2,1)S(1)} %collective-permute-done.17), channel_id=1, source_target_pairs={{8,0},{16,8},{24,16},{28,24},{20,28},{12,20},{4,12},{0,4},{9,1},{1... | collective-permute-start | bytes 1228808 | tf_op jit(solution)/shard_map/ppermute | solution.py:510
  214.8 21.8 %collective-permute-start.20 = (bf16[160,1280]{1,0:T(8,128)(2,1)S(1)}, bf16[160,1280]{1,0:T(8,128)(2,1)S(1)}, u32[]{:S(2)}, u32[]{:S(2)}) collective-permute-start(bf16[160,1280]{1,0:T(8,128)(2,1)S(1)} %collective-permute-done.18), channel_id=1, source_target_pairs={{0,8},{8,16},{16,24},{24,28},{28,20},{20,12},{12,4},{4,0},{1,9},{9... | collective-permute-start | bytes 1228808 | tf_op jit(solution)/shard_map/ppermute | solution.py:510
  214.8 21.8 %collective-permute-start.21 = (bf16[160,1280]{1,0:T(8,128)(2,1)S(1)}, bf16[160,1280]{1,0:T(8,128)(2,1)S(1)}, u32[]{:S(2)}, u32[]{:S(2)}) collective-permute-start(bf16[160,1280]{1,0:T(8,128)(2,1)S(1)} %collective-permute-done.19), channel_id=1, source_target_pairs={{8,0},{16,8},{24,16},{28,24},{20,28},{12,20},{4,12},{0,4},{9,1},{1... | collective-permute-start | bytes 1228808 | tf_op jit(solution)/shard_map/ppermute | solution.py:510
  236.6 8.9 %collective-permute-start.22 = (bf16[160,1280]{1,0:T(8,128)(2,1)S(1)}, bf16[160,1280]{1,0:T(8,128)(2,1)S(1)}, u32[]{:S(2)}, u32[]{:S(2)}) collective-permute-start(bf16[160,1280]{1,0:T(8,128)(2,1)S(1)} %collective-permute-done.20), channel_id=1, source_target_pairs={{0,8},{8,16},{16,24},{24,28},{28,20},{20,12},{12,4},{4,0},{1,9},{9... | collective-permute-start | bytes 1228808 | tf_op jit(solution)/shard_map/ppermute | solution.py:510
  236.7 8.8 %collective-permute-start.23 = (bf16[160,1280]{1,0:T(8,128)(2,1)S(1)}, bf16[160,1280]{1,0:T(8,128)(2,1)S(1)}, u32[]{:S(2)}, u32[]{:S(2)}) collective-permute-start(bf16[160,1280]{1,0:T(8,128)(2,1)S(1)} %collective-permute-done.21), channel_id=1, source_target_pairs={{8,0},{16,8},{24,16},{28,24},{20,28},{12,20},{4,12},{0,4},{9,1},{1... | collective-permute-start | bytes 1228808 | tf_op jit(solution)/shard_map/ppermute | solution.py:510
  247.1 8.6 %collective-permute-start.25 = (bf16[160,1280]{1,0:T(8,128)(2,1)S(1)}, bf16[160,1280]{1,0:T(8,128)(2,1)S(1)}, u32[]{:S(2)}, u32[]{:S(2)}) collective-permute-start(bf16[160,1280]{1,0:T(8,128)(2,1)S(1)} %collective-permute-done.23), channel_id=1, source_target_pairs={{8,0},{16,8},{24,16},{28,24},{20,28},{12,20},{4,12},{0,4},{9,1},{1... | collective-permute-start | bytes 1228808 | tf_op jit(solution)/shard_map/ppermute | solution.py:510
  337.7 13.2 %collective-permute-start.28 = (bf16[160,1280]{1,0:T(8,128)(2,1)S(1)}, bf16[160,1280]{1,0:T(8,128)(2,1)S(1)}, u32[]{:S(2)}, u32[]{:S(2)}) collective-permute-start(bf16[160,1280]{1,0:T(8,128)(2,1)S(1)} %get-tuple-element.360), channel_id=1, source_target_pairs={{0,8},{8,16},{16,24},{24,28},{28,20},{20,12},{12,4},{4,0},{1,9},{9... | collective-permute-start | bytes 1228808 | tf_op jit(solution)/shard_map/ppermute | solution.py:543
  339.8 15.8 %collective-permute-start.29 = (bf16[160,1280]{1,0:T(8,128)(2,1)S(1)}, bf16[160,1280]{1,0:T(8,128)(2,1)S(1)}, u32[]{:S(2)}, u32[]{:S(2)}) collective-permute-start(bf16[160,1280]{1,0:T(8,128)(2,1)S(1)} %get-tuple-element.359), channel_id=1, source_target_pairs={{8,0},{16,8},{24,16},{28,24},{20,28},{12,20},{4,12},{0,4},{9,1},{1... | collective-permute-start | bytes 1228808 | tf_op jit(solution)/shard_map/ppermute | solution.py:543
  339.8 271.9 %reduce-scatter.8.cloned.1.call-start = ((), (), s32[]{:S(2)}) async-start(), calls=%async_computation.7 | async-start | bytes 2211840 | tf_op jit(solution)/shard_map/reduce_scatter | solution.py:587
  357.0 17.3 %collective-permute-start.30 = (bf16[160,1280]{1,0:T(8,128)(2,1)S(1)}, bf16[160,1280]{1,0:T(8,128)(2,1)S(1)}, u32[]{:S(2)}, u32[]{:S(2)}) collective-permute-start(bf16[160,1280]{1,0:T(8,128)(2,1)S(1)} %get-tuple-element.218), channel_id=1, source_target_pairs={{0,8},{8,16},{16,24},{24,28},{28,20},{20,12},{12,4},{4,0},{1,9},{9... | collective-permute-start | bytes 1228808 | tf_op jit(solution)/shard_map/ppermute | solution.py:543
  357.1 30.2 %collective-permute-start.31 = (bf16[160,1280]{1,0:T(8,128)(2,1)S(1)}, bf16[160,1280]{1,0:T(8,128)(2,1)S(1)}, u32[]{:S(2)}, u32[]{:S(2)}) collective-permute-start(bf16[160,1280]{1,0:T(8,128)(2,1)S(1)} %get-tuple-element.219), channel_id=1, source_target_pairs={{8,0},{16,8},{24,16},{28,24},{20,28},{12,20},{4,12},{0,4},{9,1},{1... | collective-permute-start | bytes 1228808 | tf_op jit(solution)/shard_map/ppermute | solution.py:543
  374.3 125.6 %collective-permute-start.38 = (bf16[2,640,1024]{2,1,0:T(8,128)(2,1)}, bf16[2,640,1024]{2,1,0:T(8,128)(2,1)}, u32[]{:S(2)}, u32[]{:S(2)}) collective-permute-start(bf16[2,640,1024]{2,1,0:T(8,128)(2,1)} %dynamic-slice_bitcast_fusion), channel_id=1, source_target_pairs={{0,1},{1,0},{2,3},{3,2},{4,5},{5,4},{6,7},{7,6},{8,9},{9,8},{10,11... | collective-permute-start | bytes 7864328 | tf_op jit(solution)/shard_map/ppermute | solution.py:571
  387.5 22.1 %collective-permute-start.32 = (bf16[160,1280]{1,0:T(8,128)(2,1)S(1)}, bf16[160,1280]{1,0:T(8,128)(2,1)S(1)}, u32[]{:S(2)}, u32[]{:S(2)}) collective-permute-start(bf16[160,1280]{1,0:T(8,128)(2,1)S(1)} %get-tuple-element.221), channel_id=1, source_target_pairs={{0,8},{8,16},{16,24},{24,28},{28,20},{20,12},{12,4},{4,0},{1,9},{9... | collective-permute-start | bytes 1228808 | tf_op jit(solution)/shard_map/ppermute | solution.py:543
  387.5 29.3 %collective-permute-start.33 = (bf16[160,1280]{1,0:T(8,128)(2,1)S(1)}, bf16[160,1280]{1,0:T(8,128)(2,1)S(1)}, u32[]{:S(2)}, u32[]{:S(2)}) collective-permute-start(bf16[160,1280]{1,0:T(8,128)(2,1)S(1)} %get-tuple-element.222), channel_id=1, source_target_pairs={{8,0},{16,8},{24,16},{28,24},{20,28},{12,20},{4,12},{0,4},{9,1},{1... | collective-permute-start | bytes 1228808 | tf_op jit(solution)/shard_map/ppermute | solution.py:543
  417.0 22.9 %collective-permute-start.34 = (bf16[160,1280]{1,0:T(8,128)(2,1)S(1)}, bf16[160,1280]{1,0:T(8,128)(2,1)S(1)}, u32[]{:S(2)}, u32[]{:S(2)}) collective-permute-start(bf16[160,1280]{1,0:T(8,128)(2,1)S(1)} %get-tuple-element.235), channel_id=1, source_target_pairs={{0,8},{8,16},{16,24},{24,28},{28,20},{20,12},{12,4},{4,0},{1,9},{9... | collective-permute-start | bytes 1228808 | tf_op jit(solution)/shard_map/ppermute | solution.py:543
  417.0 22.8 %collective-permute-start.35 = (bf16[160,1280]{1,0:T(8,128)(2,1)S(1)}, bf16[160,1280]{1,0:T(8,128)(2,1)S(1)}, u32[]{:S(2)}, u32[]{:S(2)}) collective-permute-start(bf16[160,1280]{1,0:T(8,128)(2,1)S(1)} %get-tuple-element.236), channel_id=1, source_target_pairs={{8,0},{16,8},{24,16},{28,24},{20,28},{12,20},{4,12},{0,4},{9,1},{1... | collective-permute-start | bytes 1228808 | tf_op jit(solution)/shard_map/ppermute | solution.py:543
  440.1 14.8 %collective-permute-start.36 = (bf16[160,1280]{1,0:T(8,128)(2,1)S(1)}, bf16[160,1280]{1,0:T(8,128)(2,1)S(1)}, u32[]{:S(2)}, u32[]{:S(2)}) collective-permute-start(bf16[160,1280]{1,0:T(8,128)(2,1)S(1)} %get-tuple-element.237), channel_id=1, source_target_pairs={{0,8},{8,16},{16,24},{24,28},{28,20},{20,12},{12,4},{4,0},{1,9},{9... | collective-permute-start | bytes 1228808 | tf_op jit(solution)/shard_map/ppermute | solution.py:543
  440.2 14.6 %collective-permute-start.37 = (bf16[160,1280]{1,0:T(8,128)(2,1)S(1)}, bf16[160,1280]{1,0:T(8,128)(2,1)S(1)}, u32[]{:S(2)}, u32[]{:S(2)}) collective-permute-start(bf16[160,1280]{1,0:T(8,128)(2,1)S(1)} %get-tuple-element.238), channel_id=1, source_target_pairs={{8,0},{16,8},{24,16},{28,24},{20,28},{12,20},{4,12},{0,4},{9,1},{1... | collective-permute-start | bytes 1228808 | tf_op jit(solution)/shard_map/ppermute | solution.py:543
  455.1 15.6 %collective-permute-start.42 = (bf16[160,1280]{1,0:T(8,128)(2,1)S(1)}, bf16[160,1280]{1,0:T(8,128)(2,1)S(1)}, u32[]{:S(2)}, u32[]{:S(2)}) collective-permute-start(bf16[160,1280]{1,0:T(8,128)(2,1)S(1)} %get-tuple-element.246), channel_id=1, source_target_pairs={{0,8},{8,16},{16,24},{24,28},{28,20},{20,12},{12,4},{4,0},{1,9},{9... | collective-permute-start | bytes 1228808 | tf_op jit(solution)/shard_map/ppermute | solution.py:543
  455.2 15.5 %collective-permute-start.43 = (bf16[160,1280]{1,0:T(8,128)(2,1)S(1)}, bf16[160,1280]{1,0:T(8,128)(2,1)S(1)}, u32[]{:S(2)}, u32[]{:S(2)}) collective-permute-start(bf16[160,1280]{1,0:T(8,128)(2,1)S(1)} %get-tuple-element.247), channel_id=1, source_target_pairs={{8,0},{16,8},{24,16},{28,24},{20,28},{12,20},{4,12},{0,4},{9,1},{1... | collective-permute-start | bytes 1228808 | tf_op jit(solution)/shard_map/ppermute | solution.py:543
  457.2 26.5 %collective-permute-start.40 = (bf16[160,1280]{1,0:T(8,128)(2,1)S(1)}, bf16[160,1280]{1,0:T(8,128)(2,1)S(1)}, u32[]{:S(2)}, u32[]{:S(2)}) collective-permute-start(bf16[160,1280]{1,0:T(8,128)(2,1)S(1)} %get-tuple-element.244), channel_id=1, source_target_pairs={{0,8},{8,16},{16,24},{24,28},{28,20},{20,12},{12,4},{4,0},{1,9},{9... | collective-permute-start | bytes 1228808 | tf_op jit(solution)/shard_map/ppermute | solution.py:543
  457.3 33.4 %collective-permute-start.41 = (bf16[160,1280]{1,0:T(8,128)(2,1)S(1)}, bf16[160,1280]{1,0:T(8,128)(2,1)S(1)}, u32[]{:S(2)}, u32[]{:S(2)}) collective-permute-start(bf16[160,1280]{1,0:T(8,128)(2,1)S(1)} %get-tuple-element.245), channel_id=1, source_target_pairs={{8,0},{16,8},{24,16},{28,24},{20,28},{12,20},{4,12},{0,4},{9,1},{1... | collective-permute-start | bytes 1228808 | tf_op jit(solution)/shard_map/ppermute | solution.py:543
  492.0 27.7 %collective-permute-start.46 = (bf16[160,1280]{1,0:T(8,128)(2,1)S(1)}, bf16[160,1280]{1,0:T(8,128)(2,1)S(1)}, u32[]{:S(2)}, u32[]{:S(2)}) collective-permute-start(bf16[160,1280]{1,0:T(8,128)(2,1)S(1)} %get-tuple-element.258), channel_id=1, source_target_pairs={{0,8},{8,16},{16,24},{24,28},{28,20},{20,12},{12,4},{4,0},{1,9},{9... | collective-permute-start | bytes 1228808 | tf_op jit(solution)/shard_map/ppermute | solution.py:543
  497.1 22.5 %collective-permute-start.47 = (bf16[160,1280]{1,0:T(8,128)(2,1)S(1)}, bf16[160,1280]{1,0:T(8,128)(2,1)S(1)}, u32[]{:S(2)}, u32[]{:S(2)}) collective-permute-start(bf16[160,1280]{1,0:T(8,128)(2,1)S(1)} %get-tuple-element.259), channel_id=1, source_target_pairs={{8,0},{16,8},{24,16},{28,24},{20,28},{12,20},{4,12},{0,4},{9,1},{1... | collective-permute-start | bytes 1228808 | tf_op jit(solution)/shard_map/ppermute | solution.py:543
  497.1 24.8 %collective-permute-start.44 = (bf16[160,1280]{1,0:T(8,128)(2,1)S(1)}, bf16[160,1280]{1,0:T(8,128)(2,1)S(1)}, u32[]{:S(2)}, u32[]{:S(2)}) collective-permute-start(bf16[160,1280]{1,0:T(8,128)(2,1)S(1)} %get-tuple-element.256), channel_id=1, source_target_pairs={{0,8},{8,16},{16,24},{24,28},{28,20},{20,12},{12,4},{4,0},{1,9},{9... | collective-permute-start | bytes 1228808 | tf_op jit(solution)/shard_map/ppermute | solution.py:543
  500.0 21.9 %collective-permute-start.45 = (bf16[160,1280]{1,0:T(8,128)(2,1)S(1)}, bf16[160,1280]{1,0:T(8,128)(2,1)S(1)}, u32[]{:S(2)}, u32[]{:S(2)}) collective-permute-start(bf16[160,1280]{1,0:T(8,128)(2,1)S(1)} %get-tuple-element.257), channel_id=1, source_target_pairs={{8,0},{16,8},{24,16},{28,24},{20,28},{12,20},{4,12},{0,4},{9,1},{1... | collective-permute-start | bytes 1228808 | tf_op jit(solution)/shard_map/ppermute | solution.py:543
  503.9 20.2 %collective-permute-start.39 = (bf16[1,640,1024]{2,1,0:T(8,128)(2,1)S(1)}, bf16[1,640,1024]{2,1,0:T(8,128)(2,1)S(1)}, u32[]{:S(2)}, u32[]{:S(2)}) collective-permute-start(bf16[1,640,1024]{2,1,0:T(8,128)(2,1)S(1)} %constant_dynamic-slice_fusion), channel_id=1, source_target_pairs={{0,2},{1,3},{2,0},{3,1},{4,6},{5,7},{6,4},{7,5},{8,10},{9,11},{10,... | collective-permute-start | bytes 3932168 | tf_op jit(solution)/shard_map/ppermute | solution.py:571
  539.7 124.7 %reduce-scatter.4.cloned.1.call-start = ((), (), s32[]{:S(2)}) async-start(), calls=%async_computation.5 | async-start | bytes 6553600 | tf_op jit(solution)/shard_map/reduce_scatter | solution.py:740
  558.1 15.3 %collective-permute-start.51 = (bf16[160,1280]{1,0:T(8,128)(2,1)S(1)}, bf16[160,1280]{1,0:T(8,128)(2,1)S(1)}, u32[]{:S(2)}, u32[]{:S(2)}) collective-permute-start(bf16[160,1280]{1,0:T(8,128)(2,1)S(1)} %copy-done.15), channel_id=1, source_target_pairs={{0,8},{8,16},{16,24},{24,28},{28,20},{20,12},{12,4},{4,0},{1,9},{9... | collective-permute-start | bytes 1228808 | tf_op jit(solution)/shard_map/ppermute | solution.py:543
  558.3 15.8 %collective-permute-start.52 = (bf16[160,1280]{1,0:T(8,128)(2,1)S(1)}, bf16[160,1280]{1,0:T(8,128)(2,1)}, u32[]{:S(2)}, u32[]{:S(2)}) collective-permute-start(bf16[160,1280]{1,0:T(8,128)(2,1)S(1)} %copy-done.14), channel_id=1, source_target_pairs={{8,0},{16,8},{24,16},{28,24},{20,28},{12,20},{4,12},{0,4},{9,1},{1... | collective-permute-start | bytes 1228808 | tf_op jit(solution)/shard_map/ppermute | solution.py:543
  576.4 37.2 %collective-permute-start.53 = (bf16[160,1280]{1,0:T(8,128)(2,1)}, bf16[160,1280]{1,0:T(8,128)(2,1)}, u32[]{:S(2)}, u32[]{:S(2)}) collective-permute-start(bf16[160,1280]{1,0:T(8,128)(2,1)} %get-tuple-element.266), channel_id=1, source_target_pairs={{0,8},{8,16},{16,24},{24,28},{28,20},{20,12},{12,4},{4,0},{1,9},{9... | collective-permute-start | bytes 1228808 | tf_op jit(solution)/shard_map/ppermute | solution.py:543
  580.2 9.9 %collective-permute-start.61 = (f32[9020]{0:T(1024)S(1)}, f32[9020]{0:T(1024)S(1)}, u32[]{:S(2)}, u32[]{:S(2)}) collective-permute-start(f32[9020]{0:T(1024)S(1)} %concatenate.47), channel_id=1, source_target_pairs={{0,4},{4,0},{8,12},{12,8},{16,20},{20,16},{24,28},{28,24},{1,5},{5... | collective-permute-start | bytes 108248 | tf_op jit(solution)/shard_map/ppermute | solution.py:581
  612.9 12.1 %collective-permute-start.57 = (bf16[160,1280]{1,0:T(8,128)(2,1)}, bf16[160,1280]{1,0:T(8,128)(2,1)S(1)}, u32[]{:S(2)}, u32[]{:S(2)}) collective-permute-start(bf16[160,1280]{1,0:T(8,128)(2,1)} %get-tuple-element.267), channel_id=1, source_target_pairs={{8,0},{16,8},{24,16},{28,24},{20,28},{12,20},{4,12},{0,4},{9,1},{1... | collective-permute-start | bytes 1228808 | tf_op jit(solution)/shard_map/ppermute | solution.py:543
  614.8 11.6 %collective-permute-start.54 = (bf16[160,1280]{1,0:T(8,128)(2,1)S(1)}, bf16[160,1280]{1,0:T(8,128)(2,1)S(1)}, u32[]{:S(2)}, u32[]{:S(2)}) collective-permute-start(bf16[160,1280]{1,0:T(8,128)(2,1)S(1)} %add_convert_fusion.8), channel_id=1, source_target_pairs={{0,8},{8,16},{16,24},{24,28},{28,20},{20,12},{12,4},{4,0},{1,9},{9... | collective-permute-start | bytes 1228808 | tf_op jit(solution)/shard_map/ppermute | solution.py:543
  618.7 13.7 %collective-permute-start.65 = (f32[325,256]{1,0:T(8,128)S(1)}, f32[325,256]{1,0:T(8,128)}, u32[]{:S(2)}, u32[]{:S(2)}) collective-permute-start(f32[325,256]{1,0:T(8,128)S(1)} %fusion.29), channel_id=1, source_target_pairs={{0,2},{1,3},{2,0},{3,1},{4,6},{5,7},{6,4},{7,5},{8,10},{9,11},{10,... | collective-permute-start | bytes 998408 | tf_op jit(solution)/shard_map/ppermute | solution.py:581
  627.7 10.9 %collective-permute-start.55 = (bf16[160,1280]{1,0:T(8,128)(2,1)S(1)}, bf16[160,1280]{1,0:T(8,128)(2,1)S(1)}, u32[]{:S(2)}, u32[]{:S(2)}) collective-permute-start(bf16[160,1280]{1,0:T(8,128)(2,1)S(1)} %get-tuple-element.335), channel_id=1, source_target_pairs={{0,8},{8,16},{16,24},{24,28},{28,20},{20,12},{12,4},{4,0},{1,9},{9... | collective-permute-start | bytes 1228808 | tf_op jit(solution)/shard_map/ppermute | solution.py:543
  629.2 10.7 %collective-permute-start.58 = (bf16[160,1280]{1,0:T(8,128)(2,1)S(1)}, bf16[160,1280]{1,0:T(8,128)(2,1)}, u32[]{:S(2)}, u32[]{:S(2)}) collective-permute-start(bf16[160,1280]{1,0:T(8,128)(2,1)S(1)} %get-tuple-element.336), channel_id=1, source_target_pairs={{8,0},{16,8},{24,16},{28,24},{20,28},{12,20},{4,12},{0,4},{9,1},{1... | collective-permute-start | bytes 1228808 | tf_op jit(solution)/shard_map/ppermute | solution.py:543
  642.0 26.5 %collective-permute-start.56 = (bf16[160,1280]{1,0:T(8,128)(2,1)}, bf16[160,1280]{1,0:T(8,128)(2,1)S(1)}, u32[]{:S(2)}, u32[]{:S(2)}) collective-permute-start(bf16[160,1280]{1,0:T(8,128)(2,1)} %get-tuple-element.333), channel_id=1, source_target_pairs={{0,8},{8,16},{16,24},{24,28},{28,20},{20,12},{12,4},{4,0},{1,9},{9... | collective-permute-start | bytes 1228808 | tf_op jit(solution)/shard_map/ppermute | solution.py:543
  642.8 26.6 %collective-permute-start.59 = (bf16[160,1280]{1,0:T(8,128)(2,1)S(1)}, bf16[160,1280]{1,0:T(8,128)(2,1)}, u32[]{:S(2)}, u32[]{:S(2)}) collective-permute-start(bf16[160,1280]{1,0:T(8,128)(2,1)S(1)} %get-tuple-element.334), channel_id=1, source_target_pairs={{8,0},{16,8},{24,16},{28,24},{20,28},{12,20},{4,12},{0,4},{9,1},{1... | collective-permute-start | bytes 1228808 | tf_op jit(solution)/shard_map/ppermute | solution.py:543
  671.7 24.2 %collective-permute-start.60 = (bf16[160,1280]{1,0:T(8,128)(2,1)}, bf16[160,1280]{1,0:T(8,128)(2,1)}, u32[]{:S(2)}, u32[]{:S(2)}) collective-permute-start(bf16[160,1280]{1,0:T(8,128)(2,1)} %get-tuple-element.332), channel_id=1, source_target_pairs={{8,0},{16,8},{24,16},{28,24},{20,28},{12,20},{4,12},{0,4},{9,1},{1... | collective-permute-start | bytes 1228808 | tf_op jit(solution)/shard_map/ppermute | solution.py:543
  672.2 10.7 %collective-permute-start.49 = (f32[640]{0:T(1024)S(1)}, f32[640]{0:T(1024)S(1)}, u32[]{:S(2)}, u32[]{:S(2)}) collective-permute-start(f32[640]{0:T(1024)S(1)} %add.758), channel_id=1, source_target_pairs={{0,8},{4,12},{8,0},{12,4},{16,24},{20,28},{24,16},{28,20},{1,9},{5... | collective-permute-start | bytes 7688 | tf_op jit(solution)/shard_map/ppermute | solution.py:581
  683.0 12.3 %collective-permute-start.50 = (f32[640]{0:T(1024)S(1)}, f32[640]{0:T(1024)S(1)}, u32[]{:S(2)}, u32[]{:S(2)}) collective-permute-start(f32[640]{0:T(1024)S(1)} %add.759), channel_id=1, source_target_pairs={{0,16},{4,20},{8,24},{12,28},{16,0},{20,4},{24,8},{28,12},{1,17},{... | collective-permute-start | bytes 7688 | tf_op jit(solution)/shard_map/ppermute | solution.py:581
  (41 other events, 846.3 us)
Sparse Core Ops, SparseCore 0:
  9.6 43.0 all-gather.2
  111.3 121.3 all-gather.4
  339.9 161.4 reduce-scatter.5
  539.8 71.8 reduce-scatter.7
  614.1 50.2 reduce-scatter.3

commit v8 on v6

--- a/solution.py
+++ b/solution.py
@@ -500,20 +500,25 @@
         self.half = self.rows // 2
         self.taken = 0
         self.held = (shard[: self.half], shard[self.half :])
+        self.waiting = []
         full = jnp.zeros((self.count * self.rows, width), shard.dtype)
         self.full = lax.dynamic_update_slice(full, shard, (me * self.rows, 0))
 
-    def step(self, times=1):
+    def step(self, times=1, place=True):
         for _ in range(min(times, self.count - 1 - self.taken)):
             self.taken += 1
-            arrived = tuple(
+            self.held = tuple(
                 lax.ppermute(held, "gx", move) for held, move in zip(self.held, self.moves)
             )
-            self.held, self.full = lax.optimization_barrier((arrived, self.full))
             for piece, sign, offset in zip(self.held, (-1, 1), (0, self.half)):
                 owner = ring_index(self.place + sign * self.taken, self.count)
-                start = owner * self.rows + offset
-                self.full = lax.dynamic_update_slice(self.full, piece, (start, 0))
+                self.waiting.append((piece, owner * self.rows + offset))
+            if place:
+                if len(self.waiting) > 2:
+                    self.held, self.full = lax.optimization_barrier((self.held, self.full))
+                for piece, start in self.waiting:
+                    self.full = lax.dynamic_update_slice(self.full, piece, (start, 0))
+                self.waiting = []
         return self.held
 
     def finish(self):
@@ -610,25 +615,21 @@
     state_cols = state_weight.shape[1]
     col_start = lax.axis_index("gy") * col_width
 
-    state_step_weight = jnp.concatenate([state_weight, step_weight], 1)
-    full_state = lax.all_gather(state_step_weight, "gx", axis=0, tiled=True)
+    inner = gate_weight.shape[1]
     upstream = lax.all_gather(cotangent, "gy", axis=1, tiled=True)
-    value_gather = RingGather(value_weight)
+    value_gather = RingGather(jnp.concatenate([value_weight, state_weight, step_weight], 1))
     value_gather.step()
     tokens = tie(layer_input, value_gather).astype(wide)
     scale_in = lax.rsqrt(jnp.mean(tokens * tokens, axis=1, keepdims=True) + epsilon)
     normed = (tokens * scale_in * norm_gain).astype(low)
     value_gather.step()
     normed = tie(normed, value_gather)
-    value_gather.step(value_gather.count)
-    gate_shard = tie(gate_weight, value_gather)
-    full_gate = lax.all_gather(gate_shard, "gx", axis=0, tiled=True)
-    full_value = value_gather.finish()
-
-    out_gather = RingGather(tie(out_weight.T, value_gather))
-    out_gather.step()
-    normed = tie(normed, out_gather)
-    state_step = dot(normed, full_state)
+    full_value_state = value_gather.finish()
+
+    gate_gather = RingGather(tie(gate_weight, value_gather))
+    gate_gather.step(place=False)
+    normed = tie(normed, gate_gather)
+    state_step = dot(normed, full_value_state[:, inner:])
     mixer = Mixer(
         state_step[:, :state_cols],
         state_step[:, state_cols:],
@@ -638,23 +639,28 @@
         decay_log,
         segment_ids,
     )
-    out_gather.step()
+    gate_gather.step(place=False)
     normed, mixer.g = together(normed, mixer.g)
+    normed = tie(normed, gate_gather)
+    value_in = dot(normed, full_value_state[:, :inner])
+    gate_gather.step(place=False)
+    value_in = tie(value_in, gate_gather)
+    mixed = mixer.forward(value_in, conv_value, conv_value_bias, skip_scale)
+    gate_gather.step(place=False)
+    mixed = mixer.mixed = tie(mixer.mixed, gate_gather)
+    mixed = mixed[:, : mixer.inner]
+    full_gate = gate_gather.finish()
+    out_gather = RingGather(tie(out_weight.T, gate_gather))
+    out_gather.step(place=False)
     normed = tie(normed, out_gather)
-    value_in = dot(normed, full_value)
-    out_gather.step()
-    value_in = tie(value_in, out_gather)
-    mixed = mixer.forward(value_in, conv_value, conv_value_bias, skip_scale)
-    out_gather.step()
-    mixed = mixer.mixed = tie(mixer.mixed, out_gather)
-    mixed = mixed[:, : mixer.inner]
+    gate_in = dot(normed, full_gate)
+    out_gather.step(place=False)
+    gate_in = tie(gate_in, out_gather)
     full_out = out_gather.finish()
-    full_value_state = jnp.concatenate([full_value, full_state], 1)
-    gate_in = dot(normed, full_gate)
+    up_back = dot(upstream, full_out)
     gate_open = jax.nn.sigmoid(gate_in)
     gate_act = gate_in * gate_open
     gated = mixed * gate_act
-    up_back = dot(upstream, full_out)
 
     sums_out = lax.psum(
         jnp.stack(

time: 659 us -> 657 us (level)
  matrix products: 123 us -> 111 us
  starting transfers between devices: 92.4 us -> 102 us
    ppermute x28 -> x42, starting transfers between devices: 30.6 us -> 40.5 us  [step(): lax.ppermute(held, 'gx', move)]
    dot_general x4, matrix products: 45.8 us -> 36.1 us  [dot(): jnp.dot(left, right, preferred_element_type=wide, precision=precision)]
    dynamic_update_slice x28 -> x42, local copies, waits for them, and re-layouts: 23.1 us -> 29.6 us  [step(): self.full = lax.dynamic_update_slice(self.full, piece, (start, 0))]
    unnamed x90 -> x96, local copies, waits for them, and re-layouts: 18.2 us -> 13.5 us
    ppermute x28 -> x42, waiting for transfers between devices: 123 us -> 126 us  [step(): lax.ppermute(held, 'gx', move)]
  transfers between devices with their start and end apart: 84 -> 96, of which waited for: 37 -> 48; matrix products, arithmetic and copies ran while one was open for 38% -> 35% of each run, Pallas kernels for 13% -> 13%
where the time goes in v8:
time: 657 us; the launch traced here: 651 us
  waiting for transfers between devices  177 us (27%)
  matrix products  111 us (17%)
  starting transfers between devices  102 us (16%)
  other arithmetic  84.2 us (13%)
  Pallas kernels  83.3 us (13%)
  local copies, waits for them, and re-layouts  66.9 us (10%)
  between operations  15.5 us (2%)
  blocking collectives  11.4 us (2%)
    ppermute x42, waiting for transfers between devices, step(): lax.ppermute(held, 'gx', move)  126 us
    pallas_call x5, Pallas kernels, call(): pl.pallas_call(kernel, out_shape=shapes, scratch_shapes=list(scratch), co...  83.3 us
    ppermute x42, starting transfers between devices, step(): lax.ppermute(held, 'gx', move).astype(wide)  53.1 us
    ppermute x42, waiting for transfers between devices, step(): lax.ppermute(held, 'gx', move).astype(wide)  44 us
    ppermute x42, starting transfers between devices, step(): lax.ppermute(held, 'gx', move)  40.5 us
    dot_general x3, matrix products, contract_cols(): lax.dot_general(left, right, (((1,), (1,)), ((), ())), preferred_element_...  39.4 us
    dot_general x4, matrix products, dot(): jnp.dot(left, right, preferred_element_type=wide, precision=precision)  36.1 us
    dot_general x4, matrix products, contract_rows(): lax.dot_general(left, right, (((0,), (0,)), ((), ())), preferred_element_...  35.2 us
  transfers between devices with their start and end apart: 96, of which 48 were waited for; matrix products, arithmetic and copies ran while one was open for 35% of the time, Pallas kernels for 13%

profile of v8, /device:TPU:0, one launch (start us, length us, event | category | flops | bytes accessed | tf_op | source)
XLA Modules:
  0.0 650.8 jit_solution(2539041457785456031)
XLA Ops:
  9.2 3.1 collective-permute-start
  12.6 11.7 %collective-permute-done = bf16[160,1556]{1,0:T(8,128)(2,1)S(1)} collective-permute-done((bf16[160,1556]{1,0:T(8,128)(2,1)S(1)}, bf16[160,1556]{1,0:T(8,128)(2,1)S(1)}, u32[]{:S(2)}, u32[]{:S(2)}) %collective-permute-start) | collective-permute-done | bytes 497952 | tf_op jit(solution)/shard_map/ppermute | solution.py:511
  29.6 3.6 fusion.2
  33.1 5.3 collective-permute-done.2
  44.4 7.4 %collective-permute-done.4 = bf16[160,1556]{1,0:T(8,128)(2,1)} collective-permute-done((bf16[160,1556]{1,0:T(8,128)(2,1)S(1)}, bf16[160,1556]{1,0:T(8,128)(2,1)}, u32[]{:S(2)}, u32[]{:S(2)}) %collective-permute-start.4) | collective-permute-done | bytes 497952 | tf_op jit(solution)/shard_map/ppermute | solution.py:511
  56.4 7.9 %collective-permute-done.5 = bf16[160,1556]{1,0:T(8,128)(2,1)S(1)} collective-permute-done((bf16[160,1556]{1,0:T(8,128)(2,1)}, bf16[160,1556]{1,0:T(8,128)(2,1)S(1)}, u32[]{:S(2)}, u32[]{:S(2)}) %collective-permute-start.5) | collective-permute-done | bytes 497952 | tf_op jit(solution)/shard_map/ppermute | solution.py:511
  70.9 5.6 collective-permute-done.6
  81.2 8.3 %collective-permute-done.7 = bf16[160,1556]{1,0:T(8,128)(2,1)S(1)} collective-permute-done((bf16[160,1556]{1,0:T(8,128)(2,1)S(1)}, bf16[160,1556]{1,0:T(8,128)(2,1)S(1)}, u32[]{:S(2)}, u32[]{:S(2)}) %collective-permute-start.7) | collective-permute-done | bytes 497952 | tf_op jit(solution)/shard_map/ppermute | solution.py:511
  94.1 7.3 %collective-permute-done.8 = bf16[160,1556]{1,0:T(8,128)(2,1)S(1)} collective-permute-done((bf16[160,1556]{1,0:T(8,128)(2,1)S(1)}, bf16[160,1556]{1,0:T(8,128)(2,1)S(1)}, u32[]{:S(2)}, u32[]{:S(2)}) %collective-permute-start.8) | collective-permute-done | bytes 497952 | tf_op jit(solution)/shard_map/ppermute | solution.py:511
  103.4 2.8 collective-permute-start.14
  107.8 7.9 %collective-permute-done.14 = bf16[160,1280]{1,0:T(8,128)(2,1)S(1)} collective-permute-done((bf16[160,1280]{1,0:T(8,128)(2,1)S(1)}, bf16[160,1280]{1,0:T(8,128)(2,1)S(1)}, u32[]{:S(2)}, u32[]{:S(2)}) %collective-permute-start.14) | collective-permute-done | bytes 409632 | tf_op jit(solution)/shard_map/ppermute | solution.py:511
  120.3 4.4 fusion.19
  128.5 17.5 %shard_map.288 = (bf16[1024,128]{1,0:T(8,128)(2,1)}, bf16[1024,128]{1,0:T(8,128)(2,1)}, bf16[128,1024]{1,0:T(8,128)(2,1)}, bf16[128,1024]{1,0:T(8,128)(2,1)}, f3...) custom-call(f32[1024,256]{1,0:T(8,128)} %slice.164.state_ref, ...), custom_call_target="tpu_custom_call" | custom-call | flops 2013265920 | bytes 17315840 | tf_op jit(solution)/shard_map/pallas_call | solution.py:293
  148.2 11.5 %fusion.4.value_ref = f32[1024,1280]{1,0:T(8,128)} fusion(bf16[1024,2560]{1,0:T(8,128)(2,1)S(1)} %bitcast.72, bf16[2560,1556]{1,0:T(8,128)(2,1)} %constant_dynamic-update-slice_fusion.30), kind=kOutput, calls=%fused_computation.11 | convolution fusion | flops 6710886400 | bytes 17039360 | tf_op jit(solution)/shard_map/dot_general | solution.py:25
  164.7 18.1 %shard_map.289.mixed_ref = f32[1024,1280]{1,0:T(8,128)} custom-call(f32[1024,1280]{1,0:T(8,128)} %fusion.4.value_ref, f32[4,1280]{1,0:T(4,128)} %taps_ref.8, f32[1,1280]{1,0:T(1,128)} %broadcast_in_dim.54.bias_ref, f32[1,1280]{1,0:T(1,128)} %broadcast_in_dim_reshape.3.skip_ref, f32[1024,1280]{1,0:T(8,128)} %get-tuple-element.135.dtx_ref, ...), custom_call_target="tpu_custom_call" | custom-call | flops 3355443200 | bytes 24754176 | tf_op jit(solution)/shard_map/pallas_call | solution.py:293
  185.6 9.4 %collective-permute-done.22 = bf16[160,1280]{1,0:T(8,128)(2,1)} collective-permute-done((bf16[160,1280]{1,0:T(8,128)(2,1)S(1)}, bf16[160,1280]{1,0:T(8,128)(2,1)}, u32[]{:S(2)}, u32[]{:S(2)}) %collective-permute-start.22) | collective-permute-done | bytes 409632 | tf_op jit(solution)/shard_map/ppermute | solution.py:511
  201.6 4.6 collective-permute-done.24
  208.4 8.0 %collective-permute-done.25 = bf16[160,1280]{1,0:T(8,128)(2,1)S(1)} collective-permute-done((bf16[160,1280]{1,0:T(8,128)(2,1)S(1)}, bf16[160,1280]{1,0:T(8,128)(2,1)S(1)}, u32[]{:S(2)}, u32[]{:S(2)}) %collective-permute-start.25) | collective-permute-done | bytes 409632 | tf_op jit(solution)/shard_map/ppermute | solution.py:511
  218.9 3.2 broadcast.80
  223.1 2.7 collective-permute-done.28
  229.6 6.9 %fusion.36 = f32[1024,1280]{1,0:T(8,128)S(1)} fusion(bf16[1024,2560]{1,0:T(8,128)(2,1)S(1)} %bitcast.74, bf16[2560,1280]{1,0:T(8,128)(2,1)S(1)} %constant_dynamic-update-slice_fusion.15), kind=kOutput, calls=%fused_computation.176 | convolution fusion | flops 6710886400 | bytes 17039360 | tf_op jit(solution)/shard_map/dot_general | solution.py:25
  240.9 3.2 multiply_convert_fusion.3
  244.1 5.1 collective-permute-done.32
  256.0 5.0 collective-permute-done.34
  264.6 4.3 collective-permute-done.36
  272.6 4.3 collective-permute-done.38
  280.5 4.3 collective-permute-done.40
  287.5 13.2 %multiply_reduce_fusion.2 = (f32[1024]{0:T(1024)S(1)}, f32[1024]{0:T(1024)S(1)}, f32[1024,1280]{1,0:T(8,128)}) fusion(f32[1024,1280]{1,0:T(8,128)} %get-tuple-element.277, f32[1280]{0:T(1024)S(1)} %copy-done.25, bf16[1024,2560]{1,0:T(8,128)(2,1)} %all-gather.2.cloned.1.call-done, bf16[2560,1280]{1,0:T(8,128)(2,1)} %constant_dynamic-update-slice_fusion), kind=kOutput, calls=%fused_computation.18 | convolution fusion | flops 6717437952 | bytes 22295552 | tf_op jit(solution)/shard_map/dot_general | solution.py:25
  300.7 5.8 psum.14
  306.5 11.1 %fusion.3 = bf16[2560,1280]{1,0:T(8,128)(2,1)S(1)} fusion(bf16[1024,2560]{1,0:T(8,128)(2,1)} %all-gather.2.cloned.1.call-done, f32[1024,1280]{1,0:T(8,128)} %get-tuple-element.277, f32[1024]{0:T(1024)S(1)} %bitcast.89, f32[1280]{0:T(1024)S(1)} %copy-done.25), kind=kOutput, calls=%fused_computation.10 | convolution fusion | flops 6718095360 | bytes 17048576 | tf_op jit(solution)/shard_map/dot_general | solution.py:29
  317.6 2.7 copy-done.5
  322.8 11.8 %multiply_convert_fusion = bf16[2560,1024]{1,0:T(8,128)(2,1)} fusion(bf16[2560,1280]{1,0:T(8,128)(2,1)} %constant_dynamic-update-slice_fusion, bf16[1024,1280]{1,0:T(8,128)(2,1)S(1)} %get-tuple-element.159, f32[1024]{0:T(1024)S(1)} %bitcast.90), kind=kOutput, calls=%fused_computation.9 | convolution fusion | flops 6716129280 | bytes 14422016 | tf_op jit(solution)/shard_map/dot_general | solution.py:35
  338.3 14.6 %multiply_convert_fusion.1 = (bf16[1024,1280]{1,0:T(8,128)(2,1)S(1)}, f32[1024,1280]{1,0:T(8,128)}, f32[1280]{0:T(1024)}) fusion(f32[1024,1280]{1,0:T(8,128)} %copy-done, f32[1024,1280]{1,0:T(8,128)} %shard_map.289.mixed_ref, f32[1024,1280]{1,0:T(8,128)} %get-tuple-element.277, f32[1024]{0:T(1024)S(1)} %fusion.25, f32[1024,1280]{1,0:T(8,128)} %get-tuple-element.163, ...), kind=kLoop, calls=%fused_computation.14 | loop fusion | flops 24902400 | bytes 28854272 | tf_op jit(solution)/shard_map/convert_element_type | solution.py:690
  357.0 7.3 %convolution_convert_fusion.1 = bf16[2560,1280]{1,0:T(8,128)(2,1)S(1)} fusion(bf16[1024,2560]{1,0:T(8,128)(2,1)S(1)} %bitcast.76, bf16[1024,1280]{1,0:T(8,128)(2,1)S(1)} %get-tuple-element.211), kind=kOutput, calls=%fused_computation.3 | convolution fusion | flops 6714163200 | bytes 14417920 | tf_op jit(solution)/shard_map/dot_general | solution.py:29
  365.2 2.7 add_convert_fusion.31
  372.1 20.1 %shard_map.290 = (bf16[1024,1280]{1,0:T(8,128)(2,1)}, f32[8,1280]{1,0:T(8,128)}, f32[1024,128]{1,0:T(8,128)}, f32[1024,128]{1,0:T(8,128)}, f32[1024,128]{1,0:T(8...) custom-call(f32[1024,1280]{1,0:T(8,128)} %fusion.4.value_ref, f32[1024,1280]{1,0:T(8,128)} %shard_map.289.mixed_ref, ...), custom_call_target="tpu_custom_call" | custom-call | flops 5033164800 | bytes 35805184 | tf_op jit(solution)/shard_map/pallas_call | solution.py:293
  400.0 20.6 %shard_map.291 = (bf16[1024,1280]{1,0:T(8,128)(2,1)}, f32[8,1280]{1,0:T(8,128)}, f32[1024,128]{1,0:T(8,128)}, f32[1024,128]{1,0:T(8,128)}, f32[1024,128]{1,0:T(8...) custom-call(f32[1024,1280]{1,0:T(8,128)} %fusion.4.value_ref, ...), custom_call_target="tpu_custom_call", output_to_operand_aliasing={{0}: (15, {}), {1}: (16, {})} | custom-call | flops 5033164800 | bytes 41089024 | tf_op jit(solution)/shard_map/pallas_call | solution.py:293
  427.8 9.8 %convolution_convert_fusion = bf16[2560,1280]{1,0:T(8,128)(2,1)S(1)} fusion(bf16[1024,2560]{1,0:T(8,128)(2,1)} %fusion.2, bf16[1024,1280]{1,0:T(8,128)(2,1)} %get-tuple-element.185), kind=kOutput, calls=%fused_computation.2 | convolution fusion | flops 6714163200 | bytes 14417920 | tf_op jit(solution)/shard_map/dot_general | solution.py:29
  448.5 7.0 %shard_map.292 = (bf16[1024,256]{1,0:T(8,128)(2,1)}, bf16[1024,128]{1,0:T(8,128)(2,1)}, f32[8,256]{1,0:T(8,128)}, f32[8,128]{1,0:T(8,128)}) custom-call(f32[1024,256]{1,0:T(8,128)} %slice.164.state_ref, f32[1024,128]{1,0:T(8,128)} %pad.13.step_ref, f32[4,256]{1,0:T(4,128)} %taps_ref.9, f32[1,256]{1,0:T(1,128)} %bitcast.101, f32[1,128]{1,0:T(1,128)} %pad.14.step_bias_ref, ...), custom_call_target="tpu_custom_call" | custom-call | flops 2013265920 | bytes 8153088 | tf_op jit(solution)/shard_map/pallas_call | solution.py:293
  455.6 7.0 %convolution_convert_fusion.3 = bf16[2560,276]{1,0:T(8,128)(2,1)} fusion(bf16[1024,2560]{1,0:T(8,128)(2,1)} %fusion.2, bf16[1024,20]{1,0:T(8,128)(2,1)} %bitcast.87, bf16[1024,256]{1,0:T(8,128)(2,1)} %get-tuple-element.201), kind=kOutput, calls=%fused_computation.27 | convolution fusion | flops 1448871936 | bytes 7221248 | tf_op jit(solution)/shard_map/dot_general | solution.py:29
  462.7 3.0 pad_maximum_fusion
  470.8 11.7 %fusion.37 = f32[2560,1024]{1,0:T(8,128)} fusion(bf16[2560,1280]{1,0:T(8,128)(2,1)} %copy-done.6, bf16[1024,1280]{1,0:T(8,128)(2,1)S(1)} %copy-done.14), kind=kOutput, calls=%fused_computation.177 | convolution fusion | flops 6710886400 | bytes 19660800 | tf_op jit(solution)/shard_map/dot_general | solution.py:35
  482.5 2.6 convert_add_fusion.5
  487.7 15.9 %add_convert_fusion = bf16[2560,1024]{1,0:T(8,128)(2,1)} fusion(f32[2560,1024]{1,0:T(8,128)} %fusion.37, bf16[2560,1556]{1,0:T(8,128)(2,1)} %constant_dynamic-update-slice_fusion.30, bf16[1024,1556]{1,0:T(8,128)(2,1)S(1)} %copy-done.9), kind=kOutput, calls=%fused_computation.8 | convolution fusion | flops 8163164160 | bytes 26882048 | tf_op jit(solution)/shard_map/dot_general | solution.py:35
  509.6 3.6 collective-permute-done.88
  520.7 2.6 collective-permute-start.81
  529.6 6.8 %collective-permute-done.81 = bf16[160,1280]{1,0:T(8,128)(2,1)S(1)} collective-permute-done((bf16[160,1280]{1,0:T(8,128)(2,1)}, bf16[160,1280]{1,0:T(8,128)(2,1)S(1)}, u32[]{:S(2)}, u32[]{:S(2)}) %collective-permute-start.81) | collective-permute-done | bytes 409632 | tf_op jit(solution)/shard_map/ppermute | solution.py:548
  540.0 4.4 collective-permute-done.69
  547.9 5.1 collective-permute-done.77
  557.5 4.3 collective-permute-done.70
  563.1 2.6 collective-permute-start.71
  566.3 4.3 collective-permute-done.78
  571.9 2.5 collective-permute-start.79
  575.1 4.3 collective-permute-done.71
  580.7 3.1 collective-permute-start.74
  584.1 2.8 collective-permute-done.84
  591.1 3.2 collective-permute-done.74
  597.3 2.8 collective-permute-done.85
  600.1 2.6 convert_add_fusion.2
  608.3 3.8 collective-permute-done.86
  613.4 2.6 fusion.13
  624.6 5.6 psum.15
  632.4 5.1 fusion.10
  637.5 3.2 copy.64
  (397 shorter events, 209.8 us)
Async XLA Ops:
  7.2 280.3 %all-gather.2.cloned.1.call-start = ((), (), s32[]{:S(2)}) async-start(), calls=%async_computation.3 | async-start | bytes 6553600 | tf_op jit(solution)/shard_map/all_gather | solution.py:619
  9.2 15.1 %collective-permute-start = (bf16[160,1556]{1,0:T(8,128)(2,1)S(1)}, bf16[160,1556]{1,0:T(8,128)(2,1)S(1)}, u32[]{:S(2)}, u32[]{:S(2)}) collective-permute-start(bf16[160,1556]{1,0:T(8,128)(2,1)S(1)} %get-tuple-element.330), channel_id=1, source_target_pairs={{0,8},{8,16},{16,24},{24,28},{28,20},{20,12},{12,4},{4,0},{1,9},{9... | collective-permute-start | bytes 1493768 | tf_op jit(solution)/shard_map/ppermute | solution.py:511
  12.3 13.6 %collective-permute-start.1 = (bf16[160,1556]{1,0:T(8,128)(2,1)S(1)}, bf16[160,1556]{1,0:T(8,128)(2,1)S(1)}, u32[]{:S(2)}, u32[]{:S(2)}) collective-permute-start(bf16[160,1556]{1,0:T(8,128)(2,1)S(1)} %get-tuple-element.329), channel_id=1, source_target_pairs={{8,0},{16,8},{24,16},{28,24},{20,28},{12,20},{4,12},{0,4},{9,1},{1... | collective-permute-start | bytes 1493768 | tf_op jit(solution)/shard_map/ppermute | solution.py:511
  25.8 12.6 %collective-permute-start.2 = (bf16[160,1556]{1,0:T(8,128)(2,1)S(1)}, bf16[160,1556]{1,0:T(8,128)(2,1)S(1)}, u32[]{:S(2)}, u32[]{:S(2)}) collective-permute-start(bf16[160,1556]{1,0:T(8,128)(2,1)S(1)} %collective-permute-done), channel_id=1, source_target_pairs={{0,8},{8,16},{16,24},{24,28},{28,20},{20,12},{12,4},{4,0},{1,9},{9... | collective-permute-start | bytes 1493768 | tf_op jit(solution)/shard_map/ppermute | solution.py:511
  27.4 12.4 %collective-permute-start.3 = (bf16[160,1556]{1,0:T(8,128)(2,1)S(1)}, bf16[160,1556]{1,0:T(8,128)(2,1)S(1)}, u32[]{:S(2)}, u32[]{:S(2)}) collective-permute-start(bf16[160,1556]{1,0:T(8,128)(2,1)S(1)} %collective-permute-done.1), channel_id=1, source_target_pairs={{8,0},{16,8},{24,16},{28,24},{20,28},{12,20},{4,12},{0,4},{9,1},{1... | collective-permute-start | bytes 1493768 | tf_op jit(solution)/shard_map/ppermute | solution.py:511
  39.8 12.1 %collective-permute-start.4 = (bf16[160,1556]{1,0:T(8,128)(2,1)S(1)}, bf16[160,1556]{1,0:T(8,128)(2,1)}, u32[]{:S(2)}, u32[]{:S(2)}) collective-permute-start(bf16[160,1556]{1,0:T(8,128)(2,1)S(1)} %collective-permute-done.2), channel_id=1, source_target_pairs={{0,8},{8,16},{16,24},{24,28},{28,20},{20,12},{12,4},{4,0},{1,9},{9... | collective-permute-start | bytes 1493768 | tf_op jit(solution)/shard_map/ppermute | solution.py:511
  41.3 12.1 %collective-permute-start.9 = (bf16[160,1556]{1,0:T(8,128)(2,1)S(1)}, bf16[160,1556]{1,0:T(8,128)(2,1)}, u32[]{:S(2)}, u32[]{:S(2)}) collective-permute-start(bf16[160,1556]{1,0:T(8,128)(2,1)S(1)} %collective-permute-done.3), channel_id=1, source_target_pairs={{8,0},{16,8},{24,16},{28,24},{20,28},{12,20},{4,12},{0,4},{9,1},{1... | collective-permute-start | bytes 1493768 | tf_op jit(solution)/shard_map/ppermute | solution.py:511
  51.8 12.5 %collective-permute-start.5 = (bf16[160,1556]{1,0:T(8,128)(2,1)}, bf16[160,1556]{1,0:T(8,128)(2,1)S(1)}, u32[]{:S(2)}, u32[]{:S(2)}) collective-permute-start(bf16[160,1556]{1,0:T(8,128)(2,1)} %collective-permute-done.4), channel_id=1, source_target_pairs={{0,8},{8,16},{16,24},{24,28},{28,20},{20,12},{12,4},{4,0},{1,9},{9... | collective-permute-start | bytes 1493768 | tf_op jit(solution)/shard_map/ppermute | solution.py:511
  53.4 12.5 %collective-permute-start.10 = (bf16[160,1556]{1,0:T(8,128)(2,1)}, bf16[160,1556]{1,0:T(8,128)(2,1)S(1)}, u32[]{:S(2)}, u32[]{:S(2)}) collective-permute-start(bf16[160,1556]{1,0:T(8,128)(2,1)} %collective-permute-done.9), channel_id=1, source_target_pairs={{8,0},{16,8},{24,16},{28,24},{20,28},{12,20},{4,12},{0,4},{9,1},{1... | collective-permute-start | bytes 1493768 | tf_op jit(solution)/shard_map/ppermute | solution.py:511
  64.3 12.3 %collective-permute-start.6 = (bf16[160,1556]{1,0:T(8,128)(2,1)S(1)}, bf16[160,1556]{1,0:T(8,128)(2,1)S(1)}, u32[]{:S(2)}, u32[]{:S(2)}) collective-permute-start(bf16[160,1556]{1,0:T(8,128)(2,1)S(1)} %collective-permute-done.5), channel_id=1, source_target_pairs={{0,8},{8,16},{16,24},{24,28},{28,20},{20,12},{12,4},{4,0},{1,9},{9... | collective-permute-start | bytes 1493768 | tf_op jit(solution)/shard_map/ppermute | solution.py:511
  65.9 12.3 %collective-permute-start.11 = (bf16[160,1556]{1,0:T(8,128)(2,1)S(1)}, bf16[160,1556]{1,0:T(8,128)(2,1)S(1)}, u32[]{:S(2)}, u32[]{:S(2)}) collective-permute-start(bf16[160,1556]{1,0:T(8,128)(2,1)S(1)} %collective-permute-done.10), channel_id=1, source_target_pairs={{8,0},{16,8},{24,16},{28,24},{20,28},{12,20},{4,12},{0,4},{9,1},{1... | collective-permute-start | bytes 1493768 | tf_op jit(solution)/shard_map/ppermute | solution.py:511
  76.6 12.9 %collective-permute-start.7 = (bf16[160,1556]{1,0:T(8,128)(2,1)S(1)}, bf16[160,1556]{1,0:T(8,128)(2,1)S(1)}, u32[]{:S(2)}, u32[]{:S(2)}) collective-permute-start(bf16[160,1556]{1,0:T(8,128)(2,1)S(1)} %collective-permute-done.6), channel_id=1, source_target_pairs={{0,8},{8,16},{16,24},{24,28},{28,20},{20,12},{12,4},{4,0},{1,9},{9... | collective-permute-start | bytes 1493768 | tf_op jit(solution)/shard_map/ppermute | solution.py:511
  78.1 12.9 %collective-permute-start.12 = (bf16[160,1556]{1,0:T(8,128)(2,1)S(1)}, bf16[160,1556]{1,0:T(8,128)(2,1)S(1)}, u32[]{:S(2)}, u32[]{:S(2)}) collective-permute-start(bf16[160,1556]{1,0:T(8,128)(2,1)S(1)} %collective-permute-done.11), channel_id=1, source_target_pairs={{8,0},{16,8},{24,16},{28,24},{20,28},{12,20},{4,12},{0,4},{9,1},{1... | collective-permute-start | bytes 1493768 | tf_op jit(solution)/shard_map/ppermute | solution.py:511
  89.4 12.0 %collective-permute-start.8 = (bf16[160,1556]{1,0:T(8,128)(2,1)S(1)}, bf16[160,1556]{1,0:T(8,128)(2,1)S(1)}, u32[]{:S(2)}, u32[]{:S(2)}) collective-permute-start(bf16[160,1556]{1,0:T(8,128)(2,1)S(1)} %collective-permute-done.7), channel_id=1, source_target_pairs={{0,8},{8,16},{16,24},{24,28},{28,20},{20,12},{12,4},{4,0},{1,9},{9... | collective-permute-start | bytes 1493768 | tf_op jit(solution)/shard_map/ppermute | solution.py:511
  91.0 12.3 %collective-permute-start.13 = (bf16[160,1556]{1,0:T(8,128)(2,1)S(1)}, bf16[160,1556]{1,0:T(8,128)(2,1)S(1)}, u32[]{:S(2)}, u32[]{:S(2)}) collective-permute-start(bf16[160,1556]{1,0:T(8,128)(2,1)S(1)} %collective-permute-done.12), channel_id=1, source_target_pairs={{8,0},{16,8},{24,16},{28,24},{20,28},{12,20},{4,12},{0,4},{9,1},{1... | collective-permute-start | bytes 1493768 | tf_op jit(solution)/shard_map/ppermute | solution.py:511
  103.4 12.3 %collective-permute-start.14 = (bf16[160,1280]{1,0:T(8,128)(2,1)S(1)}, bf16[160,1280]{1,0:T(8,128)(2,1)S(1)}, u32[]{:S(2)}, u32[]{:S(2)}) collective-permute-start(bf16[160,1280]{1,0:T(8,128)(2,1)S(1)} %get-tuple-element.334), channel_id=1, source_target_pairs={{0,8},{8,16},{16,24},{24,28},{28,20},{20,12},{12,4},{4,0},{1,9},{9... | collective-permute-start | bytes 1228808 | tf_op jit(solution)/shard_map/ppermute | solution.py:511
  117.7 28.2 %collective-permute-start.16 = (bf16[160,1280]{1,0:T(8,128)(2,1)S(1)}, bf16[160,1280]{1,0:T(8,128)(2,1)S(1)}, u32[]{:S(2)}, u32[]{:S(2)}) collective-permute-start(bf16[160,1280]{1,0:T(8,128)(2,1)S(1)} %collective-permute-done.14), channel_id=1, source_target_pairs={{0,8},{8,16},{16,24},{24,28},{28,20},{20,12},{12,4},{4,0},{1,9},{9... | collective-permute-start | bytes 1228808 | tf_op jit(solution)/shard_map/ppermute | solution.py:511
  118.2 27.8 %collective-permute-start.17 = (bf16[160,1280]{1,0:T(8,128)(2,1)S(1)}, bf16[160,1280]{1,0:T(8,128)(2,1)S(1)}, u32[]{:S(2)}, u32[]{:S(2)}) collective-permute-start(bf16[160,1280]{1,0:T(8,128)(2,1)S(1)} %collective-permute-done.15), channel_id=1, source_target_pairs={{8,0},{16,8},{24,16},{28,24},{20,28},{12,20},{4,12},{0,4},{9,1},{1... | collective-permute-start | bytes 1228808 | tf_op jit(solution)/shard_map/ppermute | solution.py:511
  146.0 13.8 %collective-permute-start.18 = (bf16[160,1280]{1,0:T(8,128)(2,1)S(1)}, bf16[160,1280]{1,0:T(8,128)(2,1)S(1)}, u32[]{:S(2)}, u32[]{:S(2)}) collective-permute-start(bf16[160,1280]{1,0:T(8,128)(2,1)S(1)} %collective-permute-done.16), channel_id=1, source_target_pairs={{0,8},{8,16},{16,24},{24,28},{28,20},{20,12},{12,4},{4,0},{1,9},{9... | collective-permute-start | bytes 1228808 | tf_op jit(solution)/shard_map/ppermute | solution.py:511
  146.5 13.2 %collective-permute-start.19 = (bf16[160,1280]{1,0:T(8,128)(2,1)S(1)}, bf16[160,1280]{1,0:T(8,128)(2,1)}, u32[]{:S(2)}, u32[]{:S(2)}) collective-permute-start(bf16[160,1280]{1,0:T(8,128)(2,1)S(1)} %collective-permute-done.17), channel_id=1, source_target_pairs={{8,0},{16,8},{24,16},{28,24},{20,28},{12,20},{4,12},{0,4},{9,1},{1... | collective-permute-start | bytes 1228808 | tf_op jit(solution)/shard_map/ppermute | solution.py:511
  159.8 23.1 %collective-permute-start.20 = (bf16[160,1280]{1,0:T(8,128)(2,1)S(1)}, bf16[160,1280]{1,0:T(8,128)(2,1)S(1)}, u32[]{:S(2)}, u32[]{:S(2)}) collective-permute-start(bf16[160,1280]{1,0:T(8,128)(2,1)S(1)} %collective-permute-done.18), channel_id=1, source_target_pairs={{0,8},{8,16},{16,24},{24,28},{28,20},{20,12},{12,4},{4,0},{1,9},{9... | collective-permute-start | bytes 1228808 | tf_op jit(solution)/shard_map/ppermute | solution.py:511
  160.3 22.6 %collective-permute-start.21 = (bf16[160,1280]{1,0:T(8,128)(2,1)}, bf16[160,1280]{1,0:T(8,128)(2,1)}, u32[]{:S(2)}, u32[]{:S(2)}) collective-permute-start(bf16[160,1280]{1,0:T(8,128)(2,1)} %collective-permute-done.19), channel_id=1, source_target_pairs={{8,0},{16,8},{24,16},{28,24},{20,28},{12,20},{4,12},{0,4},{9,1},{1... | collective-permute-start | bytes 1228808 | tf_op jit(solution)/shard_map/ppermute | solution.py:511
  182.9 12.1 %collective-permute-start.22 = (bf16[160,1280]{1,0:T(8,128)(2,1)S(1)}, bf16[160,1280]{1,0:T(8,128)(2,1)}, u32[]{:S(2)}, u32[]{:S(2)}) collective-permute-start(bf16[160,1280]{1,0:T(8,128)(2,1)S(1)} %collective-permute-done.20), channel_id=1, source_target_pairs={{0,8},{8,16},{16,24},{24,28},{28,20},{20,12},{12,4},{4,0},{1,9},{9... | collective-permute-start | bytes 1228808 | tf_op jit(solution)/shard_map/ppermute | solution.py:511
  185.0 302.6 %reduce-scatter.4.cloned.1.call-start = ((), (), s32[]{:S(2)}) async-start(), calls=%async_computation.4 | async-start | bytes 6553600 | tf_op jit(solution)/shard_map/reduce_scatter | solution.py:681
  249.2 13.6 %collective-permute-start.35 = (bf16[160,1280]{1,0:T(8,128)(2,1)S(1)}, bf16[160,1280]{1,0:T(8,128)(2,1)S(1)}, u32[]{:S(2)}, u32[]{:S(2)}) collective-permute-start(bf16[160,1280]{1,0:T(8,128)(2,1)S(1)} %collective-permute-done.33), channel_id=1, source_target_pairs={{8,0},{16,8},{24,16},{28,24},{20,28},{12,20},{4,12},{0,4},{9,1},{1... | collective-permute-start | bytes 1228808 | tf_op jit(solution)/shard_map/ppermute | solution.py:511
  320.3 14.3 %collective-permute-start.42 = (bf16[160,1280]{1,0:T(8,128)(2,1)S(1)}, bf16[160,1280]{1,0:T(8,128)(2,1)}, u32[]{:S(2)}, u32[]{:S(2)}) collective-permute-start(bf16[160,1280]{1,0:T(8,128)(2,1)S(1)} %get-tuple-element.161), channel_id=1, source_target_pairs={{0,8},{8,16},{16,24},{24,28},{28,20},{20,12},{12,4},{4,0},{1,9},{9... | collective-permute-start | bytes 1228808 | tf_op jit(solution)/shard_map/ppermute | solution.py:548
  321.3 13.4 %collective-permute-start.43 = (bf16[160,1280]{1,0:T(8,128)(2,1)S(1)}, bf16[160,1280]{1,0:T(8,128)(2,1)}, u32[]{:S(2)}, u32[]{:S(2)}) collective-permute-start(bf16[160,1280]{1,0:T(8,128)(2,1)S(1)} %get-tuple-element.162), channel_id=1, source_target_pairs={{8,0},{16,8},{24,16},{28,24},{20,28},{12,20},{4,12},{0,4},{9,1},{1... | collective-permute-start | bytes 1228808 | tf_op jit(solution)/shard_map/ppermute | solution.py:548
  334.6 260.8 %reduce-scatter.8.cloned.1.call-start = ((), (), s32[]{:S(2)}) async-start(), calls=%async_computation.6 | async-start | bytes 2211840 | tf_op jit(solution)/shard_map/reduce_scatter | solution.py:576
  336.3 16.6 %collective-permute-start.44 = (bf16[160,1280]{1,0:T(8,128)(2,1)S(1)}, bf16[160,1280]{1,0:T(8,128)(2,1)S(1)}, u32[]{:S(2)}, u32[]{:S(2)}) collective-permute-start(bf16[160,1280]{1,0:T(8,128)(2,1)S(1)} %get-tuple-element.164), channel_id=1, source_target_pairs={{0,8},{8,16},{16,24},{24,28},{28,20},{20,12},{12,4},{4,0},{1,9},{9... | collective-permute-start | bytes 1228808 | tf_op jit(solution)/shard_map/ppermute | solution.py:548
  337.2 15.7 %collective-permute-start.45 = (bf16[160,1280]{1,0:T(8,128)(2,1)S(1)}, bf16[160,1280]{1,0:T(8,128)(2,1)S(1)}, u32[]{:S(2)}, u32[]{:S(2)}) collective-permute-start(bf16[160,1280]{1,0:T(8,128)(2,1)S(1)} %get-tuple-element.165), channel_id=1, source_target_pairs={{8,0},{16,8},{24,16},{28,24},{20,28},{12,20},{4,12},{0,4},{9,1},{1... | collective-permute-start | bytes 1228808 | tf_op jit(solution)/shard_map/ppermute | solution.py:548
  367.9 24.3 %collective-permute-start.50 = (bf16[160,1280]{1,0:T(8,128)(2,1)S(1)}, bf16[160,1280]{1,0:T(8,128)(2,1)S(1)}, u32[]{:S(2)}, u32[]{:S(2)}) collective-permute-start(bf16[160,1280]{1,0:T(8,128)(2,1)S(1)} %get-tuple-element.172), channel_id=1, source_target_pairs={{0,8},{8,16},{16,24},{24,28},{28,20},{20,12},{12,4},{4,0},{1,9},{9... | collective-permute-start | bytes 1228808 | tf_op jit(solution)/shard_map/ppermute | solution.py:548
  369.5 23.5 %collective-permute-start.51 = (bf16[160,1280]{1,0:T(8,128)(2,1)S(1)}, bf16[160,1280]{1,0:T(8,128)(2,1)}, u32[]{:S(2)}, u32[]{:S(2)}) collective-permute-start(bf16[160,1280]{1,0:T(8,128)(2,1)S(1)} %get-tuple-element.173), channel_id=1, source_target_pairs={{8,0},{16,8},{24,16},{28,24},{20,28},{12,20},{4,12},{0,4},{9,1},{1... | collective-permute-start | bytes 1228808 | tf_op jit(solution)/shard_map/ppermute | solution.py:548
  369.9 24.3 %collective-permute-start.48 = (bf16[160,1280]{1,0:T(8,128)(2,1)}, bf16[160,1280]{1,0:T(8,128)(2,1)}, u32[]{:S(2)}, u32[]{:S(2)}) collective-permute-start(bf16[160,1280]{1,0:T(8,128)(2,1)} %get-tuple-element.170), channel_id=1, source_target_pairs={{0,8},{8,16},{16,24},{24,28},{28,20},{20,12},{12,4},{4,0},{1,9},{9... | collective-permute-start | bytes 1228808 | tf_op jit(solution)/shard_map/ppermute | solution.py:548
  371.5 22.8 %collective-permute-start.49 = (bf16[160,1280]{1,0:T(8,128)(2,1)S(1)}, bf16[160,1280]{1,0:T(8,128)(2,1)}, u32[]{:S(2)}, u32[]{:S(2)}) collective-permute-start(bf16[160,1280]{1,0:T(8,128)(2,1)S(1)} %get-tuple-element.171), channel_id=1, source_target_pairs={{8,0},{16,8},{24,16},{28,24},{20,28},{12,20},{4,12},{0,4},{9,1},{1... | collective-permute-start | bytes 1228808 | tf_op jit(solution)/shard_map/ppermute | solution.py:548
  395.8 24.7 %collective-permute-start.54 = (bf16[160,1280]{1,0:T(8,128)(2,1)S(1)}, bf16[160,1280]{1,0:T(8,128)(2,1)}, u32[]{:S(2)}, u32[]{:S(2)}) collective-permute-start(bf16[160,1280]{1,0:T(8,128)(2,1)S(1)} %get-tuple-element.189), channel_id=1, source_target_pairs={{0,8},{8,16},{16,24},{24,28},{28,20},{20,12},{12,4},{4,0},{1,9},{9... | collective-permute-start | bytes 1228808 | tf_op jit(solution)/shard_map/ppermute | solution.py:548
  397.5 23.1 %collective-permute-start.55 = (bf16[160,1280]{1,0:T(8,128)(2,1)S(1)}, bf16[160,1280]{1,0:T(8,128)(2,1)}, u32[]{:S(2)}, u32[]{:S(2)}) collective-permute-start(bf16[160,1280]{1,0:T(8,128)(2,1)S(1)} %get-tuple-element.190), channel_id=1, source_target_pairs={{8,0},{16,8},{24,16},{28,24},{20,28},{12,20},{4,12},{0,4},{9,1},{1... | collective-permute-start | bytes 1228808 | tf_op jit(solution)/shard_map/ppermute | solution.py:548
  397.9 24.0 %collective-permute-start.52 = (bf16[160,1280]{1,0:T(8,128)(2,1)S(1)}, bf16[160,1280]{1,0:T(8,128)(2,1)}, u32[]{:S(2)}, u32[]{:S(2)}) collective-permute-start(bf16[160,1280]{1,0:T(8,128)(2,1)S(1)} %get-tuple-element.187), channel_id=1, source_target_pairs={{0,8},{8,16},{16,24},{24,28},{28,20},{20,12},{12,4},{4,0},{1,9},{9... | collective-permute-start | bytes 1228808 | tf_op jit(solution)/shard_map/ppermute | solution.py:548
  399.5 22.5 %collective-permute-start.53 = (bf16[160,1280]{1,0:T(8,128)(2,1)S(1)}, bf16[160,1280]{1,0:T(8,128)(2,1)}, u32[]{:S(2)}, u32[]{:S(2)}) collective-permute-start(bf16[160,1280]{1,0:T(8,128)(2,1)S(1)} %get-tuple-element.188), channel_id=1, source_target_pairs={{8,0},{16,8},{24,16},{28,24},{20,28},{12,20},{4,12},{0,4},{9,1},{1... | collective-permute-start | bytes 1228808 | tf_op jit(solution)/shard_map/ppermute | solution.py:548
  423.5 15.0 %collective-permute-start.58 = (bf16[160,1280]{1,0:T(8,128)(2,1)S(1)}, bf16[160,1280]{1,0:T(8,128)(2,1)S(1)}, u32[]{:S(2)}, u32[]{:S(2)}) collective-permute-start(bf16[160,1280]{1,0:T(8,128)(2,1)S(1)} %get-tuple-element.193), channel_id=1, source_target_pairs={{0,8},{8,16},{16,24},{24,28},{28,20},{20,12},{12,4},{4,0},{1,9},{9... | collective-permute-start | bytes 1228808 | tf_op jit(solution)/shard_map/ppermute | solution.py:548
  425.1 13.4 %collective-permute-start.59 = (bf16[160,1280]{1,0:T(8,128)(2,1)S(1)}, bf16[160,1280]{1,0:T(8,128)(2,1)S(1)}, u32[]{:S(2)}, u32[]{:S(2)}) collective-permute-start(bf16[160,1280]{1,0:T(8,128)(2,1)S(1)} %get-tuple-element.194), channel_id=1, source_target_pairs={{8,0},{16,8},{24,16},{28,24},{20,28},{12,20},{4,12},{0,4},{9,1},{1... | collective-permute-start | bytes 1228808 | tf_op jit(solution)/shard_map/ppermute | solution.py:548
  425.6 15.1 %collective-permute-start.56 = (bf16[160,1280]{1,0:T(8,128)(2,1)S(1)}, bf16[160,1280]{1,0:T(8,128)(2,1)S(1)}, u32[]{:S(2)}, u32[]{:S(2)}) collective-permute-start(bf16[160,1280]{1,0:T(8,128)(2,1)S(1)} %get-tuple-element.191), channel_id=1, source_target_pairs={{0,8},{8,16},{16,24},{24,28},{28,20},{20,12},{12,4},{4,0},{1,9},{9... | collective-permute-start | bytes 1228808 | tf_op jit(solution)/shard_map/ppermute | solution.py:548
  427.2 13.5 %collective-permute-start.57 = (bf16[160,1280]{1,0:T(8,128)(2,1)S(1)}, bf16[160,1280]{1,0:T(8,128)(2,1)S(1)}, u32[]{:S(2)}, u32[]{:S(2)}) collective-permute-start(bf16[160,1280]{1,0:T(8,128)(2,1)S(1)} %get-tuple-element.192), channel_id=1, source_target_pairs={{8,0},{16,8},{24,16},{28,24},{20,28},{12,20},{4,12},{0,4},{9,1},{1... | collective-permute-start | bytes 1228808 | tf_op jit(solution)/shard_map/ppermute | solution.py:548
  442.9 42.2 %collective-permute-start.62 = (bf16[160,1280]{1,0:T(8,128)(2,1)}, bf16[160,1280]{1,0:T(8,128)(2,1)}, u32[]{:S(2)}, u32[]{:S(2)}) collective-permute-start(bf16[160,1280]{1,0:T(8,128)(2,1)} %get-tuple-element.205), channel_id=1, source_target_pairs={{0,8},{8,16},{16,24},{24,28},{28,20},{20,12},{12,4},{4,0},{1,9},{9... | collective-permute-start | bytes 1228808 | tf_op jit(solution)/shard_map/ppermute | solution.py:548
  444.5 40.6 %collective-permute-start.63 = (bf16[160,1280]{1,0:T(8,128)(2,1)}, bf16[160,1280]{1,0:T(8,128)(2,1)}, u32[]{:S(2)}, u32[]{:S(2)}) collective-permute-start(bf16[160,1280]{1,0:T(8,128)(2,1)} %get-tuple-element.206), channel_id=1, source_target_pairs={{8,0},{16,8},{24,16},{28,24},{20,28},{12,20},{4,12},{0,4},{9,1},{1... | collective-permute-start | bytes 1228808 | tf_op jit(solution)/shard_map/ppermute | solution.py:548
  445.0 37.5 %collective-permute-start.60 = (bf16[160,1280]{1,0:T(8,128)(2,1)}, bf16[160,1280]{1,0:T(8,128)(2,1)}, u32[]{:S(2)}, u32[]{:S(2)}) collective-permute-start(bf16[160,1280]{1,0:T(8,128)(2,1)} %get-tuple-element.203), channel_id=1, source_target_pairs={{0,8},{8,16},{16,24},{24,28},{28,20},{20,12},{12,4},{4,0},{1,9},{9... | collective-permute-start | bytes 1228808 | tf_op jit(solution)/shard_map/ppermute | solution.py:548
  446.5 20.1 %collective-permute-start.64 = (bf16[160,1280]{1,0:T(8,128)(2,1)}, bf16[160,1280]{1,0:T(8,128)(2,1)}, u32[]{:S(2)}, u32[]{:S(2)}) collective-permute-start(bf16[160,1280]{1,0:T(8,128)(2,1)} %get-tuple-element.209), channel_id=1, source_target_pairs={{0,8},{8,16},{16,24},{24,28},{28,20},{20,12},{12,4},{4,0},{1,9},{9... | collective-permute-start | bytes 1228808 | tf_op jit(solution)/shard_map/ppermute | solution.py:548
  447.7 20.6 %collective-permute-start.65 = (bf16[160,1280]{1,0:T(8,128)(2,1)S(1)}, bf16[160,1280]{1,0:T(8,128)(2,1)}, u32[]{:S(2)}, u32[]{:S(2)}) collective-permute-start(bf16[160,1280]{1,0:T(8,128)(2,1)S(1)} %get-tuple-element.210), channel_id=1, source_target_pairs={{8,0},{16,8},{24,16},{28,24},{20,28},{12,20},{4,12},{0,4},{9,1},{1... | collective-permute-start | bytes 1228808 | tf_op jit(solution)/shard_map/ppermute | solution.py:548
  462.6 150.8 %reduce-scatter.6.cloned.1.call-start = ((), (), s32[]{:S(2)}) async-start(), calls=%async_computation.5 | async-start | bytes 6553600 | tf_op jit(solution)/shard_map/reduce_scatter | solution.py:732
  466.6 15.9 %collective-permute-start.61 = (bf16[160,1280]{1,0:T(8,128)(2,1)S(1)}, bf16[160,1280]{1,0:T(8,128)(2,1)S(1)}, u32[]{:S(2)}, u32[]{:S(2)}) collective-permute-start(bf16[160,1280]{1,0:T(8,128)(2,1)S(1)} %copy-done.18), channel_id=1, source_target_pairs={{8,0},{16,8},{24,16},{28,24},{20,28},{12,20},{4,12},{0,4},{9,1},{1... | collective-permute-start | bytes 1228808 | tf_op jit(solution)/shard_map/ppermute | solution.py:548
  505.2 18.1 %collective-permute-start.75 = (bf16[160,1280]{1,0:T(8,128)(2,1)}, bf16[160,1280]{1,0:T(8,128)(2,1)}, u32[]{:S(2)}, u32[]{:S(2)}) collective-permute-start(bf16[160,1280]{1,0:T(8,128)(2,1)} %get-tuple-element.215), channel_id=1, source_target_pairs={{0,8},{8,16},{16,24},{24,28},{28,20},{20,12},{12,4},{4,0},{1,9},{9... | collective-permute-start | bytes 1228808 | tf_op jit(solution)/shard_map/ppermute | solution.py:548
  520.7 15.7 %collective-permute-start.81 = (bf16[160,1280]{1,0:T(8,128)(2,1)}, bf16[160,1280]{1,0:T(8,128)(2,1)S(1)}, u32[]{:S(2)}, u32[]{:S(2)}) collective-permute-start(bf16[160,1280]{1,0:T(8,128)(2,1)} %get-tuple-element.216), channel_id=1, source_target_pairs={{8,0},{16,8},{24,16},{28,24},{20,28},{12,20},{4,12},{0,4},{9,1},{1... | collective-permute-start | bytes 1228808 | tf_op jit(solution)/shard_map/ppermute | solution.py:548
  525.2 19.2 %collective-permute-start.69 = (bf16[160,1280]{1,0:T(8,128)(2,1)}, bf16[160,1280]{1,0:T(8,128)(2,1)S(1)}, u32[]{:S(2)}, u32[]{:S(2)}) collective-permute-start(bf16[160,1280]{1,0:T(8,128)(2,1)} %get-tuple-element.213), channel_id=1, source_target_pairs={{0,8},{8,16},{16,24},{24,28},{28,20},{20,12},{12,4},{4,0},{1,9},{9... | collective-permute-start | bytes 1228808 | tf_op jit(solution)/shard_map/ppermute | solution.py:548
  526.6 30.9 %collective-permute-start.72 = (bf16[160,1280]{1,0:T(8,128)(2,1)}, bf16[160,1280]{1,0:T(8,128)(2,1)S(1)}, u32[]{:S(2)}, u32[]{:S(2)}) collective-permute-start(bf16[160,1280]{1,0:T(8,128)(2,1)} %get-tuple-element.214), channel_id=1, source_target_pairs={{8,0},{16,8},{24,16},{28,24},{20,28},{12,20},{4,12},{0,4},{9,1},{1... | collective-permute-start | bytes 1228808 | tf_op jit(solution)/shard_map/ppermute | solution.py:548
  537.7 15.3 %collective-permute-start.77 = (bf16[160,1280]{1,0:T(8,128)(2,1)S(1)}, bf16[160,1280]{1,0:T(8,128)(2,1)S(1)}, u32[]{:S(2)}, u32[]{:S(2)}) collective-permute-start(bf16[160,1280]{1,0:T(8,128)(2,1)S(1)} %get-tuple-element.289), channel_id=1, source_target_pairs={{0,8},{8,16},{16,24},{24,28},{28,20},{20,12},{12,4},{4,0},{1,9},{9... | collective-permute-start | bytes 1228808 | tf_op jit(solution)/shard_map/ppermute | solution.py:548
  539.4 13.6 %collective-permute-start.82 = (bf16[160,1280]{1,0:T(8,128)(2,1)S(1)}, bf16[160,1280]{1,0:T(8,128)(2,1)S(1)}, u32[]{:S(2)}, u32[]{:S(2)}) collective-permute-start(bf16[160,1280]{1,0:T(8,128)(2,1)S(1)} %get-tuple-element.290), channel_id=1, source_target_pairs={{8,0},{16,8},{24,16},{28,24},{20,28},{12,20},{4,12},{0,4},{9,1},{1... | collective-permute-start | bytes 1228808 | tf_op jit(solution)/shard_map/ppermute | solution.py:548
  545.5 16.3 %collective-permute-start.70 = (bf16[160,1280]{1,0:T(8,128)(2,1)S(1)}, bf16[160,1280]{1,0:T(8,128)(2,1)S(1)}, u32[]{:S(2)}, u32[]{:S(2)}) collective-permute-start(bf16[160,1280]{1,0:T(8,128)(2,1)S(1)} %add_convert_fusion.14), channel_id=1, source_target_pairs={{0,8},{8,16},{16,24},{24,28},{28,20},{20,12},{12,4},{4,0},{1,9},{9... | collective-permute-start | bytes 1228808 | tf_op jit(solution)/shard_map/ppermute | solution.py:548
  554.5 16.1 %collective-permute-start.78 = (bf16[160,1280]{1,0:T(8,128)(2,1)S(1)}, bf16[160,1280]{1,0:T(8,128)(2,1)S(1)}, u32[]{:S(2)}, u32[]{:S(2)}) collective-permute-start(bf16[160,1280]{1,0:T(8,128)(2,1)S(1)} %get-tuple-element.287), channel_id=1, source_target_pairs={{0,8},{8,16},{16,24},{24,28},{28,20},{20,12},{12,4},{4,0},{1,9},{9... | collective-permute-start | bytes 1228808 | tf_op jit(solution)/shard_map/ppermute | solution.py:548
  557.0 13.6 %collective-permute-start.83 = (bf16[160,1280]{1,0:T(8,128)(2,1)S(1)}, bf16[160,1280]{1,0:T(8,128)(2,1)S(1)}, u32[]{:S(2)}, u32[]{:S(2)}) collective-permute-start(bf16[160,1280]{1,0:T(8,128)(2,1)S(1)} %get-tuple-element.288), channel_id=1, source_target_pairs={{8,0},{16,8},{24,16},{28,24},{20,28},{12,20},{4,12},{0,4},{9,1},{1... | collective-permute-start | bytes 1228808 | tf_op jit(solution)/shard_map/ppermute | solution.py:548
  563.1 16.2 %collective-permute-start.71 = (bf16[160,1280]{1,0:T(8,128)(2,1)S(1)}, bf16[160,1280]{1,0:T(8,128)(2,1)S(1)}, u32[]{:S(2)}, u32[]{:S(2)}) collective-permute-start(bf16[160,1280]{1,0:T(8,128)(2,1)S(1)} %get-tuple-element.293), channel_id=1, source_target_pairs={{0,8},{8,16},{16,24},{24,28},{28,20},{20,12},{12,4},{4,0},{1,9},{9... | collective-permute-start | bytes 1228808 | tf_op jit(solution)/shard_map/ppermute | solution.py:548
  565.7 13.7 %collective-permute-start.73 = (bf16[160,1280]{1,0:T(8,128)(2,1)S(1)}, bf16[160,1280]{1,0:T(8,128)(2,1)S(1)}, u32[]{:S(2)}, u32[]{:S(2)}) collective-permute-start(bf16[160,1280]{1,0:T(8,128)(2,1)S(1)} %get-tuple-element.294), channel_id=1, source_target_pairs={{8,0},{16,8},{24,16},{28,24},{20,28},{12,20},{4,12},{0,4},{9,1},{1... | collective-permute-start | bytes 1228808 | tf_op jit(solution)/shard_map/ppermute | solution.py:548
  571.9 12.2 %collective-permute-start.79 = (bf16[160,1280]{1,0:T(8,128)(2,1)S(1)}, bf16[160,1280]{1,0:T(8,128)(2,1)S(1)}, u32[]{:S(2)}, u32[]{:S(2)}) collective-permute-start(bf16[160,1280]{1,0:T(8,128)(2,1)S(1)} %get-tuple-element.285), channel_id=1, source_target_pairs={{0,8},{8,16},{16,24},{24,28},{28,20},{20,12},{12,4},{4,0},{1,9},{9... | collective-permute-start | bytes 1228808 | tf_op jit(solution)/shard_map/ppermute | solution.py:548
  574.4 12.4 %collective-permute-start.84 = (bf16[160,1280]{1,0:T(8,128)(2,1)S(1)}, bf16[160,1280]{1,0:T(8,128)(2,1)S(1)}, u32[]{:S(2)}, u32[]{:S(2)}) collective-permute-start(bf16[160,1280]{1,0:T(8,128)(2,1)S(1)} %get-tuple-element.286), channel_id=1, source_target_pairs={{8,0},{16,8},{24,16},{28,24},{20,28},{12,20},{4,12},{0,4},{9,1},{1... | collective-permute-start | bytes 1228808 | tf_op jit(solution)/shard_map/ppermute | solution.py:548
  580.7 13.6 %collective-permute-start.74 = (bf16[160,1280]{1,0:T(8,128)(2,1)S(1)}, bf16[160,1280]{1,0:T(8,128)(2,1)S(1)}, u32[]{:S(2)}, u32[]{:S(2)}) collective-permute-start(bf16[160,1280]{1,0:T(8,128)(2,1)S(1)} %get-tuple-element.292), channel_id=1, source_target_pairs={{8,0},{16,8},{24,16},{28,24},{20,28},{12,20},{4,12},{0,4},{9,1},{1... | collective-permute-start | bytes 1228808 | tf_op jit(solution)/shard_map/ppermute | solution.py:548
  630.3 12.8 %collective-permute-start.68 = (f32[640]{0:T(1024)S(1)}, f32[640]{0:T(1024)S(1)}, u32[]{:S(2)}, u32[]{:S(2)}) collective-permute-start(f32[640]{0:T(1024)S(1)} %add.907), channel_id=1, source_target_pairs={{0,16},{4,20},{8,24},{12,28},{16,0},{20,4},{24,8},{28,12},{1,17},{... | collective-permute-start | bytes 7688 | tf_op jit(solution)/shard_map/ppermute | solution.py:570
  (76 other events, 1117.6 us)
Sparse Core Ops, SparseCore 0:
  185.1 37.6 all-gather.1
  334.7 50.3 reduce-scatter.3
  462.7 68.3 reduce-scatter.7
  533.5 51.0 reduce-scatter.5

commit v9 on v8

--- a/solution.py
+++ b/solution.py
@@ -693,14 +693,19 @@
     normed = tie(normed, out_ring)
     gate_ring = RingSum(row_major(contract_rows(normed, grad_gate_in).astype(low)))
 
-    half = (mixer.pairs + 1) // 2
+    first = (mixer.pairs + 2) // 3
+    second = (first + mixer.pairs + 1) // 2
     out_ring.step()
     grad_mixed = tie(grad_mixed, out_ring, gate_ring)
-    part = mixer.backward_part(grad_mixed, 0, half)
+    part = mixer.backward_part(grad_mixed, 0, first)
     out_ring.step()
     gate_ring.step()
     grad_mixed = tie(grad_mixed, out_ring, gate_ring)
-    value_grad, value_sums, *totals = mixer.backward_part(grad_mixed, half, mixer.pairs, part)
+    part = mixer.backward_part(grad_mixed, first, second, part)
+    out_ring.step()
+    gate_ring.step()
+    grad_mixed = tie(grad_mixed, out_ring, gate_ring)
+    value_grad, value_sums, *totals = mixer.backward_part(grad_mixed, second, mixer.pairs, part)
     grad_value_in = value_grad[:, : gate_weight.shape[1]]
     out_ring.step()
     gate_ring.step()

time: 657 us -> 677 us (1.030)
  waiting for transfers between devices: 177 us -> 200 us
  starting transfers between devices: 102 us -> 93.9 us
    ppermute x42, waiting for transfers between devices: 44 us -> 58.2 us  [step(): lax.ppermute(held, 'gx', move).astype(wide)]
    ppermute x8, waiting for transfers between devices: 6.07 us -> 14.7 us  [butterfly_sum(): v = v + lax.ppermute(v, axis, flips(count, bit))]
    ppermute x42, starting transfers between devices: 53.1 us -> 45.6 us  [step(): lax.ppermute(held, 'gx', move).astype(wide)]
    pallas_call x5 -> x6, Pallas kernels: 83.3 us -> 88.9 us  [call(): pl.pallas_call(kernel, out_shape=shapes, scratch_shapes=list(scratch), co...]
  transfers between devices with their start and end apart: 96 -> 96, of which waited for: 48 -> 51; matrix products, arithmetic and copies ran while one was open for 35% -> 34% of each run, Pallas kernels for 13% -> 13%
where the time goes in v9:
time: 677 us; the launch traced here: 669 us
  waiting for transfers between devices  200 us (30%)
  matrix products  110 us (16%)
  starting transfers between devices  93.9 us (14%)
  Pallas kernels  88.9 us (13%)
  other arithmetic  82.4 us (12%)
  local copies, waits for them, and re-layouts  68.2 us (10%)
  between operations  15.1 us (2%)
  blocking collectives  11.4 us (2%)
    ppermute x42, waiting for transfers between devices, step(): lax.ppermute(held, 'gx', move)  127 us
    pallas_call x6, Pallas kernels, call(): pl.pallas_call(kernel, out_shape=shapes, scratch_shapes=list(scratch), co...  88.9 us
    ppermute x42, waiting for transfers between devices, step(): lax.ppermute(held, 'gx', move).astype(wide)  58.2 us
    ppermute x42, starting transfers between devices, step(): lax.ppermute(held, 'gx', move).astype(wide)  45.6 us
    ppermute x42, starting transfers between devices, step(): lax.ppermute(held, 'gx', move)  40.5 us
    dot_general x3, matrix products, contract_cols(): lax.dot_general(left, right, (((1,), (1,)), ((), ())), preferred_element_...  39.1 us
    dot_general x4, matrix products, dot(): jnp.dot(left, right, preferred_element_type=wide, precision=precision)  36.1 us
    dot_general x4, matrix products, contract_rows(): lax.dot_general(left, right, (((0,), (0,)), ((), ())), preferred_element_...  34.6 us
  transfers between devices with their start and end apart: 96, of which 51 were waited for; matrix products, arithmetic and copies ran while one was open for 34% of the time, Pallas kernels for 13%

profile of v9, /device:TPU:0, one launch (start us, length us, event | category | flops | bytes accessed | tf_op | source)
XLA Modules:
  0.0 669.2 jit_solution(991200856519196850)
XLA Ops:
  9.2 3.1 collective-permute-start
  12.6 11.7 %collective-permute-done = bf16[160,1556]{1,0:T(8,128)(2,1)S(1)} collective-permute-done((bf16[160,1556]{1,0:T(8,128)(2,1)S(1)}, bf16[160,1556]{1,0:T(8,128)(2,1)S(1)}, u32[]{:S(2)}, u32[]{:S(2)}) %collective-permute-start) | collective-permute-done | bytes 497952 | tf_op jit(solution)/shard_map/ppermute | solution.py:511
  29.6 3.6 fusion.2
  33.1 5.3 collective-permute-done.2
  44.4 7.4 %collective-permute-done.4 = bf16[160,1556]{1,0:T(8,128)(2,1)} collective-permute-done((bf16[160,1556]{1,0:T(8,128)(2,1)S(1)}, bf16[160,1556]{1,0:T(8,128)(2,1)}, u32[]{:S(2)}, u32[]{:S(2)}) %collective-permute-start.4) | collective-permute-done | bytes 497952 | tf_op jit(solution)/shard_map/ppermute | solution.py:511
  56.4 7.9 %collective-permute-done.5 = bf16[160,1556]{1,0:T(8,128)(2,1)S(1)} collective-permute-done((bf16[160,1556]{1,0:T(8,128)(2,1)}, bf16[160,1556]{1,0:T(8,128)(2,1)S(1)}, u32[]{:S(2)}, u32[]{:S(2)}) %collective-permute-start.5) | collective-permute-done | bytes 497952 | tf_op jit(solution)/shard_map/ppermute | solution.py:511
  70.9 5.6 collective-permute-done.6
  81.1 8.3 %collective-permute-done.7 = bf16[160,1556]{1,0:T(8,128)(2,1)S(1)} collective-permute-done((bf16[160,1556]{1,0:T(8,128)(2,1)S(1)}, bf16[160,1556]{1,0:T(8,128)(2,1)S(1)}, u32[]{:S(2)}, u32[]{:S(2)}) %collective-permute-start.7) | collective-permute-done | bytes 497952 | tf_op jit(solution)/shard_map/ppermute | solution.py:511
  94.1 7.4 %collective-permute-done.8 = bf16[160,1556]{1,0:T(8,128)(2,1)S(1)} collective-permute-done((bf16[160,1556]{1,0:T(8,128)(2,1)S(1)}, bf16[160,1556]{1,0:T(8,128)(2,1)S(1)}, u32[]{:S(2)}, u32[]{:S(2)}) %collective-permute-start.8) | collective-permute-done | bytes 497952 | tf_op jit(solution)/shard_map/ppermute | solution.py:511
  103.4 2.8 collective-permute-start.14
  107.9 7.8 %collective-permute-done.14 = bf16[160,1280]{1,0:T(8,128)(2,1)S(1)} collective-permute-done((bf16[160,1280]{1,0:T(8,128)(2,1)S(1)}, bf16[160,1280]{1,0:T(8,128)(2,1)S(1)}, u32[]{:S(2)}, u32[]{:S(2)}) %collective-permute-start.14) | collective-permute-done | bytes 409632 | tf_op jit(solution)/shard_map/ppermute | solution.py:511
  120.3 4.4 fusion.19
  128.5 17.5 %shard_map.288 = (bf16[1024,128]{1,0:T(8,128)(2,1)}, bf16[1024,128]{1,0:T(8,128)(2,1)}, bf16[128,1024]{1,0:T(8,128)(2,1)}, bf16[128,1024]{1,0:T(8,128)(2,1)}, f3...) custom-call(f32[1024,256]{1,0:T(8,128)} %slice.164.state_ref, ...), custom_call_target="tpu_custom_call" | custom-call | flops 2013265920 | bytes 17315840 | tf_op jit(solution)/shard_map/pallas_call | solution.py:293
  148.2 11.6 %fusion.4.value_ref = f32[1024,1280]{1,0:T(8,128)} fusion(bf16[1024,2560]{1,0:T(8,128)(2,1)S(1)} %bitcast.72, bf16[2560,1556]{1,0:T(8,128)(2,1)} %constant_dynamic-update-slice_fusion.30), kind=kOutput, calls=%fused_computation.11 | convolution fusion | flops 6710886400 | bytes 17039360 | tf_op jit(solution)/shard_map/dot_general | solution.py:25
  164.8 18.1 %shard_map.289.mixed_ref = f32[1024,1280]{1,0:T(8,128)} custom-call(f32[1024,1280]{1,0:T(8,128)} %fusion.4.value_ref, f32[4,1280]{1,0:T(4,128)} %taps_ref.10, f32[1,1280]{1,0:T(1,128)} %broadcast_in_dim.54.bias_ref, f32[1,1280]{1,0:T(1,128)} %broadcast_in_dim_reshape.3.skip_ref, f32[1024,1280]{1,0:T(8,128)} %get-tuple-element.147.dtx_ref, ...), custom_call_target="tpu_custom_call" | custom-call | flops 3355443200 | bytes 24754176 | tf_op jit(solution)/shard_map/pallas_call | solution.py:293
  185.6 9.4 %collective-permute-done.22 = bf16[160,1280]{1,0:T(8,128)(2,1)} collective-permute-done((bf16[160,1280]{1,0:T(8,128)(2,1)S(1)}, bf16[160,1280]{1,0:T(8,128)(2,1)}, u32[]{:S(2)}, u32[]{:S(2)}) %collective-permute-start.22) | collective-permute-done | bytes 409632 | tf_op jit(solution)/shard_map/ppermute | solution.py:511
  201.7 4.6 collective-permute-done.24
  208.4 8.0 %collective-permute-done.25 = bf16[160,1280]{1,0:T(8,128)(2,1)S(1)} collective-permute-done((bf16[160,1280]{1,0:T(8,128)(2,1)S(1)}, bf16[160,1280]{1,0:T(8,128)(2,1)S(1)}, u32[]{:S(2)}, u32[]{:S(2)}) %collective-permute-start.25) | collective-permute-done | bytes 409632 | tf_op jit(solution)/shard_map/ppermute | solution.py:511
  219.0 3.2 broadcast.80
  223.1 2.7 collective-permute-done.28
  229.7 6.9 %fusion.36 = f32[1024,1280]{1,0:T(8,128)S(1)} fusion(bf16[1024,2560]{1,0:T(8,128)(2,1)S(1)} %bitcast.74, bf16[2560,1280]{1,0:T(8,128)(2,1)S(1)} %constant_dynamic-update-slice_fusion.15), kind=kOutput, calls=%fused_computation.176 | convolution fusion | flops 6710886400 | bytes 17039360 | tf_op jit(solution)/shard_map/dot_general | solution.py:25
  240.9 3.1 multiply_convert_fusion.3
  244.1 5.2 collective-permute-done.32
  256.0 5.0 collective-permute-done.34
  264.6 4.3 collective-permute-done.36
  272.6 4.3 collective-permute-done.38
  280.5 4.4 collective-permute-done.40
  287.5 13.2 %multiply_reduce_fusion.2 = (f32[1024]{0:T(1024)S(1)}, f32[1024]{0:T(1024)S(1)}, f32[1024,1280]{1,0:T(8,128)}) fusion(f32[1024,1280]{1,0:T(8,128)} %get-tuple-element.301, f32[1280]{0:T(1024)S(1)} %copy-done.23, bf16[1024,2560]{1,0:T(8,128)(2,1)} %all-gather.2.cloned.1.call-done, bf16[2560,1280]{1,0:T(8,128)(2,1)} %constant_dynamic-update-slice_fusion), kind=kOutput, calls=%fused_computation.18 | convolution fusion | flops 6717437952 | bytes 22295552 | tf_op jit(solution)/shard_map/dot_general | solution.py:25
  300.8 5.8 psum.14
  306.6 11.1 %fusion.3 = bf16[2560,1280]{1,0:T(8,128)(2,1)S(1)} fusion(bf16[1024,2560]{1,0:T(8,128)(2,1)} %all-gather.2.cloned.1.call-done, f32[1024,1280]{1,0:T(8,128)} %get-tuple-element.301, f32[1024]{0:T(1024)S(1)} %bitcast.91, f32[1280]{0:T(1024)S(1)} %copy-done.23), kind=kOutput, calls=%fused_computation.10 | convolution fusion | flops 6718095360 | bytes 17048576 | tf_op jit(solution)/shard_map/dot_general | solution.py:29
  317.6 2.7 copy-done.5
  322.8 11.6 %multiply_convert_fusion = bf16[2560,1024]{1,0:T(8,128)(2,1)} fusion(bf16[2560,1280]{1,0:T(8,128)(2,1)} %constant_dynamic-update-slice_fusion, bf16[1024,1280]{1,0:T(8,128)(2,1)S(1)} %get-tuple-element.171, f32[1024]{0:T(1024)S(1)} %bitcast.92), kind=kOutput, calls=%fused_computation.9 | convolution fusion | flops 6716129280 | bytes 14422016 | tf_op jit(solution)/shard_map/dot_general | solution.py:35
  338.2 14.6 %multiply_convert_fusion.1 = (bf16[1024,1280]{1,0:T(8,128)(2,1)S(1)}, f32[1024,1280]{1,0:T(8,128)}, f32[1280]{0:T(1024)}) fusion(f32[1024,1280]{1,0:T(8,128)} %copy-done.1, f32[1024,1280]{1,0:T(8,128)} %shard_map.289.mixed_ref, f32[1024,1280]{1,0:T(8,128)} %get-tuple-element.301, f32[1024]{0:T(1024)S(1)} %fusion.25, f32[1024,1280]{1,0:T(8,128)} %get-tuple-element.175, ...), kind=kLoop, calls=%fused_computation.14 | loop fusion | flops 24902400 | bytes 28854272 | tf_op jit(solution)/shard_map/convert_element_type | solution.py:690
  356.9 7.4 %convolution_convert_fusion.1 = bf16[2560,1280]{1,0:T(8,128)(2,1)S(1)} fusion(bf16[1024,2560]{1,0:T(8,128)(2,1)S(1)} %bitcast.76, bf16[1024,1280]{1,0:T(8,128)(2,1)S(1)} %get-tuple-element.235), kind=kOutput, calls=%fused_computation.3 | convolution fusion | flops 6714163200 | bytes 14417920 | tf_op jit(solution)/shard_map/dot_general | solution.py:29
  371.2 8.3 %collective-permute-done.50 = bf16[160,1280]{1,0:T(8,128)(2,1)S(1)} collective-permute-done((bf16[160,1280]{1,0:T(8,128)(2,1)S(1)}, bf16[160,1280]{1,0:T(8,128)(2,1)S(1)}, u32[]{:S(2)}, u32[]{:S(2)}) %collective-permute-start.50) | collective-permute-done | bytes 409632 | tf_op jit(solution)/shard_map/ppermute | solution.py:548
  381.4 3.5 collective-permute-done.48
  389.5 17.0 %shard_map.290 = (bf16[1024,1280]{1,0:T(8,128)(2,1)}, f32[8,1280]{1,0:T(8,128)}, f32[1024,128]{1,0:T(8,128)}, f32[1024,128]{1,0:T(8,128)}, f32[1024,128]{1,0:T(8...) custom-call(f32[1024,1280]{1,0:T(8,128)} %fusion.4.value_ref, f32[1024,1280]{1,0:T(8,128)} %shard_map.289.mixed_ref, ...), custom_call_target="tpu_custom_call" | custom-call | flops 4026531840 | bytes 35805184 | tf_op jit(solution)/shard_map/pallas_call | solution.py:293
  409.8 5.7 collective-permute-done.52
  419.5 14.7 %shard_map.291 = (bf16[1024,1280]{1,0:T(8,128)(2,1)}, f32[8,1280]{1,0:T(8,128)}, f32[1024,128]{1,0:T(8,128)}, f32[1024,128]{1,0:T(8,128)}, f32[1024,128]{1,0:T(8...) custom-call(f32[1024,1280]{1,0:T(8,128)} %fusion.4.value_ref, ...), custom_call_target="tpu_custom_call", output_to_operand_aliasing={{0}: (15, {}), {1}: (16, {})} | custom-call | flops 3019898880 | bytes 41089024 | tf_op jit(solution)/shard_map/pallas_call | solution.py:293
  436.3 14.6 %shard_map.292 = (bf16[1024,1280]{1,0:T(8,128)(2,1)}, f32[8,1280]{1,0:T(8,128)}, f32[1024,128]{1,0:T(8,128)}, f32[1024,128]{1,0:T(8,128)}, f32[1024,128]{1,0:T(8...) custom-call(f32[1024,1280]{1,0:T(8,128)} %fusion.4.value_ref, ...), custom_call_target="tpu_custom_call", output_to_operand_aliasing={{0}: (15, {}), {1}: (16, {})} | custom-call | flops 3019898880 | bytes 41089024 | tf_op jit(solution)/shard_map/pallas_call | solution.py:293
  458.2 9.0 %convolution_convert_fusion = bf16[2560,1280]{1,0:T(8,128)(2,1)S(1)} fusion(bf16[1024,2560]{1,0:T(8,128)(2,1)S(1)} %bitcast.78, bf16[1024,1280]{1,0:T(8,128)(2,1)} %get-tuple-element.209), kind=kOutput, calls=%fused_computation.2 | convolution fusion | flops 6714163200 | bytes 14417920 | tf_op jit(solution)/shard_map/dot_general | solution.py:29
  467.3 2.8 copy-done.4
  473.1 2.5 convert_add_fusion.5
  479.6 7.0 %shard_map.293 = (bf16[1024,256]{1,0:T(8,128)(2,1)}, bf16[1024,128]{1,0:T(8,128)(2,1)}, f32[8,256]{1,0:T(8,128)}, f32[8,128]{1,0:T(8,128)}) custom-call(f32[1024,256]{1,0:T(8,128)} %slice.164.state_ref, f32[1024,128]{1,0:T(8,128)} %pad.13.step_ref, f32[4,256]{1,0:T(4,128)} %taps_ref.11, f32[1,256]{1,0:T(1,128)} %bitcast.103, f32[1,128]{1,0:T(1,128)} %pad.14.step_bias_ref, ...), custom_call_target="tpu_custom_call" | custom-call | flops 2013265920 | bytes 8153088 | tf_op jit(solution)/shard_map/pallas_call | solution.py:293
  486.6 7.0 %convolution_convert_fusion.3 = bf16[2560,276]{1,0:T(8,128)(2,1)} fusion(bf16[1024,2560]{1,0:T(8,128)(2,1)} %fusion.2, bf16[1024,20]{1,0:T(8,128)(2,1)} %bitcast.89, bf16[1024,256]{1,0:T(8,128)(2,1)} %get-tuple-element.225), kind=kOutput, calls=%fused_computation.27 | convolution fusion | flops 1448871936 | bytes 7221248 | tf_op jit(solution)/shard_map/dot_general | solution.py:29
  494.1 3.0 pad_maximum_fusion
  499.6 11.6 %fusion.37 = f32[2560,1024]{1,0:T(8,128)} fusion(bf16[2560,1280]{1,0:T(8,128)(2,1)} %copy-done.6, bf16[1024,1280]{1,0:T(8,128)(2,1)S(1)} %copy-done.14), kind=kOutput, calls=%fused_computation.177 | convolution fusion | flops 6710886400 | bytes 19660800 | tf_op jit(solution)/shard_map/dot_general | solution.py:35
  511.2 2.5 add_convert_fusion.15
  513.7 15.8 %add_convert_fusion = bf16[2560,1024]{1,0:T(8,128)(2,1)} fusion(f32[2560,1024]{1,0:T(8,128)} %fusion.37, bf16[2560,1556]{1,0:T(8,128)(2,1)} %constant_dynamic-update-slice_fusion.30, bf16[1024,1556]{1,0:T(8,128)(2,1)S(1)} %copy-done.9), kind=kOutput, calls=%fused_computation.8 | convolution fusion | flops 8163164160 | bytes 26882048 | tf_op jit(solution)/shard_map/dot_general | solution.py:35
  534.0 9.4 %collective-permute-done.75 = bf16[160,1280]{1,0:T(8,128)(2,1)S(1)} collective-permute-done((bf16[160,1280]{1,0:T(8,128)(2,1)}, bf16[160,1280]{1,0:T(8,128)(2,1)S(1)}, u32[]{:S(2)}, u32[]{:S(2)}) %collective-permute-start.75) | collective-permute-done | bytes 409632 | tf_op jit(solution)/shard_map/ppermute | solution.py:548
  545.6 13.8 %collective-permute-done.88 = f32[9020]{0:T(1024)S(1)} collective-permute-done((f32[9020]{0:T(1024)S(1)}, f32[9020]{0:T(1024)S(1)}, u32[]{:S(2)}, u32[]{:S(2)}) %collective-permute-start.88) | collective-permute-done | bytes 36112 | tf_op jit(solution)/shard_map/ppermute | solution.py:570
  567.5 2.5 collective-permute-start.77
  575.1 4.9 collective-permute-done.77
  581.3 2.5 collective-permute-start.78
  583.8 5.0 collective-permute-done.71
  592.4 2.7 collective-permute-done.78
  603.8 4.4 collective-permute-done.79
  615.7 3.3 collective-permute-done.80
  620.9 2.6 convert_add_fusion.2
  629.4 2.5 collective-permute-done.86
  633.2 2.6 fusion.13
  643.4 5.6 psum.15
  651.1 5.1 fusion.10
  656.2 3.2 copy.66
  (399 shorter events, 209.0 us)
Async XLA Ops:
  7.2 280.3 %all-gather.2.cloned.1.call-start = ((), (), s32[]{:S(2)}) async-start(), calls=%async_computation.3 | async-start | bytes 6553600 | tf_op jit(solution)/shard_map/all_gather | solution.py:619
  9.2 15.1 %collective-permute-start = (bf16[160,1556]{1,0:T(8,128)(2,1)S(1)}, bf16[160,1556]{1,0:T(8,128)(2,1)S(1)}, u32[]{:S(2)}, u32[]{:S(2)}) collective-permute-start(bf16[160,1556]{1,0:T(8,128)(2,1)S(1)} %get-tuple-element.354), channel_id=1, source_target_pairs={{0,8},{8,16},{16,24},{24,28},{28,20},{20,12},{12,4},{4,0},{1,9},{9... | collective-permute-start | bytes 1493768 | tf_op jit(solution)/shard_map/ppermute | solution.py:511
  12.3 13.6 %collective-permute-start.1 = (bf16[160,1556]{1,0:T(8,128)(2,1)S(1)}, bf16[160,1556]{1,0:T(8,128)(2,1)S(1)}, u32[]{:S(2)}, u32[]{:S(2)}) collective-permute-start(bf16[160,1556]{1,0:T(8,128)(2,1)S(1)} %get-tuple-element.353), channel_id=1, source_target_pairs={{8,0},{16,8},{24,16},{28,24},{20,28},{12,20},{4,12},{0,4},{9,1},{1... | collective-permute-start | bytes 1493768 | tf_op jit(solution)/shard_map/ppermute | solution.py:511
  25.8 12.6 %collective-permute-start.2 = (bf16[160,1556]{1,0:T(8,128)(2,1)S(1)}, bf16[160,1556]{1,0:T(8,128)(2,1)S(1)}, u32[]{:S(2)}, u32[]{:S(2)}) collective-permute-start(bf16[160,1556]{1,0:T(8,128)(2,1)S(1)} %collective-permute-done), channel_id=1, source_target_pairs={{0,8},{8,16},{16,24},{24,28},{28,20},{20,12},{12,4},{4,0},{1,9},{9... | collective-permute-start | bytes 1493768 | tf_op jit(solution)/shard_map/ppermute | solution.py:511
  27.4 12.4 %collective-permute-start.3 = (bf16[160,1556]{1,0:T(8,128)(2,1)S(1)}, bf16[160,1556]{1,0:T(8,128)(2,1)S(1)}, u32[]{:S(2)}, u32[]{:S(2)}) collective-permute-start(bf16[160,1556]{1,0:T(8,128)(2,1)S(1)} %collective-permute-done.1), channel_id=1, source_target_pairs={{8,0},{16,8},{24,16},{28,24},{20,28},{12,20},{4,12},{0,4},{9,1},{1... | collective-permute-start | bytes 1493768 | tf_op jit(solution)/shard_map/ppermute | solution.py:511
  39.8 12.1 %collective-permute-start.4 = (bf16[160,1556]{1,0:T(8,128)(2,1)S(1)}, bf16[160,1556]{1,0:T(8,128)(2,1)}, u32[]{:S(2)}, u32[]{:S(2)}) collective-permute-start(bf16[160,1556]{1,0:T(8,128)(2,1)S(1)} %collective-permute-done.2), channel_id=1, source_target_pairs={{0,8},{8,16},{16,24},{24,28},{28,20},{20,12},{12,4},{4,0},{1,9},{9... | collective-permute-start | bytes 1493768 | tf_op jit(solution)/shard_map/ppermute | solution.py:511
  41.3 12.1 %collective-permute-start.9 = (bf16[160,1556]{1,0:T(8,128)(2,1)S(1)}, bf16[160,1556]{1,0:T(8,128)(2,1)}, u32[]{:S(2)}, u32[]{:S(2)}) collective-permute-start(bf16[160,1556]{1,0:T(8,128)(2,1)S(1)} %collective-permute-done.3), channel_id=1, source_target_pairs={{8,0},{16,8},{24,16},{28,24},{20,28},{12,20},{4,12},{0,4},{9,1},{1... | collective-permute-start | bytes 1493768 | tf_op jit(solution)/shard_map/ppermute | solution.py:511
  51.8 12.5 %collective-permute-start.5 = (bf16[160,1556]{1,0:T(8,128)(2,1)}, bf16[160,1556]{1,0:T(8,128)(2,1)S(1)}, u32[]{:S(2)}, u32[]{:S(2)}) collective-permute-start(bf16[160,1556]{1,0:T(8,128)(2,1)} %collective-permute-done.4), channel_id=1, source_target_pairs={{0,8},{8,16},{16,24},{24,28},{28,20},{20,12},{12,4},{4,0},{1,9},{9... | collective-permute-start | bytes 1493768 | tf_op jit(solution)/shard_map/ppermute | solution.py:511
  53.4 12.5 %collective-permute-start.10 = (bf16[160,1556]{1,0:T(8,128)(2,1)}, bf16[160,1556]{1,0:T(8,128)(2,1)S(1)}, u32[]{:S(2)}, u32[]{:S(2)}) collective-permute-start(bf16[160,1556]{1,0:T(8,128)(2,1)} %collective-permute-done.9), channel_id=1, source_target_pairs={{8,0},{16,8},{24,16},{28,24},{20,28},{12,20},{4,12},{0,4},{9,1},{1... | collective-permute-start | bytes 1493768 | tf_op jit(solution)/shard_map/ppermute | solution.py:511
  64.3 12.3 %collective-permute-start.6 = (bf16[160,1556]{1,0:T(8,128)(2,1)S(1)}, bf16[160,1556]{1,0:T(8,128)(2,1)S(1)}, u32[]{:S(2)}, u32[]{:S(2)}) collective-permute-start(bf16[160,1556]{1,0:T(8,128)(2,1)S(1)} %collective-permute-done.5), channel_id=1, source_target_pairs={{0,8},{8,16},{16,24},{24,28},{28,20},{20,12},{12,4},{4,0},{1,9},{9... | collective-permute-start | bytes 1493768 | tf_op jit(solution)/shard_map/ppermute | solution.py:511
  65.9 12.3 %collective-permute-start.11 = (bf16[160,1556]{1,0:T(8,128)(2,1)S(1)}, bf16[160,1556]{1,0:T(8,128)(2,1)S(1)}, u32[]{:S(2)}, u32[]{:S(2)}) collective-permute-start(bf16[160,1556]{1,0:T(8,128)(2,1)S(1)} %collective-permute-done.10), channel_id=1, source_target_pairs={{8,0},{16,8},{24,16},{28,24},{20,28},{12,20},{4,12},{0,4},{9,1},{1... | collective-permute-start | bytes 1493768 | tf_op jit(solution)/shard_map/ppermute | solution.py:511
  76.6 12.9 %collective-permute-start.7 = (bf16[160,1556]{1,0:T(8,128)(2,1)S(1)}, bf16[160,1556]{1,0:T(8,128)(2,1)S(1)}, u32[]{:S(2)}, u32[]{:S(2)}) collective-permute-start(bf16[160,1556]{1,0:T(8,128)(2,1)S(1)} %collective-permute-done.6), channel_id=1, source_target_pairs={{0,8},{8,16},{16,24},{24,28},{28,20},{20,12},{12,4},{4,0},{1,9},{9... | collective-permute-start | bytes 1493768 | tf_op jit(solution)/shard_map/ppermute | solution.py:511
  78.1 12.9 %collective-permute-start.12 = (bf16[160,1556]{1,0:T(8,128)(2,1)S(1)}, bf16[160,1556]{1,0:T(8,128)(2,1)S(1)}, u32[]{:S(2)}, u32[]{:S(2)}) collective-permute-start(bf16[160,1556]{1,0:T(8,128)(2,1)S(1)} %collective-permute-done.11), channel_id=1, source_target_pairs={{8,0},{16,8},{24,16},{28,24},{20,28},{12,20},{4,12},{0,4},{9,1},{1... | collective-permute-start | bytes 1493768 | tf_op jit(solution)/shard_map/ppermute | solution.py:511
  89.4 12.0 %collective-permute-start.8 = (bf16[160,1556]{1,0:T(8,128)(2,1)S(1)}, bf16[160,1556]{1,0:T(8,128)(2,1)S(1)}, u32[]{:S(2)}, u32[]{:S(2)}) collective-permute-start(bf16[160,1556]{1,0:T(8,128)(2,1)S(1)} %collective-permute-done.7), channel_id=1, source_target_pairs={{0,8},{8,16},{16,24},{24,28},{28,20},{20,12},{12,4},{4,0},{1,9},{9... | collective-permute-start | bytes 1493768 | tf_op jit(solution)/shard_map/ppermute | solution.py:511
  91.0 12.3 %collective-permute-start.13 = (bf16[160,1556]{1,0:T(8,128)(2,1)S(1)}, bf16[160,1556]{1,0:T(8,128)(2,1)S(1)}, u32[]{:S(2)}, u32[]{:S(2)}) collective-permute-start(bf16[160,1556]{1,0:T(8,128)(2,1)S(1)} %collective-permute-done.12), channel_id=1, source_target_pairs={{8,0},{16,8},{24,16},{28,24},{20,28},{12,20},{4,12},{0,4},{9,1},{1... | collective-permute-start | bytes 1493768 | tf_op jit(solution)/shard_map/ppermute | solution.py:511
  103.4 12.3 %collective-permute-start.14 = (bf16[160,1280]{1,0:T(8,128)(2,1)S(1)}, bf16[160,1280]{1,0:T(8,128)(2,1)S(1)}, u32[]{:S(2)}, u32[]{:S(2)}) collective-permute-start(bf16[160,1280]{1,0:T(8,128)(2,1)S(1)} %get-tuple-element.358), channel_id=1, source_target_pairs={{0,8},{8,16},{16,24},{24,28},{28,20},{20,12},{12,4},{4,0},{1,9},{9... | collective-permute-start | bytes 1228808 | tf_op jit(solution)/shard_map/ppermute | solution.py:511
  106.1 11.6 %collective-permute-start.15 = (bf16[160,1280]{1,0:T(8,128)(2,1)S(1)}, bf16[160,1280]{1,0:T(8,128)(2,1)S(1)}, u32[]{:S(2)}, u32[]{:S(2)}) collective-permute-start(bf16[160,1280]{1,0:T(8,128)(2,1)S(1)} %get-tuple-element.357), channel_id=1, source_target_pairs={{8,0},{16,8},{24,16},{28,24},{20,28},{12,20},{4,12},{0,4},{9,1},{1... | collective-permute-start | bytes 1228808 | tf_op jit(solution)/shard_map/ppermute | solution.py:511
  117.7 28.3 %collective-permute-start.16 = (bf16[160,1280]{1,0:T(8,128)(2,1)S(1)}, bf16[160,1280]{1,0:T(8,128)(2,1)S(1)}, u32[]{:S(2)}, u32[]{:S(2)}) collective-permute-start(bf16[160,1280]{1,0:T(8,128)(2,1)S(1)} %collective-permute-done.14), channel_id=1, source_target_pairs={{0,8},{8,16},{16,24},{24,28},{28,20},{20,12},{12,4},{4,0},{1,9},{9... | collective-permute-start | bytes 1228808 | tf_op jit(solution)/shard_map/ppermute | solution.py:511
  118.2 27.8 %collective-permute-start.17 = (bf16[160,1280]{1,0:T(8,128)(2,1)S(1)}, bf16[160,1280]{1,0:T(8,128)(2,1)S(1)}, u32[]{:S(2)}, u32[]{:S(2)}) collective-permute-start(bf16[160,1280]{1,0:T(8,128)(2,1)S(1)} %collective-permute-done.15), channel_id=1, source_target_pairs={{8,0},{16,8},{24,16},{28,24},{20,28},{12,20},{4,12},{0,4},{9,1},{1... | collective-permute-start | bytes 1228808 | tf_op jit(solution)/shard_map/ppermute | solution.py:511
  146.0 13.8 %collective-permute-start.18 = (bf16[160,1280]{1,0:T(8,128)(2,1)S(1)}, bf16[160,1280]{1,0:T(8,128)(2,1)S(1)}, u32[]{:S(2)}, u32[]{:S(2)}) collective-permute-start(bf16[160,1280]{1,0:T(8,128)(2,1)S(1)} %collective-permute-done.16), channel_id=1, source_target_pairs={{0,8},{8,16},{16,24},{24,28},{28,20},{20,12},{12,4},{4,0},{1,9},{9... | collective-permute-start | bytes 1228808 | tf_op jit(solution)/shard_map/ppermute | solution.py:511
  146.6 13.3 %collective-permute-start.19 = (bf16[160,1280]{1,0:T(8,128)(2,1)S(1)}, bf16[160,1280]{1,0:T(8,128)(2,1)}, u32[]{:S(2)}, u32[]{:S(2)}) collective-permute-start(bf16[160,1280]{1,0:T(8,128)(2,1)S(1)} %collective-permute-done.17), channel_id=1, source_target_pairs={{8,0},{16,8},{24,16},{28,24},{20,28},{12,20},{4,12},{0,4},{9,1},{1... | collective-permute-start | bytes 1228808 | tf_op jit(solution)/shard_map/ppermute | solution.py:511
  159.8 23.1 %collective-permute-start.20 = (bf16[160,1280]{1,0:T(8,128)(2,1)S(1)}, bf16[160,1280]{1,0:T(8,128)(2,1)S(1)}, u32[]{:S(2)}, u32[]{:S(2)}) collective-permute-start(bf16[160,1280]{1,0:T(8,128)(2,1)S(1)} %collective-permute-done.18), channel_id=1, source_target_pairs={{0,8},{8,16},{16,24},{24,28},{28,20},{20,12},{12,4},{4,0},{1,9},{9... | collective-permute-start | bytes 1228808 | tf_op jit(solution)/shard_map/ppermute | solution.py:511
  160.3 22.6 %collective-permute-start.21 = (bf16[160,1280]{1,0:T(8,128)(2,1)}, bf16[160,1280]{1,0:T(8,128)(2,1)}, u32[]{:S(2)}, u32[]{:S(2)}) collective-permute-start(bf16[160,1280]{1,0:T(8,128)(2,1)} %collective-permute-done.19), channel_id=1, source_target_pairs={{8,0},{16,8},{24,16},{28,24},{20,28},{12,20},{4,12},{0,4},{9,1},{1... | collective-permute-start | bytes 1228808 | tf_op jit(solution)/shard_map/ppermute | solution.py:511
  182.9 12.1 %collective-permute-start.22 = (bf16[160,1280]{1,0:T(8,128)(2,1)S(1)}, bf16[160,1280]{1,0:T(8,128)(2,1)}, u32[]{:S(2)}, u32[]{:S(2)}) collective-permute-start(bf16[160,1280]{1,0:T(8,128)(2,1)S(1)} %collective-permute-done.20), channel_id=1, source_target_pairs={{0,8},{8,16},{16,24},{24,28},{28,20},{20,12},{12,4},{4,0},{1,9},{9... | collective-permute-start | bytes 1228808 | tf_op jit(solution)/shard_map/ppermute | solution.py:511
  183.5 11.8 %collective-permute-start.23 = (bf16[160,1280]{1,0:T(8,128)(2,1)}, bf16[160,1280]{1,0:T(8,128)(2,1)}, u32[]{:S(2)}, u32[]{:S(2)}) collective-permute-start(bf16[160,1280]{1,0:T(8,128)(2,1)} %collective-permute-done.21), channel_id=1, source_target_pairs={{8,0},{16,8},{24,16},{28,24},{20,28},{12,20},{4,12},{0,4},{9,1},{1... | collective-permute-start | bytes 1228808 | tf_op jit(solution)/shard_map/ppermute | solution.py:511
  185.0 328.7 %reduce-scatter.4.cloned.1.call-start = ((), (), s32[]{:S(2)}) async-start(), calls=%async_computation.4 | async-start | bytes 6553600 | tf_op jit(solution)/shard_map/reduce_scatter | solution.py:681
  249.3 11.7 %collective-permute-start.34 = (bf16[160,1280]{1,0:T(8,128)(2,1)S(1)}, bf16[160,1280]{1,0:T(8,128)(2,1)S(1)}, u32[]{:S(2)}, u32[]{:S(2)}) collective-permute-start(bf16[160,1280]{1,0:T(8,128)(2,1)S(1)} %collective-permute-done.32), channel_id=1, source_target_pairs={{0,8},{8,16},{16,24},{24,28},{28,20},{20,12},{12,4},{4,0},{1,9},{9... | collective-permute-start | bytes 1228808 | tf_op jit(solution)/shard_map/ppermute | solution.py:511
  249.3 13.6 %collective-permute-start.35 = (bf16[160,1280]{1,0:T(8,128)(2,1)S(1)}, bf16[160,1280]{1,0:T(8,128)(2,1)S(1)}, u32[]{:S(2)}, u32[]{:S(2)}) collective-permute-start(bf16[160,1280]{1,0:T(8,128)(2,1)S(1)} %collective-permute-done.33), channel_id=1, source_target_pairs={{8,0},{16,8},{24,16},{28,24},{20,28},{12,20},{4,12},{0,4},{9,1},{1... | collective-permute-start | bytes 1228808 | tf_op jit(solution)/shard_map/ppermute | solution.py:511
  320.4 14.1 %collective-permute-start.42 = (bf16[160,1280]{1,0:T(8,128)(2,1)S(1)}, bf16[160,1280]{1,0:T(8,128)(2,1)}, u32[]{:S(2)}, u32[]{:S(2)}) collective-permute-start(bf16[160,1280]{1,0:T(8,128)(2,1)S(1)} %get-tuple-element.173), channel_id=1, source_target_pairs={{0,8},{8,16},{16,24},{24,28},{28,20},{20,12},{12,4},{4,0},{1,9},{9... | collective-permute-start | bytes 1228808 | tf_op jit(solution)/shard_map/ppermute | solution.py:548
  321.3 13.2 %collective-permute-start.43 = (bf16[160,1280]{1,0:T(8,128)(2,1)S(1)}, bf16[160,1280]{1,0:T(8,128)(2,1)}, u32[]{:S(2)}, u32[]{:S(2)}) collective-permute-start(bf16[160,1280]{1,0:T(8,128)(2,1)S(1)} %get-tuple-element.174), channel_id=1, source_target_pairs={{8,0},{16,8},{24,16},{28,24},{20,28},{12,20},{4,12},{0,4},{9,1},{1... | collective-permute-start | bytes 1228808 | tf_op jit(solution)/shard_map/ppermute | solution.py:548
  334.5 279.4 %reduce-scatter.8.cloned.1.call-start = ((), (), s32[]{:S(2)}) async-start(), calls=%async_computation.6 | async-start | bytes 2211840 | tf_op jit(solution)/shard_map/reduce_scatter | solution.py:576
  336.1 16.6 %collective-permute-start.44 = (bf16[160,1280]{1,0:T(8,128)(2,1)S(1)}, bf16[160,1280]{1,0:T(8,128)(2,1)S(1)}, u32[]{:S(2)}, u32[]{:S(2)}) collective-permute-start(bf16[160,1280]{1,0:T(8,128)(2,1)S(1)} %get-tuple-element.176), channel_id=1, source_target_pairs={{0,8},{8,16},{16,24},{24,28},{28,20},{20,12},{12,4},{4,0},{1,9},{9... | collective-permute-start | bytes 1228808 | tf_op jit(solution)/shard_map/ppermute | solution.py:548
  337.1 15.7 %collective-permute-start.45 = (bf16[160,1280]{1,0:T(8,128)(2,1)S(1)}, bf16[160,1280]{1,0:T(8,128)(2,1)S(1)}, u32[]{:S(2)}, u32[]{:S(2)}) collective-permute-start(bf16[160,1280]{1,0:T(8,128)(2,1)S(1)} %get-tuple-element.177), channel_id=1, source_target_pairs={{8,0},{16,8},{24,16},{28,24},{20,28},{12,20},{4,12},{0,4},{9,1},{1... | collective-permute-start | bytes 1228808 | tf_op jit(solution)/shard_map/ppermute | solution.py:548
  367.1 12.5 %collective-permute-start.50 = (bf16[160,1280]{1,0:T(8,128)(2,1)S(1)}, bf16[160,1280]{1,0:T(8,128)(2,1)S(1)}, u32[]{:S(2)}, u32[]{:S(2)}) collective-permute-start(bf16[160,1280]{1,0:T(8,128)(2,1)S(1)} %get-tuple-element.184), channel_id=1, source_target_pairs={{0,8},{8,16},{16,24},{24,28},{28,20},{20,12},{12,4},{4,0},{1,9},{9... | collective-permute-start | bytes 1228808 | tf_op jit(solution)/shard_map/ppermute | solution.py:548
  368.8 12.4 %collective-permute-start.51 = (bf16[160,1280]{1,0:T(8,128)(2,1)S(1)}, bf16[160,1280]{1,0:T(8,128)(2,1)S(1)}, u32[]{:S(2)}, u32[]{:S(2)}) collective-permute-start(bf16[160,1280]{1,0:T(8,128)(2,1)S(1)} %get-tuple-element.185), channel_id=1, source_target_pairs={{8,0},{16,8},{24,16},{28,24},{20,28},{12,20},{4,12},{0,4},{9,1},{1... | collective-permute-start | bytes 1228808 | tf_op jit(solution)/shard_map/ppermute | solution.py:548
  369.2 15.7 %collective-permute-start.48 = (bf16[160,1280]{1,0:T(8,128)(2,1)S(1)}, bf16[160,1280]{1,0:T(8,128)(2,1)S(1)}, u32[]{:S(2)}, u32[]{:S(2)}) collective-permute-start(bf16[160,1280]{1,0:T(8,128)(2,1)S(1)} %get-tuple-element.182), channel_id=1, source_target_pairs={{0,8},{8,16},{16,24},{24,28},{28,20},{20,12},{12,4},{4,0},{1,9},{9... | collective-permute-start | bytes 1228808 | tf_op jit(solution)/shard_map/ppermute | solution.py:548
  370.8 15.1 %collective-permute-start.49 = (bf16[160,1280]{1,0:T(8,128)(2,1)S(1)}, bf16[160,1280]{1,0:T(8,128)(2,1)S(1)}, u32[]{:S(2)}, u32[]{:S(2)}) collective-permute-start(bf16[160,1280]{1,0:T(8,128)(2,1)S(1)} %get-tuple-element.183), channel_id=1, source_target_pairs={{8,0},{16,8},{24,16},{28,24},{20,28},{12,20},{4,12},{0,4},{9,1},{1... | collective-permute-start | bytes 1228808 | tf_op jit(solution)/shard_map/ppermute | solution.py:548
  387.2 21.3 %collective-permute-start.54 = (bf16[160,1280]{1,0:T(8,128)(2,1)S(1)}, bf16[160,1280]{1,0:T(8,128)(2,1)S(1)}, u32[]{:S(2)}, u32[]{:S(2)}) collective-permute-start(bf16[160,1280]{1,0:T(8,128)(2,1)S(1)} %get-tuple-element.189), channel_id=1, source_target_pairs={{0,8},{8,16},{16,24},{24,28},{28,20},{20,12},{12,4},{4,0},{1,9},{9... | collective-permute-start | bytes 1228808 | tf_op jit(solution)/shard_map/ppermute | solution.py:548
  388.1 20.4 %collective-permute-start.55 = (bf16[160,1280]{1,0:T(8,128)(2,1)S(1)}, bf16[160,1280]{1,0:T(8,128)(2,1)S(1)}, u32[]{:S(2)}, u32[]{:S(2)}) collective-permute-start(bf16[160,1280]{1,0:T(8,128)(2,1)S(1)} %get-tuple-element.190), channel_id=1, source_target_pairs={{8,0},{16,8},{24,16},{28,24},{20,28},{12,20},{4,12},{0,4},{9,1},{1... | collective-permute-start | bytes 1228808 | tf_op jit(solution)/shard_map/ppermute | solution.py:548
  417.4 33.5 %collective-permute-start.58 = (bf16[160,1280]{1,0:T(8,128)(2,1)S(1)}, bf16[160,1280]{1,0:T(8,128)(2,1)S(1)}, u32[]{:S(2)}, u32[]{:S(2)}) collective-permute-start(bf16[160,1280]{1,0:T(8,128)(2,1)S(1)} %get-tuple-element.213), channel_id=1, source_target_pairs={{0,8},{8,16},{16,24},{24,28},{28,20},{20,12},{12,4},{4,0},{1,9},{9... | collective-permute-start | bytes 1228808 | tf_op jit(solution)/shard_map/ppermute | solution.py:548
  418.6 32.4 %collective-permute-start.59 = (bf16[160,1280]{1,0:T(8,128)(2,1)S(1)}, bf16[160,1280]{1,0:T(8,128)(2,1)S(1)}, u32[]{:S(2)}, u32[]{:S(2)}) collective-permute-start(bf16[160,1280]{1,0:T(8,128)(2,1)S(1)} %get-tuple-element.214), channel_id=1, source_target_pairs={{8,0},{16,8},{24,16},{28,24},{20,28},{12,20},{4,12},{0,4},{9,1},{1... | collective-permute-start | bytes 1228808 | tf_op jit(solution)/shard_map/ppermute | solution.py:548
  434.3 18.0 %collective-permute-start.56 = (bf16[160,1280]{1,0:T(8,128)(2,1)S(1)}, bf16[160,1280]{1,0:T(8,128)(2,1)}, u32[]{:S(2)}, u32[]{:S(2)}) collective-permute-start(bf16[160,1280]{1,0:T(8,128)(2,1)S(1)} %get-tuple-element.211), channel_id=1, source_target_pairs={{0,8},{8,16},{16,24},{24,28},{28,20},{20,12},{12,4},{4,0},{1,9},{9... | collective-permute-start | bytes 1228808 | tf_op jit(solution)/shard_map/ppermute | solution.py:548
  435.4 16.9 %collective-permute-start.57 = (bf16[160,1280]{1,0:T(8,128)(2,1)S(1)}, bf16[160,1280]{1,0:T(8,128)(2,1)}, u32[]{:S(2)}, u32[]{:S(2)}) collective-permute-start(bf16[160,1280]{1,0:T(8,128)(2,1)S(1)} %get-tuple-element.212), channel_id=1, source_target_pairs={{8,0},{16,8},{24,16},{28,24},{20,28},{12,20},{4,12},{0,4},{9,1},{1... | collective-permute-start | bytes 1228808 | tf_op jit(solution)/shard_map/ppermute | solution.py:548
  453.9 17.0 %collective-permute-start.62 = (bf16[160,1280]{1,0:T(8,128)(2,1)S(1)}, bf16[160,1280]{1,0:T(8,128)(2,1)S(1)}, u32[]{:S(2)}, u32[]{:S(2)}) collective-permute-start(bf16[160,1280]{1,0:T(8,128)(2,1)S(1)} %get-tuple-element.217), channel_id=1, source_target_pairs={{0,8},{8,16},{16,24},{24,28},{28,20},{20,12},{12,4},{4,0},{1,9},{9... | collective-permute-start | bytes 1228808 | tf_op jit(solution)/shard_map/ppermute | solution.py:548
  455.1 15.8 %collective-permute-start.63 = (bf16[160,1280]{1,0:T(8,128)(2,1)S(1)}, bf16[160,1280]{1,0:T(8,128)(2,1)S(1)}, u32[]{:S(2)}, u32[]{:S(2)}) collective-permute-start(bf16[160,1280]{1,0:T(8,128)(2,1)S(1)} %get-tuple-element.218), channel_id=1, source_target_pairs={{8,0},{16,8},{24,16},{28,24},{20,28},{12,20},{4,12},{0,4},{9,1},{1... | collective-permute-start | bytes 1228808 | tf_op jit(solution)/shard_map/ppermute | solution.py:548
  456.0 17.1 %collective-permute-start.60 = (bf16[160,1280]{1,0:T(8,128)(2,1)S(1)}, bf16[160,1280]{1,0:T(8,128)(2,1)S(1)}, u32[]{:S(2)}, u32[]{:S(2)}) collective-permute-start(bf16[160,1280]{1,0:T(8,128)(2,1)S(1)} %get-tuple-element.215), channel_id=1, source_target_pairs={{0,8},{8,16},{16,24},{24,28},{28,20},{20,12},{12,4},{4,0},{1,9},{9... | collective-permute-start | bytes 1228808 | tf_op jit(solution)/shard_map/ppermute | solution.py:548
  457.1 16.0 %collective-permute-start.61 = (bf16[160,1280]{1,0:T(8,128)(2,1)S(1)}, bf16[160,1280]{1,0:T(8,128)(2,1)S(1)}, u32[]{:S(2)}, u32[]{:S(2)}) collective-permute-start(bf16[160,1280]{1,0:T(8,128)(2,1)S(1)} %get-tuple-element.216), channel_id=1, source_target_pairs={{8,0},{16,8},{24,16},{28,24},{20,28},{12,20},{4,12},{0,4},{9,1},{1... | collective-permute-start | bytes 1228808 | tf_op jit(solution)/shard_map/ppermute | solution.py:548
  475.5 35.7 %collective-permute-start.64 = (bf16[160,1280]{1,0:T(8,128)(2,1)}, bf16[160,1280]{1,0:T(8,128)(2,1)}, u32[]{:S(2)}, u32[]{:S(2)}) collective-permute-start(bf16[160,1280]{1,0:T(8,128)(2,1)} %get-tuple-element.229), channel_id=1, source_target_pairs={{0,8},{8,16},{16,24},{24,28},{28,20},{20,12},{12,4},{4,0},{1,9},{9... | collective-permute-start | bytes 1228808 | tf_op jit(solution)/shard_map/ppermute | solution.py:548
  476.7 34.5 %collective-permute-start.65 = (bf16[160,1280]{1,0:T(8,128)(2,1)}, bf16[160,1280]{1,0:T(8,128)(2,1)}, u32[]{:S(2)}, u32[]{:S(2)}) collective-permute-start(bf16[160,1280]{1,0:T(8,128)(2,1)} %get-tuple-element.230), channel_id=1, source_target_pairs={{8,0},{16,8},{24,16},{28,24},{20,28},{12,20},{4,12},{0,4},{9,1},{1... | collective-permute-start | bytes 1228808 | tf_op jit(solution)/shard_map/ppermute | solution.py:548
  477.6 19.5 %collective-permute-start.66 = (bf16[160,1280]{1,0:T(8,128)(2,1)}, bf16[160,1280]{1,0:T(8,128)(2,1)}, u32[]{:S(2)}, u32[]{:S(2)}) collective-permute-start(bf16[160,1280]{1,0:T(8,128)(2,1)} %get-tuple-element.233), channel_id=1, source_target_pairs={{0,8},{8,16},{16,24},{24,28},{28,20},{20,12},{12,4},{4,0},{1,9},{9... | collective-permute-start | bytes 1228808 | tf_op jit(solution)/shard_map/ppermute | solution.py:548
  478.7 18.4 %collective-permute-start.67 = (bf16[160,1280]{1,0:T(8,128)(2,1)S(1)}, bf16[160,1280]{1,0:T(8,128)(2,1)}, u32[]{:S(2)}, u32[]{:S(2)}) collective-permute-start(bf16[160,1280]{1,0:T(8,128)(2,1)S(1)} %get-tuple-element.234), channel_id=1, source_target_pairs={{8,0},{16,8},{24,16},{28,24},{20,28},{12,20},{4,12},{0,4},{9,1},{1... | collective-permute-start | bytes 1228808 | tf_op jit(solution)/shard_map/ppermute | solution.py:548
  493.6 139.5 %reduce-scatter.6.cloned.1.call-start = ((), (), s32[]{:S(2)}) async-start(), calls=%async_computation.5 | async-start | bytes 6553600 | tf_op jit(solution)/shard_map/reduce_scatter | solution.py:737
  529.9 13.5 %collective-permute-start.75 = (bf16[160,1280]{1,0:T(8,128)(2,1)}, bf16[160,1280]{1,0:T(8,128)(2,1)S(1)}, u32[]{:S(2)}, u32[]{:S(2)}) collective-permute-start(bf16[160,1280]{1,0:T(8,128)(2,1)} %get-tuple-element.239), channel_id=1, source_target_pairs={{0,8},{8,16},{16,24},{24,28},{28,20},{20,12},{12,4},{4,0},{1,9},{9... | collective-permute-start | bytes 1228808 | tf_op jit(solution)/shard_map/ppermute | solution.py:548
  532.0 13.3 %collective-permute-start.87 = (f32[9020]{0:T(1024)S(1)}, f32[9020]{0:T(1024)S(1)}, u32[]{:S(2)}, u32[]{:S(2)}) collective-permute-start(f32[9020]{0:T(1024)S(1)} %concatenate.50), channel_id=1, source_target_pairs={{0,4},{4,0},{8,12},{12,8},{16,20},{20,16},{24,28},{28,24},{1,5},{5... | collective-permute-start | bytes 108248 | tf_op jit(solution)/shard_map/ppermute | solution.py:570
  532.8 33.1 %collective-permute-start.81 = (bf16[160,1280]{1,0:T(8,128)(2,1)}, bf16[160,1280]{1,0:T(8,128)(2,1)}, u32[]{:S(2)}, u32[]{:S(2)}) collective-permute-start(bf16[160,1280]{1,0:T(8,128)(2,1)} %get-tuple-element.240), channel_id=1, source_target_pairs={{8,0},{16,8},{24,16},{28,24},{20,28},{12,20},{4,12},{0,4},{9,1},{1... | collective-permute-start | bytes 1228808 | tf_op jit(solution)/shard_map/ppermute | solution.py:548
  545.3 20.6 %collective-permute-start.76 = (bf16[160,1280]{1,0:T(8,128)(2,1)}, bf16[160,1280]{1,0:T(8,128)(2,1)}, u32[]{:S(2)}, u32[]{:S(2)}) collective-permute-start(bf16[160,1280]{1,0:T(8,128)(2,1)} %add_convert_fusion.10), channel_id=1, source_target_pairs={{0,8},{8,16},{16,24},{24,28},{28,20},{20,12},{12,4},{4,0},{1,9},{9... | collective-permute-start | bytes 1228808 | tf_op jit(solution)/shard_map/ppermute | solution.py:548
  545.3 14.0 %collective-permute-start.88 = (f32[9020]{0:T(1024)S(1)}, f32[9020]{0:T(1024)S(1)}, u32[]{:S(2)}, u32[]{:S(2)}) collective-permute-start(f32[9020]{0:T(1024)S(1)} %add.927), channel_id=1, source_target_pairs={{0,8},{4,12},{8,0},{12,4},{16,24},{20,28},{24,16},{28,20},{1,9},{5... | collective-permute-start | bytes 108248 | tf_op jit(solution)/shard_map/ppermute | solution.py:570
  567.5 12.5 %collective-permute-start.77 = (bf16[160,1280]{1,0:T(8,128)(2,1)S(1)}, bf16[160,1280]{1,0:T(8,128)(2,1)S(1)}, u32[]{:S(2)}, u32[]{:S(2)}) collective-permute-start(bf16[160,1280]{1,0:T(8,128)(2,1)S(1)} %get-tuple-element.313), channel_id=1, source_target_pairs={{0,8},{8,16},{16,24},{24,28},{28,20},{20,12},{12,4},{4,0},{1,9},{9... | collective-permute-start | bytes 1228808 | tf_op jit(solution)/shard_map/ppermute | solution.py:548
  570.6 18.2 %collective-permute-start.71 = (bf16[160,1280]{1,0:T(8,128)(2,1)}, bf16[160,1280]{1,0:T(8,128)(2,1)S(1)}, u32[]{:S(2)}, u32[]{:S(2)}) collective-permute-start(bf16[160,1280]{1,0:T(8,128)(2,1)} %get-tuple-element.237), channel_id=1, source_target_pairs={{0,8},{8,16},{16,24},{24,28},{28,20},{20,12},{12,4},{4,0},{1,9},{9... | collective-permute-start | bytes 1228808 | tf_op jit(solution)/shard_map/ppermute | solution.py:548
  572.7 27.0 %collective-permute-start.73 = (bf16[160,1280]{1,0:T(8,128)(2,1)}, bf16[160,1280]{1,0:T(8,128)(2,1)S(1)}, u32[]{:S(2)}, u32[]{:S(2)}) collective-permute-start(bf16[160,1280]{1,0:T(8,128)(2,1)} %get-tuple-element.238), channel_id=1, source_target_pairs={{8,0},{16,8},{24,16},{28,24},{20,28},{12,20},{4,12},{0,4},{9,1},{1... | collective-permute-start | bytes 1228808 | tf_op jit(solution)/shard_map/ppermute | solution.py:548
  581.3 13.8 %collective-permute-start.78 = (bf16[160,1280]{1,0:T(8,128)(2,1)S(1)}, bf16[160,1280]{1,0:T(8,128)(2,1)S(1)}, u32[]{:S(2)}, u32[]{:S(2)}) collective-permute-start(bf16[160,1280]{1,0:T(8,128)(2,1)S(1)} %get-tuple-element.311), channel_id=1, source_target_pairs={{0,8},{8,16},{16,24},{24,28},{28,20},{20,12},{12,4},{4,0},{1,9},{9... | collective-permute-start | bytes 1228808 | tf_op jit(solution)/shard_map/ppermute | solution.py:548
  583.8 12.4 %collective-permute-start.83 = (bf16[160,1280]{1,0:T(8,128)(2,1)S(1)}, bf16[160,1280]{1,0:T(8,128)(2,1)S(1)}, u32[]{:S(2)}, u32[]{:S(2)}) collective-permute-start(bf16[160,1280]{1,0:T(8,128)(2,1)S(1)} %get-tuple-element.312), channel_id=1, source_target_pairs={{8,0},{16,8},{24,16},{28,24},{20,28},{12,20},{4,12},{0,4},{9,1},{1... | collective-permute-start | bytes 1228808 | tf_op jit(solution)/shard_map/ppermute | solution.py:548
  627.5 11.5 %collective-permute-start.91 = (f32[325,256]{1,0:T(8,128)}, f32[325,256]{1,0:T(8,128)}, u32[]{:S(2)}, u32[]{:S(2)}) collective-permute-start(f32[325,256]{1,0:T(8,128)} %fusion.29), channel_id=1, source_target_pairs={{0,2},{1,3},{2,0},{3,1},{4,6},{5,7},{6,4},{7,5},{8,10},{9,11},{10,... | collective-permute-start | bytes 998408 | tf_op jit(solution)/shard_map/ppermute | solution.py:570
  649.0 12.8 %collective-permute-start.70 = (f32[640]{0:T(1024)S(1)}, f32[640]{0:T(1024)S(1)}, u32[]{:S(2)}, u32[]{:S(2)}) collective-permute-start(f32[640]{0:T(1024)S(1)} %add.909), channel_id=1, source_target_pairs={{0,16},{4,20},{8,24},{12,28},{16,0},{20,4},{24,8},{28,12},{1,17},{... | collective-permute-start | bytes 7688 | tf_op jit(solution)/shard_map/ppermute | solution.py:570
  (76 other events, 1148.6 us)
Sparse Core Ops, SparseCore 0:
  185.2 37.6 all-gather.1
  334.6 50.3 reduce-scatter.3
  493.7 70.8 reduce-scatter.7
  567.1 50.6 reduce-scatter.5
